TPU v7x, 128 devices: a whole 4x4x4 slice. The times are simulated.
128 devices in a mesh: expert: 32 (over y, z, core), fsdp: 4 (over x).
Axes of the slice: x: 4, y: 4, z: 4, core: 2. Of those that a mesh axis runs over, the one named last changes fastest.
Arguments:
- tokens: bfloat16 [25216, 768], P(('expert', 'fsdp')), may hold values from -6 to 6
- qkv_weight: bfloat16 [2, 3, 768, 768], P(None, None, 'fsdp'), may hold values from -0.21875 to 0.21875
- out_weight: bfloat16 [2, 768, 768], P(None, 'fsdp'), may hold values from -1.75 to 1.75
- norm_gain: bfloat16 [2, 2, 768], P(None, None, 'fsdp'), may hold values from 0.5 to 1.5
- mixer_bias: bfloat16 [2, 5, 768], P(None, None, 'fsdp'), may hold values from -1.25 to 1.25
- router_weight: bfloat16 [2, 768, 32], P(None, 'fsdp'), may hold values from -0.21875 to 0.21875
- router_bias: bfloat16 [2, 32], P(None, 'fsdp'), may hold values from -0.625 to 0.625
- expert_in: bfloat16 [2, 32, 768, 3072], P(None, 'expert', None, 'fsdp'), may hold values from -0.21875 to 0.21875
- expert_in_bias: bfloat16 [2, 32, 3072], P(None, 'expert', 'fsdp'), may hold values from -0.625 to 0.625
- expert_out: bfloat16 [2, 32, 3072, 768], P(None, 'expert', 'fsdp'), may hold values from -1.75 to 1.75
- expert_out_bias: bfloat16 [2, 32, 768], P(None, 'expert'), may hold values from -6 to 6
- routes: int32 [2, 25216, 2], P(None, ('expert', 'fsdp')), may hold values from 0 to 31, all different within a row; in each aligned block of 197 rows (0 to 196, 197 to 393, ..., all dimensions but the last counted through in order) at most 19 rows name the same one
- cotangent: bfloat16 [25216, 768], P(('expert', 'fsdp')), may hold values from -6 to 6
Outputs:
- activations: bfloat16 [25216, 768], P(('expert', 'fsdp'))
- tokens_grad: float32 [25216, 768], P(('expert', 'fsdp'))
- qkv_weight_grad: float32 [2, 3, 768, 768], P(None, None, 'fsdp')
- out_weight_grad: float32 [2, 768, 768], P(None, 'fsdp')
- norm_gain_grad: float32 [2, 2, 768], P(None, None, 'fsdp')
- mixer_bias_grad: float32 [2, 5, 768], P(None, None, 'fsdp')
- router_weight_grad: float32 [2, 768, 32], P(None, 'fsdp')
- router_bias_grad: float32 [2, 32], P(None, 'fsdp')
- expert_in_grad: float32 [2, 32, 768, 3072], P(None, 'expert', None, 'fsdp')
- expert_in_bias_grad: float32 [2, 32, 3072], P(None, 'expert', 'fsdp')
- expert_out_grad: float32 [2, 32, 3072, 768], P(None, 'expert', 'fsdp')
- expert_out_bias_grad: float32 [2, 32, 768], P(None, 'expert')
Inputs may be any that keep to these rules, and one draw needn't show every extreme that they name: `routes`: the two experts of a token differ. Among the 197 tokens of one block in one layer at most 19 name one expert, and some block and expert reach 19 in every draw.
All inputs are finite; a program needn't handle non-finite values.
Results may differ from a plain program's by a relative error of at most 0.033.
Values may be sent and summed in bfloat16 or wider, within the bound.
No kernel may reach another device: no remote copies, remote signals or barrier semaphores. Data moves between devices by JAX's collectives and lax.ppermute only.
A program may use at most 256 MiB of HBM per device.

v0:
```python
from functools import partial

import jax
import jax.numpy as jnp
from jax import lax
from jax.sharding import PartitionSpec as P

HEADS = 12
IMG_LEN = 197
LAYERS = 2


epsilon = 1e-06


def contract(left, right, left_dim, right_dim):
    return lax.dot_general(
        left, right, (((left_dim,), (right_dim,)), ((), ())), preferred_element_type=jnp.float32
    )


def layer_norm(values, gain, shift):
    centred = values - jnp.mean(values, axis=-1, keepdims=True)
    inverse = lax.rsqrt(jnp.mean(centred * centred, axis=-1, keepdims=True) + epsilon)
    scaled = centred * inverse
    return (scaled * gain + shift, scaled, inverse)


def norm_backward(grad_out, scaled, inverse, gain):
    grad_scaled = grad_out * gain
    mean_grad = jnp.mean(grad_scaled, axis=-1, keepdims=True)
    mean_cross = jnp.mean(grad_scaled * scaled, axis=-1, keepdims=True)
    grad_input = inverse * (grad_scaled - mean_grad - scaled * mean_cross)
    return (grad_input, jnp.sum(grad_out * scaled, axis=0), jnp.sum(grad_out, axis=0))


def slot_targets(routes_layer, experts, capacity):
    flat_routes = routes_layer.reshape(-1)
    onehot = (flat_routes[:, None] == jnp.arange(experts, dtype=jnp.int32)[None, :]).astype(
        jnp.int32
    )
    earlier = jnp.cumsum(onehot, axis=0) - onehot
    return flat_routes * capacity + jnp.sum(earlier * onehot, axis=1)


def attention_forward(normed, qkv_full, shifts, image_shape):
    token_count, model_width = normed.shape
    projected = jnp.einsum("td,kde->kte", normed, qkv_full, preferred_element_type=jnp.float32)
    query = (projected[0] + shifts[1]).astype(jnp.bfloat16)
    keyset = projected[1].astype(jnp.bfloat16)
    values = (projected[2] + shifts[2]).astype(jnp.bfloat16)
    scale = image_shape[-1] ** (-0.5)
    scores = (
        jnp.einsum(
            "bqhd,bkhd->bhqk",
            query.reshape(image_shape),
            keyset.reshape(image_shape),
            preferred_element_type=jnp.float32,
        )
        * scale
    )
    row_max = jnp.max(scores, axis=-1, keepdims=True)
    exponent = jnp.exp(scores - row_max)
    row_total = jnp.sum(exponent, axis=-1, keepdims=True)
    weights = (exponent / row_total).astype(jnp.bfloat16)
    log_total = row_max + jnp.log(row_total)
    mixed = jnp.einsum(
        "bhqk,bkhd->bqhd", weights, values.reshape(image_shape), preferred_element_type=jnp.float32
    )
    return (
        query,
        keyset,
        values,
        mixed.reshape(token_count, model_width).astype(jnp.bfloat16),
        log_total,
    )


def attention_backward(grad_mixed, query, keyset, values, log_total, image_shape):
    token_count, model_width = grad_mixed.shape
    scale = image_shape[-1] ** (-0.5)
    query_heads = query.reshape(image_shape)
    key_heads = keyset.reshape(image_shape)
    value_heads = values.reshape(image_shape)
    grad_heads = grad_mixed.reshape(image_shape)
    scores = (
        jnp.einsum("bqhd,bkhd->bhqk", query_heads, key_heads, preferred_element_type=jnp.float32)
        * scale
    )
    weights = jnp.exp(scores - log_total)
    grad_values = jnp.einsum(
        "bhqk,bqhd->bkhd",
        weights.astype(jnp.bfloat16),
        grad_heads,
        preferred_element_type=jnp.float32,
    )
    grad_weights = jnp.einsum(
        "bqhd,bkhd->bhqk", grad_heads, value_heads, preferred_element_type=jnp.float32
    )
    grad_scores = (
        weights * (grad_weights - jnp.sum(grad_weights * weights, axis=-1, keepdims=True))
    ).astype(jnp.bfloat16)
    grad_query = (
        jnp.einsum("bhqk,bkhd->bqhd", grad_scores, key_heads, preferred_element_type=jnp.float32)
        * scale
    )
    grad_keys = (
        jnp.einsum("bhqk,bqhd->bkhd", grad_scores, query_heads, preferred_element_type=jnp.float32)
        * scale
    )
    stacked = jnp.stack([grad_query, grad_keys, grad_values]).reshape(3, token_count, model_width)
    return stacked.astype(jnp.bfloat16)


def layer_forward(hidden_state, layer_params, expert_params, routes_layer, capacity, image_shape):
    token_count, model_width = hidden_state.shape
    qkv_full, out_full, gain_full, bias_full, router_full, router_bias_full = (
        lax.all_gather(layer_params[0], "fsdp", axis=1, tiled=True),
        lax.all_gather(layer_params[1], "fsdp", axis=0, tiled=True),
        lax.all_gather(layer_params[2], "fsdp", axis=1, tiled=True),
        lax.all_gather(layer_params[3], "fsdp", axis=1, tiled=True),
        lax.all_gather(layer_params[4], "fsdp", axis=0, tiled=True),
        lax.all_gather(layer_params[5], "fsdp", axis=0, tiled=True),
    )
    gain_rows = gain_full.astype(jnp.float32)
    shifts = bias_full.astype(jnp.float32)
    normed_first, scaled_first, inverse_first = layer_norm(hidden_state, gain_rows[0], shifts[0])
    normed_first = normed_first.astype(jnp.bfloat16)
    query, keyset, values, mixed, log_total = attention_forward(
        normed_first, qkv_full, shifts, image_shape
    )
    hidden_state = (
        hidden_state + jnp.dot(mixed, out_full, preferred_element_type=jnp.float32) + shifts[3]
    )
    normed_second, scaled_second, inverse_second = layer_norm(hidden_state, gain_rows[1], shifts[4])
    normed_second = normed_second.astype(jnp.bfloat16)
    logits = jnp.dot(
        normed_second, router_full, preferred_element_type=jnp.float32
    ) + router_bias_full.astype(jnp.float32)
    router_probs = jax.nn.softmax(logits, axis=-1)
    experts = router_probs.shape[1]
    onehot_routes = (
        routes_layer[:, :, None] == jnp.arange(experts, dtype=jnp.int32)[None, None, :]
    ).astype(jnp.float32)
    gates = jnp.sum(onehot_routes * router_probs[:, None, :], axis=2)
    targets = slot_targets(routes_layer, experts, capacity)
    send_rows = (
        jnp.zeros((experts * capacity, model_width), jnp.bfloat16)
        .at[targets]
        .set(jnp.repeat(normed_second, 2, axis=0))
    )
    received = lax.all_to_all(
        send_rows.reshape(experts, capacity, model_width),
        "expert",
        split_axis=0,
        concat_axis=0,
        tiled=True,
    )
    own_rows = received.reshape(-1, model_width)
    weight_in, bias_in, weight_out, bias_out = expert_params
    group_rows = lax.all_gather(own_rows, "fsdp", axis=0, tiled=True)
    pre_active = jnp.dot(
        group_rows, weight_in, preferred_element_type=jnp.float32
    ) + bias_in.astype(jnp.float32)
    active = jax.nn.gelu(pre_active, approximate=False).astype(jnp.bfloat16)
    expert_sum = lax.psum_scatter(
        jnp.dot(active, weight_out, preferred_element_type=jnp.float32).astype(jnp.bfloat16),
        "fsdp",
        scatter_dimension=0,
        tiled=True,
    ).astype(jnp.float32)
    expert_weights = (weight_in, weight_out)
    expert_result = (expert_sum + bias_out.astype(jnp.float32)).astype(jnp.bfloat16)
    returned = lax.all_to_all(
        expert_result.reshape(-1, capacity, model_width),
        "expert",
        split_axis=0,
        concat_axis=0,
        tiled=True,
    )
    picked = (
        returned.reshape(experts * capacity, model_width)[targets]
        .reshape(token_count, 2, model_width)
        .astype(jnp.float32)
    )
    hidden_state = hidden_state + jnp.sum(gates[:, :, None] * picked, axis=1)
    kept_values = (
        qkv_full,
        out_full,
        gain_rows,
        router_full,
        normed_first,
        scaled_first,
        inverse_first,
        query,
        keyset,
        values,
        mixed,
        log_total,
        normed_second,
        scaled_second,
        inverse_second,
        router_probs,
        onehot_routes,
        gates,
        targets,
        group_rows,
        pre_active,
        active,
        picked,
        expert_weights,
    )
    return (hidden_state, kept_values)


def layer_backward(grad_state, kept_values, capacity, image_shape):
    (
        qkv_full,
        out_full,
        gain_rows,
        router_full,
        normed_first,
        scaled_first,
        inverse_first,
        query,
        keyset,
        values,
        mixed,
        log_total,
        normed_second,
        scaled_second,
        inverse_second,
        router_probs,
        onehot_routes,
        gates,
        targets,
        group_rows,
        pre_active,
        active,
        picked,
        expert_weights,
    ) = kept_values
    token_count, model_width = grad_state.shape
    experts = router_probs.shape[1]
    grad_picked = (gates[:, :, None] * grad_state[:, None, :]).astype(jnp.bfloat16)
    grad_gates = jnp.sum(grad_state[:, None, :] * picked, axis=2)
    grad_send = (
        jnp.zeros((experts * capacity, model_width), jnp.bfloat16)
        .at[targets]
        .set(grad_picked.reshape(-1, model_width))
    )
    grad_received = lax.all_to_all(
        grad_send.reshape(experts, capacity, model_width),
        "expert",
        split_axis=0,
        concat_axis=0,
        tiled=True,
    )
    grad_own = grad_received.reshape(-1, model_width)
    gelu_fn = partial(jax.nn.gelu, approximate=False)
    weight_in, weight_out = expert_weights
    grad_group = lax.all_gather(grad_own, "fsdp", axis=0, tiled=True)
    grad_active = contract(grad_group, weight_out, 1, 1)
    unused, gelu_back = jax.vjp(gelu_fn, pre_active)
    grad_pre = gelu_back(grad_active)[0].astype(jnp.bfloat16)
    out_grad = contract(active, grad_group, 0, 0)
    in_grad = contract(group_rows, grad_pre, 0, 0)
    in_bias_grad = jnp.sum(grad_pre.astype(jnp.float32), axis=0)
    out_bias_grad = jnp.sum(grad_group.astype(jnp.float32), axis=0)
    grad_rows_sum = lax.psum_scatter(
        contract(grad_pre, weight_in, 1, 1).astype(jnp.bfloat16),
        "fsdp",
        scatter_dimension=0,
        tiled=True,
    )
    grad_back = lax.all_to_all(
        grad_rows_sum.reshape(-1, capacity, model_width),
        "expert",
        split_axis=0,
        concat_axis=0,
        tiled=True,
    )
    grad_entries = grad_back.reshape(experts * capacity, model_width)[targets].astype(jnp.float32)
    grad_normed = jnp.sum(grad_entries.reshape(token_count, 2, model_width), axis=1)
    grad_probs = jnp.sum(onehot_routes * grad_gates[:, :, None], axis=1)
    grad_logits = router_probs * (
        grad_probs - jnp.sum(grad_probs * router_probs, axis=-1, keepdims=True)
    )
    grad_logits = grad_logits.astype(jnp.bfloat16)
    router_grad = contract(normed_second, grad_logits, 0, 0)
    router_bias_grad = jnp.sum(grad_logits.astype(jnp.float32), axis=0)
    grad_normed = grad_normed + contract(grad_logits, router_full, 1, 1)
    grad_middle, gain_second, shift_second = norm_backward(
        grad_normed, scaled_second, inverse_second, gain_rows[1]
    )
    grad_middle = grad_middle + grad_state
    grad_branch = grad_middle.astype(jnp.bfloat16)
    out_weight_grad = contract(mixed, grad_branch, 0, 0)
    out_shift_grad = jnp.sum(grad_middle, axis=0)
    grad_mixed = contract(grad_branch, out_full, 1, 1).astype(jnp.bfloat16)
    grad_qkv = attention_backward(grad_mixed, query, keyset, values, log_total, image_shape)
    qkv_grad = jnp.einsum("td,kte->kde", normed_first, grad_qkv, preferred_element_type=jnp.float32)
    qkv_bias_grad = jnp.sum(grad_qkv.astype(jnp.float32), axis=1)
    grad_normed_first = jnp.einsum(
        "kte,kde->td", grad_qkv, qkv_full, preferred_element_type=jnp.float32
    )
    grad_input, gain_first, shift_first = norm_backward(
        grad_normed_first, scaled_first, inverse_first, gain_rows[0]
    )
    grad_input = grad_input + grad_middle
    gain_grad = jnp.stack([gain_first, gain_second])
    shift_grad = jnp.stack(
        [shift_first, qkv_bias_grad[0], qkv_bias_grad[2], out_shift_grad, shift_second]
    )
    reduced = (
        lax.psum_scatter(
            qkv_grad.astype(jnp.bfloat16), "fsdp", scatter_dimension=1, tiled=True
        ).astype(jnp.float32),
        lax.psum_scatter(
            out_weight_grad.astype(jnp.bfloat16), "fsdp", scatter_dimension=0, tiled=True
        ).astype(jnp.float32),
        lax.psum_scatter(
            gain_grad.astype(jnp.bfloat16), "fsdp", scatter_dimension=1, tiled=True
        ).astype(jnp.float32),
        lax.psum_scatter(
            shift_grad.astype(jnp.bfloat16), "fsdp", scatter_dimension=1, tiled=True
        ).astype(jnp.float32),
        lax.psum_scatter(
            router_grad.astype(jnp.bfloat16), "fsdp", scatter_dimension=0, tiled=True
        ).astype(jnp.float32),
        lax.psum_scatter(
            router_bias_grad.astype(jnp.bfloat16), "fsdp", scatter_dimension=0, tiled=True
        ).astype(jnp.float32),
    )
    totals = (
        lax.psum(reduced[0].astype(jnp.bfloat16), "expert").astype(jnp.float32),
        lax.psum(reduced[1].astype(jnp.bfloat16), "expert").astype(jnp.float32),
        lax.psum(reduced[2].astype(jnp.bfloat16), "expert").astype(jnp.float32),
        lax.psum(reduced[3].astype(jnp.bfloat16), "expert").astype(jnp.float32),
        lax.psum(reduced[4].astype(jnp.bfloat16), "expert").astype(jnp.float32),
        lax.psum(reduced[5].astype(jnp.bfloat16), "expert").astype(jnp.float32),
    )
    return (grad_input, totals, (in_grad, in_bias_grad, out_grad, out_bias_grad))


def shards(
    tokens,
    qkv_weight,
    out_weight,
    norm_gain,
    mixer_bias,
    router_weight,
    router_bias,
    expert_in,
    expert_in_bias,
    expert_out,
    expert_out_bias,
    routes,
    cotangent,
):
    token_count, model_width = tokens.shape
    experts = lax.axis_size("expert") * expert_in.shape[1]
    capacity = max(2, (3 * token_count + experts - 1) // experts)
    image_shape = (token_count // IMG_LEN, IMG_LEN, HEADS, model_width // HEADS)
    hidden_state = tokens.astype(jnp.float32)
    saved_layers = []
    for layer_index in range(LAYERS):
        layer_params = (
            qkv_weight[layer_index],
            out_weight[layer_index],
            norm_gain[layer_index],
            mixer_bias[layer_index],
            router_weight[layer_index],
            router_bias[layer_index],
        )
        expert_params = (
            expert_in[layer_index][0],
            expert_in_bias[layer_index][0],
            expert_out[layer_index][0],
            expert_out_bias[layer_index][0],
        )
        hidden_state, kept_values = layer_forward(
            hidden_state, layer_params, expert_params, routes[layer_index], capacity, image_shape
        )
        saved_layers.append(kept_values)
    result = hidden_state.astype(jnp.bfloat16)
    grad_state = cotangent.astype(jnp.float32)
    mixer_parts = [None] * LAYERS
    expert_parts = [None] * LAYERS
    for layer_index in reversed(range(LAYERS)):
        grad_state, mixer_parts[layer_index], expert_parts[layer_index] = layer_backward(
            grad_state, saved_layers[layer_index], capacity, image_shape
        )
    qkv_all = jnp.stack([parts[0] for parts in mixer_parts])
    out_all = jnp.stack([parts[1] for parts in mixer_parts])
    gain_all = jnp.stack([parts[2] for parts in mixer_parts])
    shift_all = jnp.stack([parts[3] for parts in mixer_parts])
    router_all = jnp.stack([parts[4] for parts in mixer_parts])
    router_bias_all = jnp.stack([parts[5] for parts in mixer_parts])
    in_all = jnp.stack([parts[0] for parts in expert_parts])[:, None]
    in_bias_all = jnp.stack([parts[1] for parts in expert_parts])[:, None]
    out_expert_all = jnp.stack([parts[2] for parts in expert_parts])[:, None]
    out_bias_all = jnp.stack([parts[3] for parts in expert_parts])[:, None]
    return (
        result,
        grad_state,
        qkv_all,
        out_all,
        gain_all,
        shift_all,
        router_all,
        router_bias_all,
        in_all,
        in_bias_all,
        out_expert_all,
        out_bias_all,
    )


def solution(mesh):
    placed = (
        P(("expert", "fsdp"), None),
        P(None, None, "fsdp", None),
        P(None, "fsdp", None),
        P(None, None, "fsdp"),
        P(None, None, "fsdp"),
        P(None, "fsdp", None),
        P(None, "fsdp"),
        P(None, "expert", None, "fsdp"),
        P(None, "expert", "fsdp"),
        P(None, "expert", "fsdp", None),
        P(None, "expert", None),
        P(None, ("expert", "fsdp"), None),
        P(("expert", "fsdp"), None),
    )
    return jax.shard_map(
        shards,
        mesh=mesh,
        in_specs=placed,
        out_specs=(
            P(("expert", "fsdp"), None),
            P(("expert", "fsdp"), None),
            P(None, None, "fsdp", None),
            P(None, "fsdp", None),
            P(None, None, "fsdp"),
            P(None, None, "fsdp"),
            P(None, "fsdp", None),
            P(None, "fsdp"),
            P(None, "expert", None, "fsdp"),
            P(None, "expert", "fsdp"),
            P(None, "expert", "fsdp", None),
            P(None, "expert", None),
        ),
        check_vma=False,
    )
```

profile of v0, /device:TPU:1, one launch (start us, length us, event | category | flops | bytes accessed | tf_op | source)
XLA Modules:
  0.0 1162.6 jit_solution(3902370646355225702)
XLA Ops:
  11.3 11.9 %all-gather.1 = bf16[1,5,768]{1,0,2:T(2,128)(2,1)S(1)} all-gather(bf16[1,5,192]{1,0,2:T(2,128)(2,1)S(1)} %copy.305), channel_id=3, replica_groups=mesh['expert'=32,'fsdp'=4] {'fsdp'}, dimensions={2}, use_global_device_ids=true | all-gather | bytes 9600 | tf_op jit(solution)/shard_map/all_gather | solution.py:121
  23.5 11.8 %slice_reduce_fusion.7 = (f32[768]{0:T(1024)S(1)}, f32[768]{0:T(1024)S(1)}, f32[768]{0:T(1024)S(1)}, f32[768]{0:T(1024)S(1)}, f32[768]{0:T(1024)S(1)}) fusion(f32[1,5,768]{1,0,2:T(1,128)S(1)} %convert_element_type.453), kind=kLoop, calls=%fused_computation.214 | loop fusion | bytes 30720 | tf_op jit(solution)/shard_map/slice | solution.py:135
  35.5 12.4 %all-gather = bf16[1,2,768]{1,0,2:T(2,128)(2,1)S(1)} all-gather(bf16[1,2,192]{1,0,2:T(2,128)(2,1)S(1)} %copy.304), channel_id=2, replica_groups=mesh['expert'=32,'fsdp'=4] {'fsdp'}, dimensions={2}, use_global_device_ids=true | all-gather | bytes 3840 | tf_op jit(solution)/shard_map/all_gather | solution.py:120
  51.4 4.6 slice_reduce_fusion.8
  56.0 3.5 all-gather.29.cloned.1.call-done
  68.0 17.4 %all-gather.31.cloned.1.call-done = bf16[1,768,768]{2,1,0:T(8,128)(2,1)} async-done(((bf16[1,192,768]{2,1,0:T(8,128)(2,1)}), bf16[1,768,768]{2,1,0:T(8,128)(2,1)}) %all-gather.31.cloned.1.call-update) | async-done | bytes 1179664 | tf_op jit(solution)/shard_map/all_gather | solution.py:119
  93.4 27.9 %all_to_all.40 = bf16[32,19,768]{2,1,0:T(8,128)(2,1)S(1)} all-to-all(bf16[32,19,768]{2,1,0:T(8,128)(2,1)S(1)} %reshape.575), channel_id=1, replica_groups=mesh['expert'=32,'fsdp'=4] {'expert'}, dimensions={0} | all-to-all | bytes 1867776 | tf_op jit(solution)/shard_map/all_to_all | solution.py:152
  123.1 40.6 %all-gather.21.cloned.1.call-done = bf16[2432,768]{1,0:T(8,128)(2,1)} async-done(((bf16[608,768]{1,0:T(8,128)(2,1)}), bf16[2432,768]{1,0:T(8,128)(2,1)}) %all-gather.21.cloned.1.call-update) | async-done | bytes 3735568 | tf_op jit(solution)/shard_map/all_gather | solution.py:161
  163.7 21.8 %multiply_convert_fusion.1 = (bf16[2432,768]{1,0:T(8,128)(2,1)S(1)}, f32[2432,768]{1,0:T(8,128)}, f32[2432,768]{1,0:T(8,128)}) fusion(f32[768]{0:T(1024)S(1)} %get-tuple-element.119, bf16[2432,768]{1,0:T(8,128)(2,1)} %all-gather.21.cloned.1.call-done, bf16[2,1,768,768]{3,2,1,0:T(8,128)(2,1)} %param.20), kind=kOutput, calls=%fused_computation.31 | convolution fusion | flops 2992177152 | bytes 23596032 | tf_op jit(solution)/shard_map/dot_general | solution.py:162
  187.3 4.5 convolution_convert_fusion.3
  193.2 9.6 all-gather.7
  203.2 11.8 %slice_reduce_fusion = (f32[768]{0:T(1024)S(1)}, f32[768]{0:T(1024)S(1)}, f32[768]{0:T(1024)S(1)}, f32[768]{0:T(1024)S(1)}, f32[768]{0:T(1024)S(1)}) fusion(f32[1,5,768]{1,0,2:T(1,128)S(1)} %convert_element_type.456), kind=kLoop, calls=%fused_computation.207 | loop fusion | bytes 30720 | tf_op jit(solution)/shard_map/slice | solution.py:135
  217.5 9.4 all-reduce.9
  227.0 11.6 all-gather.4
  239.2 9.9 all-gather.6
  249.5 4.6 slice_reduce_fusion.1
  259.0 16.8 %all-to-all-start.1 = ((bf16[32,19,768]{2,1,0:T(8,128)(2,1)}), bf16[32,19,768]{2,1,0:T(8,128)(2,1)S(1)}, u32[]{:S(2)}, u32[]{:S(2)}) async-start(bf16[32,19,768]{2,1,0:T(8,128)(2,1)} %reshape.577), calls=%async_computation.2 | async-start | bytes 2359296 | tf_op jit(solution)/shard_map/all_to_all | solution.py:174
  276.8 17.4 %all-to-all-done.1 = bf16[32,19,768]{2,1,0:T(8,128)(2,1)S(1)} async-done(((bf16[32,19,768]{2,1,0:T(8,128)(2,1)}), bf16[32,19,768]{2,1,0:T(8,128)(2,1)S(1)}, u32[]{:S(2)}, u32[]{:S(2)}) %all-to-all-start.1) | async-done | bytes 933920 | tf_op jit(solution)/shard_map/all_to_all | solution.py:174
  316.0 3.7 scatter_custom_fusion.1
  321.9 24.7 %all_to_all.41 = bf16[32,19,768]{2,1,0:T(8,128)(2,1)} all-to-all(bf16[32,19,768]{2,1,0:T(8,128)(2,1)} %reshape.582), channel_id=1, replica_groups=mesh['expert'=32,'fsdp'=4] {'expert'}, dimensions={0} | all-to-all | bytes 1867776 | tf_op jit(solution)/shard_map/all_to_all | solution.py:152
  353.8 11.7 %all-gather.10 = bf16[1,768,32]{2,0,1:T(2,128)(2,1)S(1)} all-gather(bf16[1,192,32]{2,0,1:T(2,128)(2,1)S(1)} %copy.309), channel_id=12, replica_groups=mesh['expert'=32,'fsdp'=4] {'fsdp'}, dimensions={1}, use_global_device_ids=true | all-gather | bytes 61440 | tf_op jit(solution)/shard_map/all_gather | solution.py:122
  367.2 3.3 scatter_custom_fusion.2
  371.7 26.0 %all_to_all.42 = bf16[32,19,768]{2,1,0:T(8,128)(2,1)} all-to-all(bf16[32,19,768]{2,1,0:T(8,128)(2,1)} %reshape.586), channel_id=1, replica_groups=mesh['expert'=32,'fsdp'=4] {'expert'}, dimensions={0} | all-to-all | bytes 1867776 | tf_op jit(solution)/shard_map/all_to_all | solution.py:252
  399.9 21.9 %multiply_convert_fusion = (bf16[2432,768]{1,0:T(8,128)(2,1)}, f32[2432,768]{1,0:T(8,128)}, f32[2432,768]{1,0:T(8,128)}) fusion(f32[768]{0:T(1024)S(1)} %copy-done.142, bf16[2432,768]{1,0:T(8,128)(2,1)} %all-gather.23.cloned.1.call-done, bf16[2,1,768,768]{3,2,1,0:T(8,128)(2,1)} %param.20), kind=kOutput, calls=%fused_computation.18 | convolution fusion | flops 2992177152 | bytes 23596032 | tf_op jit(solution)/shard_map/dot_general | solution.py:162
  421.8 18.8 %all-gather.25.cloned.1.call-done = bf16[2432,768]{1,0:T(8,128)(2,1)} async-done(((bf16[608,768]{1,0:T(8,128)(2,1)}), bf16[2432,768]{1,0:T(8,128)(2,1)}) %all-gather.25.cloned.1.call-update) | async-done | bytes 3735568 | tf_op jit(solution)/shard_map/all_gather | solution.py:262
  440.6 11.2 convert_reduce_fusion.2
  453.6 4.6 convolution_convert_fusion.1
  458.2 7.4 convolution_convert_fusion.2
  465.6 36.1 %reduce-scatter.35.cloned.1.call-done = bf16[608,768]{1,0:T(8,128)(2,1)} async-done(((bf16[2432,768]{1,0:T(8,128)(2,1)}), bf16[608,768]{1,0:T(8,128)(2,1)}) %reduce-scatter.35.cloned.1.call-update) | async-done | bytes 933904 | tf_op jit(solution)/shard_map/reduce_scatter | solution.py:270
  503.9 7.7 all-to-all-start.5
  511.6 35.2 %reduce-scatter.33.cloned.1.call-done = bf16[608,768]{1,0:T(8,128)(2,1)} async-done(((bf16[2432,768]{1,0:T(8,128)(2,1)}), bf16[608,768]{1,0:T(8,128)(2,1)}) %reduce-scatter.33.cloned.1.call-update) | async-done | bytes 933904 | tf_op jit(solution)/shard_map/reduce_scatter | solution.py:166
  549.3 7.7 all-to-all-start.3
  568.0 7.4 all-to-all-done.3
  582.7 4.7 multiply_reduce_fusion.5
  591.1 3.5 reduce_sum.516
  605.9 4.2 multiply_reduce_fusion.9
  612.6 3.3 scatter_custom_fusion.3
  616.3 22.8 %all_to_all.43 = bf16[32,19,768]{2,1,0:T(8,128)(2,1)} all-to-all(bf16[32,19,768]{2,1,0:T(8,128)(2,1)S(1)} %reshape.591), channel_id=1, replica_groups=mesh['expert'=32,'fsdp'=4] {'expert'}, dimensions={0} | all-to-all | bytes 1867776 | tf_op jit(solution)/shard_map/all_to_all | solution.py:252
  641.3 40.3 %all-gather.27.cloned.1.call-done = bf16[2432,768]{1,0:T(8,128)(2,1)} async-done(((bf16[608,768]{1,0:T(8,128)(2,1)}), bf16[2432,768]{1,0:T(8,128)(2,1)}) %all-gather.27.cloned.1.call-update) | async-done | bytes 3735568 | tf_op jit(solution)/shard_map/all_gather | solution.py:262
  681.6 11.7 %convert_reduce_fusion.3 = (f32[768]{0:T(1024)}, bf16[2432,768]{1,0:T(8,128)(2,1)S(1)}) fusion(f32[2432,768]{1,0:T(8,128)} %get-tuple-element.149, bf16[2432,768]{1,0:T(8,128)(2,1)} %all-gather.27.cloned.1.call-done, bf16[2,1,768,768]{3,2,1,0:T(8,128)(2,1)} %param.22, f32[2432,768]{1,0:T(8,128)} %get-tuple-element.183, f32[768]{0:T(1024)S(1)} %copy-done.141), kind=kOutput, calls=%fused_computation.15 | convolution fusion | flops 2900655360 | bytes 23599104 | tf_op jit(solution)/shard_map/dot_general | solution.py:17
  695.2 4.6 convolution_convert_fusion
  705.7 4.3 convert_bitcast_fusion
  710.0 8.1 copy.290
  718.1 4.9 copy.315
  723.1 20.3 %reduce-scatter.37.cloned.1.call-done = bf16[608,768]{1,0:T(8,128)(2,1)} async-done(((bf16[2432,768]{1,0:T(8,128)(2,1)}), bf16[608,768]{1,0:T(8,128)(2,1)}) %reduce-scatter.37.cloned.1.call-update) | async-done | bytes 933904 | tf_op jit(solution)/shard_map/reduce_scatter | solution.py:270
  745.6 7.6 all-to-all-start.7
  753.4 18.3 %all-to-all-done.7 = bf16[32,19,768]{2,1,0:T(8,128)(2,1)S(1)} async-done(((bf16[32,19,768]{2,1,0:T(8,128)(2,1)}), bf16[32,19,768]{2,1,0:T(8,128)(2,1)S(1)}, u32[]{:S(2)}, u32[]{:S(2)}) %all-to-all-start.7) | async-done | bytes 933920 | tf_op jit(solution)/shard_map/all_to_all | solution.py:276
  795.1 8.1 copy.288
  803.2 4.9 copy.314
  813.4 6.7 convolution_bitcast_fusion.2
  820.2 4.8 convolution_bitcast_fusion
  825.1 7.6 all-reduce.8
  840.1 6.6 convolution_bitcast_fusion.3
  851.8 4.7 convolution_bitcast_fusion.1
  867.6 31.4 %reduce-scatter.43.cloned.1.call-done = bf16[192,2304]{1,0:T(8,128)(2,1)} async-done(((bf16[768,2304]{1,0:T(8,128)(2,1)}), bf16[192,2304]{1,0:T(8,128)(2,1)}) %reduce-scatter.43.cloned.1.call-update) | async-done | bytes 884752
  903.3 20.7 %reduce-scatter.41.cloned.1.call-done = bf16[192,768]{1,0:T(8,128)(2,1)} async-done(((bf16[768,768]{1,0:T(8,128)(2,1)}), bf16[192,768]{1,0:T(8,128)(2,1)}) %reduce-scatter.41.cloned.1.call-update) | async-done | bytes 294928 | tf_op jit(solution)/shard_map/reduce_scatter | solution.py:319
  924.0 26.5 %reduce-scatter.39.cloned.1.call-done = bf16[192,768]{1,0:T(8,128)(2,1)} async-done(((bf16[768,768]{1,0:T(8,128)(2,1)}), bf16[192,768]{1,0:T(8,128)(2,1)}) %reduce-scatter.39.cloned.1.call-update) | async-done | bytes 294928 | tf_op jit(solution)/shard_map/reduce_scatter | solution.py:319
  950.5 4.2 maximum_bitcast_fusion.1
  955.8 16.1 %reduce-scatter.47.cloned.1.call-done = bf16[192,2]{1,0:T(8,128)(2,1)} async-done(((bf16[768,2]{1,0:T(8,128)(2,1)}), bf16[192,2]{1,0:T(8,128)(2,1)}) %reduce-scatter.47.cloned.1.call-update) | async-done | bytes 784
  972.8 21.8 %reduce-scatter.53.cloned.1.call-done = bf16[192,5]{1,0:T(8,128)(2,1)} async-done(((bf16[768,5]{1,0:T(8,128)(2,1)}), bf16[192,5]{1,0:T(8,128)(2,1)}) %reduce-scatter.53.cloned.1.call-update) | async-done | bytes 1936
  995.5 21.8 %reduce-scatter.51.cloned.1.call-done = bf16[192,5]{1,0:T(8,128)(2,1)} async-done(((bf16[768,5]{1,0:T(8,128)(2,1)}), bf16[192,5]{1,0:T(8,128)(2,1)}) %reduce-scatter.51.cloned.1.call-update) | async-done | bytes 1936
  1018.2 123.9 %all-reduce.6 = (bf16[1,2,192]{2,1,0:T(2,128)(2,1)S(1)}, bf16[1,2,192]{2,1,0:T(2,128)(2,1)S(1)}, bf16[1,5,192]{2,1,0:T(8,128)(2,1)S(1)}, bf16[1,5,192]{2,1,0:T(8...) all-reduce(bf16[1,2,192]{2,1,0:T(2,128)(2,1)S(1)} %bitcast.338, ...), channel_id=1, replica_groups=mesh['expert'=32,'fsdp'=4] {'expert'}, use_global_device_ids=true, to_apply=%region_67.68 | all-reduce | flops 14992 | bytes 59968 | tf_op jit(solution)/shard_map/psum | solution.py:338
  1144.5 4.4 maximum_convert_fusion
  1148.9 5.7 copy.276
  (625 shorter events, 191.0 us)
Async XLA Ops:
  7.2 52.2 %all-gather.29.cloned.1.call-start = ((), (), s32[]{:S(2)}) async-start(), calls=%async_computation.32 | async-start | bytes 4423680 | tf_op jit(solution)/shard_map/all_gather | solution.py:118
  10.0 25.3 %copy-start.147 = (bf16[2,2,192]{2,1,0:T(2,128)(2,1)S(1)}, bf16[2,2,192]{2,1,0:T(2,128)(2,1)}, u32[]{:S(2)}) copy-start(bf16[2,2,192]{2,1,0:T(2,128)(2,1)} %param.16) | copy-start | bytes 4612
  10.0 38.3 %copy-start.17 = (bf16[197,768]{1,0:T(8,128)(2,1)S(1)}, bf16[197,768]{1,0:T(8,128)(2,1)}, u32[]{:S(2)}) copy-start(bf16[197,768]{1,0:T(8,128)(2,1)} %param.13) | copy-start | bytes 907780
  10.1 38.9 %copy-start.145 = (s32[2,197,2]{1,2,0:T(2,128)S(1)}, s32[2,197,2]{1,2,0:T(2,128)}, u32[]{:S(2)}) copy-start(s32[2,197,2]{1,2,0:T(2,128)} %param.24) | copy-start | bytes 9460
  10.1 75.3 %all-gather.31.cloned.1.call-start = ((), (), s32[]{:S(2)}) async-start(), calls=%async_computation.33 | async-start | bytes 1474560 | tf_op jit(solution)/shard_map/all_gather | solution.py:119
  11.0 152.6 %all-gather.21.cloned.1.call-start = ((), (), s32[]{:S(2)}) async-start(), calls=%async_computation.22 | async-start | bytes 4669440 | tf_op jit(solution)/shard_map/all_gather | solution.py:161
  35.3 27.1 %copy-start.106 = (f32[768]{0:T(1024)}, f32[768]{0:T(1024)S(1)}, u32[]{:S(2)}) copy-start(f32[768]{0:T(1024)S(1)} %get-tuple-element.115) | copy-start | bytes 9220
  48.9 227.3 %copy-start.101 = (s32[197,2]{0,1:T(2,128)}, s32[197,2]{0,1:T(2,128)S(1)}, u32[]{:S(2)}) copy-start(s32[197,2]{0,1:T(2,128)S(1)} %get-tuple-element.168) | copy-start | bytes 4732
  49.0 317.1 %copy-start.103 = (s32[197,2]{0,1:T(2,128)}, s32[197,2]{0,1:T(2,128)S(1)}, u32[]{:S(2)}) copy-start(s32[197,2]{0,1:T(2,128)S(1)} %get-tuple-element.167) | copy-start | bytes 4732
  51.3 141.6 %copy-start.130 = (s32[394,1]{0,1:T(1,128)}, s32[394,1]{0,1:T(1,128)S(1)}, u32[]{:S(2)}) copy-start(s32[394,1]{0,1:T(1,128)S(1)} %compare_select_fusion.1) | copy-start | bytes 4732
  55.9 31.5 %copy-start.80 = (f32[768]{0:T(1024)}, f32[768]{0:T(1024)S(1)}, u32[]{:S(2)}) copy-start(f32[768]{0:T(1024)S(1)} %get-tuple-element.109) | copy-start | bytes 9220
  87.2 211.8 %copy-start.2 = (f32[197,768]{1,0:T(8,128)}, f32[197,768]{1,0:T(8,128)S(1)}, u32[]{:S(2)}) copy-start(f32[197,768]{1,0:T(8,128)S(1)} %get-tuple-element.182) | copy-start | bytes 1815556
  87.5 33.8 %copy-start.114 = (f32[197]{0:T(256)}, f32[197]{0:T(256)S(1)}, u32[]{:S(2)}) copy-start(f32[197]{0:T(256)S(1)} %add_rsqrt_fusion.2) | copy-start | bytes 2368
  88.0 187.9 %copy-start.23 = (bf16[197,768]{1,0:T(8,128)(2,1)}, bf16[197,768]{1,0:T(8,128)(2,1)S(1)}, u32[]{:S(2)}) copy-start(bf16[197,768]{1,0:T(8,128)(2,1)S(1)} %add_convert_fusion.11) | copy-start | bytes 907780
  93.0 29.4 %copy-start.123 = (bf16[2,1,768]{2,0,1:T(2,128)(2,1)S(1)}, bf16[2,1,768]{2,0,1:T(2,128)(2,1)}, u32[]{:S(2)}) copy-start(bf16[2,1,768]{2,0,1:T(2,128)(2,1)} %param.21) | copy-start | bytes 9220
  122.4 134.0 %reduce-scatter.31.cloned.1.call-start = ((), (), s32[]{:S(2)}) async-start(), calls=%async_computation.23 | async-start | bytes 4669440 | tf_op jit(solution)/shard_map/reduce_scatter | solution.py:166
  123.1 62.3 %copy-start.140 = (f32[768]{0:T(1024)}, f32[768]{0:T(1024)S(1)}, u32[]{:S(2)}) copy-start(f32[768]{0:T(1024)S(1)} %get-tuple-element.119) | copy-start | bytes 9220
  191.8 23.9 %copy-start.146 = (u32[128]{0:T(128)S(1)}, u32[128]{0:T(128)}, u32[]{:S(2)}) copy-start(u32[128]{0:T(128)} %constant.127) | copy-start | bytes 1540
  191.8 35.1 %copy-start.92 = (bf16[2,192,32]{1,2,0:T(8,128)(2,1)S(1)}, bf16[2,192,32]{1,2,0:T(8,128)(2,1)}, u32[]{:S(2)}) copy-start(bf16[2,192,32]{1,2,0:T(8,128)(2,1)} %param.18) | copy-start | bytes 73732
  191.8 107.7 %all-gather.33.cloned.1.call-start = ((), (), s32[]{:S(2)}) async-start(), calls=%async_computation.34 | async-start | bytes 4423680 | tf_op jit(solution)/shard_map/all_gather | solution.py:118
  192.4 118.6 %all-gather.35.cloned.1.call-start = ((), (), s32[]{:S(2)}) async-start(), calls=%async_computation.35 | async-start | bytes 1474560 | tf_op jit(solution)/shard_map/all_gather | solution.py:119
  193.0 101.5 %copy-start.104 = (s32[1024]{0:T(1024)}, s32[1024]{0:T(1024)S(1)}, u32[]{:S(2)}) copy-start(s32[1024]{0:T(1024)S(1)} %pad_clamp_fusion.1) | copy-start | bytes 12292
  215.0 84.4 %copy-start.119 = (f32[768]{0:T(1024)}, f32[768]{0:T(1024)S(1)}, u32[]{:S(2)}) copy-start(f32[768]{0:T(1024)S(1)} %get-tuple-element.108) | copy-start | bytes 9220
  239.0 36.9 %copy-start.66 = (bf16[1,768,32]{1,2,0:T(8,128)(2,1)}, bf16[1,768,32]{1,2,0:T(8,128)(2,1)S(1)}, u32[]{:S(2)}) copy-start(bf16[1,768,32]{1,2,0:T(8,128)(2,1)S(1)} %copy.239) | copy-start | bytes 147460
  254.1 45.4 %copy-start.87 = (f32[768]{0:T(1024)}, f32[768]{0:T(1024)S(1)}, u32[]{:S(2)}) copy-start(f32[768]{0:T(1024)S(1)} %get-tuple-element.103) | copy-start | bytes 9220
  254.3 55.9 %copy-start.90 = (f32[12,64]{1,0:T(8,128)}, f32[12,64]{1,0:T(8,128)S(1)}, u32[]{:S(2)}) copy-start(f32[12,64]{1,0:T(8,128)S(1)} %add.371) | copy-start | bytes 9220
  259.0 35.2 %all-to-all-start.1 = ((bf16[32,19,768]{2,1,0:T(8,128)(2,1)}), bf16[32,19,768]{2,1,0:T(8,128)(2,1)S(1)}, u32[]{:S(2)}, u32[]{:S(2)}) async-start(bf16[32,19,768]{2,1,0:T(8,128)(2,1)} %reshape.577), calls=%async_computation.2 | async-start | bytes 2359296 | tf_op jit(solution)/shard_map/all_to_all | solution.py:174
  275.8 124.1 %all-gather.23.cloned.1.call-start = ((), (), s32[]{:S(2)}) async-start(), calls=%async_computation.24 | async-start | bytes 4669440 | tf_op jit(solution)/shard_map/all_gather | solution.py:161
  275.9 40.1 %copy-start.131 = (s32[394,1]{0,1:T(1,128)}, s32[394,1]{0,1:T(1,128)S(1)}, u32[]{:S(2)}) copy-start(s32[394,1]{0,1:T(1,128)S(1)} %compare_select_fusion) | copy-start | bytes 4732
  312.9 33.7 %copy-start.97 = (f32[197]{0:T(256)}, f32[197]{0:T(256)S(1)}, u32[]{:S(2)}) copy-start(f32[197]{0:T(256)S(1)} %broadcast_multiply_fusion.10) | copy-start | bytes 2368
  313.2 33.5 %copy-start.116 = (f32[197]{0:T(256)}, f32[197]{0:T(256)S(1)}, u32[]{:S(2)}) copy-start(f32[197]{0:T(256)S(1)} %add_rsqrt_fusion) | copy-start | bytes 2368
  313.9 51.8 %copy-start.25 = (bf16[197,768]{1,0:T(8,128)(2,1)}, bf16[197,768]{1,0:T(8,128)(2,1)S(1)}, u32[]{:S(2)}) copy-start(bf16[197,768]{1,0:T(8,128)(2,1)S(1)} %add_convert_fusion.9) | copy-start | bytes 907780
  319.7 29.7 %copy-start.38 = (bf16[197,768]{1,0:T(8,128)(2,1)S(1)}, bf16[197,768]{1,0:T(8,128)(2,1)}, u32[]{:S(2)}) copy-start(bf16[197,768]{1,0:T(8,128)(2,1)} %param.25) | copy-start | bytes 907780
  348.9 91.7 %all-gather.25.cloned.1.call-start = ((), (), s32[]{:S(2)}) async-start(), calls=%async_computation.26 | async-start | bytes 4669440 | tf_op jit(solution)/shard_map/all_gather | solution.py:262
  366.0 33.8 %copy-start.99 = (f32[197]{0:T(256)}, f32[197]{0:T(256)S(1)}, u32[]{:S(2)}) copy-start(f32[197]{0:T(256)S(1)} %get-tuple-element.191) | copy-start | bytes 2368
  366.1 33.8 %copy-start.110 = (f32[197]{0:T(256)}, f32[197]{0:T(256)S(1)}, u32[]{:S(2)}) copy-start(f32[197]{0:T(256)S(1)} %fusion.123) | copy-start | bytes 2368
  370.5 29.5 %copy-start.142 = (f32[768]{0:T(1024)S(1)}, f32[768]{0:T(1024)}, u32[]{:S(2)}) copy-start(f32[768]{0:T(1024)} %get-tuple-element.118) | copy-start | bytes 9220
  399.8 101.8 %reduce-scatter.35.cloned.1.call-start = ((), (), s32[]{:S(2)}) async-start(), calls=%async_computation.27 | async-start | bytes 4669440 | tf_op jit(solution)/shard_map/reduce_scatter | solution.py:270
  458.2 88.6 %reduce-scatter.33.cloned.1.call-start = ((), (), s32[]{:S(2)}) async-start(), calls=%async_computation.25 | async-start | bytes 4669440 | tf_op jit(solution)/shard_map/reduce_scatter | solution.py:166
  465.6 81.2 %copy-start.118 = (f32[768]{0:T(1024)S(1)}, f32[768]{0:T(1024)}, u32[]{:S(2)}) copy-start(f32[768]{0:T(1024)} %get-tuple-element.116) | copy-start | bytes 9220
  503.9 45.4 %all-to-all-start.5 = ((bf16[32,19,768]{2,1,0:T(8,128)(2,1)}), bf16[32,19,768]{2,1,0:T(8,128)(2,1)}, u32[]{:S(2)}, u32[]{:S(2)}) async-start(bf16[32,19,768]{2,1,0:T(8,128)(2,1)} %reshape.588), calls=%async_computation.8 | async-start | bytes 2359296 | tf_op jit(solution)/shard_map/all_to_all | solution.py:276
  511.6 47.9 %copy-start.59 = (f32[197,2]{1,0:T(8,128)S(1)}, f32[197,2]{1,0:T(8,128)}, u32[]{:S(2)}) copy-start(f32[197,2]{1,0:T(8,128)} %copy-done.58) | copy-start | bytes 4732
  549.3 26.1 %all-to-all-start.3 = ((bf16[32,19,768]{2,1,0:T(8,128)(2,1)}), bf16[32,19,768]{2,1,0:T(8,128)(2,1)}, u32[]{:S(2)}, u32[]{:S(2)}) async-start(bf16[32,19,768]{2,1,0:T(8,128)(2,1)} %reshape.584), calls=%async_computation.5 | async-start | bytes 2359296 | tf_op jit(solution)/shard_map/all_to_all | solution.py:174
  557.0 124.6 %all-gather.27.cloned.1.call-start = ((), (), s32[]{:S(2)}) async-start(), calls=%async_computation.28 | async-start | bytes 4669440 | tf_op jit(solution)/shard_map/all_gather | solution.py:262
  610.3 89.6 %copy-start.16 = (f32[197,768]{1,0:T(8,128)}, f32[197,768]{1,0:T(8,128)S(1)}, u32[]{:S(2)}) copy-start(f32[197,768]{1,0:T(8,128)S(1)} %multiply_add_fusion.1) | copy-start | bytes 1815556
  615.9 65.7 %copy-start.141 = (f32[768]{0:T(1024)S(1)}, f32[768]{0:T(1024)}, u32[]{:S(2)}) copy-start(f32[768]{0:T(1024)} %copy-done.140) | copy-start | bytes 9220
  641.2 102.2 %reduce-scatter.37.cloned.1.call-start = ((), (), s32[]{:S(2)}) async-start(), calls=%async_computation.29 | async-start | bytes 4669440 | tf_op jit(solution)/shard_map/reduce_scatter | solution.py:270
  699.9 132.9 %reduce-scatter.49.cloned.1.call-start = ((), (), s32[]{:S(2)}) async-start(), calls=%async_computation.39 | async-start | bytes 245760
  703.0 130.7 %reduce-scatter.57.cloned.1.call-start = ((), (), s32[]{:S(2)}) async-start(), calls=%async_computation.43 | async-start | bytes 245760
  704.6 130.0 %reduce-scatter.55.cloned.1.call-start = ((), (), s32[]{:S(2)}) async-start(), calls=%async_computation.42 | async-start | bytes 245760
  705.6 157.7 %reduce-scatter.45.cloned.1.call-start = ((), (), s32[]{:S(2)}) async-start(), calls=%async_computation.37 | async-start | bytes 4423680
  723.0 30.3 %copy-start.74 = (f32[12,197]{1,0:T(8,128)S(1)}, f32[12,197]{1,0:T(8,128)}, u32[]{:S(2)}) copy-start(f32[12,197]{1,0:T(8,128)} %copy-done.73) | copy-start | bytes 28372
  723.0 30.3 %copy-start.83 = (f32[12,197]{1,0:T(8,128)S(1)}, f32[12,197]{1,0:T(8,128)}, u32[]{:S(2)}) copy-start(f32[12,197]{1,0:T(8,128)} %copy-done.82) | copy-start | bytes 28372
  723.1 49.1 %copy-start.105 = (s32[1024]{0:T(1024)S(1)}, s32[1024]{0:T(1024)}, u32[]{:S(2)}) copy-start(s32[1024]{0:T(1024)} %copy-done.104) | copy-start | bytes 12292
  745.6 26.0 %all-to-all-start.7 = ((bf16[32,19,768]{2,1,0:T(8,128)(2,1)}), bf16[32,19,768]{2,1,0:T(8,128)(2,1)S(1)}, u32[]{:S(2)}, u32[]{:S(2)}) async-start(bf16[32,19,768]{2,1,0:T(8,128)(2,1)} %reshape.593), calls=%async_computation.11 | async-start | bytes 2359296 | tf_op jit(solution)/shard_map/all_to_all | solution.py:276
  753.3 145.7 %reduce-scatter.43.cloned.1.call-start = ((), (), s32[]{:S(2)}) async-start(), calls=%async_computation.36 | async-start | bytes 4423680
  753.3 31.3 %copy-start.71 = (f32[12,197]{1,0:T(8,128)}, f32[12,197]{1,0:T(8,128)S(1)}, u32[]{:S(2)}) copy-start(f32[12,197]{1,0:T(8,128)S(1)} %log_add_fusion.1) | copy-start | bytes 28372
  808.2 115.8 %reduce-scatter.41.cloned.1.call-start = ((), (), s32[]{:S(2)}) async-start(), calls=%async_computation.31 | async-start | bytes 1474560 | tf_op jit(solution)/shard_map/reduce_scatter | solution.py:319
  813.2 137.3 %reduce-scatter.39.cloned.1.call-start = ((), (), s32[]{:S(2)}) async-start(), calls=%async_computation.30 | async-start | bytes 1474560 | tf_op jit(solution)/shard_map/reduce_scatter | solution.py:319
  839.8 132.1 %reduce-scatter.47.cloned.1.call-start = ((), (), s32[]{:S(2)}) async-start(), calls=%async_computation.38 | async-start | bytes 245760
  860.1 134.6 %reduce-scatter.53.cloned.1.call-start = ((), (), s32[]{:S(2)}) async-start(), calls=%async_computation.41 | async-start | bytes 245760
  861.0 156.3 %reduce-scatter.51.cloned.1.call-start = ((), (), s32[]{:S(2)}) async-start(), calls=%async_computation.40 | async-start | bytes 245760
  862.1 282.4 %all-reduce.12.cloned.1.call-start = ((), (), s32[]{:S(2)}) async-start(), calls=%async_computation.44 | async-start | bytes 5898240 | tf_op jit(solution)/shard_map/psum | solution.py:336
  903.3 47.2 %copy-start.40 = (f32[1,768,768]{2,1,0:T(8,128)S(1)}, f32[1,768,768]{2,1,0:T(8,128)}, u32[]{:S(2)}) copy-start(f32[1,768,768]{2,1,0:T(8,128)} %convolution_bitcast_fusion) | copy-start | bytes 7077892
  (124 other events, 719.9 us)
Sparse Core Ops, SparseCore 0:
  10.3 49.1 all-gather.28
  61.7 23.6 all-gather.30
  122.5 41.0 all-gather.20
  191.9 45.1 reduce-scatter.30
  239.3 43.2 all-gather.32
  284.8 23.2 all-gather.34
  349.0 43.1 all-gather.22
  400.0 40.5 all-gather.24
  458.3 43.3 reduce-scatter.34
  503.9 42.7 reduce-scatter.32
  641.4 40.2 all-gather.26
  700.0 43.3 reduce-scatter.36
  745.8 18.4 reduce-scatter.48
  766.6 19.6 reduce-scatter.56
  788.5 20.2 reduce-scatter.54
  811.8 43.6 reduce-scatter.44
  857.9 41.0 reduce-scatter.42
  901.4 22.5 reduce-scatter.40
  926.6 23.8 reduce-scatter.38
  952.8 19.1 reduce-scatter.46
  974.3 20.2 reduce-scatter.52
  997.1 20.1 reduce-scatter.50
  1021.7 111.9 all-reduce.11
where the time goes:
time: 1180 us; the launch traced here: 1160 us
  waiting for transfers between devices  395 us (33%)
  blocking collectives  309 us (26%)
  local copies, waits for them, and re-layouts  178 us (15%)
  matrix products  156 us (13%)
  other arithmetic  64.3 us (5%)
  starting transfers between devices  41.7 us (4%)
  between operations  18.6 us (2%)
    psum x1, blocking collectives, layer_backward(): lax.psum(reduced[2].astype(jnp.bfloat16), 'expert').astype(jnp.float32)  124 us
    unnamed x31, waiting for transfers between devices  92.5 us
    unnamed x356, local copies, waits for them, and re-layouts  70.7 us
    dot_general x16, matrix products, contract(): lax.dot_general(left, right, (((left_dim,), (right_dim,)), ((), ())), pre...  65.1 us
    all_gather x2, waiting for transfers between devices, layer_backward(): grad_group = lax.all_gather(grad_own, 'fsdp', axis=0, tiled=True)  59.1 us
    reduce_scatter x2, waiting for transfers between devices, layer_backward(): lax.psum_scatter(contract(grad_pre, weight_in, 1, 1).astype(jnp.bfloat16)...  56.4 us
    all_to_all x2, blocking collectives, layer_forward(): lax.all_to_all(send_rows.reshape(experts, capacity, model_width), 'expert...  52.6 us
    all_to_all x2, blocking collectives, layer_backward(): lax.all_to_all(grad_send.reshape(experts, capacity, model_width), 'expert...  48.7 us
  transfers between devices with their start and end apart: 27, of which 17 were waited for; matrix products, arithmetic and copies ran while one was open for 21% of the time, Pallas kernels for 0%

commit v1 on v0

v1 whole, which is shorter than its diff:
```python
import functools

import jax
import jax.numpy as jnp
from jax import lax
from jax.experimental import pallas as pl
from jax.experimental.pallas import tpu as pltpu
from jax.sharding import PartitionSpec as P

HEADS = 12
LAYERS = 2
EPSILON = 1e-06
BF16 = jnp.bfloat16
F32 = jnp.float32
VMEM_LIMIT = 56 * 1024 * 1024


def dot(left, right, left_dim=1, right_dim=0):
    return lax.dot_general(
        left, right, (((left_dim,), (right_dim,)), ((), ())), preferred_element_type=F32
    )


def shaped(shape, kind):
    return jax.ShapeDtypeStruct(shape, kind)


def standardize(values):
    centred = values - jnp.mean(values, axis=-1, keepdims=True)
    inverse = lax.rsqrt(jnp.mean(centred * centred, axis=-1, keepdims=True) + EPSILON)
    return centred * inverse, inverse


def norm_backward(grad_out, scaled, inverse, gain):
    grad_scaled = grad_out * gain
    mean_grad = jnp.mean(grad_scaled, axis=-1, keepdims=True)
    mean_cross = jnp.mean(grad_scaled * scaled, axis=-1, keepdims=True)
    grad_input = inverse * (grad_scaled - mean_grad - scaled * mean_cross)
    return (
        grad_input,
        jnp.sum(grad_out * scaled, axis=0, keepdims=True),
        jnp.sum(grad_out, axis=0, keepdims=True),
    )


def gelu_both(pre):
    size = jnp.abs(pre) * (0.5**0.5)
    t = 1.0 / (1.0 + 0.3275911 * size)
    poly = t * (
        0.254829592
        + t * (-0.284496736 + t * (1.421413741 + t * (-1.453152027 + t * 1.061405429)))
    )
    bell = jnp.exp(-(size * size))
    tail = (0.5 * poly) * bell
    cdf = jnp.where(pre >= 0.0, 1.0 - tail, tail)
    return pre * cdf, cdf + pre * bell * 0.3989422804014327


def slot_targets(routes_layer, experts, stride):
    flat = routes_layer.reshape(-1)
    count = flat.shape[0]
    onehot = (flat[:, None] == jnp.arange(experts, dtype=jnp.int32)[None, :]).astype(BF16)
    below = (jnp.arange(count)[None, :] < jnp.arange(count)[:, None]).astype(BF16)
    earlier = dot(below, onehot)
    position = jnp.sum(earlier * onehot.astype(F32), axis=1).astype(jnp.int32)
    return (flat * stride + position).reshape(-1, 2)


def slot_rows(targets_row, rows, which):
    tokens = targets_row.shape[1]
    slots = lax.broadcasted_iota(jnp.int32, (rows, tokens), 0)
    return (slots == targets_row[which : which + 1, :]).astype(F32).astype(BF16)


def slot_columns(targets, rows, which):
    tokens = targets.shape[0]
    slots = lax.broadcasted_iota(jnp.int32, (tokens, rows), 1)
    return (slots == targets[:, which : which + 1]).astype(F32).astype(BF16)


def expert_hot(routes, experts, which):
    places = lax.broadcasted_iota(jnp.int32, (routes.shape[0], experts), 1)
    return (places == routes[:, which : which + 1]).astype(F32)


def pair_lanes(tokens, head):
    lanes = lax.broadcasted_iota(jnp.int32, (tokens, 128), 1)
    return (lanes // 64) == head % 2


def place_weights(here_ref, own_ref, mine, theirs, full_ref):
    _, part, _ = own_ref.shape
    parts = full_ref.shape[1] // part
    me, core = here_ref[0], here_ref[1]

    def spot(ahead):
        return pl.ds(pl.multiple_of(lax.rem(me + ahead, parts) * part, part), part)

    for kind in range(4):
        full_ref[kind, spot(0), :] = own_ref[kind]
    for ahead, (mine_ref, theirs_ref) in enumerate(zip(mine, theirs), start=1):
        for half in range(2):
            full_ref[2 * core + half, spot(ahead), :] = mine_ref[half]
            full_ref[2 * (1 - core) + half, spot(ahead), :] = theirs_ref[half]


def mixer_forward_body(first, count, scale, experts, *refs):
    here_ref, own_ref = refs[:2]
    full_ref = refs[-1]
    place_weights(here_ref, own_ref, refs[2:5], refs[5:8], full_ref)
    refs = refs[8:-1]
    if first:
        (x_ref, lane_ref, router_ref, rbias_ref, routes_ref, row_ref) = refs[:6]
        outs = refs[6:]
        x = x_ref[...]
    else:
        (
            middle_ref,
            back_ref,
            gates_prev_ref,
            targets_prev_ref,
            cot_ref,
            lane_ref,
            router_ref,
            rbias_ref,
            routes_ref,
            row_ref,
        ) = refs[:10]
        outs = refs[10:]
        x = middle_ref[...]
        back = back_ref[...]
        for j in range(2):
            picked = dot(slot_columns(targets_prev_ref[...], back.shape[0], j), back)
            x = x + gates_prev_ref[:, j : j + 1] * picked
    middle_out, send_out, q_out, k_out, v_out, m_out, lse_out, probs_out, gates_out = outs[:9]
    if not first:
        outs[9][...] = x
    tokens, width = x.shape
    lane = lane_ref[...]
    scaled, _ = standardize(x)
    normed = (scaled * lane[0:1] + lane[2:3]).astype(BF16)
    q_out[...] = (dot(normed, full_ref[0]) + lane[3:4]).astype(BF16)
    k_out[...] = dot(normed, full_ref[1]).astype(BF16)
    v_out[...] = (dot(normed, full_ref[2]) + lane[4:5]).astype(BF16)
    valid = lax.broadcasted_iota(jnp.int32, (tokens, tokens), 1) < count
    log_totals = jnp.zeros((tokens, 128), F32)
    head_lanes = lax.broadcasted_iota(jnp.int32, (tokens, 128), 1)
    for pair in range(HEADS // 2):
        cols = slice(pair * 128, pair * 128 + 128)
        q, k, v = q_out[:, cols], k_out[:, cols], v_out[:, cols]
        mixed = jnp.zeros((tokens, 128), F32)
        for head in (2 * pair, 2 * pair + 1):
            keep = pair_lanes(tokens, head)
            scores = dot(jnp.where(keep, q, jnp.zeros_like(q)), k, 1, 1) * scale
            scores = jnp.where(valid, scores, -1e30)
            top = jnp.max(scores, axis=-1, keepdims=True)
            exponent = jnp.exp(scores - top)
            total = jnp.sum(exponent, axis=-1, keepdims=True)
            weights = (exponent / total).astype(BF16)
            mixed = mixed + dot(weights, jnp.where(keep, v, jnp.zeros_like(v)))
            log_totals = jnp.where(head_lanes == head, top + jnp.log(total), log_totals)
        m_out[:, cols] = mixed.astype(BF16)
    lse_out[...] = log_totals
    middle = x + dot(m_out[...], full_ref[3]) + lane[5:6]
    middle_out[...] = middle
    scaled, _ = standardize(middle)
    normed = (scaled * lane[1:2] + lane[6:7]).astype(BF16)
    logits = dot(normed, router_ref[...], 1, 1) + rbias_ref[...]
    exponent = jnp.exp(logits - jnp.max(logits, axis=-1, keepdims=True))
    probs = exponent / jnp.sum(exponent, axis=-1, keepdims=True)
    probs_out[...] = probs
    gates = [
        jnp.sum(expert_hot(routes_ref[...], experts, j) * probs, axis=-1, keepdims=True)
        for j in range(2)
    ]
    for j in range(2):
        gates_out[:, j : j + 1] = gates[j]
    rows = send_out.shape[0]
    picks = [slot_rows(row_ref[...], rows, j) for j in range(2)]
    send_out[:, :width] = dot(picks[0] + picks[1], normed).astype(BF16)
    if not first:
        cot = cot_ref[...]
        sent = sum(dot(picks[j], (gates[j] * cot).astype(BF16)) for j in range(2))
        send_out[:, width:] = sent.astype(BF16)


def mixer_backward_body(last, count, scale, experts, *refs):
    (
        g_ref,
        back_ref,
        x_ref,
        middle_ref,
        q_ref,
        k_ref,
        v_ref,
        m_ref,
        lse_ref,
        probs_ref,
        gates_ref,
        routes_ref,
        targets_ref,
        here_ref,
        full_ref,
        lane_ref,
        router_ref,
    ) = refs[:17]
    if last:
        row_prev_ref, gates_prev_ref, g_out, keep_out, give_out, small_out = refs[17:23]
        act_out, send_out = refs[23:25]
        dq_ref, dk_ref, dv_ref, dm_ref = refs[25:]
        y_back, d_back = back_ref[:, : g_ref.shape[1]], back_ref[:, g_ref.shape[1] :]
    else:
        y_ref, g_out, keep_out, give_out, small_out = refs[17:22]
        dq_ref, dk_ref, dv_ref, dm_ref = refs[22:]
        y_back, d_back = y_ref[...], back_ref[...]
    tokens, width = g_ref.shape
    rows = y_back.shape[0]
    lane = lane_ref[...]
    g = g_ref[...]
    middle = middle_ref[...]
    picks = [slot_columns(targets_ref[...], rows, j) for j in range(2)]
    dprobs = jnp.zeros((tokens, experts), F32)
    added = middle
    for j in range(2):
        picked = dot(picks[j], y_back)
        if last:
            added = added + gates_ref[:, j : j + 1] * picked
        dgate = jnp.sum(g * picked, axis=-1, keepdims=True)
        dprobs = dprobs + expert_hot(routes_ref[...], experts, j) * dgate
    if last:
        act_out[...] = added.astype(BF16)
    probs = probs_ref[...]
    dz = (probs * (dprobs - jnp.sum(dprobs * probs, axis=-1, keepdims=True))).astype(BF16)
    scaled, inverse = standardize(middle)
    normed = (scaled * lane[1:2] + lane[6:7]).astype(BF16)
    small_out[7 : 7 + experts, :] = dot(dz, normed, 0, 0)
    rbias_grad = jnp.sum(dz.astype(F32), axis=0, keepdims=True)
    small_out[7 + experts :, :] = jnp.zeros((small_out.shape[0] - 7 - experts, width), F32)
    small_out[7 + experts : 8 + experts, :experts] = rbias_grad
    dn = dot(dz, router_ref[...]) + dot(picks[0] + picks[1], d_back)
    dmiddle, gain_second, shift_second = norm_backward(dn, scaled, inverse, lane[1:2])
    dmiddle = dmiddle + g
    small_out[1:2, :] = gain_second
    small_out[6:7, :] = shift_second
    small_out[5:6, :] = jnp.sum(dmiddle, axis=0, keepdims=True)
    branch = dmiddle.astype(BF16)
    parts = keep_out.shape[0]
    part = width // parts
    core = here_ref[1]

    def store_dense(which, value):
        def store(target):
            for f in range(parts):
                target[f, which % 2] = value[f * part : (f + 1) * part, :].astype(BF16)

        pl.when(core == which // 2)(lambda: store(keep_out))
        pl.when(core != which // 2)(lambda: store(give_out))

    store_dense(3, dot(m_ref[...], branch, 0, 0))
    dm_ref[...] = dot(branch, full_ref[3], 1, 1).astype(BF16)
    valid = lax.broadcasted_iota(jnp.int32, (tokens, tokens), 1) < count
    for pair in range(HEADS // 2):
        cols = slice(pair * 128, pair * 128 + 128)
        q, k, v, dm = q_ref[:, cols], k_ref[:, cols], v_ref[:, cols], dm_ref[:, cols]
        dq = jnp.zeros((tokens, 128), F32)
        dk = jnp.zeros((tokens, 128), F32)
        dv = jnp.zeros((tokens, 128), F32)
        zero = jnp.zeros_like(q)
        for head in (2 * pair, 2 * pair + 1):
            keep = pair_lanes(tokens, head)
            q_one, k_one = jnp.where(keep, q, zero), jnp.where(keep, k, zero)
            dm_one = jnp.where(keep, dm, zero)
            scores = dot(q_one, k, 1, 1) * scale
            weights = jnp.where(
                valid, jnp.exp(scores - lse_ref[:, head : head + 1]), 0.0
            )
            dv = dv + dot(weights.astype(BF16), dm_one, 0, 0)
            dp = dot(dm_one, v, 1, 1)
            ds = weights * (dp - jnp.sum(dp * weights, axis=-1, keepdims=True))
            ds = ds.astype(BF16)
            dq = dq + dot(ds, k_one)
            dk = dk + dot(ds, q_one, 0, 0)
        dq_ref[:, cols] = (dq * scale).astype(BF16)
        dk_ref[:, cols] = (dk * scale).astype(BF16)
        dv_ref[:, cols] = dv.astype(BF16)
    small_out[3:4, :] = jnp.sum(dq_ref[...].astype(F32), axis=0, keepdims=True)
    small_out[4:5, :] = jnp.sum(dv_ref[...].astype(F32), axis=0, keepdims=True)
    scaled, inverse = standardize(x_ref[...])
    normed = (scaled * lane[0:1] + lane[2:3]).astype(BF16)
    dn = jnp.zeros((tokens, width), F32)
    for i, ref in enumerate((dq_ref, dk_ref, dv_ref)):
        store_dense(i, dot(normed, ref[...], 0, 0))
        dn = dn + dot(ref[...], full_ref[i], 1, 1)
    dx, gain_first, shift_first = norm_backward(dn, scaled, inverse, lane[0:1])
    small_out[0:1, :] = gain_first
    small_out[2:3, :] = shift_first
    dx = dx + dmiddle
    g_out[...] = dx
    if last:
        sent = sum(
            dot(
                slot_rows(row_prev_ref[...], send_out.shape[0], j),
                (gates_prev_ref[:, j : j + 1] * dx).astype(BF16),
            )
            for j in range(2)
        )
        send_out[...] = sent.astype(BF16)


CHUNK = 256
BLOCK = 256


def expert_pieces(rows, grads, pieces, biases, slopes, total, back, outs, finish):
    count, width = (grads if rows is None else rows).shape
    part = pieces[0][0].shape[1]
    forward, backward = rows is not None, grads is not None
    keep = forward and not backward
    operands, names = [], []

    def give(name, value):
        if value is not None:
            names.append(name)
            operands.append(value)

    give("rows", rows)
    give("grads", grads)
    for i, (weight_in, weight_out) in enumerate(pieces):
        give(("in", i), weight_in)
        give(("out", i), weight_out)
    give("biases", biases)
    give("slopes", slopes)
    give("total", total)
    give("back", back)
    kind = BF16 if finish else F32
    shapes = []
    if forward and backward:
        shapes.append(("both", shaped((count, 2 * width), kind)))
    elif forward:
        shapes.append(("y", shaped((count, width), kind)))
        shapes.append(("kept", shaped((len(pieces), count, part), BF16)))
    else:
        shapes.append(("d", shaped((count, width), kind)))
    scratch = [pltpu.VMEM((count, width), F32)] * (forward + backward)

    def body(*refs):
        at = dict(zip(names + [n for n, _ in shapes], refs))
        sums = list(refs[len(names) + len(shapes) :])
        y_sum = sums.pop(0) if forward else None
        d_sum = sums.pop(0) if backward else None
        if forward:
            y_sum[...] = at["total"][...] if "total" in at else jnp.zeros_like(y_sum)
        if backward:
            d_sum[...] = at["back"][...] if "back" in at else jnp.zeros_like(d_sum)
        for i in range(len(pieces)):

            def step(c, carry):
                cols = pl.ds(pl.multiple_of(c * CHUNK, CHUNK), CHUNK)
                weight_in, weight_out = at["in", i][:, cols], at["out", i][cols, :]
                for start in range(0, count, BLOCK):
                    here = slice(start, start + BLOCK)
                    if forward:
                        pre = dot(at["rows"][here, :], weight_in) + at["biases"][i : i + 1, cols]
                        active, slope = gelu_both(pre)
                        y_sum[here, :] += dot(active.astype(BF16), weight_out)
                        if keep:
                            at["kept"][i, here, cols] = slope.astype(BF16)
                    else:
                        slope = at["slopes"][i, here, cols].astype(F32)
                    if backward:
                        grad = dot(at["grads"][here, :], weight_out, 1, 1)
                        d_sum[here, :] += dot((grad * slope).astype(BF16), weight_in, 1, 1)
                return carry

            lax.fori_loop(0, part // CHUNK, step, 0)
        if forward and backward:
            at["both"][:, :width] = y_sum[...].astype(kind)
            at["both"][:, width:] = d_sum[...].astype(kind)
        elif forward:
            at["y"][...] = y_sum[...].astype(kind)
        else:
            at["d"][...] = d_sum[...].astype(kind)

    return pl.pallas_call(
        body,
        out_shape=[s for _, s in shapes],
        scratch_shapes=scratch,
        compiler_params=pltpu.CompilerParams(vmem_limit_bytes=VMEM_LIMIT),
        cost_estimate=pl.CostEstimate(
            flops=4 * (forward + backward) * count * width * part * len(pieces),
            bytes_accessed=20_000_000,
            transcendentals=0,
        ),
    )(*operands)


def expert_grads(rows, grads, weight_in, bias_column, weight_out):
    pieces = len(rows)
    count, width = rows[0].shape
    part = weight_in.shape[1]

    def body(*refs):
        rows_refs, grads_refs = refs[:pieces], refs[pieces : 2 * pieces]
        in_ref, bias_ref, out_ref, in_out, bias_out, w_out, sum_out, turned, total = refs[
            2 * pieces :
        ]
        turned[...] = in_ref[...].astype(F32).T.astype(BF16)

        def step(c, carry):
            here = pl.ds(pl.multiple_of(c * CHUNK, CHUNK), CHUNK)
            weight_grad = jnp.zeros((CHUNK, width), F32)
            turned_grad = jnp.zeros((CHUNK, width), F32)
            bias_grad = jnp.zeros((CHUNK, 1), F32)
            for rows_ref, grads_ref in zip(rows_refs, grads_refs):
                pre = dot(turned[here, :], rows_ref[...], 1, 1) + bias_ref[here, :]
                active, slope = gelu_both(pre)
                weight_grad += dot(active.astype(BF16), grads_ref[...])
                grad = (dot(out_ref[here, :], grads_ref[...], 1, 1) * slope).astype(BF16)
                bias_grad += jnp.sum(grad.astype(F32), axis=1, keepdims=True)
                turned_grad += dot(grad, rows_ref[...])
            w_out[here, :] = weight_grad
            total[here, :] = turned_grad
            bias_out[here, :] = bias_grad
            return carry

        lax.fori_loop(0, part // CHUNK, step, 0)
        sum_out[...] = sum(
            jnp.sum(ref[...].astype(F32), axis=0, keepdims=True) for ref in grads_refs
        )
        in_out[...] = total[...].T

    return pl.pallas_call(
        body,
        out_shape=(
            shaped((width, part), F32),
            shaped((part, 1), F32),
            shaped((part, width), F32),
            shaped((1, width), F32),
        ),
        scratch_shapes=[pltpu.VMEM((part, width), BF16), pltpu.VMEM((part, width), F32)],
        compiler_params=pltpu.CompilerParams(vmem_limit_bytes=VMEM_LIMIT),
        cost_estimate=pl.CostEstimate(
            flops=8 * pieces * count * width * part, bytes_accessed=20_000_000, transcendentals=0
        ),
    )(*rows, *grads, weight_in, bias_column, weight_out)


def ahead(value, steps, axis="fsdp"):
    size = lax.axis_size(axis)
    return lax.ppermute(value, axis, [((i + steps) % size, i) for i in range(size)])


def other_core(value):
    size = lax.axis_size("expert")
    return lax.ppermute(value, "expert", [(i ^ 1, i) for i in range(size)])


def ring_pair(first, second):
    next_first, next_second = ahead(first, 1), ahead(second, 1)
    last_first, last_second = ahead(first, 3), ahead(second, 3)
    far_first, far_second = ahead(next_first, 1), ahead(last_second, 3)
    return [
        (first, second),
        (next_first, next_second),
        (far_first, far_second),
        (last_first, last_second),
    ]


def ring_weights(packed, core):
    half = lax.dynamic_slice_in_dim(packed, 2 * core, 2, axis=0)
    after, before = ahead(half, 1), ahead(half, 3)
    far = jnp.concatenate([ahead(after[0:1], 1), ahead(before[1:2], 3)], axis=0)
    mine = [after, far, before]
    return [packed] + mine + [other_core(a) for a in mine]


def swap(rows, stride):
    width = rows.shape[-1]
    moved = lax.all_to_all(
        rows.reshape(-1, stride, width), "expert", split_axis=0, concat_axis=0, tiled=True
    )
    return moved.reshape(-1, width)


def pack_small(norm_gain, mixer_bias, router_weight, router_bias, expert_in_bias):
    part = norm_gain.shape[-1]
    lanes = jnp.concatenate([norm_gain, mixer_bias], axis=1)
    return jnp.concatenate(
        [
            lanes.reshape(-1, part),
            jnp.swapaxes(router_weight, 1, 2).reshape(-1, part),
            jnp.pad(router_bias, ((0, 0), (0, part - router_bias.shape[1]))),
            expert_in_bias.reshape(-1, part),
        ],
        axis=0,
    )


def shards(
    tokens,
    qkv_weight,
    out_weight,
    norm_gain,
    mixer_bias,
    router_weight,
    router_bias,
    expert_in,
    expert_in_bias,
    expert_out,
    expert_out_bias,
    routes,
    cotangent,
):
    count, width = tokens.shape
    parts = lax.axis_size("fsdp")
    experts = lax.axis_size("expert") * expert_in.shape[1]
    capacity = max(2, (3 * count + experts - 1) // experts)
    stride = -(-capacity // 8) * 8
    rows = experts * stride
    held = -(-count // 16) * 16
    part = width // parts
    scale = (width // HEADS) ** (-0.5)
    gather = lambda a: lax.all_gather(a, "fsdp", axis=0, tiled=False)
    fill = ((0, held - count), (0, 0))

    small_all = gather(
        pack_small(norm_gain, mixer_bias, router_weight, router_bias, expert_in_bias)
    )
    at_router = 7 * LAYERS
    at_rbias = at_router + LAYERS * experts
    at_ebias = at_rbias + LAYERS
    lanes = jnp.swapaxes(small_all[:, :at_rbias], 0, 1).reshape(at_rbias, width)
    lane_rows = lanes[:at_router].astype(F32).reshape(LAYERS, 7, width)
    routers = lanes[at_router:].reshape(LAYERS, experts, width)
    rbias = small_all[:, at_rbias:at_ebias, : router_bias.shape[1]]
    rbias = jnp.swapaxes(rbias, 0, 1).reshape(LAYERS, 1, experts).astype(F32)
    ebias = small_all[:, at_ebias:].reshape(parts, LAYERS, -1).astype(F32)

    me, core = lax.axis_index("fsdp"), lax.axis_index("expert") % 2
    here = jnp.stack([me, core]).astype(jnp.int32)
    packed = [
        jnp.concatenate([qkv_weight[layer], out_weight[layer][None]], axis=0)
        for layer in range(LAYERS)
    ]
    weights0 = ring_weights(packed[0], core)
    wide0 = ring_pair(expert_in[0, 0], expert_out[0, 0])
    weights1 = ring_weights(packed[1], core)
    wide1 = ring_pair(expert_in[1, 0], expert_out[1, 0])
    order = (me + jnp.arange(parts)) % parts
    hidden_bias = [jnp.take(ebias[:, layer], order, axis=0) for layer in range(LAYERS)]
    targets = [
        jnp.pad(slot_targets(routes[layer], experts, stride), fill, constant_values=-1)
        for layer in range(LAYERS)
    ]
    turned = [a.T for a in targets]
    named = [jnp.pad(routes[layer], fill) for layer in range(LAYERS)]
    bias_out = [expert_out_bias[layer].astype(F32) for layer in range(LAYERS)]
    x0 = jnp.pad(tokens, fill).astype(F32)
    cot = jnp.pad(cotangent, fill).astype(F32)

    kept_shapes = [shaped((held, width), BF16)] * 4 + [
        shaped((held, 128), F32),
        shaped((held, experts), F32),
        shaped((held, 2), F32),
    ]
    full_rows = shaped((held, width), F32)

    full_shape = shaped((4, width, width), BF16)

    def mixer_forward(first, args, outs):
        return pl.pallas_call(
            functools.partial(mixer_forward_body, first, count, scale, experts),
            out_shape=outs + [full_shape],
            in_specs=[pl.BlockSpec(memory_space=pltpu.SMEM)]
            + [pl.BlockSpec(memory_space=pltpu.VMEM)] * (len(args) - 1),
            compiler_params=pltpu.CompilerParams(vmem_limit_bytes=VMEM_LIMIT),
            cost_estimate=pl.CostEstimate(
                flops=2_000_000_000, bytes_accessed=20_000_000, transcendentals=0
            ),
        )(*args)

    middle0, send, *kept0 = mixer_forward(
        True,
        (here, *weights0, x0, lane_rows[0], routers[0], rbias[0], named[0], turned[0]),
        [full_rows, shaped((rows, width), BF16)] + kept_shapes,
    )
    full0 = kept0.pop()
    rows0 = swap(send, stride)
    near = [wide0[0], wide0[1], wide0[3]]
    near_bias = jnp.stack([hidden_bias[0][0], hidden_bias[0][1], hidden_bias[0][3]])
    start = jnp.broadcast_to(bias_out[0], (rows, width))
    total, near_slopes = expert_pieces(
        rows0, None, near, near_bias, None, start, None, None, False
    )
    result, far_slopes = expert_pieces(
        rows0, None, [wide0[2]], hidden_bias[0][2:3], None, total, None, None, True
    )
    y0 = swap(result, stride)
    gates0 = kept0[6]
    middle1, send, *kept1 = mixer_forward(
        False,
        (here, *weights1, middle0, y0, gates0, targets[0], cot)
        + (lane_rows[1], routers[1], rbias[1], named[1], turned[1]),
        [full_rows, shaped((rows, 2 * width), BF16)] + kept_shapes + [full_rows],
    )
    full1 = kept1.pop()
    x1 = kept1.pop()
    both = swap(send, stride)
    rows1, grads1 = both[:, :width], both[:, width:]
    start = jnp.broadcast_to(bias_out[1], (rows, width))
    (both,) = expert_pieces(
        rows1, grads1, wide1, hidden_bias[1], None, start, None, None, True
    )
    both = swap(both, stride)

    half_shape = shaped((parts, 2, part, width), BF16)
    small_shape = shaped((40, width), F32)
    scratch = [pltpu.VMEM((held, width), BF16)] * 4

    def mixer_backward(last, args, outs):
        specs = [pl.BlockSpec(memory_space=pltpu.VMEM)] * len(args)
        specs[13] = pl.BlockSpec(memory_space=pltpu.SMEM)
        return pl.pallas_call(
            functools.partial(mixer_backward_body, last, count, scale, experts),
            out_shape=outs,
            in_specs=specs,
            scratch_shapes=scratch,
            compiler_params=pltpu.CompilerParams(vmem_limit_bytes=VMEM_LIMIT),
            cost_estimate=pl.CostEstimate(
                flops=4_000_000_000, bytes_accessed=20_000_000, transcendentals=0
            ),
        )(*args)

    q, k, v, m, lse, probs, gates = kept1
    g, keep1, give1, small1, activations, send = mixer_backward(
        True,
        (cot, both, x1, middle1, q, k, v, m, lse, probs, gates, named[1], targets[1])
        + (here, full1, lane_rows[1], routers[1], turned[0], gates0),
        [
            full_rows,
            half_shape,
            half_shape,
            small_shape,
            shaped((held, width), BF16),
            shaped((rows, width), BF16),
        ],
    )
    grads0 = swap(send, stride)
    near_back = expert_pieces(
        None,
        grads0,
        near + [wide0[2]],
        None,
        jnp.concatenate([near_slopes, far_slopes]),
        None,
        None,
        None,
        True,
    )
    back0 = swap(near_back[0], stride)
    q, k, v, m, lse, probs, gates = kept0
    g, keep0, give0, small0 = mixer_backward(
        False,
        (g, back0, x0, middle0, q, k, v, m, lse, probs, gates, named[0], targets[0])
        + (here, full0, lane_rows[0], routers[0], y0),
        [full_rows, half_shape, half_shape, small_shape],
    )

    size = lax.axis_size("expert")
    same_core = [[i for i in range(size) if i % 2 == c] for c in range(2)]

    def reduce_dense(keep, give, more=None):
        chip = (keep.astype(F32) + other_core(give).astype(F32)).astype(BF16)
        chip = chip.reshape(parts, 2 * part, width)
        if more is not None:
            extra = more.shape[0] // 2
            paired = more.astype(BF16).reshape(2, extra, width)
            mine = lax.dynamic_index_in_dim(paired, core, 0, keepdims=False).astype(F32)
            theirs = lax.dynamic_index_in_dim(paired, 1 - core, 0, keepdims=False)
            mine = (mine + other_core(theirs).astype(F32)).astype(BF16)
            chip = jnp.concatenate(
                [chip, jnp.broadcast_to(mine[None], (parts, extra, width))], axis=1
            )
        lines = chip.shape[1]
        got = lax.all_to_all(chip, "fsdp", split_axis=0, concat_axis=0, tiled=True)
        summed = jnp.sum(got.astype(F32), axis=0).astype(BF16)
        each = 2 * lines // size
        got = lax.all_to_all(
            summed.reshape(size // 2, each, width),
            "expert",
            split_axis=0,
            concat_axis=0,
            tiled=True,
            axis_index_groups=same_core,
        )
        final = jnp.sum(got.astype(F32), axis=0).astype(BF16)
        got = lax.all_to_all(
            jnp.broadcast_to(final[None], (size, each, width)),
            "expert",
            split_axis=0,
            concat_axis=0,
            tiled=True,
        )
        got = got.reshape(size // 2, 2, each, width).swapaxes(0, 1).reshape(2, lines, width)
        return got[:, : 2 * part].reshape(4, part, width), got[:, 2 * part :].reshape(-1, width)

    def own_grads(layer, pieces):
        a, b, c, d = expert_grads(
            [p[0] for p in pieces],
            [p[1] for p in pieces],
            expert_in[layer, 0],
            expert_in_bias[layer, 0].astype(F32)[:, None],
            expert_out[layer, 0],
        )
        return a, b[:, 0], c, d[0]

    own1 = own_grads(1, ring_pair(rows1, grads1))
    own0 = own_grads(0, ring_pair(rows0, grads0))
    dense1, _ = reduce_dense(keep1, give1)
    smalls = jnp.concatenate([small0, small1, jnp.zeros((-80 % size, width), F32)])
    dense0, smalls = reduce_dense(keep0, give0, smalls)
    dense_sum = jnp.stack([dense0, dense1]).astype(F32)
    small_sum = smalls[:80].astype(F32).reshape(LAYERS, 40, width)
    mine = lax.dynamic_slice_in_dim(small_sum, me * part, part, axis=2)
    router_grad = jnp.swapaxes(mine[:, 7 : 7 + experts], 1, 2)
    rbias_grad = lax.dynamic_slice_in_dim(
        small_sum[:, 7 + experts], me * router_bias.shape[1], router_bias.shape[1], axis=1
    )
    in_grad, in_bias_grad, out_grad, out_bias_grad = (
        jnp.stack([a, b])[:, None] for a, b in zip(own0, own1)
    )
    return (
        activations[:count],
        g[:count],
        dense_sum[:, :3],
        dense_sum[:, 3],
        mine[:, :2],
        mine[:, 2:7],
        router_grad,
        rbias_grad,
        in_grad,
        in_bias_grad,
        out_grad,
        out_bias_grad,
    )


def solution(mesh):
    tokens_spec = P(("expert", "fsdp"), None)
    params = (
        P(None, None, "fsdp", None),
        P(None, "fsdp", None),
        P(None, None, "fsdp"),
        P(None, None, "fsdp"),
        P(None, "fsdp", None),
        P(None, "fsdp"),
        P(None, "expert", None, "fsdp"),
        P(None, "expert", "fsdp"),
        P(None, "expert", "fsdp", None),
        P(None, "expert", None),
    )
    return jax.shard_map(
        shards,
        mesh=mesh,
        in_specs=(tokens_spec,) + params + (P(None, ("expert", "fsdp"), None), tokens_spec),
        out_specs=(tokens_spec, tokens_spec) + params,
        check_vma=False,
    )
```

time: 1180 us -> 735 us (0.62)
  blocking collectives: 309 us -> 101 us
  Pallas kernels: 0 us -> 188 us
  waiting for transfers between devices: 395 us -> 233 us
  matrix products: 156 us -> 0.44 us
  local copies, waits for them, and re-layouts: 178 us -> 56.6 us
  starting transfers between devices: 41.7 us -> 106 us
  other arithmetic: 64.3 us -> 35.5 us
  between operations: 18.6 us -> 2.02 us
    pallas_call x0 -> x10, Pallas kernels: none -> 188 us  [the longest x4 80.2 us: expert_pieces(): pl.pallas_call(body, out_shape=[s for _, s in shapes], scratch_shapes=scr...]
    ppermute x0 -> x41, waiting for transfers between devices: none -> 187 us  [the longest x32 186 us: ahead(): lax.ppermute(value, axis, [((i + steps) % size, i) for i in range(size)])]
    dot_general x42 -> x2, matrix products: 156 us -> 0.44 us  [dot(): lax.dot_general(left, right, (((left_dim,), (right_dim,)), ((), ())), pre...]
    reduce_scatter x6 -> x0, waiting for transfers between devices: 139 us -> none  [the longest x2 56.4 us: layer_backward(): lax.psum_scatter(contract(grad_pre, weight_in, 1, 1).astype(jnp.bfloat16)...]
    psum x1 -> x0, blocking collectives: 124 us -> none  [layer_backward(): lax.psum(reduced[2].astype(jnp.bfloat16), 'expert').astype(jnp.float32)]
    all_gather x8 -> x0, waiting for transfers between devices: 121 us -> none  [the longest x2 59.1 us: layer_backward(): grad_group = lax.all_gather(grad_own, 'fsdp', axis=0, tiled=True)]
    unnamed x31 -> x0, waiting for transfers between devices: 92.5 us -> none
    unnamed x356 -> x80, local copies, waits for them, and re-layouts: 70.7 us -> 7.35 us
  transfers between devices with their start and end apart: 27 -> 51, of which waited for: 17 -> 18; matrix products, arithmetic and copies ran while one was open for 21% -> 11% of each run, Pallas kernels for 0% -> 18%
where the time goes in v1:
time: 735 us; the launch traced here: 722 us
  waiting for transfers between devices  233 us (32%)
  Pallas kernels  188 us (26%)
  starting transfers between devices  106 us (14%)
  blocking collectives  101 us (14%)
  local copies, waits for them, and re-layouts  56.6 us (8%)
  other arithmetic  35.5 us (5%)
    ppermute x32, waiting for transfers between devices, ahead(): lax.ppermute(value, axis, [((i + steps) % size, i) for i in range(size)])  186 us
    pallas_call x4, Pallas kernels, expert_pieces(): pl.pallas_call(body, out_shape=[s for _, s in shapes], scratch_shapes=scr...  80.2 us
    all_to_all x2, blocking collectives, swap(): lax.all_to_all(rows.reshape(-1, stride, width), 'expert', split_axis=0, c...  63.5 us
    pallas_call x2, Pallas kernels, expert_grads(): pl.pallas_call(body, out_shape=(shaped((width, part), F32), shaped((part,...  56.2 us
    all_gather x1, blocking collectives, shards(): gather = lambda a: lax.all_gather(a, 'fsdp', axis=0, tiled=False)  37.8 us
    ppermute x32, starting transfers between devices, ahead(): lax.ppermute(value, axis, [((i + steps) % size, i) for i in range(size)])  36.1 us
    pallas_call x2, Pallas kernels, mixer_backward(): pl.pallas_call(functools.partial(mixer_backward_body, last, count, scale,...  33.4 us
    all_to_all x4, starting transfers between devices, swap(): lax.all_to_all(rows.reshape(-1, stride, width), 'expert', split_axis=0, c...  30.5 us
  transfers between devices with their start and end apart: 51, of which 18 were waited for; matrix products, arithmetic and copies ran while one was open for 11% of the time, Pallas kernels for 18%

profile of v1, /device:TPU:1, one launch (start us, length us, event | category | flops | bytes accessed | tf_op | source)
XLA Modules:
  0.0 722.0 jit_solution(17635491538663466256)
XLA Ops:
  3.5 3.4 collective-permute-start.7
  6.9 3.2 slice_bitcast_fusion.1
  10.2 2.7 collective-permute-start.14
  12.9 1.6 slice_bitcast_fusion
  14.7 37.8 %all-gather = bf16[352,192]{1,0:T(8,128)(2,1)S(1)} all-gather(bf16[88,192]{1,0:T(8,128)(2,1)S(1)} %fusion.10), channel_id=2, replica_groups=mesh['expert'=32,'fsdp'=4] {'fsdp'}, dimensions={0}, use_global_device_ids=true | all-gather | bytes 168960 | tf_op jit(solution)/shard_map/all_gather | solution.py:524
  55.8 1.7 slice.221
  64.3 1.6 squeeze.67.refs_10_.refs_16_
  68.8 4.2 collective-permute-start.11
  78.8 2.4 collective-permute-start
  81.2 7.6 %shard_map.220 = (f32[208,768]{1,0:T(8,128)}, bf16[768,768]{1,0:T(8,128)(2,1)}, bf16[208,768]{1,0:T(8,128)(2,1)}, bf16[208,768]{1,0:T(8,128)(2,1)}, bf16[208,768...) custom-call(s32[2]{0:T(128)} %pad_add_fusion.refs_0_.refs_13_, ...), custom_call_target="tpu_custom_call" | custom-call | flops 2000000000 | bytes 20000000 | tf_op jit(solution)/shard_map/pallas_call | solution.py:572
  88.9 9.0 %all-to-all-start = ((bf16[32,24,768]{2,1,0:T(8,128)(2,1)}), bf16[32,24,768]{2,1,0:T(8,128)(2,1)}, u32[]{:S(2)}, u32[]{:S(2)}) async-start(bf16[32,24,768]{2,1,0:T(8,128)(2,1)} %bitcast.119), calls=%async_computation | async-start | bytes 2359296 | tf_op jit(solution)/shard_map/all_to_all | solution.py:480
  102.6 15.3 %collective-permute-done.refs_2_ = bf16[2,192,768]{2,1,0:T(8,128)(2,1)S(1)} collective-permute-done((bf16[2,192,768]{2,1,0:T(8,128)(2,1)}, bf16[2,192,768]{2,1,0:T(8,128)(2,1)S(1)}, u32[]{:S(2)}, u32[]{:S(2)}) %collective-permute-start) | collective-permute-done | bytes 589856 | tf_op jit(solution)/shard_map/ppermute | solution.py:450
  118.9 2.7 collective-permute-start.1
  121.5 1.6 broadcast_in_dim.29.refs_8_
  123.1 20.1 %shard_map.221 = (f32[768,768]{1,0:T(8,128)}, bf16[3,768,768]{2,1,0:T(8,128)(2,1)}) custom-call(bf16[768,768]{1,0:T(8,128)(2,1)} %bitcast.12.refs_0_, bf16[768,768]{1,0:T(8,128)(2,1)} %get-tuple-element.166.refs_1_.refs_8_, bf16[768,768]{1,0:T(8,128)(2,1)} %get-tuple-element.164.refs_2_.refs_10_, bf16[768,768]{1,0:T(8,128)(2,1)} %collective-permute-done.14.refs_3_, ...), custom_call_target="tpu_custom_call" | custom-call | flops 5435817984 | bytes 20000000 | tf_op jit(solution)/shard_map/pallas_call | solution.py:384
  143.2 8.6 %shard_map.222 = (bf16[768,768]{1,0:T(8,128)(2,1)}, bf16[1,768,768]{2,1,0:T(8,128)(2,1)}) custom-call(bf16[768,768]{1,0:T(8,128)(2,1)} %bitcast.12.refs_0_, bf16[768,768]{1,0:T(8,128)(2,1)} %collective-permute-done.15.refs_1_.refs_7_, bf16[768,768]{1,0:T(8,128)(2,1)} %collective-permute-done.17.refs_2_.refs_8_, f32[1,768]{1,0:T(1,128)} %get-tuple-element.184.refs_3_, ...), custom_call_target="tpu_custom_call" | custom-call | flops 1811939328 | bytes 20000000 | tf_op jit(solution)/shard_map/pallas_call | solution.py:384
  151.8 9.9 %all-to-all-start.1 = ((bf16[32,24,768]{2,1,0:T(8,128)(2,1)}), bf16[32,24,768]{2,1,0:T(8,128)(2,1)S(1)}, u32[]{:S(2)}, u32[]{:S(2)}) async-start(bf16[32,24,768]{2,1,0:T(8,128)(2,1)} %bitcast.118), calls=%async_computation.1 | async-start | bytes 2359296 | tf_op jit(solution)/shard_map/all_to_all | solution.py:480
  161.7 1.7 slice.220
  167.5 1.7 constant_dynamic-update-slice_fusion.1
  169.1 4.2 collective-permute-done.3
  173.4 1.7 constant_dynamic-update-slice_fusion.refs_3_
  181.1 10.3 %shard_map.223 = (f32[208,768]{1,0:T(8,128)}, bf16[768,1536]{1,0:T(8,128)(2,1)}, bf16[208,768]{1,0:T(8,128)(2,1)}, bf16[208,768]{1,0:T(8,128)(2,1)}, bf16[208,76...) custom-call(s32[2]{0:T(128)} %pad_add_fusion.refs_0_.refs_13_, ...), custom_call_target="tpu_custom_call" | custom-call | flops 2000000000 | bytes 20000000 | tf_op jit(solution)/shard_map/pallas_call | solution.py:572
  191.4 7.0 all-to-all-start.2
  200.0 1.9 collective-permute-start.21
  201.9 24.1 %collective-permute-done.20.refs_4_ = bf16[768,768]{1,0:T(8,128)(2,1)} collective-permute-done((bf16[768,768]{1,0:T(8,128)(2,1)S(1)}, bf16[768,768]{1,0:T(8,128)(2,1)}, u32[]{:S(2)}, u32[]{:S(2)}) %collective-permute-start.20) | collective-permute-done | bytes 1179680 | tf_op jit(solution)/shard_map/ppermute | solution.py:450
  226.0 1.9 collective-permute-start.22
  229.6 1.6 fusion.14
  231.2 20.1 %collective-permute-done.21.refs_5_ = bf16[768,768]{1,0:T(8,128)(2,1)} collective-permute-done((bf16[768,768]{1,0:T(8,128)(2,1)}, bf16[768,768]{1,0:T(8,128)(2,1)}, u32[]{:S(2)}, u32[]{:S(2)}) %collective-permute-start.21) | collective-permute-done | bytes 1179680 | tf_op jit(solution)/shard_map/ppermute | solution.py:450
  251.3 1.8 collective-permute-done.25.refs_8_
  253.0 23.5 %collective-permute-done.22.refs_6_ = bf16[768,768]{1,0:T(8,128)(2,1)} collective-permute-done((bf16[768,768]{1,0:T(8,128)(2,1)}, bf16[768,768]{1,0:T(8,128)(2,1)}, u32[]{:S(2)}, u32[]{:S(2)}) %collective-permute-start.22) | collective-permute-done | bytes 1179680 | tf_op jit(solution)/shard_map/ppermute | solution.py:450
  276.5 1.8 collective-permute-done.24.refs_7_
  278.3 1.6 broadcast_in_dim.30.refs_11_
  279.9 32.0 %shard_map.224 = bf16[768,1536]{1,0:T(8,128)(2,1)} custom-call(bf16[768,768]{1,0:T(8,128)(2,1)} %get-tuple-element.168.refs_0_, bf16[768,768]{1,0:T(8,128)(2,1)} %get-tuple-element.167.refs_1_.refs_4_, bf16[768,768]{1,0:T(8,128)(2,1)} %get-tuple-element.165.refs_2_.refs_8_, bf16[768,768]{1,0:T(8,128)(2,1)} %get-tuple-element.163.refs_3_.refs_10_, ...), custom_call_target="tpu_custom_call" | custom-call | flops 14495514624 | bytes 20000000 | tf_op jit(solution)/shard_map/pallas_call | solution.py:384
  311.9 39.9 %all_to_all.60 = bf16[32,24,1536]{2,1,0:T(8,128)(2,1)} all-to-all(bf16[32,24,1536]{2,1,0:T(8,128)(2,1)} %bitcast.111), channel_id=1, replica_groups=mesh['expert'=32,'fsdp'=4] {'expert'}, dimensions={0} | all-to-all | bytes 4718592 | tf_op jit(solution)/shard_map/all_to_all | solution.py:480
  351.9 16.9 %shard_map.225 = (f32[208,768]{1,0:T(8,128)}, bf16[4,2,192,768]{3,2,1,0:T(8,128)(2,1)}, bf16[4,2,192,768]{3,2,1,0:T(8,128)(2,1)}, f32[40,768]{1,0:T(8,128)}, bf1...) custom-call(f32[208,768]{1,0:T(8,128)} %pad_convert_fusion.1.refs_12_.refs_0_, bf16[768,1536]{1,0:T(8,128)(2,1)} %bitcast.110, ...), custom_call_target="tpu_custom_call" | custom-call | flops 4000000000 | bytes 20000000 | tf_op jit(solution)/shard_map/pallas_call | solution.py:624
  368.8 4.5 all-to-all-start.4
  373.3 3.9 pad_maximum_fusion.refs_9_
  377.9 13.8 %all-to-all-done.4 = bf16[32,24,768]{2,1,0:T(8,128)(2,1)} async-done(((bf16[32,24,768]{2,1,0:T(8,128)(2,1)}), bf16[32,24,768]{2,1,0:T(8,128)(2,1)}, u32[]{:S(2)}, u32[]{:S(2)}) %all-to-all-start.4) | async-done | bytes 1179680 | tf_op jit(solution)/shard_map/all_to_all | solution.py:480
  391.7 19.6 %shard_map.226 = bf16[768,768]{1,0:T(8,128)(2,1)} custom-call(bf16[768,768]{1,0:T(8,128)(2,1)} %bitcast.28.refs_0_.refs_4_, bf16[768,768]{1,0:T(8,128)(2,1)} %get-tuple-element.166.refs_1_.refs_8_, bf16[768,768]{1,0:T(8,128)(2,1)} %get-tuple-element.164.refs_2_.refs_10_, bf16[768,768]{1,0:T(8,128)(2,1)} %collective-permute-done.14.refs_3_, ...), custom_call_target="tpu_custom_call" | custom-call | flops 7247757312 | bytes 20000000 | tf_op jit(solution)/shard_map/pallas_call | solution.py:384
  411.3 23.6 %all_to_all.61 = bf16[32,24,768]{2,1,0:T(8,128)(2,1)} all-to-all(bf16[32,24,768]{2,1,0:T(8,128)(2,1)} %bitcast.122), channel_id=1, replica_groups=mesh['expert'=32,'fsdp'=4] {'expert'}, dimensions={0} | all-to-all | bytes 2359296 | tf_op jit(solution)/shard_map/all_to_all | solution.py:480
  434.9 16.5 %shard_map.227 = (f32[208,768]{1,0:T(8,128)}, bf16[4,2,192,768]{3,2,1,0:T(8,128)(2,1)}, bf16[4,2,192,768]{3,2,1,0:T(8,128)(2,1)}, f32[40,768]{1,0:T(8,128)}) custom-call(f32[208,768]{1,0:T(8,128)} %get-tuple-element.73.refs_0_, bf16[768,768]{1,0:T(8,128)(2,1)} %bitcast.121, f32[208,768]{1,0:T(8,128)} %pad_convert_fusion.refs_8_.refs_2_, ...), custom_call_target="tpu_custom_call" | custom-call | flops 4000000000 | bytes 20000000 | tf_op jit(solution)/shard_map/pallas_call | solution.py:624
  451.9 2.0 add_convert_fusion
  453.9 3.8 all-to-all-start.9
  459.3 2.9 add_convert_fusion.1
  462.2 1.7 pad_maximum_fusion.1
  463.9 22.8 %all-to-all-done.9 = bf16[4,384,768]{2,1,0:T(8,128)(2,1)S(1)} async-done(((bf16[4,384,768]{2,1,0:T(8,128)(2,1)}), bf16[4,384,768]{2,1,0:T(8,128)(2,1)S(1)}, u32[]{:S(2)}, u32[]{:S(2)}) %all-to-all-start.9) | async-done | bytes 2359328 | tf_op jit(solution)/shard_map/all_to_all | solution.py:686
  488.1 3.7 all-to-all-start.6
  491.8 2.6 collective-permute-start.35
  496.0 2.6 collective-permute-start.38
  498.6 48.5 %collective-permute-done.35.refs_1_ = bf16[768,768]{1,0:T(8,128)(2,1)} collective-permute-done((bf16[768,768]{1,0:T(8,128)(2,1)}, bf16[768,768]{1,0:T(8,128)(2,1)}, u32[]{:S(2)}, u32[]{:S(2)}) %collective-permute-start.35) | collective-permute-done | bytes 1179680 | tf_op jit(solution)/shard_map/ppermute | solution.py:450
  548.6 23.8 %collective-permute-done.29.refs_1_ = bf16[768,768]{1,0:T(8,128)(2,1)} collective-permute-done((bf16[768,768]{1,0:T(8,128)(2,1)}, bf16[768,768]{1,0:T(8,128)(2,1)}, u32[]{:S(2)}, u32[]{:S(2)}) %collective-permute-start.29) | collective-permute-done | bytes 1179680 | tf_op jit(solution)/shard_map/ppermute | solution.py:450
  574.5 3.0 reduce_sum.70
  577.4 4.3 all-to-all-start.10
  583.7 7.4 %all-to-all-done.10 = bf16[16,24,768]{2,1,0:T(8,128)(2,1)} async-done(((bf16[16,24,768]{2,1,0:T(8,128)(2,1)}), bf16[16,24,768]{2,1,0:T(8,128)(2,1)}, u32[]{:S(2)}, u32[]{:S(2)}) %all-to-all-start.10) | async-done | bytes 589856 | tf_op jit(solution)/shard_map/all_to_all | solution.py:689
  591.0 3.6 all-to-all-start.7
  598.8 2.4 collective-permute-start.30
  601.2 21.7 %collective-permute-done.36.refs_2_ = bf16[768,768]{1,0:T(8,128)(2,1)} collective-permute-done((bf16[768,768]{1,0:T(8,128)(2,1)}, bf16[768,768]{1,0:T(8,128)(2,1)}, u32[]{:S(2)}, u32[]{:S(2)}) %collective-permute-start.36) | collective-permute-done | bytes 1179680 | tf_op jit(solution)/shard_map/ppermute | solution.py:450
  625.5 7.8 %all-to-all-start.11 = ((bf16[32,24,768]{2,1,0:T(8,128)(2,1)}), bf16[32,24,768]{2,1,0:T(8,128)(2,1)S(1)}, u32[]{:S(2)}, u32[]{:S(2)}) async-start(bf16[32,24,768]{2,1,0:T(8,128)(2,1)} %broadcast_in_dim.34), calls=%async_computation.11 | async-start | bytes 2359296 | tf_op jit(solution)/shard_map/all_to_all | solution.py:698
  633.3 28.0 %shard_map.229 = (f32[768,768]{1,0:T(8,128)}, f32[768,1]{1,0:T(8,128)}, f32[768,768]{1,0:T(8,128)}, f32[1,768]{1,0:T(1,128)}) custom-call(bf16[768,768]{1,0:T(8,128)(2,1)} %get-tuple-element.168.refs_0_, bf16[768,768]{1,0:T(8,128)(2,1)} %collective-permute-done.35.refs_1_, bf16[768,768]{1,0:T(8,128)(2,1)} %collective-permute-done.36.refs_2_, ...), custom_call_target="tpu_custom_call" | custom-call | flops 14495514624 | bytes 20000000 | tf_op jit(solution)/shard_map/pallas_call | solution.py:432
  665.1 7.9 %all-to-all-start.8 = ((bf16[32,27,768]{2,1,0:T(8,128)(2,1)}), bf16[32,27,768]{2,1,0:T(8,128)(2,1)S(1)}, u32[]{:S(2)}, u32[]{:S(2)}) async-start(bf16[32,27,768]{2,1,0:T(8,128)(2,1)} %broadcast_in_dim.33), calls=%async_computation.8 | async-start | bytes 3145728 | tf_op jit(solution)/shard_map/all_to_all | solution.py:698
  673.9 28.2 %shard_map.228 = (f32[768,768]{1,0:T(8,128)}, f32[768,1]{1,0:T(8,128)}, f32[768,768]{1,0:T(8,128)}, f32[1,768]{1,0:T(1,128)}) custom-call(bf16[768,768]{1,0:T(8,128)(2,1)} %bitcast.12.refs_0_, bf16[768,768]{1,0:T(8,128)(2,1)} %collective-permute-done.29.refs_1_, bf16[768,768]{1,0:T(8,128)(2,1)} %collective-permute-done.30.refs_2_, ...), custom_call_target="tpu_custom_call" | custom-call | flops 14495514624 | bytes 20000000 | tf_op jit(solution)/shard_map/pallas_call | solution.py:432
  705.2 5.0 maximum_bitcast_fusion
  710.2 2.5 maximum_bitcast_fusion.1
  716.8 2.0 slice.241
  (251 shorter events, 73.0 us)
Async XLA Ops:
  3.5 52.2 %collective-permute-start.7 = (bf16[2,192,768]{2,1,0:T(8,128)(2,1)S(1)}, bf16[2,192,768]{2,1,0:T(8,128)(2,1)}, u32[]{:S(2)}, u32[]{:S(2)}) collective-permute-start(bf16[2,192,768]{2,1,0:T(8,128)(2,1)S(1)} %fusion.2), channel_id=1, source_target_pairs={{1,0},{2,1},{3,2},{0,3},{5,4},{6,5},{7,6},{4,7},{9,8},{10,9},{11,1... | collective-permute-start | bytes 1769480 | tf_op jit(solution)/shard_map/ppermute | solution.py:450
  6.9 51.8 %collective-permute-start.9 = (bf16[2,192,768]{2,1,0:T(8,128)(2,1)S(1)}, bf16[2,192,768]{2,1,0:T(8,128)(2,1)}, u32[]{:S(2)}, u32[]{:S(2)}) collective-permute-start(bf16[2,192,768]{2,1,0:T(8,128)(2,1)S(1)} %fusion.2), channel_id=1, source_target_pairs={{3,0},{0,1},{1,2},{2,3},{7,4},{4,5},{5,6},{6,7},{11,8},{8,9},{9,10... | collective-permute-start | bytes 1769480 | tf_op jit(solution)/shard_map/ppermute | solution.py:450
  10.2 43.6 %copy-start.28 = (s32[2,197,2]{1,2,0:T(2,128)S(1)}, s32[2,197,2]{1,2,0:T(2,128)}, u32[]{:S(2)}) copy-start(s32[2,197,2]{1,2,0:T(2,128)} %param.26) | copy-start | bytes 9460
  10.2 88.9 %collective-permute-start.14 = (bf16[768,768]{1,0:T(8,128)(2,1)}, bf16[768,768]{1,0:T(8,128)(2,1)}, u32[]{:S(2)}, u32[]{:S(2)}) collective-permute-start(bf16[768,768]{1,0:T(8,128)(2,1)} %get-tuple-element.166.refs_1_.refs_8_), channel_id=1, source_target_pairs={{1,0},{2,1},{3,2},{0,3},{5,4},{6,5},{7,6},{4,7},{9,8},{10,9},{11,1... | collective-permute-start | bytes 3538952 | tf_op jit(solution)/shard_map/ppermute | solution.py:450
  14.5 85.2 %collective-permute-start.16 = (bf16[768,768]{1,0:T(8,128)(2,1)}, bf16[768,768]{1,0:T(8,128)(2,1)}, u32[]{:S(2)}, u32[]{:S(2)}) collective-permute-start(bf16[768,768]{1,0:T(8,128)(2,1)} %get-tuple-element.164.refs_2_.refs_10_), channel_id=1, source_target_pairs={{3,0},{0,1},{1,2},{2,3},{7,4},{4,5},{5,6},{6,7},{11,8},{8,9},{9,10... | collective-permute-start | bytes 3538952 | tf_op jit(solution)/shard_map/ppermute | solution.py:450
  57.5 15.4 %collective-permute-start.8 = (bf16[1,192,768]{2,1,0:T(8,128)(2,1)}, bf16[1,192,768]{2,1,0:T(8,128)(2,1)}, u32[]{:S(2)}, u32[]{:S(2)}) collective-permute-start(bf16[1,192,768]{2,1,0:T(8,128)(2,1)} %slice.221), channel_id=1, source_target_pairs={{1,0},{2,1},{3,2},{0,3},{5,4},{6,5},{7,6},{4,7},{9,8},{10,9},{11,1... | collective-permute-start | bytes 884744 | tf_op jit(solution)/shard_map/ppermute | solution.py:450
  59.7 14.2 %collective-permute-start.10 = (bf16[1,192,768]{2,1,0:T(8,128)(2,1)S(1)}, bf16[1,192,768]{2,1,0:T(8,128)(2,1)S(1)}, u32[]{:S(2)}, u32[]{:S(2)}) collective-permute-start(bf16[1,192,768]{2,1,0:T(8,128)(2,1)S(1)} %slice.222), channel_id=1, source_target_pairs={{3,0},{0,1},{1,2},{2,3},{7,4},{4,5},{5,6},{6,7},{11,8},{8,9},{9,10... | collective-permute-start | bytes 884744 | tf_op jit(solution)/shard_map/ppermute | solution.py:450
  68.8 8.5 %collective-permute-start.11 = (bf16[2,192,768]{2,1,0:T(8,128)(2,1)}, bf16[2,192,768]{2,1,0:T(8,128)(2,1)S(1)}, u32[]{:S(2)}, u32[]{:S(2)}) collective-permute-start(bf16[2,192,768]{2,1,0:T(8,128)(2,1)} %collective-permute-done.7.refs_2_), channel_id=1, source_target_pairs={{4,0},{0,4},{12,8},{8,12},{20,16},{16,20},{28,24},{24,28},{36,32},... | collective-permute-start | bytes 1769480 | tf_op jit(solution)/shard_map/ppermute | solution.py:455
  72.9 5.6 collective-permute-start.13
  74.0 4.9 collective-permute-start.12
  77.3 41.6 %collective-permute-start.18 = (bf16[768,768]{1,0:T(8,128)(2,1)}, bf16[768,768]{1,0:T(8,128)(2,1)S(1)}, u32[]{:S(2)}, u32[]{:S(2)}) collective-permute-start(bf16[768,768]{1,0:T(8,128)(2,1)} %get-tuple-element.164.refs_2_.refs_10_), channel_id=1, source_target_pairs={{1,0},{2,1},{3,2},{0,3},{5,4},{6,5},{7,6},{4,7},{9,8},{10,9},{11,1... | collective-permute-start | bytes 3538952 | tf_op jit(solution)/shard_map/ppermute | solution.py:450
  78.5 43.0 %collective-permute-start.19 = (bf16[768,768]{1,0:T(8,128)(2,1)}, bf16[768,768]{1,0:T(8,128)(2,1)}, u32[]{:S(2)}, u32[]{:S(2)}) collective-permute-start(bf16[768,768]{1,0:T(8,128)(2,1)} %get-tuple-element.166.refs_1_.refs_8_), channel_id=1, source_target_pairs={{3,0},{0,1},{1,2},{2,3},{7,4},{4,5},{5,6},{6,7},{11,8},{8,9},{9,10... | collective-permute-start | bytes 3538952 | tf_op jit(solution)/shard_map/ppermute | solution.py:450
  78.8 39.1 %collective-permute-start = (bf16[2,192,768]{2,1,0:T(8,128)(2,1)}, bf16[2,192,768]{2,1,0:T(8,128)(2,1)S(1)}, u32[]{:S(2)}, u32[]{:S(2)}) collective-permute-start(bf16[2,192,768]{2,1,0:T(8,128)(2,1)} %fusion.3), channel_id=1, source_target_pairs={{1,0},{2,1},{3,2},{0,3},{5,4},{6,5},{7,6},{4,7},{9,8},{10,9},{11,1... | collective-permute-start | bytes 1769480 | tf_op jit(solution)/shard_map/ppermute | solution.py:450
  88.9 13.7 %copy-start.24 = (bf16[2,1,768]{2,0,1:T(2,128)(2,1)S(1)}, bf16[2,1,768]{2,0,1:T(2,128)(2,1)}, u32[]{:S(2)}) copy-start(bf16[2,1,768]{2,0,1:T(2,128)(2,1)} %param.25) | copy-start | bytes 9220
  88.9 32.6 %all-to-all-start = ((bf16[32,24,768]{2,1,0:T(8,128)(2,1)}), bf16[32,24,768]{2,1,0:T(8,128)(2,1)}, u32[]{:S(2)}, u32[]{:S(2)}) async-start(bf16[32,24,768]{2,1,0:T(8,128)(2,1)} %bitcast.119), calls=%async_computation | async-start | bytes 2359296 | tf_op jit(solution)/shard_map/all_to_all | solution.py:480
  99.1 44.0 %collective-permute-start.15 = (bf16[768,768]{1,0:T(8,128)(2,1)}, bf16[768,768]{1,0:T(8,128)(2,1)}, u32[]{:S(2)}, u32[]{:S(2)}) collective-permute-start(bf16[768,768]{1,0:T(8,128)(2,1)} %collective-permute-done.14.refs_3_), channel_id=1, source_target_pairs={{1,0},{2,1},{3,2},{0,3},{5,4},{6,5},{7,6},{4,7},{9,8},{10,9},{11,1... | collective-permute-start | bytes 3538952 | tf_op jit(solution)/shard_map/ppermute | solution.py:450
  99.7 43.5 %collective-permute-start.17 = (bf16[768,768]{1,0:T(8,128)(2,1)}, bf16[768,768]{1,0:T(8,128)(2,1)}, u32[]{:S(2)}, u32[]{:S(2)}) collective-permute-start(bf16[768,768]{1,0:T(8,128)(2,1)} %collective-permute-done.16.refs_6_), channel_id=1, source_target_pairs={{3,0},{0,1},{1,2},{2,3},{7,4},{4,5},{5,6},{6,7},{11,8},{8,9},{9,10... | collective-permute-start | bytes 3538952 | tf_op jit(solution)/shard_map/ppermute | solution.py:450
  117.9 48.9 %copy-start.9 = (bf16[2,192,768]{2,1,0:T(8,128)(2,1)}, bf16[2,192,768]{2,1,0:T(8,128)(2,1)S(1)}, u32[]{:S(2)}) copy-start(bf16[2,192,768]{2,1,0:T(8,128)(2,1)S(1)} %collective-permute-done.refs_2_) | copy-start | bytes 1769476
  117.9 43.8 %collective-permute-start.2 = (bf16[2,192,768]{2,1,0:T(8,128)(2,1)}, bf16[2,192,768]{2,1,0:T(8,128)(2,1)}, u32[]{:S(2)}, u32[]{:S(2)}) collective-permute-start(bf16[2,192,768]{2,1,0:T(8,128)(2,1)} %fusion.3), channel_id=1, source_target_pairs={{3,0},{0,1},{1,2},{2,3},{7,4},{4,5},{5,6},{6,7},{11,8},{8,9},{9,10... | collective-permute-start | bytes 1769480 | tf_op jit(solution)/shard_map/ppermute | solution.py:450
  118.9 48.6 %collective-permute-start.1 = (bf16[1,192,768]{2,1,0:T(8,128)(2,1)}, bf16[1,192,768]{2,1,0:T(8,128)(2,1)}, u32[]{:S(2)}, u32[]{:S(2)}) collective-permute-start(bf16[1,192,768]{2,1,0:T(8,128)(2,1)} %slice.219), channel_id=1, source_target_pairs={{1,0},{2,1},{3,2},{0,3},{5,4},{6,5},{7,6},{4,7},{9,8},{10,9},{11,1... | collective-permute-start | bytes 884744 | tf_op jit(solution)/shard_map/ppermute | solution.py:450
  151.7 12.4 %copy-start.15 = (bf16[32,4,192]{2,0,1:T(8,128)(2,1)S(1)}, bf16[32,4,192]{2,0,1:T(8,128)(2,1)}, u32[]{:S(2)}) copy-start(bf16[32,4,192]{2,0,1:T(8,128)(2,1)} %get-tuple-element.173) | copy-start | bytes 147460
  151.7 13.2 %copy-start.26 = (f32[4,8]{1,0:T(4,128)S(1)}, f32[4,8]{1,0:T(4,128)}, u32[]{:S(2)}) copy-start(f32[4,8]{1,0:T(4,128)} %get-tuple-element.159) | copy-start | bytes 388
  151.7 13.8 %copy-start.25 = (s32[1,197,2]{1,2,0:T(2,128)S(1)}, s32[1,197,2]{1,2,0:T(2,128)}, u32[]{:S(2)}) copy-start(s32[1,197,2]{1,2,0:T(2,128)} %get-tuple-element.185) | copy-start | bytes 4732
  151.8 28.3 %all-to-all-start.1 = ((bf16[32,24,768]{2,1,0:T(8,128)(2,1)}), bf16[32,24,768]{2,1,0:T(8,128)(2,1)S(1)}, u32[]{:S(2)}, u32[]{:S(2)}) async-start(bf16[32,24,768]{2,1,0:T(8,128)(2,1)} %bitcast.118), calls=%async_computation.1 | async-start | bytes 2359296 | tf_op jit(solution)/shard_map/all_to_all | solution.py:480
  161.7 16.1 %copy-start.13 = (bf16[197,768]{1,0:T(8,128)(2,1)S(1)}, bf16[197,768]{1,0:T(8,128)(2,1)}, u32[]{:S(2)}) copy-start(bf16[197,768]{1,0:T(8,128)(2,1)} %param.27) | copy-start | bytes 907780
  163.5 9.9 %collective-permute-start.3 = (bf16[1,192,768]{2,1,0:T(8,128)(2,1)}, bf16[1,192,768]{2,1,0:T(8,128)(2,1)}, u32[]{:S(2)}, u32[]{:S(2)}) collective-permute-start(bf16[1,192,768]{2,1,0:T(8,128)(2,1)} %slice.220), channel_id=1, source_target_pairs={{3,0},{0,1},{1,2},{2,3},{7,4},{4,5},{5,6},{6,7},{11,8},{8,9},{9,10... | collective-permute-start | bytes 884744 | tf_op jit(solution)/shard_map/ppermute | solution.py:450
  166.9 12.9 %collective-permute-start.4 = (bf16[2,192,768]{2,1,0:T(8,128)(2,1)S(1)}, bf16[2,192,768]{2,1,0:T(8,128)(2,1)}, u32[]{:S(2)}, u32[]{:S(2)}) collective-permute-start(bf16[2,192,768]{2,1,0:T(8,128)(2,1)S(1)} %collective-permute-done.refs_2_), channel_id=1, source_target_pairs={{4,0},{0,4},{12,8},{8,12},{20,16},{16,20},{28,24},{24,28},{36,32},... | collective-permute-start | bytes 1769480 | tf_op jit(solution)/shard_map/ppermute | solution.py:455
  167.2 12.6 %collective-permute-start.6 = (bf16[2,192,768]{2,1,0:T(8,128)(2,1)}, bf16[2,192,768]{2,1,0:T(8,128)(2,1)}, u32[]{:S(2)}, u32[]{:S(2)}) collective-permute-start(bf16[2,192,768]{2,1,0:T(8,128)(2,1)} %collective-permute-done.2.refs_4_), channel_id=1, source_target_pairs={{4,0},{0,4},{12,8},{8,12},{20,16},{16,20},{28,24},{24,28},{36,32},... | collective-permute-start | bytes 1769480 | tf_op jit(solution)/shard_map/ppermute | solution.py:455
  175.1 4.8 collective-permute-start.5
  191.4 38.2 %all-to-all-start.2 = ((bf16[32,24,1536]{2,1,0:T(8,128)(2,1)}), bf16[32,24,1536]{2,1,0:T(8,128)(2,1)S(1)}, u32[]{:S(2)}, u32[]{:S(2)}) async-start(bf16[32,24,1536]{2,1,0:T(8,128)(2,1)} %bitcast.109), calls=%async_computation.2 | async-start | bytes 4718592 | tf_op jit(solution)/shard_map/all_to_all | solution.py:480
  198.5 27.5 %collective-permute-start.20 = (bf16[768,768]{1,0:T(8,128)(2,1)S(1)}, bf16[768,768]{1,0:T(8,128)(2,1)}, u32[]{:S(2)}, u32[]{:S(2)}) collective-permute-start(bf16[768,768]{1,0:T(8,128)(2,1)S(1)} %copy-done.10), channel_id=1, source_target_pairs={{1,0},{2,1},{3,2},{0,3},{5,4},{6,5},{7,6},{4,7},{9,8},{10,9},{11,1... | collective-permute-start | bytes 3538952 | tf_op jit(solution)/shard_map/ppermute | solution.py:450
  199.2 28.7 %collective-permute-start.23 = (bf16[768,768]{1,0:T(8,128)(2,1)}, bf16[768,768]{1,0:T(8,128)(2,1)}, u32[]{:S(2)}, u32[]{:S(2)}) collective-permute-start(bf16[768,768]{1,0:T(8,128)(2,1)} %get-tuple-element.163.refs_3_.refs_10_), channel_id=1, source_target_pairs={{3,0},{0,1},{1,2},{2,3},{7,4},{4,5},{5,6},{6,7},{11,8},{8,9},{9,10... | collective-permute-start | bytes 3538952 | tf_op jit(solution)/shard_map/ppermute | solution.py:450
  200.0 51.3 %collective-permute-start.21 = (bf16[768,768]{1,0:T(8,128)(2,1)}, bf16[768,768]{1,0:T(8,128)(2,1)}, u32[]{:S(2)}, u32[]{:S(2)}) collective-permute-start(bf16[768,768]{1,0:T(8,128)(2,1)} %get-tuple-element.163.refs_3_.refs_10_), channel_id=1, source_target_pairs={{1,0},{2,1},{3,2},{0,3},{5,4},{6,5},{7,6},{4,7},{9,8},{10,9},{11,1... | collective-permute-start | bytes 3538952 | tf_op jit(solution)/shard_map/ppermute | solution.py:450
  201.9 51.1 %collective-permute-start.25 = (bf16[768,768]{1,0:T(8,128)(2,1)S(1)}, bf16[768,768]{1,0:T(8,128)(2,1)}, u32[]{:S(2)}, u32[]{:S(2)}) collective-permute-start(bf16[768,768]{1,0:T(8,128)(2,1)S(1)} %copy-done.10), channel_id=1, source_target_pairs={{3,0},{0,1},{1,2},{2,3},{7,4},{4,5},{5,6},{6,7},{11,8},{8,9},{9,10... | collective-permute-start | bytes 3538952 | tf_op jit(solution)/shard_map/ppermute | solution.py:450
  226.0 50.6 %collective-permute-start.22 = (bf16[768,768]{1,0:T(8,128)(2,1)}, bf16[768,768]{1,0:T(8,128)(2,1)}, u32[]{:S(2)}, u32[]{:S(2)}) collective-permute-start(bf16[768,768]{1,0:T(8,128)(2,1)} %collective-permute-done.20.refs_4_), channel_id=1, source_target_pairs={{1,0},{2,1},{3,2},{0,3},{5,4},{6,5},{7,6},{4,7},{9,8},{10,9},{11,1... | collective-permute-start | bytes 3538952 | tf_op jit(solution)/shard_map/ppermute | solution.py:450
  227.9 50.4 %collective-permute-start.24 = (bf16[768,768]{1,0:T(8,128)(2,1)}, bf16[768,768]{1,0:T(8,128)(2,1)}, u32[]{:S(2)}, u32[]{:S(2)}) collective-permute-start(bf16[768,768]{1,0:T(8,128)(2,1)} %collective-permute-done.23.refs_9_), channel_id=1, source_target_pairs={{3,0},{0,1},{1,2},{2,3},{7,4},{4,5},{5,6},{6,7},{11,8},{8,9},{9,10... | collective-permute-start | bytes 3538952 | tf_op jit(solution)/shard_map/ppermute | solution.py:450
  351.8 21.4 %copy-start.4 = (bf16[3,768,768]{2,1,0:T(8,128)(2,1)S(1)}, bf16[3,768,768]{2,1,0:T(8,128)(2,1)}, u32[]{:S(2)}) copy-start(bf16[3,768,768]{2,1,0:T(8,128)(2,1)} %get-tuple-element.75) | copy-start | bytes 10616836
  368.8 23.0 %all-to-all-start.4 = ((bf16[32,24,768]{2,1,0:T(8,128)(2,1)}), bf16[32,24,768]{2,1,0:T(8,128)(2,1)}, u32[]{:S(2)}, u32[]{:S(2)}) async-start(bf16[32,24,768]{2,1,0:T(8,128)(2,1)} %bitcast.120), calls=%async_computation.4 | async-start | bytes 2359296 | tf_op jit(solution)/shard_map/all_to_all | solution.py:480
  377.1 74.8 %collective-permute-start.28 = (bf16[4,2,192,768]{3,2,1,0:T(8,128)(2,1)}, bf16[4,2,192,768]{3,2,1,0:T(8,128)(2,1)S(1)}, u32[]{:S(2)}, u32[]{:S(2)}) collective-permute-start(bf16[4,2,192,768]{3,2,1,0:T(8,128)(2,1)} %get-tuple-element.90), channel_id=1, source_target_pairs={{4,0},{0,4},{12,8},{8,12},{20,16},{16,20},{28,24},{24,28},{36,32},... | collective-permute-start | bytes 7077896 | tf_op jit(solution)/shard_map/ppermute | solution.py:455
  434.9 17.0 %copy-start.5 = (bf16[4,2,192,768]{3,2,1,0:T(8,128)(2,1)S(1)}, bf16[4,2,192,768]{3,2,1,0:T(8,128)(2,1)}, u32[]{:S(2)}) copy-start(bf16[4,2,192,768]{3,2,1,0:T(8,128)(2,1)} %get-tuple-element.89) | copy-start | bytes 7077892
  451.4 7.8 %collective-permute-start.26 = (bf16[4,2,192,768]{3,2,1,0:T(8,128)(2,1)}, bf16[4,2,192,768]{3,2,1,0:T(8,128)(2,1)}, u32[]{:S(2)}, u32[]{:S(2)}) collective-permute-start(bf16[4,2,192,768]{3,2,1,0:T(8,128)(2,1)} %get-tuple-element.86), channel_id=1, source_target_pairs={{4,0},{0,4},{12,8},{8,12},{20,16},{16,20},{28,24},{24,28},{36,32},... | collective-permute-start | bytes 7077896 | tf_op jit(solution)/shard_map/ppermute | solution.py:455
  453.9 32.9 %all-to-all-start.9 = ((bf16[4,384,768]{2,1,0:T(8,128)(2,1)}), bf16[4,384,768]{2,1,0:T(8,128)(2,1)S(1)}, u32[]{:S(2)}, u32[]{:S(2)}) async-start(bf16[4,384,768]{2,1,0:T(8,128)(2,1)} %bitcast.40), calls=%async_computation.9 | async-start | bytes 4718592 | tf_op jit(solution)/shard_map/all_to_all | solution.py:686
  457.9 1.3 collective-permute-start.27
  488.1 89.3 %all-to-all-start.6 = ((bf16[4,432,768]{2,1,0:T(8,128)(2,1)}), bf16[4,432,768]{2,1,0:T(8,128)(2,1)S(1)}, u32[]{:S(2)}, u32[]{:S(2)}) async-start(bf16[4,432,768]{2,1,0:T(8,128)(2,1)} %pad_maximum_fusion.1), calls=%async_computation.6 | async-start | bytes 5308416 | tf_op jit(solution)/shard_map/all_to_all | solution.py:686
  491.8 55.3 %collective-permute-start.35 = (bf16[768,768]{1,0:T(8,128)(2,1)}, bf16[768,768]{1,0:T(8,128)(2,1)}, u32[]{:S(2)}, u32[]{:S(2)}) collective-permute-start(bf16[768,768]{1,0:T(8,128)(2,1)} %get-tuple-element.168.refs_0_), channel_id=1, source_target_pairs={{1,0},{2,1},{3,2},{0,3},{5,4},{6,5},{7,6},{4,7},{9,8},{10,9},{11,1... | collective-permute-start | bytes 3538952 | tf_op jit(solution)/shard_map/ppermute | solution.py:450
  494.5 77.9 %collective-permute-start.29 = (bf16[768,768]{1,0:T(8,128)(2,1)}, bf16[768,768]{1,0:T(8,128)(2,1)}, u32[]{:S(2)}, u32[]{:S(2)}) collective-permute-start(bf16[768,768]{1,0:T(8,128)(2,1)} %bitcast.12.refs_0_), channel_id=1, source_target_pairs={{1,0},{2,1},{3,2},{0,3},{5,4},{6,5},{7,6},{4,7},{9,8},{10,9},{11,1... | collective-permute-start | bytes 3538952 | tf_op jit(solution)/shard_map/ppermute | solution.py:450
  495.0 78.5 %collective-permute-start.39 = (bf16[768,768]{1,0:T(8,128)(2,1)}, bf16[768,768]{1,0:T(8,128)(2,1)}, u32[]{:S(2)}, u32[]{:S(2)}) collective-permute-start(bf16[768,768]{1,0:T(8,128)(2,1)} %get-tuple-element.167.refs_1_.refs_4_), channel_id=1, source_target_pairs={{3,0},{0,1},{1,2},{2,3},{7,4},{4,5},{5,6},{6,7},{11,8},{8,9},{9,10... | collective-permute-start | bytes 3538952 | tf_op jit(solution)/shard_map/ppermute | solution.py:450
  495.9 102.5 %collective-permute-start.37 = (bf16[768,768]{1,0:T(8,128)(2,1)}, bf16[768,768]{1,0:T(8,128)(2,1)}, u32[]{:S(2)}, u32[]{:S(2)}) collective-permute-start(bf16[768,768]{1,0:T(8,128)(2,1)} %get-tuple-element.168.refs_0_), channel_id=1, source_target_pairs={{3,0},{0,1},{1,2},{2,3},{7,4},{4,5},{5,6},{6,7},{11,8},{8,9},{9,10... | collective-permute-start | bytes 3538952 | tf_op jit(solution)/shard_map/ppermute | solution.py:450
  496.0 102.9 %collective-permute-start.38 = (bf16[768,768]{1,0:T(8,128)(2,1)}, bf16[768,768]{1,0:T(8,128)(2,1)}, u32[]{:S(2)}, u32[]{:S(2)}) collective-permute-start(bf16[768,768]{1,0:T(8,128)(2,1)} %get-tuple-element.167.refs_1_.refs_4_), channel_id=1, source_target_pairs={{1,0},{2,1},{3,2},{0,3},{5,4},{6,5},{7,6},{4,7},{9,8},{10,9},{11,1... | collective-permute-start | bytes 3538952 | tf_op jit(solution)/shard_map/ppermute | solution.py:450
  547.1 75.8 %collective-permute-start.36 = (bf16[768,768]{1,0:T(8,128)(2,1)}, bf16[768,768]{1,0:T(8,128)(2,1)}, u32[]{:S(2)}, u32[]{:S(2)}) collective-permute-start(bf16[768,768]{1,0:T(8,128)(2,1)} %collective-permute-done.35.refs_1_), channel_id=1, source_target_pairs={{1,0},{2,1},{3,2},{0,3},{5,4},{6,5},{7,6},{4,7},{9,8},{10,9},{11,1... | collective-permute-start | bytes 3538952 | tf_op jit(solution)/shard_map/ppermute | solution.py:450
  572.4 52.1 %collective-permute-start.33 = (bf16[768,768]{1,0:T(8,128)(2,1)}, bf16[768,768]{1,0:T(8,128)(2,1)}, u32[]{:S(2)}, u32[]{:S(2)}) collective-permute-start(bf16[768,768]{1,0:T(8,128)(2,1)} %bitcast.28.refs_0_.refs_4_), channel_id=1, source_target_pairs={{3,0},{0,1},{1,2},{2,3},{7,4},{4,5},{5,6},{6,7},{11,8},{8,9},{9,10... | collective-permute-start | bytes 3538952 | tf_op jit(solution)/shard_map/ppermute | solution.py:450
  573.5 59.8 %collective-permute-start.40 = (bf16[768,768]{1,0:T(8,128)(2,1)}, bf16[768,768]{1,0:T(8,128)(2,1)}, u32[]{:S(2)}, u32[]{:S(2)}) collective-permute-start(bf16[768,768]{1,0:T(8,128)(2,1)} %collective-permute-done.39.refs_7_), channel_id=1, source_target_pairs={{3,0},{0,1},{1,2},{2,3},{7,4},{4,5},{5,6},{6,7},{11,8},{8,9},{9,10... | collective-permute-start | bytes 3538952 | tf_op jit(solution)/shard_map/ppermute | solution.py:450
  577.4 13.6 %all-to-all-start.10 = ((bf16[16,24,768]{2,1,0:T(8,128)(2,1)}), bf16[16,24,768]{2,1,0:T(8,128)(2,1)}, u32[]{:S(2)}, u32[]{:S(2)}) async-start(bf16[16,24,768]{2,1,0:T(8,128)(2,1)} %bitcast.41), calls=%async_computation.10 | async-start | bytes 1179648 | tf_op jit(solution)/shard_map/all_to_all | solution.py:689
  582.5 12.1 %copy-start.22 = (bf16[2,1,768]{2,0,1:T(2,128)(2,1)S(1)}, bf16[2,1,768]{2,0,1:T(2,128)(2,1)}, u32[]{:S(2)}) copy-start(bf16[2,1,768]{2,0,1:T(2,128)(2,1)} %param.23) | copy-start | bytes 9220
  582.6 14.0 %copy-start.14 = (bf16[208,768]{1,0:T(8,128)(2,1)S(1)}, bf16[208,768]{1,0:T(8,128)(2,1)}, u32[]{:S(2)}) copy-start(bf16[208,768]{1,0:T(8,128)(2,1)} %get-tuple-element.72) | copy-start | bytes 958468
  591.0 33.4 %all-to-all-start.7 = ((bf16[16,27,768]{2,1,0:T(8,128)(2,1)}), bf16[16,27,768]{2,1,0:T(8,128)(2,1)S(1)}, u32[]{:S(2)}, u32[]{:S(2)}) async-start(bf16[16,27,768]{2,1,0:T(8,128)(2,1)} %reshape.219), calls=%async_computation.7 | async-start | bytes 1572864 | tf_op jit(solution)/shard_map/all_to_all | solution.py:689
  598.5 74.5 %collective-permute-start.31 = (bf16[768,768]{1,0:T(8,128)(2,1)}, bf16[768,768]{1,0:T(8,128)(2,1)}, u32[]{:S(2)}, u32[]{:S(2)}) collective-permute-start(bf16[768,768]{1,0:T(8,128)(2,1)} %bitcast.12.refs_0_), channel_id=1, source_target_pairs={{3,0},{0,1},{1,2},{2,3},{7,4},{4,5},{5,6},{6,7},{11,8},{8,9},{9,10... | collective-permute-start | bytes 3538952 | tf_op jit(solution)/shard_map/ppermute | solution.py:450
  598.8 74.1 %collective-permute-start.30 = (bf16[768,768]{1,0:T(8,128)(2,1)}, bf16[768,768]{1,0:T(8,128)(2,1)}, u32[]{:S(2)}, u32[]{:S(2)}) collective-permute-start(bf16[768,768]{1,0:T(8,128)(2,1)} %collective-permute-done.29.refs_1_), channel_id=1, source_target_pairs={{1,0},{2,1},{3,2},{0,3},{5,4},{6,5},{7,6},{4,7},{9,8},{10,9},{11,1... | collective-permute-start | bytes 3538952 | tf_op jit(solution)/shard_map/ppermute | solution.py:450
  622.9 50.6 %collective-permute-start.32 = (bf16[768,768]{1,0:T(8,128)(2,1)}, bf16[768,768]{1,0:T(8,128)(2,1)}, u32[]{:S(2)}, u32[]{:S(2)}) collective-permute-start(bf16[768,768]{1,0:T(8,128)(2,1)} %bitcast.28.refs_0_.refs_4_), channel_id=1, source_target_pairs={{1,0},{2,1},{3,2},{0,3},{5,4},{6,5},{7,6},{4,7},{9,8},{10,9},{11,1... | collective-permute-start | bytes 3538952 | tf_op jit(solution)/shard_map/ppermute | solution.py:450
  624.4 49.4 %collective-permute-start.34 = (bf16[768,768]{1,0:T(8,128)(2,1)}, bf16[768,768]{1,0:T(8,128)(2,1)}, u32[]{:S(2)}, u32[]{:S(2)}) collective-permute-start(bf16[768,768]{1,0:T(8,128)(2,1)} %collective-permute-done.33.refs_7_), channel_id=1, source_target_pairs={{3,0},{0,1},{1,2},{2,3},{7,4},{4,5},{5,6},{6,7},{11,8},{8,9},{9,10... | collective-permute-start | bytes 3538952 | tf_op jit(solution)/shard_map/ppermute | solution.py:450
  625.5 38.0 %all-to-all-start.11 = ((bf16[32,24,768]{2,1,0:T(8,128)(2,1)}), bf16[32,24,768]{2,1,0:T(8,128)(2,1)S(1)}, u32[]{:S(2)}, u32[]{:S(2)}) async-start(bf16[32,24,768]{2,1,0:T(8,128)(2,1)} %broadcast_in_dim.34), calls=%async_computation.11 | async-start | bytes 2359296 | tf_op jit(solution)/shard_map/all_to_all | solution.py:698
  633.3 29.2 %copy-start.11 = (f32[208,768]{1,0:T(8,128)S(1)}, f32[208,768]{1,0:T(8,128)}, u32[]{:S(2)}) copy-start(f32[208,768]{1,0:T(8,128)} %get-tuple-element.84) | copy-start | bytes 1916932
  665.1 47.7 %all-to-all-start.8 = ((bf16[32,27,768]{2,1,0:T(8,128)(2,1)}), bf16[32,27,768]{2,1,0:T(8,128)(2,1)S(1)}, u32[]{:S(2)}, u32[]{:S(2)}) async-start(bf16[32,27,768]{2,1,0:T(8,128)(2,1)} %broadcast_in_dim.33), calls=%async_computation.8 | async-start | bytes 3145728 | tf_op jit(solution)/shard_map/all_to_all | solution.py:698
  673.0 30.9 %copy-start.29 = (f32[1,768]{1,0:T(1,128)S(1)}, f32[1,768]{1,0:T(1,128)}, u32[]{:S(2)}) copy-start(f32[1,768]{1,0:T(1,128)} %get-tuple-element.98) | copy-start | bytes 9220
  (23 other events, 109.2 us)

commit v2 on v1

--- a/solution.py
+++ b/solution.py
@@ -44,16 +44,23 @@
 
 
 def gelu_both(pre):
-    size = jnp.abs(pre) * (0.5**0.5)
-    t = 1.0 / (1.0 + 0.3275911 * size)
-    poly = t * (
-        0.254829592
-        + t * (-0.284496736 + t * (1.421413741 + t * (-1.453152027 + t * 1.061405429)))
-    )
-    bell = jnp.exp(-(size * size))
-    tail = (0.5 * poly) * bell
-    cdf = jnp.where(pre >= 0.0, 1.0 - tail, tail)
-    return pre * cdf, cdf + pre * bell * 0.3989422804014327
+    cdf = 0.5 + 0.5 * lax.erf(pre * (0.5**0.5))
+    bell = jnp.exp2(pre * pre * (-0.5 * 1.4426950408889634))
+    return pre * cdf, cdf + pre * (bell * 0.3989422804014327)
+
+
+class Fetch:
+    def __init__(self, sources, targets, semaphores):
+        self.copies = [
+            pltpu.make_async_copy(source, target, semaphores.at[i])
+            for i, (source, target) in enumerate(zip(sources, targets))
+        ]
+        for copy in self.copies:
+            copy.start()
+
+    def wait(self, *which):
+        for i in which:
+            self.copies[i].wait()
 
 
 def slot_targets(routes_layer, experts, stride):
@@ -307,31 +314,22 @@
         send_out[...] = sent.astype(BF16)
 
 
-CHUNK = 256
+CHUNK = 768
 BLOCK = 256
-
-
-def expert_pieces(rows, grads, pieces, biases, slopes, total, back, outs, finish):
-    count, width = (grads if rows is None else rows).shape
-    part = pieces[0][0].shape[1]
+GRAD_CHUNK = 256
+
+
+def expert_pieces(rows, grads, pieces, biases, slopes, total, finish):
     forward, backward = rows is not None, grads is not None
+    count = (rows if forward else grads).shape[0]
+    width, part = pieces[0][0].shape
     keep = forward and not backward
-    operands, names = [], []
-
-    def give(name, value):
-        if value is not None:
-            names.append(name)
-            operands.append(value)
-
-    give("rows", rows)
-    give("grads", grads)
-    for i, (weight_in, weight_out) in enumerate(pieces):
-        give(("in", i), weight_in)
-        give(("out", i), weight_out)
-    give("biases", biases)
-    give("slopes", slopes)
-    give("total", total)
-    give("back", back)
+    plain = [("rows" if forward else "grads", rows if forward else grads)]
+    if forward:
+        plain += [("biases", biases), ("total", total)]
+    fetched = [a for pair in pieces for a in pair]
+    slopes = slopes or []
+    spots = [(j, k) for j, value in enumerate(slopes) for k in range(value.shape[0])]
     kind = BF16 if finish else F32
     shapes = []
     if forward and backward:
@@ -341,38 +339,50 @@
         shapes.append(("kept", shaped((len(pieces), count, part), BF16)))
     else:
         shapes.append(("d", shaped((count, width), kind)))
-    scratch = [pltpu.VMEM((count, width), F32)] * (forward + backward)
+    held = [pltpu.VMEM(a.shape, BF16) for a in fetched]
+    held += [pltpu.VMEM((count, part), BF16) for _ in spots]
+    source, first = ("rows", width) if forward else ("grads", 0)
+    ends = [len(plain), len(fetched), len(slopes), len(shapes), len(held)]
 
     def body(*refs):
-        at = dict(zip(names + [n for n, _ in shapes], refs))
-        sums = list(refs[len(names) + len(shapes) :])
-        y_sum = sums.pop(0) if forward else None
-        d_sum = sums.pop(0) if backward else None
+        refs = list(refs)
+        plain_refs, far_refs, slope_refs, out_refs, held_refs = [
+            [refs.pop(0) for _ in range(n)] for n in ends
+        ]
+        at = dict(zip([n for n, _ in plain] + [n for n, _ in shapes], plain_refs + out_refs))
+        semaphores = refs.pop()
+        fetch = Fetch(
+            far_refs + [slope_refs[j].at[k] for j, k in spots], held_refs, semaphores
+        )
+        y_sum = refs.pop(0) if forward else None
+        d_sum = refs.pop(0) if backward else None
         if forward:
-            y_sum[...] = at["total"][...] if "total" in at else jnp.zeros_like(y_sum)
+            y_sum[...] = jnp.broadcast_to(at["total"][...], y_sum.shape)
         if backward:
-            d_sum[...] = at["back"][...] if "back" in at else jnp.zeros_like(d_sum)
+            d_sum[...] = jnp.zeros_like(d_sum)
         for i in range(len(pieces)):
-
-            def step(c, carry):
-                cols = pl.ds(pl.multiple_of(c * CHUNK, CHUNK), CHUNK)
-                weight_in, weight_out = at["in", i][:, cols], at["out", i][cols, :]
+            in_ref, out_ref = held_refs[2 * i], held_refs[2 * i + 1]
+            fetch.wait(2 * i, 2 * i + 1)
+            if spots:
+                slope_ref = held_refs[2 * len(pieces) + i]
+                fetch.wait(2 * len(pieces) + i)
+            for c in range(0, part, CHUNK):
+                cols = slice(c, c + CHUNK)
                 for start in range(0, count, BLOCK):
                     here = slice(start, start + BLOCK)
                     if forward:
-                        pre = dot(at["rows"][here, :], weight_in) + at["biases"][i : i + 1, cols]
-                        active, slope = gelu_both(pre)
-                        y_sum[here, :] += dot(active.astype(BF16), weight_out)
-                        if keep:
+                        pre = dot(at["rows"][here, :width], in_ref[:, cols])
+                        active, slope = gelu_both(pre + at["biases"][i : i + 1, cols])
+                        y_sum[here, :] += dot(active.astype(BF16), out_ref[cols, :])
+                        if not backward:
                             at["kept"][i, here, cols] = slope.astype(BF16)
                     else:
-                        slope = at["slopes"][i, here, cols].astype(F32)
+                        slope = slope_ref[here, cols].astype(F32)
                     if backward:
-                        grad = dot(at["grads"][here, :], weight_out, 1, 1)
-                        d_sum[here, :] += dot((grad * slope).astype(BF16), weight_in, 1, 1)
-                return carry
-
-            lax.fori_loop(0, part // CHUNK, step, 0)
+                        grad = dot(at[source][here, first : first + width], out_ref[cols, :], 1, 1)
+                        d_sum[here, :] += dot(
+                            (grad * slope).astype(BF16), in_ref[:, cols], 1, 1
+                        )
         if forward and backward:
             at["both"][:, :width] = y_sum[...].astype(kind)
             at["both"][:, width:] = d_sum[...].astype(kind)
@@ -384,65 +394,75 @@
     return pl.pallas_call(
         body,
         out_shape=[s for _, s in shapes],
-        scratch_shapes=scratch,
+        in_specs=[pl.BlockSpec(memory_space=pltpu.VMEM)] * len(plain)
+        + [pl.BlockSpec(memory_space=pl.ANY)] * (len(fetched) + len(slopes)),
+        scratch_shapes=held
+        + [pltpu.VMEM((count, width), F32)] * (forward + backward)
+        + [pltpu.SemaphoreType.DMA((len(held),))],
         compiler_params=pltpu.CompilerParams(vmem_limit_bytes=VMEM_LIMIT),
         cost_estimate=pl.CostEstimate(
             flops=4 * (forward + backward) * count * width * part * len(pieces),
             bytes_accessed=20_000_000,
             transcendentals=0,
         ),
-    )(*operands)
-
-
-def expert_grads(rows, grads, weight_in, bias_column, weight_out):
-    pieces = len(rows)
-    count, width = rows[0].shape
-    part = weight_in.shape[1]
+    )(*[a for _, a in plain], *fetched, *slopes)
+
+
+def expert_grads(pieces, weight_in, bias_column, weight_out, layer, others=()):
+    joint = not isinstance(pieces[0], tuple)
+    width, part = weight_in.shape
+    operands = list(pieces) if joint else [a for pair in pieces for a in pair]
+    held = len(operands)
+    count = sum(a.shape[0] for a in operands) // (1 if joint else 2)
 
     def body(*refs):
-        rows_refs, grads_refs = refs[:pieces], refs[pieces : 2 * pieces]
-        in_ref, bias_ref, out_ref, in_out, bias_out, w_out, sum_out, turned, total = refs[
-            2 * pieces :
-        ]
+        given, refs = refs[:held], refs[held:]
+        in_ref, bias_ref, out_ref = refs[:3]
+        in_out, bias_out, w_out, sum_out, turned, total, *here_refs = refs[3 + len(others) :]
+        fetch = Fetch(given, here_refs[:-1], here_refs[-1])
         turned[...] = in_ref[...].astype(F32).T.astype(BF16)
-
-        def step(c, carry):
-            here = pl.ds(pl.multiple_of(c * CHUNK, CHUNK), CHUNK)
-            weight_grad = jnp.zeros((CHUNK, width), F32)
-            turned_grad = jnp.zeros((CHUNK, width), F32)
-            bias_grad = jnp.zeros((CHUNK, 1), F32)
-            for rows_ref, grads_ref in zip(rows_refs, grads_refs):
+        for i in range(held if joint else held // 2):
+            if joint:
+                fetch.wait(i)
+                rows_ref, grads_ref = here_refs[i].at[:, :width], here_refs[i].at[:, width:]
+            else:
+                fetch.wait(2 * i, 2 * i + 1)
+                rows_ref, grads_ref = here_refs[2 * i], here_refs[2 * i + 1]
+
+            def add(ref, index, value):
+                ref[index] = value if i == 0 else ref[index] + value
+
+            for c in range(0, part, GRAD_CHUNK):
+                here = slice(c, c + GRAD_CHUNK)
                 pre = dot(turned[here, :], rows_ref[...], 1, 1) + bias_ref[here, :]
                 active, slope = gelu_both(pre)
-                weight_grad += dot(active.astype(BF16), grads_ref[...])
+                add(w_out, (0, here), dot(active.astype(BF16), grads_ref[...]))
                 grad = (dot(out_ref[here, :], grads_ref[...], 1, 1) * slope).astype(BF16)
-                bias_grad += jnp.sum(grad.astype(F32), axis=1, keepdims=True)
-                turned_grad += dot(grad, rows_ref[...])
-            w_out[here, :] = weight_grad
-            total[here, :] = turned_grad
-            bias_out[here, :] = bias_grad
-            return carry
-
-        lax.fori_loop(0, part // CHUNK, step, 0)
-        sum_out[...] = sum(
-            jnp.sum(ref[...].astype(F32), axis=0, keepdims=True) for ref in grads_refs
-        )
-        in_out[...] = total[...].T
-
+                add(bias_out, (0, here), jnp.sum(grad.astype(F32), axis=1, keepdims=True))
+                add(total, (here, slice(None)), dot(grad, rows_ref[...]))
+            add(sum_out, 0, jnp.sum(grads_ref[...].astype(F32), axis=0, keepdims=True))
+        in_out[0] = total[...].T
+
+    shapes = [(width, part), (part, 1), (part, width), (1, width)]
+    fixed = lambda a: pl.BlockSpec(a.shape, lambda i: (0,) * a.ndim)
+    scratch = [pltpu.VMEM(a.shape, BF16) for a in operands]
+    scratch.append(pltpu.SemaphoreType.DMA((len(operands),)))
+    small = [weight_in, bias_column, weight_out]
     return pl.pallas_call(
         body,
-        out_shape=(
-            shaped((width, part), F32),
-            shaped((part, 1), F32),
-            shaped((part, width), F32),
-            shaped((1, width), F32),
-        ),
-        scratch_shapes=[pltpu.VMEM((part, width), BF16), pltpu.VMEM((part, width), F32)],
+        grid=(1,),
+        in_specs=[pl.BlockSpec(memory_space=pl.ANY)] * held
+        + [fixed(a) for a in small]
+        + [pl.BlockSpec(memory_space=pl.ANY)] * len(others),
+        out_specs=[pl.BlockSpec((1,) + a, lambda i: (layer, 0, 0)) for a in shapes],
+        out_shape=[shaped((LAYERS,) + a, F32) for a in shapes],
+        input_output_aliases={held + len(small) + i: i for i in range(len(others))},
+        scratch_shapes=[pltpu.VMEM((part, width), BF16), pltpu.VMEM((part, width), F32)] + scratch,
         compiler_params=pltpu.CompilerParams(vmem_limit_bytes=VMEM_LIMIT),
         cost_estimate=pl.CostEstimate(
-            flops=8 * pieces * count * width * part, bytes_accessed=20_000_000, transcendentals=0
+            flops=8 * count * width * part, bytes_accessed=20_000_000, transcendentals=0
         ),
-    )(*rows, *grads, weight_in, bias_column, weight_out)
+    )(*operands, *small, *others)
 
 
 def ahead(value, steps, axis="fsdp"):
@@ -455,24 +475,22 @@
     return lax.ppermute(value, "expert", [(i ^ 1, i) for i in range(size)])
 
 
-def ring_pair(first, second):
-    next_first, next_second = ahead(first, 1), ahead(second, 1)
-    last_first, last_second = ahead(first, 3), ahead(second, 3)
-    far_first, far_second = ahead(next_first, 1), ahead(last_second, 3)
-    return [
-        (first, second),
-        (next_first, next_second),
-        (far_first, far_second),
-        (last_first, last_second),
-    ]
-
-
-def ring_weights(packed, core):
-    half = lax.dynamic_slice_in_dim(packed, 2 * core, 2, axis=0)
-    after, before = ahead(half, 1), ahead(half, 3)
-    far = jnp.concatenate([ahead(after[0:1], 1), ahead(before[1:2], 3)], axis=0)
-    mine = [after, far, before]
-    return [packed] + mine + [other_core(a) for a in mine]
+def tie(*values):
+    return lax.optimization_barrier(values)
+
+
+def ring_rows(rows):
+    half = rows.shape[0] // 2
+    after, before = ahead(rows, 1), ahead(rows, 3)
+    return after, before, lambda a, b: (ahead(a[:half], 1), ahead(b[half:], 3))
+
+
+def half_weights(packed, core):
+    return lax.dynamic_slice_in_dim(packed, 2 * core, 2, axis=0)
+
+
+def far_weights(after, before):
+    return jnp.concatenate([ahead(after[0:1], 1), ahead(before[1:2], 3)], axis=0)
 
 
 def swap(rows, stride):
@@ -521,11 +539,17 @@
     held = -(-count // 16) * 16
     part = width // parts
     scale = (width // HEADS) ** (-0.5)
-    gather = lambda a: lax.all_gather(a, "fsdp", axis=0, tiled=False)
     fill = ((0, held - count), (0, 0))
 
-    small_all = gather(
-        pack_small(norm_gain, mixer_bias, router_weight, router_bias, expert_in_bias)
+    small_local = pack_small(
+        norm_gain, mixer_bias, router_weight, router_bias, expert_in_bias
+    )
+    small_all = lax.all_to_all(
+        jnp.broadcast_to(small_local[None], (parts,) + small_local.shape),
+        "fsdp",
+        split_axis=0,
+        concat_axis=0,
+        tiled=True,
     )
     at_router = 7 * LAYERS
     at_rbias = at_router + LAYERS * experts
@@ -543,10 +567,14 @@
         jnp.concatenate([qkv_weight[layer], out_weight[layer][None]], axis=0)
         for layer in range(LAYERS)
     ]
-    weights0 = ring_weights(packed[0], core)
-    wide0 = ring_pair(expert_in[0, 0], expert_out[0, 0])
-    weights1 = ring_weights(packed[1], core)
-    wide1 = ring_pair(expert_in[1, 0], expert_out[1, 0])
+    half = half_weights(packed[0], core)
+    after, before = ahead(half, 1), ahead(half, 3)
+    far = far_weights(after, before)
+    theirs = [other_core(after), other_core(before)]
+    far, *theirs, in0, out0 = tie(far, *theirs, expert_in[0, 0], expert_out[0, 0])
+    weights0 = [packed[0], after, far, before, theirs[0], other_core(far), theirs[1]]
+    next_in, last_out = ahead(in0, 1), ahead(out0, 3)
+    next_out, last_in = ahead(out0, 1), ahead(in0, 3)
     order = (me + jnp.arange(parts)) % parts
     hidden_bias = [jnp.take(ebias[:, layer], order, axis=0) for layer in range(LAYERS)]
     targets = [
@@ -587,15 +615,35 @@
     )
     full0 = kept0.pop()
     rows0 = swap(send, stride)
-    near = [wide0[0], wide0[1], wide0[3]]
-    near_bias = jnp.stack([hidden_bias[0][0], hidden_bias[0][1], hidden_bias[0][3]])
-    start = jnp.broadcast_to(bias_out[0], (rows, width))
-    total, near_slopes = expert_pieces(
-        rows0, None, near, near_bias, None, start, None, None, False
-    )
-    result, far_slopes = expert_pieces(
-        rows0, None, [wide0[2]], hidden_bias[0][2:3], None, total, None, None, True
-    )
+    bias = hidden_bias[0]
+    total, slope_own = expert_pieces(
+        rows0, None, [(in0, out0)], bias[0:1], None, bias_out[0], False
+    )
+    total, next_in, next_out, last_in, last_out, dense_next = tie(
+        total, next_in, next_out, last_in, last_out, packed[1]
+    )
+    half = half_weights(dense_next, core)
+    after, before = ahead(half, 1), ahead(half, 3)
+    far_in, far_out = ahead(next_in, 1), ahead(last_out, 3)
+    total, slope_near = expert_pieces(
+        rows0,
+        None,
+        [(next_in, next_out), (last_in, last_out)],
+        bias[1::2],
+        None,
+        total,
+        False,
+    )
+    total, after, before = tie(total, after, before)
+    far = far_weights(after, before)
+    theirs = [other_core(after), other_core(before)]
+    result, slope_far = expert_pieces(
+        rows0, None, [(far_in, far_out)], bias[2:3], None, total, True
+    )
+    wide0 = [(in0, out0), (next_in, next_out), (far_in, far_out), (last_in, last_out)]
+    far, *theirs, in1, out1, _ = tie(far, *theirs, expert_in[1, 0], expert_out[1, 0], far_in)
+    weights1 = [packed[1], after, far, before, theirs[0], other_core(far), theirs[1]]
+    next_in, last_out = ahead(in1, 1), ahead(out1, 3)
     y0 = swap(result, stride)
     gates0 = kept0[6]
     middle1, send, *kept1 = mixer_forward(
@@ -606,13 +654,19 @@
     )
     full1 = kept1.pop()
     x1 = kept1.pop()
-    both = swap(send, stride)
-    rows1, grads1 = both[:, :width], both[:, width:]
-    start = jnp.broadcast_to(bias_out[1], (rows, width))
-    (both,) = expert_pieces(
-        rows1, grads1, wide1, hidden_bias[1], None, start, None, None, True
-    )
+    send, next_in, last_out = tie(send, next_in, last_out)
+    next_out, last_in = ahead(out1, 1), ahead(in1, 3)
+    far_in, far_out = ahead(next_in, 1), ahead(last_out, 3)
+    both1 = swap(send, stride)
+    wide1 = [(in1, out1), (next_in, next_out), (far_in, far_out), (last_in, last_out)]
+    (both,) = expert_pieces(both1, both1, wide1, hidden_bias[1], None, bias_out[1], True)
+    after1, before1, far1 = ring_rows(both1)
+    early, _ = tie(rows0, both1)
+    after0, before0, far0 = ring_rows(early)
     both = swap(both, stride)
+    both, after1, before1, after0, before0 = tie(both, after1, before1, after0, before0)
+    joint1 = [both1, after1, before1, *far1(after1, before1)]
+    rows_pieces = [rows0, after0, before0, *far0(after0, before0)]
 
     half_shape = shaped((parts, 2, part, width), BF16)
     small_shape = shaped((40, width), F32)
@@ -646,19 +700,51 @@
             shaped((rows, width), BF16),
         ],
     )
+    size = lax.axis_size("expert")
+    same_core = [[i for i in range(size) if i % 2 == c] for c in range(2)]
+
+    def chip_sum(keep, give, more=None):
+        chip = (keep.astype(F32) + other_core(give).astype(F32)).astype(BF16)
+        chip = chip.reshape(parts, 2 * part, width)
+        if more is None:
+            return chip
+        paired = more.astype(BF16).reshape(2, -1, width)
+        mine = lax.dynamic_index_in_dim(paired, core, 0, keepdims=False).astype(F32)
+        theirs = lax.dynamic_index_in_dim(paired, 1 - core, 0, keepdims=False)
+        mine = (mine + other_core(theirs).astype(F32)).astype(BF16)
+        return jnp.concatenate(
+            [chip, jnp.broadcast_to(mine[None], (parts,) + mine.shape)], axis=1
+        )
+
+    def line_sum(chip):
+        spot = lambda step: lax.dynamic_index_in_dim(
+            chip, (me + step) % parts, 0, keepdims=False
+        )
+        got = [ahead(spot(step), parts - step) for step in range(1, parts)]
+        return sum([a.astype(F32) for a in got], spot(0).astype(F32)).astype(BF16)
+
+    line1 = line_sum(chip_sum(keep1, give1))
     grads0 = swap(send, stride)
-    near_back = expert_pieces(
+    grads0, *rows_pieces = tie(grads0, *rows_pieces)
+    grads0, *joint1 = tie(grads0, *joint1)
+    (back0,) = expert_pieces(
         None,
         grads0,
-        near + [wide0[2]],
+        [wide0[i] for i in (0, 1, 3, 2)],
         None,
-        jnp.concatenate([near_slopes, far_slopes]),
-        None,
-        None,
+        [slope_own, slope_near, slope_far],
         None,
         True,
     )
-    back0 = swap(near_back[0], stride)
+    bias_columns = expert_in_bias[:, 0].astype(F32)[:, :, None]
+    back0, *joint1 = tie(back0, *joint1)
+    own = expert_grads(joint1, expert_in[1, 0], bias_columns[1], expert_out[1, 0], 1)
+    far_rows = ahead(grads0, 2)
+    grads_pieces = [grads0, ahead(grads0, 1), ahead(grads0, 3)]
+    grads_pieces += [far_rows[: rows // 2], far_rows[rows // 2 :]]
+    back0 = swap(back0, stride)
+    back0, line1, *own = tie(back0, line1, *own)
+    back0, *grads_pieces = tie(back0, *grads_pieces)
     q, k, v, m, lse, probs, gates = kept0
     g, keep0, give0, small0 = mixer_backward(
         False,
@@ -667,81 +753,81 @@
         [full_rows, half_shape, half_shape, small_shape],
     )
 
-    size = lax.axis_size("expert")
-    same_core = [[i for i in range(size) if i % 2 == c] for c in range(2)]
-
-    def reduce_dense(keep, give, more=None):
-        chip = (keep.astype(F32) + other_core(give).astype(F32)).astype(BF16)
-        chip = chip.reshape(parts, 2 * part, width)
-        if more is not None:
-            extra = more.shape[0] // 2
-            paired = more.astype(BF16).reshape(2, extra, width)
-            mine = lax.dynamic_index_in_dim(paired, core, 0, keepdims=False).astype(F32)
-            theirs = lax.dynamic_index_in_dim(paired, 1 - core, 0, keepdims=False)
-            mine = (mine + other_core(theirs).astype(F32)).astype(BF16)
-            chip = jnp.concatenate(
-                [chip, jnp.broadcast_to(mine[None], (parts, extra, width))], axis=1
-            )
-        lines = chip.shape[1]
-        got = lax.all_to_all(chip, "fsdp", split_axis=0, concat_axis=0, tiled=True)
-        summed = jnp.sum(got.astype(F32), axis=0).astype(BF16)
-        each = 2 * lines // size
-        got = lax.all_to_all(
-            summed.reshape(size // 2, each, width),
-            "expert",
-            split_axis=0,
-            concat_axis=0,
-            tiled=True,
-            axis_index_groups=same_core,
-        )
-        final = jnp.sum(got.astype(F32), axis=0).astype(BF16)
-        got = lax.all_to_all(
-            jnp.broadcast_to(final[None], (size, each, width)),
-            "expert",
-            split_axis=0,
-            concat_axis=0,
-            tiled=True,
-        )
-        got = got.reshape(size // 2, 2, each, width).swapaxes(0, 1).reshape(2, lines, width)
-        return got[:, : 2 * part].reshape(4, part, width), got[:, 2 * part :].reshape(-1, width)
-
-    def own_grads(layer, pieces):
-        a, b, c, d = expert_grads(
-            [p[0] for p in pieces],
-            [p[1] for p in pieces],
-            expert_in[layer, 0],
-            expert_in_bias[layer, 0].astype(F32)[:, None],
-            expert_out[layer, 0],
-        )
-        return a, b[:, 0], c, d[0]
-
-    own1 = own_grads(1, ring_pair(rows1, grads1))
-    own0 = own_grads(0, ring_pair(rows0, grads0))
-    dense1, _ = reduce_dense(keep1, give1)
+    own = expert_grads(
+        list(zip(rows_pieces, grads_pieces)),
+        expert_in[0, 0],
+        bias_columns[0],
+        expert_out[0, 0],
+        0,
+        own,
+    )
+    in_grad, in_bias_grad, out_grad, out_bias_grad = own
     smalls = jnp.concatenate([small0, small1, jnp.zeros((-80 % size, width), F32)])
-    dense0, smalls = reduce_dense(keep0, give0, smalls)
-    dense_sum = jnp.stack([dense0, dense1]).astype(F32)
-    small_sum = smalls[:80].astype(F32).reshape(LAYERS, 40, width)
+    line0 = line_sum(chip_sum(keep0, give0, smalls))
+    each = 2 * part * 2 // size
+    lines = jnp.concatenate(
+        [
+            line0[: 2 * part].reshape(size // 2, each, width),
+            line1.reshape(size // 2, each, width),
+            line0[2 * part :].reshape(size // 2, -1, width),
+        ],
+        axis=1,
+    )
+    got = lax.all_to_all(
+        lines, "expert", split_axis=0, concat_axis=0, tiled=True, axis_index_groups=same_core
+    )
+    final = jnp.sum(got.astype(F32), axis=0).astype(BF16)
+    got = lax.all_to_all(
+        jnp.broadcast_to(final[None], (size,) + final.shape),
+        "expert",
+        split_axis=0,
+        concat_axis=0,
+        tiled=True,
+    )
+    extra = final.shape[0] - 2 * each
+
+    def unpack_body(got_ref, qkv_out, out_out, small_ref):
+        for source in range(size):
+            place, c = source // 2, source % 2
+            kind = 2 * c + place * each // part
+            spot = pl.ds(place * each % part, each)
+            for layer in range(LAYERS):
+                lines = got_ref[source, layer * each : (layer + 1) * each, :].astype(F32)
+                if kind < 3:
+                    qkv_out[layer, kind, spot, :] = lines
+                else:
+                    out_out[layer, spot, :] = lines
+            start = (c * (size // 2) + place) * extra
+            small_ref[start : start + extra, :] = got_ref[source, 2 * each :, :].astype(F32)
+
+    qkv_grad, out_weight_grad, smalls = pl.pallas_call(
+        unpack_body,
+        out_shape=[
+            shaped((LAYERS, 3, part, width), F32),
+            shaped((LAYERS, part, width), F32),
+            shaped((size * extra, width), F32),
+        ],
+        compiler_params=pltpu.CompilerParams(vmem_limit_bytes=VMEM_LIMIT),
+        cost_estimate=pl.CostEstimate(flops=0, bytes_accessed=10_000_000, transcendentals=0),
+    )(got)
+    small_sum = smalls[:80].reshape(LAYERS, 40, width)
     mine = lax.dynamic_slice_in_dim(small_sum, me * part, part, axis=2)
     router_grad = jnp.swapaxes(mine[:, 7 : 7 + experts], 1, 2)
     rbias_grad = lax.dynamic_slice_in_dim(
         small_sum[:, 7 + experts], me * router_bias.shape[1], router_bias.shape[1], axis=1
     )
-    in_grad, in_bias_grad, out_grad, out_bias_grad = (
-        jnp.stack([a, b])[:, None] for a, b in zip(own0, own1)
-    )
     return (
         activations[:count],
         g[:count],
-        dense_sum[:, :3],
-        dense_sum[:, 3],
+        qkv_grad,
+        out_weight_grad,
         mine[:, :2],
         mine[:, 2:7],
         router_grad,
         rbias_grad,
-        in_grad,
-        in_bias_grad,
-        out_grad,
+        in_grad[:, None],
+        in_bias_grad[:, None, :, 0],
+        out_grad[:, None],
         out_bias_grad,
     )
 

time: 735 us -> 632 us (0.86)
  blocking collectives: 101 us -> 24.5 us
  waiting for transfers between devices: 233 us -> 262 us
  Pallas kernels: 188 us -> 165 us
  other arithmetic: 35.5 us -> 16.2 us
  local copies, waits for them, and re-layouts: 56.6 us -> 40.3 us
    all_to_all x2 -> x1, blocking collectives: 63.5 us -> 24.5 us  [shards(): lax.all_to_all(lines, 'expert', split_axis=0, concat_axis=0, tiled=True,...]
    all_gather x1 -> x0, blocking collectives: 37.8 us -> none  [shards(): gather = lambda a: lax.all_gather(a, 'fsdp', axis=0, tiled=False)]
    all_to_all x4 -> x6, waiting for transfers between devices: 15.6 us -> 48.4 us  [swap(): lax.all_to_all(rows.reshape(-1, stride, width), 'expert', split_axis=0, c...]
    all_to_all x6 -> x2, waiting for transfers between devices: 30.2 us -> 5.65 us  [the longest x1 5.65 us: shards(): lax.all_to_all(jnp.broadcast_to(final[None], (size,) + final.shape), 'exp...]
    pallas_call x6 -> x8, Pallas kernels: 136 us -> 114 us  [the longest x5 60.6 us: expert_pieces(): pl.pallas_call(body, out_shape=[s for _, s in shapes], in_specs=[pl.Block...]
    all_to_all x4 -> x6, starting transfers between devices: 30.5 us -> 50.9 us  [swap(): lax.all_to_all(rows.reshape(-1, stride, width), 'expert', split_axis=0, c...]
    ppermute x32 -> x37, waiting for transfers between devices: 186 us -> 205 us  [ahead(): lax.ppermute(value, axis, [((i + steps) % size, i) for i in range(size)])]
    all_to_all x6 -> x2, starting transfers between devices: 30.9 us -> 11.7 us  [the longest x1 7.6 us: shards(): lax.all_to_all(jnp.broadcast_to(final[None], (size,) + final.shape), 'exp...]
  transfers between devices with their start and end apart: 51 -> 54, of which waited for: 18 -> 25; matrix products, arithmetic and copies ran while one was open for 11% -> 7% of each run, Pallas kernels for 18% -> 19%
where the time goes in v2:
time: 632 us; the launch traced here: 623 us
  waiting for transfers between devices  262 us (41%)
  Pallas kernels  165 us (26%)
  starting transfers between devices  113 us (18%)
  local copies, waits for them, and re-layouts  40.3 us (6%)
  blocking collectives  24.5 us (4%)
  other arithmetic  16.2 us (3%)
    ppermute x37, waiting for transfers between devices, ahead(): lax.ppermute(value, axis, [((i + steps) % size, i) for i in range(size)])  205 us
    pallas_call x5, Pallas kernels, expert_pieces(): pl.pallas_call(body, out_shape=[s for _, s in shapes], in_specs=[pl.Block...  60.6 us
    all_to_all x6, starting transfers between devices, swap(): lax.all_to_all(rows.reshape(-1, stride, width), 'expert', split_axis=0, c...  50.9 us
    pallas_call x2, Pallas kernels, expert_grads(): pl.pallas_call(body, grid=(1,), in_specs=[pl.BlockSpec(memory_space=pl.AN...  49.4 us
    all_to_all x6, waiting for transfers between devices, swap(): lax.all_to_all(rows.reshape(-1, stride, width), 'expert', split_axis=0, c...  48.4 us
    ppermute x37, starting transfers between devices, ahead(): lax.ppermute(value, axis, [((i + steps) % size, i) for i in range(size)])  36.8 us
    pallas_call x2, Pallas kernels, mixer_backward(): pl.pallas_call(functools.partial(mixer_backward_body, last, count, scale,...  33 us
    all_to_all x1, blocking collectives, shards(): lax.all_to_all(lines, 'expert', split_axis=0, concat_axis=0, tiled=True,...  24.5 us
  transfers between devices with their start and end apart: 54, of which 25 were waited for; matrix products, arithmetic and copies ran while one was open for 7% of the time, Pallas kernels for 19%

profile of v2, /device:TPU:1, one launch (start us, length us, event | category | flops | bytes accessed | tf_op | source)
XLA Modules:
  0.0 623.2 jit_solution(15245358899433510700)
XLA Ops:
  0.7 1.6 slice_bitcast_fusion.4
  3.4 3.3 collective-permute-start
  7.6 4.1 all-to-all-start
  16.8 3.5 slice_bitcast_fusion
  20.3 1.7 collective-permute-start.4
  22.1 3.3 collective-permute-start.5
  29.4 1.5 collective-permute-start.3
  31.6 5.5 collective-permute-done.1
  39.7 1.7 collective-permute-start.6
  44.2 7.6 %shard_map.220 = (f32[208,768]{1,0:T(8,128)}, bf16[768,768]{1,0:T(8,128)(2,1)}, bf16[208,768]{1,0:T(8,128)(2,1)}, bf16[208,768]{1,0:T(8,128)(2,1)}, bf16[208,768...) custom-call(s32[2]{0:T(128)} %pad_add_fusion.refs_0_.refs_13_, ...), custom_call_target="tpu_custom_call" | custom-call | flops 2000000000 | bytes 20000000 | tf_op jit(solution)/shard_map/pallas_call | solution.py:600
  51.7 8.3 %all-to-all-start.1 = ((bf16[32,24,768]{2,1,0:T(8,128)(2,1)}), bf16[32,24,768]{2,1,0:T(8,128)(2,1)}, u32[]{:S(2)}, u32[]{:S(2)}) async-start(bf16[32,24,768]{2,1,0:T(8,128)(2,1)} %bitcast.115), calls=%async_computation.1 | async-start | bytes 2359296 | tf_op jit(solution)/shard_map/all_to_all | solution.py:498
  60.4 2.4 collective-permute-start.8
  62.8 1.9 collective-permute-start.9
  67.2 11.2 %all-to-all-done.1 = bf16[32,24,768]{2,1,0:T(8,128)(2,1)} async-done(((bf16[32,24,768]{2,1,0:T(8,128)(2,1)}), bf16[32,24,768]{2,1,0:T(8,128)(2,1)}, u32[]{:S(2)}, u32[]{:S(2)}) %all-to-all-start.1) | async-done | bytes 1179680 | tf_op jit(solution)/shard_map/all_to_all | solution.py:498
  78.4 6.8 %shard_map.221 = (f32[768,768]{1,0:T(8,128)}, bf16[1,768,768]{2,1,0:T(8,128)(2,1)}) custom-call(bf16[768,768]{1,0:T(8,128)(2,1)} %bitcast.13.refs_0_, f32[1,768]{1,0:T(1,128)} %get-tuple-element.290.refs_1_, f32[1,768]{1,0:T(1,128)} %get-tuple-element.296.refs_2_, bf16[768,768]{1,0:T(8,128)(2,1)} %get-tuple-element.123.refs_3_.refs_1_.refs_10_, ...), custom_call_target="tpu_custom_call" | custom-call | flops 1811939328 | bytes 20000000 | tf_op jit(solution)/shard_map/pallas_call | solution.py:394
  85.3 3.4 collective-permute-done.10.refs_6_
  88.7 24.2 %collective-permute-done.7.refs_3_ = bf16[768,768]{1,0:T(8,128)(2,1)} collective-permute-done((bf16[768,768]{1,0:T(8,128)(2,1)}, bf16[768,768]{1,0:T(8,128)(2,1)}, u32[]{:S(2)}, u32[]{:S(2)}) %collective-permute-start.7) | collective-permute-done | bytes 1179680 | tf_op jit(solution)/shard_map/ppermute | solution.py:470
  114.0 2.4 collective-permute-start.17
  116.4 2.7 collective-permute-start.11
  119.8 10.3 %shard_map.222 = (f32[768,768]{1,0:T(8,128)}, bf16[2,768,768]{2,1,0:T(8,128)(2,1)}) custom-call(bf16[768,768]{1,0:T(8,128)(2,1)} %bitcast.13.refs_0_, f32[2,768]{1,0:T(2,128)} %slice.193.refs_1_, f32[768,768]{1,0:T(8,128)} %get-tuple-element.126.refs_2_, bf16[768,768]{1,0:T(8,128)(2,1)} %collective-permute-done.7.refs_3_, ...), custom_call_target="tpu_custom_call" | custom-call | flops 3623878656 | bytes 20000000 | tf_op jit(solution)/shard_map/pallas_call | solution.py:394
  130.1 23.1 %collective-permute-done.11.refs_2_ = bf16[2,192,768]{2,1,0:T(8,128)(2,1)S(1)} collective-permute-done((bf16[2,192,768]{2,1,0:T(8,128)(2,1)S(1)}, bf16[2,192,768]{2,1,0:T(8,128)(2,1)S(1)}, u32[]{:S(2)}, u32[]{:S(2)}) %collective-permute-start.11) | collective-permute-done | bytes 589856 | tf_op jit(solution)/shard_map/ppermute | solution.py:470
  153.2 3.0 collective-permute-done.12.refs_4_
  156.1 2.6 collective-permute-start.15
  160.4 7.2 %shard_map.223 = (bf16[768,768]{1,0:T(8,128)(2,1)}, bf16[1,768,768]{2,1,0:T(8,128)(2,1)}) custom-call(bf16[768,768]{1,0:T(8,128)(2,1)} %bitcast.13.refs_0_, f32[1,768]{1,0:T(1,128)} %get-tuple-element.289.refs_1_, f32[768,768]{1,0:T(8,128)} %get-tuple-element.139.refs_2_, bf16[768,768]{1,0:T(8,128)(2,1)} %collective-permute-done.17.refs_3_.refs_7_, ...), custom_call_target="tpu_custom_call" | custom-call | flops 1811939328 | bytes 20000000 | tf_op jit(solution)/shard_map/pallas_call | solution.py:394
  167.6 8.2 %all-to-all-start.2 = ((bf16[32,24,768]{2,1,0:T(8,128)(2,1)}), bf16[32,24,768]{2,1,0:T(8,128)(2,1)S(1)}, u32[]{:S(2)}, u32[]{:S(2)}) async-start(bf16[32,24,768]{2,1,0:T(8,128)(2,1)} %bitcast.113), calls=%async_computation.2 | async-start | bytes 2359296 | tf_op jit(solution)/shard_map/all_to_all | solution.py:498
  185.1 9.1 %all-to-all-done.2 = bf16[32,24,768]{2,1,0:T(8,128)(2,1)S(1)} async-done(((bf16[32,24,768]{2,1,0:T(8,128)(2,1)}), bf16[32,24,768]{2,1,0:T(8,128)(2,1)S(1)}, u32[]{:S(2)}, u32[]{:S(2)}) %all-to-all-start.2) | async-done | bytes 1179680 | tf_op jit(solution)/shard_map/all_to_all | solution.py:498
  195.2 10.2 %shard_map.224 = (f32[208,768]{1,0:T(8,128)}, bf16[768,1536]{1,0:T(8,128)(2,1)}, bf16[208,768]{1,0:T(8,128)(2,1)}, bf16[208,768]{1,0:T(8,128)(2,1)}, bf16[208,76...) custom-call(s32[2]{0:T(128)} %pad_add_fusion.refs_0_.refs_13_, ...), custom_call_target="tpu_custom_call" | custom-call | flops 2000000000 | bytes 20000000 | tf_op jit(solution)/shard_map/pallas_call | solution.py:600
  205.5 1.5 collective-permute-done.21.refs_10_
  206.9 8.5 %all-to-all-start.3 = ((bf16[32,24,1536]{2,1,0:T(8,128)(2,1)}), bf16[32,24,1536]{2,1,0:T(8,128)(2,1)S(1)}, u32[]{:S(2)}, u32[]{:S(2)}) async-start(bf16[32,24,1536]{2,1,0:T(8,128)(2,1)} %bitcast.107), calls=%async_computation.3 | async-start | bytes 4718592 | tf_op jit(solution)/shard_map/all_to_all | solution.py:498
  215.6 1.5 collective-permute-start.25
  218.5 28.1 %all-to-all-done.3 = bf16[32,24,1536]{2,1,0:T(8,128)(2,1)S(1)} async-done(((bf16[32,24,1536]{2,1,0:T(8,128)(2,1)}), bf16[32,24,1536]{2,1,0:T(8,128)(2,1)S(1)}, u32[]{:S(2)}, u32[]{:S(2)}) %all-to-all-start.3) | async-done | bytes 2359328 | tf_op jit(solution)/shard_map/all_to_all | solution.py:498
  246.6 1.7 collective-permute-start.27
  248.3 20.0 %collective-permute-done.23.refs_7_ = bf16[768,768]{1,0:T(8,128)(2,1)} collective-permute-done((bf16[768,768]{1,0:T(8,128)(2,1)}, bf16[768,768]{1,0:T(8,128)(2,1)}, u32[]{:S(2)}, u32[]{:S(2)}) %collective-permute-start.23) | collective-permute-done | bytes 1179680 | tf_op jit(solution)/shard_map/ppermute | solution.py:470
  269.5 21.2 %shard_map.225 = bf16[768,1536]{1,0:T(8,128)(2,1)} custom-call(bf16[768,1536]{1,0:T(8,128)(2,1)} %bitcast.105, f32[4,768]{1,0:T(4,128)} %get-tuple-element.297.refs_1_, f32[1,768]{1,0:T(1,128)} %get-tuple-element.295.refs_2_, bf16[768,768]{1,0:T(8,128)(2,1)} %get-tuple-element.143.refs_3_.refs_5_, bf16[768,768]{1,0:T(8,128)(2,1)} %get-tuple-element.144.refs_4_.refs_7_, ...), custom_call_target="tpu_custom_call" | custom-call | flops 14495514624 | bytes 20000000 | tf_op jit(solution)/shard_map/pallas_call | solution.py:394
  290.8 9.4 %all-to-all-start.4 = ((bf16[32,24,1536]{2,1,0:T(8,128)(2,1)}), bf16[32,24,1536]{2,1,0:T(8,128)(2,1)}, u32[]{:S(2)}, u32[]{:S(2)}) async-start(bf16[32,24,1536]{2,1,0:T(8,128)(2,1)} %bitcast.108), calls=%async_computation.4 | async-start | bytes 4718592 | tf_op jit(solution)/shard_map/all_to_all | solution.py:498
  300.3 1.5 collective-permute-start.29
  301.7 42.4 %collective-permute-done.28.refs_2_ = bf16[768,768]{1,0:T(8,128)(2,1)} collective-permute-done((bf16[768,768]{1,0:T(8,128)(2,1)}, bf16[768,768]{1,0:T(8,128)(2,1)}, u32[]{:S(2)}, u32[]{:S(2)}) %collective-permute-start.28) | collective-permute-done | bytes 1179680 | tf_op jit(solution)/shard_map/ppermute | solution.py:470
  345.4 16.8 %shard_map.226 = (f32[208,768]{1,0:T(8,128)}, bf16[4,2,192,768]{3,2,1,0:T(8,128)(2,1)}, bf16[4,2,192,768]{3,2,1,0:T(8,128)(2,1)}, f32[40,768]{1,0:T(8,128)}, bf1...) custom-call(f32[208,768]{1,0:T(8,128)} %pad_convert_fusion.1.refs_12_.refs_0_, bf16[768,1536]{1,0:T(8,128)(2,1)} %bitcast.27.refs_1_, ...), custom_call_target="tpu_custom_call" | custom-call | flops 4000000000 | bytes 20000000 | tf_op jit(solution)/shard_map/pallas_call | solution.py:678
  366.2 1.5 collective-permute-start.33
  367.8 7.6 %all-to-all-start.5 = ((bf16[32,24,768]{2,1,0:T(8,128)(2,1)}), bf16[32,24,768]{2,1,0:T(8,128)(2,1)}, u32[]{:S(2)}, u32[]{:S(2)}) async-start(bf16[32,24,768]{2,1,0:T(8,128)(2,1)} %bitcast.28), calls=%async_computation.5 | async-start | bytes 2359296 | tf_op jit(solution)/shard_map/all_to_all | solution.py:498
  380.2 25.0 %collective-permute-done.30.refs_6_ = bf16[384,768]{1,0:T(8,128)(2,1)} collective-permute-done((bf16[384,768]{1,0:T(8,128)(2,1)S(1)}, bf16[384,768]{1,0:T(8,128)(2,1)}, u32[]{:S(2)}, u32[]{:S(2)}) %collective-permute-start.30) | collective-permute-done | bytes 589856 | tf_op jit(solution)/shard_map/ppermute | solution.py:470
  405.2 2.6 collective-permute-done.31.refs_8_
  408.4 1.9 collective-permute-start.38
  410.3 15.0 %shard_map.227 = bf16[768,768]{1,0:T(8,128)(2,1)} custom-call(bf16[768,768]{1,0:T(8,128)(2,1)} %bitcast.29.refs_0_.refs_1_, bf16[768,768]{1,0:T(8,128)(2,1)} %get-tuple-element.123.refs_3_.refs_1_.refs_10_, bf16[768,768]{1,0:T(8,128)(2,1)} %copy-done.9, bf16[768,768]{1,0:T(8,128)(2,1)} %collective-permute-done.7.refs_3_, ...), custom_call_target="tpu_custom_call" | custom-call | flops 7247757312 | bytes 20000000 | tf_op jit(solution)/shard_map/pallas_call | solution.py:394
  425.3 8.9 %all-to-all-start.6 = ((bf16[32,24,768]{2,1,0:T(8,128)(2,1)}), bf16[32,24,768]{2,1,0:T(8,128)(2,1)}, u32[]{:S(2)}, u32[]{:S(2)}) async-start(bf16[32,24,768]{2,1,0:T(8,128)(2,1)} %bitcast.114), calls=%async_computation.6 | async-start | bytes 2359296 | tf_op jit(solution)/shard_map/all_to_all | solution.py:498
  434.2 2.2 add_convert_fusion.1
  436.7 4.1 collective-permute-start.36
  441.2 24.6 %shard_map.228 = (f32[2,768,768]{2,1,0:T(8,128)}, f32[2,768,1]{2,1,0:T(8,128)}, f32[2,768,768]{2,1,0:T(8,128)}, f32[2,1,768]{2,1,0:T(1,128)}) custom-call(bf16[768,1536]{1,0:T(8,128)(2,1)} %bitcast.106, bf16[768,1536]{1,0:T(8,128)(2,1)} %collective-permute-done.26.refs_1_, bf16[768,1536]{1,0:T(8,128)(2,1)} %collective-permute-done.27.refs_2_, ...), custom_call_target="tpu_custom_call" | custom-call | flops 14495514624 | bytes 20000000 | tf_op jit(solution)/shard_map/pallas_call | solution.py:451
  467.0 9.6 %collective-permute-done.35 = bf16[384,768]{1,0:T(8,128)(2,1)S(1)} collective-permute-done((bf16[384,768]{1,0:T(8,128)(2,1)S(1)}, bf16[384,768]{1,0:T(8,128)(2,1)S(1)}, u32[]{:S(2)}, u32[]{:S(2)}) %collective-permute-start.35) | collective-permute-done | bytes 589856 | tf_op jit(solution)/shard_map/ppermute | solution.py:470
  476.6 10.4 %collective-permute-done.36 = bf16[384,768]{1,0:T(8,128)(2,1)S(1)} collective-permute-done((bf16[384,768]{1,0:T(8,128)(2,1)S(1)}, bf16[384,768]{1,0:T(8,128)(2,1)S(1)}, u32[]{:S(2)}, u32[]{:S(2)}) %collective-permute-start.36) | collective-permute-done | bytes 589856 | tf_op jit(solution)/shard_map/ppermute | solution.py:470
  487.3 16.2 %shard_map.229 = (f32[208,768]{1,0:T(8,128)}, bf16[4,2,192,768]{3,2,1,0:T(8,128)(2,1)}, bf16[4,2,192,768]{3,2,1,0:T(8,128)(2,1)}, f32[40,768]{1,0:T(8,128)}) custom-call(f32[208,768]{1,0:T(8,128)} %get-tuple-element.161.refs_0_, bf16[768,768]{1,0:T(8,128)(2,1)} %bitcast.31.refs_1_, f32[208,768]{1,0:T(8,128)} %pad_convert_fusion.refs_8_.refs_2_, ...), custom_call_target="tpu_custom_call" | custom-call | flops 4000000000 | bytes 20000000 | tf_op jit(solution)/shard_map/pallas_call | solution.py:678
  503.6 1.8 collective-permute-start.41
  506.5 3.0 collective-permute-done.42
  509.7 2.2 add_convert_fusion
  512.8 2.0 collective-permute-start.45
  514.8 28.9 %collective-permute-done.43 = bf16[432,768]{1,0:T(8,128)(2,1)S(1)} collective-permute-done((bf16[432,768]{1,0:T(8,128)(2,1)S(1)}, bf16[432,768]{1,0:T(8,128)(2,1)S(1)}, u32[]{:S(2)}, u32[]{:S(2)}) %collective-permute-start.43) | collective-permute-done | bytes 663584 | tf_op jit(solution)/shard_map/ppermute | solution.py:470
  544.6 24.5 %all_to_all.45 = bf16[16,51,768]{2,1,0:T(8,128)(2,1)S(1)} all-to-all(bf16[16,51,768]{2,1,0:T(8,128)(2,1)S(1)} %pad_maximum_fusion.1), channel_id=1, replica_groups={{0,8,16,24,32,40,48,56,64,72,80,88,96,104,112,120},{4,12,20,28,36,44,52..., dimensions={0} | all-to-all | bytes 2506752 | tf_op jit(solution)/shard_map/all_to_all | solution.py:776
  569.3 1.7 broadcast_in_dim.24
  571.1 7.6 %all-to-all-start.8 = ((bf16[32,51,768]{2,1,0:T(8,128)(2,1)}), bf16[32,51,768]{2,1,0:T(8,128)(2,1)S(1)}, u32[]{:S(2)}, u32[]{:S(2)}) async-start(bf16[32,51,768]{2,1,0:T(8,128)(2,1)} %broadcast_in_dim.24), calls=%async_computation.8 | async-start | bytes 5505024 | tf_op jit(solution)/shard_map/all_to_all | solution.py:780
  580.4 24.7 %shard_map.231 = (f32[2,768,768]{2,1,0:T(8,128)}, f32[2,768,1]{2,1,0:T(8,128)}, f32[2,768,768]{2,1,0:T(8,128)}, f32[2,1,768]{2,1,0:T(1,128)}) custom-call(bf16[768,768]{1,0:T(8,128)(2,1)} %bitcast.13.refs_0_, bf16[768,768]{1,0:T(8,128)(2,1)} %bitcast.29.refs_0_.refs_1_, ...), custom_call_target="tpu_custom_call", output_to_operand_aliasing={{0}: (13, {}), {1}: (14, {}), {2}: (15, {}), {3}: (16, {})} | custom-call | flops 14495514624 | bytes 20000000 | tf_op jit(solution)/shard_map/pallas_call | solution.py:451
  605.1 1.4 reduce.3
  608.0 5.6 all-to-all-done.8.got_ref
  613.6 1.5 copy-done
  615.2 4.1 shard_map.230
  (226 shorter events, 59.0 us)
Async XLA Ops:
  3.4 16.9 %collective-permute-start = (bf16[2,192,768]{2,1,0:T(8,128)(2,1)}, bf16[2,192,768]{2,1,0:T(8,128)(2,1)}, u32[]{:S(2)}, u32[]{:S(2)}) collective-permute-start(bf16[2,192,768]{2,1,0:T(8,128)(2,1)} %fusion.16), channel_id=1, source_target_pairs={{1,0},{2,1},{3,2},{0,3},{5,4},{6,5},{7,6},{4,7},{9,8},{10,9},{11,1... | collective-permute-start | bytes 1769480 | tf_op jit(solution)/shard_map/ppermute | solution.py:470
  6.7 15.4 %collective-permute-start.2 = (bf16[2,192,768]{2,1,0:T(8,128)(2,1)}, bf16[2,192,768]{2,1,0:T(8,128)(2,1)}, u32[]{:S(2)}, u32[]{:S(2)}) collective-permute-start(bf16[2,192,768]{2,1,0:T(8,128)(2,1)} %fusion.16), channel_id=1, source_target_pairs={{3,0},{0,1},{1,2},{2,3},{7,4},{4,5},{5,6},{6,7},{11,8},{8,9},{9,10... | collective-permute-start | bytes 1769480 | tf_op jit(solution)/shard_map/ppermute | solution.py:470
  7.6 23.3 %all-to-all-start = ((bf16[4,88,192]{2,1,0:T(8,128)(2,1)}), bf16[4,88,192]{2,1,0:T(8,128)(2,1)S(1)}, u32[]{:S(2)}, u32[]{:S(2)}) async-start(bf16[4,88,192]{2,1,0:T(8,128)(2,1)} %broadcast_in_dim.21), calls=%async_computation | async-start | bytes 360448 | tf_op jit(solution)/shard_map/all_to_all | solution.py:547
  15.8 100.6 %copy-start.1 = (bf16[4,192,768]{2,1,0:T(8,128)(2,1)}, bf16[4,192,768]{2,1,0:T(8,128)(2,1)S(1)}, u32[]{:S(2)}) copy-start(bf16[4,192,768]{2,1,0:T(8,128)(2,1)S(1)} %pad_maximum_fusion.2.refs_1_) | copy-start | bytes 3538948
  16.8 9.2 %copy-start.15 = (s32[2,208]{0,1:T(8,128)S(1)}, s32[2,208]{0,1:T(8,128)}, u32[]{:S(2)}) copy-start(s32[2,208]{0,1:T(8,128)} %get-tuple-element.284) | copy-start | bytes 4996
  20.3 40.0 %copy-start.9 = (bf16[768,768]{1,0:T(8,128)(2,1)}, bf16[768,768]{1,0:T(8,128)(2,1)S(1)}, u32[]{:S(2)}) copy-start(bf16[768,768]{1,0:T(8,128)(2,1)S(1)} %get-tuple-element.124.refs_4_.refs_2_.refs_12_) | copy-start | bytes 3538948
  20.3 19.3 %collective-permute-start.4 = (bf16[2,192,768]{2,1,0:T(8,128)(2,1)}, bf16[2,192,768]{2,1,0:T(8,128)(2,1)}, u32[]{:S(2)}, u32[]{:S(2)}) collective-permute-start(bf16[2,192,768]{2,1,0:T(8,128)(2,1)} %collective-permute-done.refs_2_), channel_id=1, source_target_pairs={{4,0},{0,4},{12,8},{8,12},{20,16},{16,20},{28,24},{24,28},{36,32},... | collective-permute-start | bytes 1769480 | tf_op jit(solution)/shard_map/ppermute | solution.py:475
  22.1 17.5 %collective-permute-start.5 = (bf16[2,192,768]{2,1,0:T(8,128)(2,1)}, bf16[2,192,768]{2,1,0:T(8,128)(2,1)}, u32[]{:S(2)}, u32[]{:S(2)}) collective-permute-start(bf16[2,192,768]{2,1,0:T(8,128)(2,1)} %collective-permute-done.2.refs_4_), channel_id=1, source_target_pairs={{4,0},{0,4},{12,8},{8,12},{20,16},{16,20},{28,24},{24,28},{36,32},... | collective-permute-start | bytes 1769480 | tf_op jit(solution)/shard_map/ppermute | solution.py:475
  28.3 8.8 %collective-permute-start.1 = (bf16[1,192,768]{2,1,0:T(8,128)(2,1)S(1)}, bf16[1,192,768]{2,1,0:T(8,128)(2,1)}, u32[]{:S(2)}, u32[]{:S(2)}) collective-permute-start(bf16[1,192,768]{2,1,0:T(8,128)(2,1)S(1)} %slice.229), channel_id=1, source_target_pairs={{1,0},{2,1},{3,2},{0,3},{5,4},{6,5},{7,6},{4,7},{9,8},{10,9},{11,1... | collective-permute-start | bytes 884744 | tf_op jit(solution)/shard_map/ppermute | solution.py:470
  29.4 9.1 %collective-permute-start.3 = (bf16[1,192,768]{2,1,0:T(8,128)(2,1)S(1)}, bf16[1,192,768]{2,1,0:T(8,128)(2,1)}, u32[]{:S(2)}, u32[]{:S(2)}) collective-permute-start(bf16[1,192,768]{2,1,0:T(8,128)(2,1)S(1)} %slice.230), channel_id=1, source_target_pairs={{3,0},{0,1},{1,2},{2,3},{7,4},{4,5},{5,6},{6,7},{11,8},{8,9},{9,10... | collective-permute-start | bytes 884744 | tf_op jit(solution)/shard_map/ppermute | solution.py:470
  39.7 4.5 collective-permute-start.6
  51.7 26.7 %all-to-all-start.1 = ((bf16[32,24,768]{2,1,0:T(8,128)(2,1)}), bf16[32,24,768]{2,1,0:T(8,128)(2,1)}, u32[]{:S(2)}, u32[]{:S(2)}) async-start(bf16[32,24,768]{2,1,0:T(8,128)(2,1)} %bitcast.115), calls=%async_computation.1 | async-start | bytes 2359296 | tf_op jit(solution)/shard_map/all_to_all | solution.py:498
  60.0 28.6 %collective-permute-start.10 = (bf16[768,768]{1,0:T(8,128)(2,1)S(1)}, bf16[768,768]{1,0:T(8,128)(2,1)}, u32[]{:S(2)}, u32[]{:S(2)}) collective-permute-start(bf16[768,768]{1,0:T(8,128)(2,1)S(1)} %get-tuple-element.124.refs_4_.refs_2_.refs_12_), channel_id=1, source_target_pairs={{3,0},{0,1},{1,2},{2,3},{7,4},{4,5},{5,6},{6,7},{11,8},{8,9},{9,10... | collective-permute-start | bytes 3538952 | tf_op jit(solution)/shard_map/ppermute | solution.py:470
  60.4 52.6 %collective-permute-start.8 = (bf16[768,768]{1,0:T(8,128)(2,1)S(1)}, bf16[768,768]{1,0:T(8,128)(2,1)}, u32[]{:S(2)}, u32[]{:S(2)}) collective-permute-start(bf16[768,768]{1,0:T(8,128)(2,1)S(1)} %get-tuple-element.124.refs_4_.refs_2_.refs_12_), channel_id=1, source_target_pairs={{1,0},{2,1},{3,2},{0,3},{5,4},{6,5},{7,6},{4,7},{9,8},{10,9},{11,1... | collective-permute-start | bytes 3538952 | tf_op jit(solution)/shard_map/ppermute | solution.py:470
  62.8 50.1 %collective-permute-start.7 = (bf16[768,768]{1,0:T(8,128)(2,1)}, bf16[768,768]{1,0:T(8,128)(2,1)}, u32[]{:S(2)}, u32[]{:S(2)}) collective-permute-start(bf16[768,768]{1,0:T(8,128)(2,1)} %get-tuple-element.123.refs_3_.refs_1_.refs_10_), channel_id=1, source_target_pairs={{1,0},{2,1},{3,2},{0,3},{5,4},{6,5},{7,6},{4,7},{9,8},{10,9},{11,1... | collective-permute-start | bytes 3538952 | tf_op jit(solution)/shard_map/ppermute | solution.py:470
  62.8 51.1 %collective-permute-start.9 = (bf16[768,768]{1,0:T(8,128)(2,1)}, bf16[768,768]{1,0:T(8,128)(2,1)}, u32[]{:S(2)}, u32[]{:S(2)}) collective-permute-start(bf16[768,768]{1,0:T(8,128)(2,1)} %get-tuple-element.123.refs_3_.refs_1_.refs_10_), channel_id=1, source_target_pairs={{3,0},{0,1},{1,2},{2,3},{7,4},{4,5},{5,6},{6,7},{11,8},{8,9},{9,10... | collective-permute-start | bytes 3538952 | tf_op jit(solution)/shard_map/ppermute | solution.py:470
  114.0 45.1 %collective-permute-start.17 = (bf16[768,768]{1,0:T(8,128)(2,1)}, bf16[768,768]{1,0:T(8,128)(2,1)}, u32[]{:S(2)}, u32[]{:S(2)}) collective-permute-start(bf16[768,768]{1,0:T(8,128)(2,1)} %collective-permute-done.7.refs_3_), channel_id=1, source_target_pairs={{1,0},{2,1},{3,2},{0,3},{5,4},{6,5},{7,6},{4,7},{9,8},{10,9},{11,1... | collective-permute-start | bytes 3538952 | tf_op jit(solution)/shard_map/ppermute | solution.py:470
  116.3 44.0 %collective-permute-start.19 = (bf16[768,768]{1,0:T(8,128)(2,1)}, bf16[768,768]{1,0:T(8,128)(2,1)}, u32[]{:S(2)}, u32[]{:S(2)}) collective-permute-start(bf16[768,768]{1,0:T(8,128)(2,1)} %collective-permute-done.10.refs_6_), channel_id=1, source_target_pairs={{3,0},{0,1},{1,2},{2,3},{7,4},{4,5},{5,6},{6,7},{11,8},{8,9},{9,10... | collective-permute-start | bytes 3538952 | tf_op jit(solution)/shard_map/ppermute | solution.py:470
  116.4 36.8 %collective-permute-start.11 = (bf16[2,192,768]{2,1,0:T(8,128)(2,1)S(1)}, bf16[2,192,768]{2,1,0:T(8,128)(2,1)S(1)}, u32[]{:S(2)}, u32[]{:S(2)}) collective-permute-start(bf16[2,192,768]{2,1,0:T(8,128)(2,1)S(1)} %constant_dynamic-slice_fusion.3), channel_id=1, source_target_pairs={{1,0},{2,1},{3,2},{0,3},{5,4},{6,5},{7,6},{4,7},{9,8},{10,9},{11,1... | collective-permute-start | bytes 1769480 | tf_op jit(solution)/shard_map/ppermute | solution.py:470
  119.1 37.0 %collective-permute-start.12 = (bf16[2,192,768]{2,1,0:T(8,128)(2,1)S(1)}, bf16[2,192,768]{2,1,0:T(8,128)(2,1)S(1)}, u32[]{:S(2)}, u32[]{:S(2)}) collective-permute-start(bf16[2,192,768]{2,1,0:T(8,128)(2,1)S(1)} %constant_dynamic-slice_fusion.3), channel_id=1, source_target_pairs={{3,0},{0,1},{1,2},{2,3},{7,4},{4,5},{5,6},{6,7},{11,8},{8,9},{9,10... | collective-permute-start | bytes 1769480 | tf_op jit(solution)/shard_map/ppermute | solution.py:470
  153.2 14.4 %copy-start.7 = (bf16[2,192,768]{2,1,0:T(8,128)(2,1)}, bf16[2,192,768]{2,1,0:T(8,128)(2,1)S(1)}, u32[]{:S(2)}) copy-start(bf16[2,192,768]{2,1,0:T(8,128)(2,1)S(1)} %collective-permute-done.11.refs_2_) | copy-start | bytes 1769476
  156.1 11.4 %copy-start.8 = (bf16[2,192,768]{2,1,0:T(8,128)(2,1)}, bf16[2,192,768]{2,1,0:T(8,128)(2,1)S(1)}, u32[]{:S(2)}) copy-start(bf16[2,192,768]{2,1,0:T(8,128)(2,1)S(1)} %collective-permute-done.12.refs_4_) | copy-start | bytes 1769476
  156.1 20.9 %collective-permute-start.15 = (bf16[2,192,768]{2,1,0:T(8,128)(2,1)S(1)}, bf16[2,192,768]{2,1,0:T(8,128)(2,1)}, u32[]{:S(2)}, u32[]{:S(2)}) collective-permute-start(bf16[2,192,768]{2,1,0:T(8,128)(2,1)S(1)} %collective-permute-done.11.refs_2_), channel_id=1, source_target_pairs={{4,0},{0,4},{12,8},{8,12},{20,16},{16,20},{28,24},{24,28},{36,32},... | collective-permute-start | bytes 1769480 | tf_op jit(solution)/shard_map/ppermute | solution.py:475
  158.8 18.2 %collective-permute-start.16 = (bf16[2,192,768]{2,1,0:T(8,128)(2,1)S(1)}, bf16[2,192,768]{2,1,0:T(8,128)(2,1)}, u32[]{:S(2)}, u32[]{:S(2)}) collective-permute-start(bf16[2,192,768]{2,1,0:T(8,128)(2,1)S(1)} %collective-permute-done.12.refs_4_), channel_id=1, source_target_pairs={{4,0},{0,4},{12,8},{8,12},{20,16},{16,20},{28,24},{24,28},{36,32},... | collective-permute-start | bytes 1769480 | tf_op jit(solution)/shard_map/ppermute | solution.py:475
  158.8 17.0 %collective-permute-start.13 = (bf16[1,192,768]{2,1,0:T(8,128)(2,1)S(1)}, bf16[1,192,768]{2,1,0:T(8,128)(2,1)}, u32[]{:S(2)}, u32[]{:S(2)}) collective-permute-start(bf16[1,192,768]{2,1,0:T(8,128)(2,1)S(1)} %slice.196), channel_id=1, source_target_pairs={{1,0},{2,1},{3,2},{0,3},{5,4},{6,5},{7,6},{4,7},{9,8},{10,9},{11,1... | collective-permute-start | bytes 884744 | tf_op jit(solution)/shard_map/ppermute | solution.py:470
  159.1 16.7 %collective-permute-start.14 = (bf16[1,192,768]{2,1,0:T(8,128)(2,1)S(1)}, bf16[1,192,768]{2,1,0:T(8,128)(2,1)}, u32[]{:S(2)}, u32[]{:S(2)}) collective-permute-start(bf16[1,192,768]{2,1,0:T(8,128)(2,1)S(1)} %slice.197), channel_id=1, source_target_pairs={{3,0},{0,1},{1,2},{2,3},{7,4},{4,5},{5,6},{6,7},{11,8},{8,9},{9,10... | collective-permute-start | bytes 884744 | tf_op jit(solution)/shard_map/ppermute | solution.py:470
  167.6 26.6 %all-to-all-start.2 = ((bf16[32,24,768]{2,1,0:T(8,128)(2,1)}), bf16[32,24,768]{2,1,0:T(8,128)(2,1)S(1)}, u32[]{:S(2)}, u32[]{:S(2)}) async-start(bf16[32,24,768]{2,1,0:T(8,128)(2,1)} %bitcast.113), calls=%async_computation.2 | async-start | bytes 2359296 | tf_op jit(solution)/shard_map/all_to_all | solution.py:498
  177.0 28.4 %collective-permute-start.20 = (bf16[768,768]{1,0:T(8,128)(2,1)}, bf16[768,768]{1,0:T(8,128)(2,1)}, u32[]{:S(2)}, u32[]{:S(2)}) collective-permute-start(bf16[768,768]{1,0:T(8,128)(2,1)} %get-tuple-element.143.refs_3_.refs_5_), channel_id=1, source_target_pairs={{1,0},{2,1},{3,2},{0,3},{5,4},{6,5},{7,6},{4,7},{9,8},{10,9},{11,1... | collective-permute-start | bytes 3538952 | tf_op jit(solution)/shard_map/ppermute | solution.py:470
  178.4 28.5 %collective-permute-start.21 = (bf16[768,768]{1,0:T(8,128)(2,1)}, bf16[768,768]{1,0:T(8,128)(2,1)}, u32[]{:S(2)}, u32[]{:S(2)}) collective-permute-start(bf16[768,768]{1,0:T(8,128)(2,1)} %get-tuple-element.144.refs_4_.refs_7_), channel_id=1, source_target_pairs={{3,0},{0,1},{1,2},{2,3},{7,4},{4,5},{5,6},{6,7},{11,8},{8,9},{9,10... | collective-permute-start | bytes 3538952 | tf_op jit(solution)/shard_map/ppermute | solution.py:470
  178.8 6.2 %collective-permute-start.18 = (bf16[2,192,768]{2,1,0:T(8,128)(2,1)S(1)}, bf16[2,192,768]{2,1,0:T(8,128)(2,1)S(1)}, u32[]{:S(2)}, u32[]{:S(2)}) collective-permute-start(bf16[2,192,768]{2,1,0:T(8,128)(2,1)S(1)} %pad_maximum_fusion.4.refs_3_), channel_id=1, source_target_pairs={{4,0},{0,4},{12,8},{8,12},{20,16},{16,20},{28,24},{24,28},{36,32},... | collective-permute-start | bytes 1769480 | tf_op jit(solution)/shard_map/ppermute | solution.py:475
  185.1 9.1 %copy-start.12 = (bf16[2,192,768]{2,1,0:T(8,128)(2,1)}, bf16[2,192,768]{2,1,0:T(8,128)(2,1)S(1)}, u32[]{:S(2)}) copy-start(bf16[2,192,768]{2,1,0:T(8,128)(2,1)S(1)} %collective-permute-done.18.refs_6_) | copy-start | bytes 1769476
  206.9 39.7 %all-to-all-start.3 = ((bf16[32,24,1536]{2,1,0:T(8,128)(2,1)}), bf16[32,24,1536]{2,1,0:T(8,128)(2,1)S(1)}, u32[]{:S(2)}, u32[]{:S(2)}) async-start(bf16[32,24,1536]{2,1,0:T(8,128)(2,1)} %bitcast.107), calls=%async_computation.3 | async-start | bytes 4718592 | tf_op jit(solution)/shard_map/all_to_all | solution.py:498
  215.5 31.1 %collective-permute-start.22 = (bf16[768,768]{1,0:T(8,128)(2,1)S(1)}, bf16[768,768]{1,0:T(8,128)(2,1)}, u32[]{:S(2)}, u32[]{:S(2)}) collective-permute-start(bf16[768,768]{1,0:T(8,128)(2,1)S(1)} %copy-done.10), channel_id=1, source_target_pairs={{1,0},{2,1},{3,2},{0,3},{5,4},{6,5},{7,6},{4,7},{9,8},{10,9},{11,1... | collective-permute-start | bytes 3538952 | tf_op jit(solution)/shard_map/ppermute | solution.py:470
  215.6 32.7 %collective-permute-start.25 = (bf16[768,768]{1,0:T(8,128)(2,1)}, bf16[768,768]{1,0:T(8,128)(2,1)}, u32[]{:S(2)}, u32[]{:S(2)}) collective-permute-start(bf16[768,768]{1,0:T(8,128)(2,1)} %get-tuple-element.143.refs_3_.refs_5_), channel_id=1, source_target_pairs={{3,0},{0,1},{1,2},{2,3},{7,4},{4,5},{5,6},{6,7},{11,8},{8,9},{9,10... | collective-permute-start | bytes 3538952 | tf_op jit(solution)/shard_map/ppermute | solution.py:470
  217.0 51.3 %collective-permute-start.23 = (bf16[768,768]{1,0:T(8,128)(2,1)}, bf16[768,768]{1,0:T(8,128)(2,1)}, u32[]{:S(2)}, u32[]{:S(2)}) collective-permute-start(bf16[768,768]{1,0:T(8,128)(2,1)} %collective-permute-done.20.refs_5_), channel_id=1, source_target_pairs={{1,0},{2,1},{3,2},{0,3},{5,4},{6,5},{7,6},{4,7},{9,8},{10,9},{11,1... | collective-permute-start | bytes 3538952 | tf_op jit(solution)/shard_map/ppermute | solution.py:470
  218.3 51.2 %collective-permute-start.24 = (bf16[768,768]{1,0:T(8,128)(2,1)}, bf16[768,768]{1,0:T(8,128)(2,1)}, u32[]{:S(2)}, u32[]{:S(2)}) collective-permute-start(bf16[768,768]{1,0:T(8,128)(2,1)} %collective-permute-done.21.refs_10_), channel_id=1, source_target_pairs={{3,0},{0,1},{1,2},{2,3},{7,4},{4,5},{5,6},{6,7},{11,8},{8,9},{9,10... | collective-permute-start | bytes 3538952 | tf_op jit(solution)/shard_map/ppermute | solution.py:470
  246.6 22.9 %copy-start.5 = (bf16[32,24,1536]{2,1,0:T(8,128)(2,1)}, bf16[32,24,1536]{2,1,0:T(8,128)(2,1)S(1)}, u32[]{:S(2)}) copy-start(bf16[32,24,1536]{2,1,0:T(8,128)(2,1)S(1)} %all-to-all-done.3) | copy-start | bytes 7077892
  246.6 98.8 %collective-permute-start.26 = (bf16[768,1536]{1,0:T(8,128)(2,1)S(1)}, bf16[768,1536]{1,0:T(8,128)(2,1)}, u32[]{:S(2)}, u32[]{:S(2)}) collective-permute-start(bf16[768,1536]{1,0:T(8,128)(2,1)S(1)} %bitcast.103), channel_id=1, source_target_pairs={{1,0},{2,1},{3,2},{0,3},{5,4},{6,5},{7,6},{4,7},{9,8},{10,9},{11,1... | collective-permute-start | bytes 7077896 | tf_op jit(solution)/shard_map/ppermute | solution.py:470
  246.6 98.8 %collective-permute-start.27 = (bf16[768,1536]{1,0:T(8,128)(2,1)S(1)}, bf16[768,1536]{1,0:T(8,128)(2,1)}, u32[]{:S(2)}, u32[]{:S(2)}) collective-permute-start(bf16[768,1536]{1,0:T(8,128)(2,1)S(1)} %bitcast.104), channel_id=1, source_target_pairs={{3,0},{0,1},{1,2},{2,3},{7,4},{4,5},{5,6},{6,7},{11,8},{8,9},{9,10... | collective-permute-start | bytes 7077896 | tf_op jit(solution)/shard_map/ppermute | solution.py:470
  290.8 54.6 %all-to-all-start.4 = ((bf16[32,24,1536]{2,1,0:T(8,128)(2,1)}), bf16[32,24,1536]{2,1,0:T(8,128)(2,1)}, u32[]{:S(2)}, u32[]{:S(2)}) async-start(bf16[32,24,1536]{2,1,0:T(8,128)(2,1)} %bitcast.108), calls=%async_computation.4 | async-start | bytes 4718592 | tf_op jit(solution)/shard_map/all_to_all | solution.py:498
  300.2 43.9 %collective-permute-start.28 = (bf16[768,768]{1,0:T(8,128)(2,1)}, bf16[768,768]{1,0:T(8,128)(2,1)}, u32[]{:S(2)}, u32[]{:S(2)}) collective-permute-start(bf16[768,768]{1,0:T(8,128)(2,1)} %bitcast.13.refs_0_), channel_id=1, source_target_pairs={{1,0},{2,1},{3,2},{0,3},{5,4},{6,5},{7,6},{4,7},{9,8},{10,9},{11,1... | collective-permute-start | bytes 3538952 | tf_op jit(solution)/shard_map/ppermute | solution.py:470
  300.3 45.1 %collective-permute-start.29 = (bf16[768,768]{1,0:T(8,128)(2,1)}, bf16[768,768]{1,0:T(8,128)(2,1)}, u32[]{:S(2)}, u32[]{:S(2)}) collective-permute-start(bf16[768,768]{1,0:T(8,128)(2,1)} %bitcast.13.refs_0_), channel_id=1, source_target_pairs={{3,0},{0,1},{1,2},{2,3},{7,4},{4,5},{5,6},{6,7},{11,8},{8,9},{9,10... | collective-permute-start | bytes 3538952 | tf_op jit(solution)/shard_map/ppermute | solution.py:470
  362.2 72.0 %collective-permute-start.34 = (bf16[4,2,192,768]{3,2,1,0:T(8,128)(2,1)}, bf16[4,2,192,768]{3,2,1,0:T(8,128)(2,1)}, u32[]{:S(2)}, u32[]{:S(2)}) collective-permute-start(bf16[4,2,192,768]{3,2,1,0:T(8,128)(2,1)} %get-tuple-element.179), channel_id=1, source_target_pairs={{4,0},{0,4},{12,8},{8,12},{20,16},{16,20},{28,24},{24,28},{36,32},... | collective-permute-start | bytes 7077896 | tf_op jit(solution)/shard_map/ppermute | solution.py:475
  364.8 43.1 %collective-permute-start.32 = (bf16[384,1536]{1,0:T(8,128)(2,1)S(1)}, bf16[384,1536]{1,0:T(8,128)(2,1)}, u32[]{:S(2)}, u32[]{:S(2)}) collective-permute-start(bf16[384,1536]{1,0:T(8,128)(2,1)S(1)} %slice.211), channel_id=1, source_target_pairs={{1,0},{2,1},{3,2},{0,3},{5,4},{6,5},{7,6},{4,7},{9,8},{10,9},{11,1... | collective-permute-start | bytes 3538952 | tf_op jit(solution)/shard_map/ppermute | solution.py:470
  366.2 41.6 %collective-permute-start.33 = (bf16[384,1536]{1,0:T(8,128)(2,1)S(1)}, bf16[384,1536]{1,0:T(8,128)(2,1)}, u32[]{:S(2)}, u32[]{:S(2)}) collective-permute-start(bf16[384,1536]{1,0:T(8,128)(2,1)S(1)} %slice.212), channel_id=1, source_target_pairs={{3,0},{0,1},{1,2},{2,3},{7,4},{4,5},{5,6},{6,7},{11,8},{8,9},{9,10... | collective-permute-start | bytes 3538952 | tf_op jit(solution)/shard_map/ppermute | solution.py:470
  367.8 40.1 %all-to-all-start.5 = ((bf16[32,24,768]{2,1,0:T(8,128)(2,1)}), bf16[32,24,768]{2,1,0:T(8,128)(2,1)}, u32[]{:S(2)}, u32[]{:S(2)}) async-start(bf16[32,24,768]{2,1,0:T(8,128)(2,1)} %bitcast.28), calls=%async_computation.5 | async-start | bytes 2359296 | tf_op jit(solution)/shard_map/all_to_all | solution.py:498
  376.5 28.7 %collective-permute-start.30 = (bf16[384,768]{1,0:T(8,128)(2,1)S(1)}, bf16[384,768]{1,0:T(8,128)(2,1)}, u32[]{:S(2)}, u32[]{:S(2)}) collective-permute-start(bf16[384,768]{1,0:T(8,128)(2,1)S(1)} %slice.209), channel_id=1, source_target_pairs={{1,0},{2,1},{3,2},{0,3},{5,4},{6,5},{7,6},{4,7},{9,8},{10,9},{11,1... | collective-permute-start | bytes 1769480 | tf_op jit(solution)/shard_map/ppermute | solution.py:470
  378.6 29.2 %collective-permute-start.31 = (bf16[384,768]{1,0:T(8,128)(2,1)S(1)}, bf16[384,768]{1,0:T(8,128)(2,1)}, u32[]{:S(2)}, u32[]{:S(2)}) collective-permute-start(bf16[384,768]{1,0:T(8,128)(2,1)S(1)} %slice.210), channel_id=1, source_target_pairs={{3,0},{0,1},{1,2},{2,3},{7,4},{4,5},{5,6},{6,7},{11,8},{8,9},{9,10... | collective-permute-start | bytes 1769480 | tf_op jit(solution)/shard_map/ppermute | solution.py:470
  407.9 32.9 %collective-permute-start.40 = (bf16[768,768]{1,0:T(8,128)(2,1)}, bf16[768,768]{1,0:T(8,128)(2,1)S(1)}, u32[]{:S(2)}, u32[]{:S(2)}) collective-permute-start(bf16[768,768]{1,0:T(8,128)(2,1)} %bitcast.29.refs_0_.refs_1_), channel_id=1, source_target_pairs={{2,0},{3,1},{0,2},{1,3},{6,4},{7,5},{4,6},{5,7},{10,8},{11,9},{8,1... | collective-permute-start | bytes 3538952 | tf_op jit(solution)/shard_map/ppermute | solution.py:470
  408.4 78.9 %collective-permute-start.38 = (bf16[768,768]{1,0:T(8,128)(2,1)}, bf16[768,768]{1,0:T(8,128)(2,1)}, u32[]{:S(2)}, u32[]{:S(2)}) collective-permute-start(bf16[768,768]{1,0:T(8,128)(2,1)} %bitcast.29.refs_0_.refs_1_), channel_id=1, source_target_pairs={{1,0},{2,1},{3,2},{0,3},{5,4},{6,5},{7,6},{4,7},{9,8},{10,9},{11,1... | collective-permute-start | bytes 3538952 | tf_op jit(solution)/shard_map/ppermute | solution.py:470
  410.3 77.0 %collective-permute-start.39 = (bf16[768,768]{1,0:T(8,128)(2,1)}, bf16[768,768]{1,0:T(8,128)(2,1)}, u32[]{:S(2)}, u32[]{:S(2)}) collective-permute-start(bf16[768,768]{1,0:T(8,128)(2,1)} %bitcast.29.refs_0_.refs_1_), channel_id=1, source_target_pairs={{3,0},{0,1},{1,2},{2,3},{7,4},{4,5},{5,6},{6,7},{11,8},{8,9},{9,10... | collective-permute-start | bytes 3538952 | tf_op jit(solution)/shard_map/ppermute | solution.py:470
  425.3 8.9 %copy-start.4 = (bf16[4,2,192,768]{3,2,1,0:T(8,128)(2,1)S(1)}, bf16[4,2,192,768]{3,2,1,0:T(8,128)(2,1)}, u32[]{:S(2)}) copy-start(bf16[4,2,192,768]{3,2,1,0:T(8,128)(2,1)} %get-tuple-element.178) | copy-start | bytes 7077892
  425.3 62.0 %all-to-all-start.6 = ((bf16[32,24,768]{2,1,0:T(8,128)(2,1)}), bf16[32,24,768]{2,1,0:T(8,128)(2,1)}, u32[]{:S(2)}, u32[]{:S(2)}) async-start(bf16[32,24,768]{2,1,0:T(8,128)(2,1)} %bitcast.114), calls=%async_computation.6 | async-start | bytes 2359296 | tf_op jit(solution)/shard_map/all_to_all | solution.py:498
  436.6 40.0 %collective-permute-start.35 = (bf16[384,768]{1,0:T(8,128)(2,1)S(1)}, bf16[384,768]{1,0:T(8,128)(2,1)S(1)}, u32[]{:S(2)}, u32[]{:S(2)}) collective-permute-start(bf16[384,768]{1,0:T(8,128)(2,1)S(1)} %get-tuple-element.266), channel_id=1, source_target_pairs={{3,0},{0,1},{1,2},{2,3},{7,4},{4,5},{5,6},{6,7},{11,8},{8,9},{9,10... | collective-permute-start | bytes 1769480 | tf_op jit(solution)/shard_map/ppermute | solution.py:470
  436.7 50.3 %collective-permute-start.36 = (bf16[384,768]{1,0:T(8,128)(2,1)S(1)}, bf16[384,768]{1,0:T(8,128)(2,1)S(1)}, u32[]{:S(2)}, u32[]{:S(2)}) collective-permute-start(bf16[384,768]{1,0:T(8,128)(2,1)S(1)} %get-tuple-element.268), channel_id=1, source_target_pairs={{2,0},{3,1},{0,2},{1,3},{6,4},{7,5},{4,6},{5,7},{10,8},{11,9},{8,1... | collective-permute-start | bytes 1769480 | tf_op jit(solution)/shard_map/ppermute | solution.py:470
  440.8 46.2 %collective-permute-start.37 = (bf16[384,768]{1,0:T(8,128)(2,1)S(1)}, bf16[384,768]{1,0:T(8,128)(2,1)S(1)}, u32[]{:S(2)}, u32[]{:S(2)}) collective-permute-start(bf16[384,768]{1,0:T(8,128)(2,1)S(1)} %get-tuple-element.267), channel_id=1, source_target_pairs={{1,0},{2,1},{3,2},{0,3},{5,4},{6,5},{7,6},{4,7},{9,8},{10,9},{11,1... | collective-permute-start | bytes 1769480 | tf_op jit(solution)/shard_map/ppermute | solution.py:470
  487.3 18.1 %copy-start.21 = (f32[40,768]{1,0:T(8,128)S(1)}, f32[40,768]{1,0:T(8,128)}, u32[]{:S(2)}) copy-start(f32[40,768]{1,0:T(8,128)} %get-tuple-element.202) | copy-start | bytes 368644
  503.6 6.1 collective-permute-start.41
  506.4 3.1 collective-permute-start.42
  512.1 31.6 %collective-permute-start.43 = (bf16[432,768]{1,0:T(8,128)(2,1)S(1)}, bf16[432,768]{1,0:T(8,128)(2,1)S(1)}, u32[]{:S(2)}, u32[]{:S(2)}) collective-permute-start(bf16[432,768]{1,0:T(8,128)(2,1)S(1)} %get-tuple-element.263), channel_id=1, source_target_pairs={{3,0},{0,1},{1,2},{2,3},{7,4},{4,5},{5,6},{6,7},{11,8},{8,9},{9,10... | collective-permute-start | bytes 1990664 | tf_op jit(solution)/shard_map/ppermute | solution.py:470
  512.2 31.5 %collective-permute-start.44 = (bf16[432,768]{1,0:T(8,128)(2,1)S(1)}, bf16[432,768]{1,0:T(8,128)(2,1)S(1)}, u32[]{:S(2)}, u32[]{:S(2)}) collective-permute-start(bf16[432,768]{1,0:T(8,128)(2,1)S(1)} %get-tuple-element.264), channel_id=1, source_target_pairs={{2,0},{3,1},{0,2},{1,3},{6,4},{7,5},{4,6},{5,7},{10,8},{11,9},{8,1... | collective-permute-start | bytes 1990664 | tf_op jit(solution)/shard_map/ppermute | solution.py:470
  512.8 31.2 %collective-permute-start.45 = (bf16[432,768]{1,0:T(8,128)(2,1)S(1)}, bf16[432,768]{1,0:T(8,128)(2,1)S(1)}, u32[]{:S(2)}, u32[]{:S(2)}) collective-permute-start(bf16[432,768]{1,0:T(8,128)(2,1)S(1)} %get-tuple-element.265), channel_id=1, source_target_pairs={{1,0},{2,1},{3,2},{0,3},{5,4},{6,5},{7,6},{4,7},{9,8},{10,9},{11,1... | collective-permute-start | bytes 1990664 | tf_op jit(solution)/shard_map/ppermute | solution.py:470
  571.1 42.6 %all-to-all-start.8 = ((bf16[32,51,768]{2,1,0:T(8,128)(2,1)}), bf16[32,51,768]{2,1,0:T(8,128)(2,1)S(1)}, u32[]{:S(2)}, u32[]{:S(2)}) async-start(bf16[32,51,768]{2,1,0:T(8,128)(2,1)} %broadcast_in_dim.24), calls=%async_computation.8 | async-start | bytes 5505024 | tf_op jit(solution)/shard_map/all_to_all | solution.py:780
  580.4 26.8 %copy-start.11 = (f32[208,768]{1,0:T(8,128)S(1)}, f32[208,768]{1,0:T(8,128)}, u32[]{:S(2)}) copy-start(f32[208,768]{1,0:T(8,128)} %get-tuple-element.198) | copy-start | bytes 1916932
  (19 other events, 82.6 us)

commit v3 on v2

--- a/solution.py
+++ b/solution.py
@@ -664,9 +664,8 @@
     early, _ = tie(rows0, both1)
     after0, before0, far0 = ring_rows(early)
     both = swap(both, stride)
-    both, after1, before1, after0, before0 = tie(both, after1, before1, after0, before0)
+    both, after1, before1 = tie(both, after1, before1)
     joint1 = [both1, after1, before1, *far1(after1, before1)]
-    rows_pieces = [rows0, after0, before0, *far0(after0, before0)]
 
     half_shape = shaped((parts, 2, part, width), BF16)
     small_shape = shaped((40, width), F32)
@@ -724,9 +723,9 @@
         return sum([a.astype(F32) for a in got], spot(0).astype(F32)).astype(BF16)
 
     line1 = line_sum(chip_sum(keep1, give1))
+    send, after0, before0 = tie(send, after0, before0)
+    rows_pieces = [rows0, after0, before0, *far0(after0, before0)]
     grads0 = swap(send, stride)
-    grads0, *rows_pieces = tie(grads0, *rows_pieces)
-    grads0, *joint1 = tie(grads0, *joint1)
     (back0,) = expert_pieces(
         None,
         grads0,
@@ -738,13 +737,13 @@
     )
     bias_columns = expert_in_bias[:, 0].astype(F32)[:, :, None]
     back0, *joint1 = tie(back0, *joint1)
+    back0, *rows_pieces = tie(back0, *rows_pieces)
     own = expert_grads(joint1, expert_in[1, 0], bias_columns[1], expert_out[1, 0], 1)
     far_rows = ahead(grads0, 2)
     grads_pieces = [grads0, ahead(grads0, 1), ahead(grads0, 3)]
     grads_pieces += [far_rows[: rows // 2], far_rows[rows // 2 :]]
     back0 = swap(back0, stride)
-    back0, line1, *own = tie(back0, line1, *own)
-    back0, *grads_pieces = tie(back0, *grads_pieces)
+    back0, *own = tie(back0, *own)
     q, k, v, m, lse, probs, gates = kept0
     g, keep0, give0, small0 = mixer_backward(
         False,
@@ -753,6 +752,7 @@
         [full_rows, half_shape, half_shape, small_shape],
     )
 
+    keep0, give0, line1, *grads_pieces = tie(keep0, give0, line1, *grads_pieces)
     own = expert_grads(
         list(zip(rows_pieces, grads_pieces)),
         expert_in[0, 0],
@@ -761,9 +761,10 @@
         0,
         own,
     )
-    in_grad, in_bias_grad, out_grad, out_bias_grad = own
     smalls = jnp.concatenate([small0, small1, jnp.zeros((-80 % size, width), F32)])
     line0 = line_sum(chip_sum(keep0, give0, smalls))
+    line0, *own = tie(line0, *own)
+    in_grad, in_bias_grad, out_grad, out_bias_grad = own
     each = 2 * part * 2 // size
     lines = jnp.concatenate(
         [
@@ -778,27 +779,33 @@
     )
     final = jnp.sum(got.astype(F32), axis=0).astype(BF16)
     got = lax.all_to_all(
-        jnp.broadcast_to(final[None], (size,) + final.shape),
+        jnp.broadcast_to(final[None], (size // 2,) + final.shape),
         "expert",
         split_axis=0,
         concat_axis=0,
         tiled=True,
-    )
+        axis_index_groups=same_core,
+    )
+    swapped = other_core(got)
     extra = final.shape[0] - 2 * each
 
-    def unpack_body(got_ref, qkv_out, out_out, small_ref):
-        for source in range(size):
-            place, c = source // 2, source % 2
-            kind = 2 * c + place * each // part
-            spot = pl.ds(place * each % part, each)
-            for layer in range(LAYERS):
-                lines = got_ref[source, layer * each : (layer + 1) * each, :].astype(F32)
-                if kind < 3:
-                    qkv_out[layer, kind, spot, :] = lines
-                else:
-                    out_out[layer, spot, :] = lines
-            start = (c * (size // 2) + place) * extra
-            small_ref[start : start + extra, :] = got_ref[source, 2 * each :, :].astype(F32)
+    def unpack_body(here_ref, mine_ref, theirs_ref, qkv_out, out_out, small_ref):
+        def unpack(c, got_ref):
+            for place in range(size // 2):
+                kind = 2 * c + place * each // part
+                spot = pl.ds(place * each % part, each)
+                for layer in range(LAYERS):
+                    lines = got_ref[place, layer * each : (layer + 1) * each, :].astype(F32)
+                    if kind < 3:
+                        qkv_out[layer, kind, spot, :] = lines
+                    else:
+                        out_out[layer, spot, :] = lines
+                start = (c * (size // 2) + place) * extra
+                small_ref[start : start + extra, :] = got_ref[place, 2 * each :, :].astype(F32)
+
+        for c in range(2):
+            pl.when(here_ref[1] == c)(functools.partial(unpack, c, mine_ref))
+            pl.when(here_ref[1] != c)(functools.partial(unpack, c, theirs_ref))
 
     qkv_grad, out_weight_grad, smalls = pl.pallas_call(
         unpack_body,
@@ -808,8 +815,10 @@
             shaped((size * extra, width), F32),
         ],
         compiler_params=pltpu.CompilerParams(vmem_limit_bytes=VMEM_LIMIT),
+        in_specs=[pl.BlockSpec(memory_space=pltpu.SMEM)]
+        + [pl.BlockSpec(memory_space=pltpu.VMEM)] * 2,
         cost_estimate=pl.CostEstimate(flops=0, bytes_accessed=10_000_000, transcendentals=0),
-    )(got)
+    )(here, got, swapped)
     small_sum = smalls[:80].reshape(LAYERS, 40, width)
     mine = lax.dynamic_slice_in_dim(small_sum, me * part, part, axis=2)
     router_grad = jnp.swapaxes(mine[:, 7 : 7 + experts], 1, 2)

time: 632 us -> 613 us (0.970)
  waiting for transfers between devices: 262 us -> 215 us
  blocking collectives: 24.5 us -> 45.6 us
  local copies, waits for them, and re-layouts: 40.3 us -> 52.6 us
    ppermute x37, waiting for transfers between devices: 205 us -> 129 us  [ahead(): lax.ppermute(value, axis, [((i + steps) % size, i) for i in range(size)])]
    all_to_all x6, waiting for transfers between devices: 48.4 us -> 83 us  [swap(): lax.all_to_all(rows.reshape(-1, stride, width), 'expert', split_axis=0, c...]
    all_to_all x0 -> x1, blocking collectives: none -> 20.9 us  [shards(): lax.all_to_all(jnp.broadcast_to(final[None], (size // 2,) + final.shape),...]
    all_to_all x1 -> x0, starting transfers between devices: 7.6 us -> none  [shards(): lax.all_to_all(jnp.broadcast_to(final[None], (size,) + final.shape), 'exp...]
    ppermute x9 -> x10, starting transfers between devices: 13.4 us -> 17.1 us  [other_core(): return lax.ppermute(value, 'expert', [(i ^ 1, i) for i in range(size)])]
  transfers between devices with their start and end apart: 54 -> 54, of which waited for: 25 -> 23; matrix products, arithmetic and copies ran while one was open for 7% -> 8% of each run, Pallas kernels for 19% -> 25%
where the time goes in v3:
time: 613 us; the launch traced here: 603 us
  waiting for transfers between devices  215 us (35%)
  Pallas kernels  166 us (27%)
  starting transfers between devices  107 us (17%)
  local copies, waits for them, and re-layouts  52.6 us (9%)
  blocking collectives  45.6 us (7%)
  other arithmetic  15.7 us (3%)
    ppermute x37, waiting for transfers between devices, ahead(): lax.ppermute(value, axis, [((i + steps) % size, i) for i in range(size)])  129 us
    all_to_all x6, waiting for transfers between devices, swap(): lax.all_to_all(rows.reshape(-1, stride, width), 'expert', split_axis=0, c...  83 us
    pallas_call x5, Pallas kernels, expert_pieces(): pl.pallas_call(body, out_shape=[s for _, s in shapes], in_specs=[pl.Block...  60.4 us
    pallas_call x2, Pallas kernels, expert_grads(): pl.pallas_call(body, grid=(1,), in_specs=[pl.BlockSpec(memory_space=pl.AN...  49.8 us
    all_to_all x6, starting transfers between devices, swap(): lax.all_to_all(rows.reshape(-1, stride, width), 'expert', split_axis=0, c...  49.3 us
    ppermute x37, starting transfers between devices, ahead(): lax.ppermute(value, axis, [((i + steps) % size, i) for i in range(size)])  36.3 us
    pallas_call x2, Pallas kernels, mixer_backward(): pl.pallas_call(functools.partial(mixer_backward_body, last, count, scale,...  33.1 us
    all_to_all x1, blocking collectives, shards(): lax.all_to_all(lines, 'expert', split_axis=0, concat_axis=0, tiled=True,...  24.7 us
  transfers between devices with their start and end apart: 54, of which 23 were waited for; matrix products, arithmetic and copies ran while one was open for 8% of the time, Pallas kernels for 25%

profile of v3, /device:TPU:1, one launch (start us, length us, event | category | flops | bytes accessed | tf_op | source)
XLA Modules:
  0.0 603.5 jit_solution(5064405592273938554)
XLA Ops:
  0.7 1.6 slice_bitcast_fusion.4
  3.4 3.3 collective-permute-start
  7.6 4.1 all-to-all-start
  16.8 3.5 slice_bitcast_fusion
  20.3 1.8 collective-permute-start.4
  22.1 3.3 collective-permute-start.5
  31.7 5.5 collective-permute-done.1
  39.8 1.7 collective-permute-start.6
  44.3 7.6 %shard_map.220 = (f32[208,768]{1,0:T(8,128)}, bf16[768,768]{1,0:T(8,128)(2,1)}, bf16[208,768]{1,0:T(8,128)(2,1)}, bf16[208,768]{1,0:T(8,128)(2,1)}, bf16[208,768...) custom-call(s32[2]{0:T(128)} %pad_add_fusion.refs_0_.refs_13_.here_r, ...), custom_call_target="tpu_custom_call" | custom-call | flops 2000000000 | bytes 20000000 | tf_op jit(solution)/shard_map/pallas_call | solution.py:600
  51.9 8.3 %all-to-all-start.1 = ((bf16[32,24,768]{2,1,0:T(8,128)(2,1)}), bf16[32,24,768]{2,1,0:T(8,128)(2,1)}, u32[]{:S(2)}, u32[]{:S(2)}) async-start(bf16[32,24,768]{2,1,0:T(8,128)(2,1)} %bitcast.122), calls=%async_computation.1 | async-start | bytes 2359296 | tf_op jit(solution)/shard_map/all_to_all | solution.py:498
  60.5 2.4 collective-permute-start.8
  63.0 1.6 collective-permute-start.9
  67.1 11.5 %all-to-all-done.1 = bf16[32,24,768]{2,1,0:T(8,128)(2,1)} async-done(((bf16[32,24,768]{2,1,0:T(8,128)(2,1)}), bf16[32,24,768]{2,1,0:T(8,128)(2,1)}, u32[]{:S(2)}, u32[]{:S(2)}) %all-to-all-start.1) | async-done | bytes 1179680 | tf_op jit(solution)/shard_map/all_to_all | solution.py:498
  78.6 6.8 %shard_map.221 = (f32[768,768]{1,0:T(8,128)}, bf16[1,768,768]{2,1,0:T(8,128)(2,1)}) custom-call(bf16[768,768]{1,0:T(8,128)(2,1)} %bitcast.13.refs_0_, f32[1,768]{1,0:T(1,128)} %get-tuple-element.292.refs_1_, f32[1,768]{1,0:T(1,128)} %get-tuple-element.298.refs_2_, bf16[768,768]{1,0:T(8,128)(2,1)} %get-tuple-element.124.refs_3_.refs_1_.refs_10_, ...), custom_call_target="tpu_custom_call" | custom-call | flops 1811939328 | bytes 20000000 | tf_op jit(solution)/shard_map/pallas_call | solution.py:394
  85.4 3.4 collective-permute-done.10.refs_6_
  88.8 24.2 %collective-permute-done.7.refs_3_ = bf16[768,768]{1,0:T(8,128)(2,1)} collective-permute-done((bf16[768,768]{1,0:T(8,128)(2,1)}, bf16[768,768]{1,0:T(8,128)(2,1)}, u32[]{:S(2)}, u32[]{:S(2)}) %collective-permute-start.7) | collective-permute-done | bytes 1179680 | tf_op jit(solution)/shard_map/ppermute | solution.py:470
  114.1 2.4 collective-permute-start.17
  116.5 2.7 collective-permute-start.11
  119.9 10.3 %shard_map.222 = (f32[768,768]{1,0:T(8,128)}, bf16[2,768,768]{2,1,0:T(8,128)(2,1)}) custom-call(bf16[768,768]{1,0:T(8,128)(2,1)} %bitcast.13.refs_0_, f32[2,768]{1,0:T(2,128)} %slice.193.refs_1_, f32[768,768]{1,0:T(8,128)} %get-tuple-element.127.refs_2_, bf16[768,768]{1,0:T(8,128)(2,1)} %collective-permute-done.7.refs_3_, ...), custom_call_target="tpu_custom_call" | custom-call | flops 3623878656 | bytes 20000000 | tf_op jit(solution)/shard_map/pallas_call | solution.py:394
  130.2 23.1 %collective-permute-done.11.refs_2_ = bf16[2,192,768]{2,1,0:T(8,128)(2,1)S(1)} collective-permute-done((bf16[2,192,768]{2,1,0:T(8,128)(2,1)S(1)}, bf16[2,192,768]{2,1,0:T(8,128)(2,1)S(1)}, u32[]{:S(2)}, u32[]{:S(2)}) %collective-permute-start.11) | collective-permute-done | bytes 589856 | tf_op jit(solution)/shard_map/ppermute | solution.py:470
  153.3 3.0 collective-permute-done.12.refs_4_
  156.3 2.6 collective-permute-start.15
  160.5 7.2 %shard_map.223 = (bf16[768,768]{1,0:T(8,128)(2,1)}, bf16[1,768,768]{2,1,0:T(8,128)(2,1)}) custom-call(bf16[768,768]{1,0:T(8,128)(2,1)} %bitcast.13.refs_0_, f32[1,768]{1,0:T(1,128)} %get-tuple-element.291.refs_1_, f32[768,768]{1,0:T(8,128)} %get-tuple-element.140.refs_2_, bf16[768,768]{1,0:T(8,128)(2,1)} %collective-permute-done.17.refs_3_.refs_7_, ...), custom_call_target="tpu_custom_call" | custom-call | flops 1811939328 | bytes 20000000 | tf_op jit(solution)/shard_map/pallas_call | solution.py:394
  167.7 8.4 %all-to-all-start.2 = ((bf16[32,24,768]{2,1,0:T(8,128)(2,1)}), bf16[32,24,768]{2,1,0:T(8,128)(2,1)S(1)}, u32[]{:S(2)}, u32[]{:S(2)}) async-start(bf16[32,24,768]{2,1,0:T(8,128)(2,1)} %bitcast.120), calls=%async_computation.2 | async-start | bytes 2359296 | tf_op jit(solution)/shard_map/all_to_all | solution.py:498
  185.4 9.1 %all-to-all-done.2 = bf16[32,24,768]{2,1,0:T(8,128)(2,1)S(1)} async-done(((bf16[32,24,768]{2,1,0:T(8,128)(2,1)}), bf16[32,24,768]{2,1,0:T(8,128)(2,1)S(1)}, u32[]{:S(2)}, u32[]{:S(2)}) %all-to-all-start.2) | async-done | bytes 1179680 | tf_op jit(solution)/shard_map/all_to_all | solution.py:498
  195.6 10.2 %shard_map.224 = (f32[208,768]{1,0:T(8,128)}, bf16[768,1536]{1,0:T(8,128)(2,1)}, bf16[208,768]{1,0:T(8,128)(2,1)}, bf16[208,768]{1,0:T(8,128)(2,1)}, bf16[208,76...) custom-call(s32[2]{0:T(128)} %pad_add_fusion.refs_0_.refs_13_.here_r, ...), custom_call_target="tpu_custom_call" | custom-call | flops 2000000000 | bytes 20000000 | tf_op jit(solution)/shard_map/pallas_call | solution.py:600
  207.3 8.5 %all-to-all-start.3 = ((bf16[32,24,1536]{2,1,0:T(8,128)(2,1)}), bf16[32,24,1536]{2,1,0:T(8,128)(2,1)S(1)}, u32[]{:S(2)}, u32[]{:S(2)}) async-start(bf16[32,24,1536]{2,1,0:T(8,128)(2,1)} %bitcast.107), calls=%async_computation.3 | async-start | bytes 4718592 | tf_op jit(solution)/shard_map/all_to_all | solution.py:498
  218.8 28.1 %all-to-all-done.3 = bf16[32,24,1536]{2,1,0:T(8,128)(2,1)S(1)} async-done(((bf16[32,24,1536]{2,1,0:T(8,128)(2,1)}), bf16[32,24,1536]{2,1,0:T(8,128)(2,1)S(1)}, u32[]{:S(2)}, u32[]{:S(2)}) %all-to-all-start.3) | async-done | bytes 2359328 | tf_op jit(solution)/shard_map/all_to_all | solution.py:498
  247.0 1.6 collective-permute-start.27
  248.6 20.0 %collective-permute-done.23.refs_7_ = bf16[768,768]{1,0:T(8,128)(2,1)} collective-permute-done((bf16[768,768]{1,0:T(8,128)(2,1)}, bf16[768,768]{1,0:T(8,128)(2,1)}, u32[]{:S(2)}, u32[]{:S(2)}) %collective-permute-start.23) | collective-permute-done | bytes 1179680 | tf_op jit(solution)/shard_map/ppermute | solution.py:470
  269.9 21.2 %shard_map.225 = bf16[768,1536]{1,0:T(8,128)(2,1)} custom-call(bf16[768,1536]{1,0:T(8,128)(2,1)} %bitcast.105, f32[4,768]{1,0:T(4,128)} %get-tuple-element.299.refs_1_, f32[1,768]{1,0:T(1,128)} %get-tuple-element.297.refs_2_, bf16[768,768]{1,0:T(8,128)(2,1)} %get-tuple-element.144.refs_3_.refs_5_, bf16[768,768]{1,0:T(8,128)(2,1)} %get-tuple-element.145.refs_4_.refs_7_, ...), custom_call_target="tpu_custom_call" | custom-call | flops 14495514624 | bytes 20000000 | tf_op jit(solution)/shard_map/pallas_call | solution.py:394
  291.1 9.4 %all-to-all-start.4 = ((bf16[32,24,1536]{2,1,0:T(8,128)(2,1)}), bf16[32,24,1536]{2,1,0:T(8,128)(2,1)}, u32[]{:S(2)}, u32[]{:S(2)}) async-start(bf16[32,24,1536]{2,1,0:T(8,128)(2,1)} %bitcast.108), calls=%async_computation.4 | async-start | bytes 4718592 | tf_op jit(solution)/shard_map/all_to_all | solution.py:498
  302.0 29.7 %all-to-all-done.4 = bf16[32,24,1536]{2,1,0:T(8,128)(2,1)} async-done(((bf16[32,24,1536]{2,1,0:T(8,128)(2,1)}), bf16[32,24,1536]{2,1,0:T(8,128)(2,1)}, u32[]{:S(2)}, u32[]{:S(2)}) %all-to-all-start.4) | async-done | bytes 2359328 | tf_op jit(solution)/shard_map/all_to_all | solution.py:498
  331.7 16.7 %shard_map.226 = (f32[208,768]{1,0:T(8,128)}, bf16[4,2,192,768]{3,2,1,0:T(8,128)(2,1)}, bf16[4,2,192,768]{3,2,1,0:T(8,128)(2,1)}, f32[40,768]{1,0:T(8,128)}, bf1...) custom-call(f32[208,768]{1,0:T(8,128)} %pad_convert_fusion.1.refs_12_.refs_0_, bf16[768,1536]{1,0:T(8,128)(2,1)} %bitcast.27.refs_1_, ...), custom_call_target="tpu_custom_call" | custom-call | flops 4000000000 | bytes 20000000 | tf_op jit(solution)/shard_map/pallas_call | solution.py:677
  349.5 4.6 all-to-all-start.5
  354.0 2.4 slice.209
  357.0 2.4 slice.210
  362.0 1.9 slice.211
  364.0 1.8 collective-permute-start.32
  365.8 1.9 slice.212
  367.7 4.7 all-to-all-done.5
  373.4 15.0 %shard_map.227 = bf16[768,768]{1,0:T(8,128)(2,1)} custom-call(bf16[768,768]{1,0:T(8,128)(2,1)} %bitcast.113, bf16[768,768]{1,0:T(8,128)(2,1)} %get-tuple-element.124.refs_3_.refs_1_.refs_10_, bf16[768,768]{1,0:T(8,128)(2,1)} %copy-done.10, bf16[768,768]{1,0:T(8,128)(2,1)} %collective-permute-done.7.refs_3_, bf16[768,768]{1,0:T(8,128)(2,1)} %collective-permute-done.8.refs_4_, ...), custom_call_target="tpu_custom_call" | custom-call | flops 7247757312 | bytes 20000000 | tf_op jit(solution)/shard_map/pallas_call | solution.py:394
  389.0 2.2 collective-permute-start.38
  391.1 5.5 collective-permute-done.32.refs_6_
  397.1 28.2 %collective-permute-done.33.refs_8_ = bf16[384,768]{1,0:T(8,128)(2,1)} collective-permute-done((bf16[384,768]{1,0:T(8,128)(2,1)}, bf16[384,768]{1,0:T(8,128)(2,1)}, u32[]{:S(2)}, u32[]{:S(2)}) %collective-permute-start.33) | collective-permute-done | bytes 589856 | tf_op jit(solution)/shard_map/ppermute | solution.py:470
  425.2 10.1 %all-to-all-start.6 = ((bf16[32,24,768]{2,1,0:T(8,128)(2,1)}), bf16[32,24,768]{2,1,0:T(8,128)(2,1)S(1)}, u32[]{:S(2)}, u32[]{:S(2)}) async-start(bf16[32,24,768]{2,1,0:T(8,128)(2,1)} %bitcast.119), calls=%async_computation.6 | async-start | bytes 2359296 | tf_op jit(solution)/shard_map/all_to_all | solution.py:498
  435.4 25.0 %shard_map.228 = (f32[2,768,768]{2,1,0:T(8,128)}, f32[2,768,1]{2,1,0:T(8,128)}, f32[2,768,768]{2,1,0:T(8,128)}, f32[2,1,768]{2,1,0:T(1,128)}) custom-call(bf16[768,1536]{1,0:T(8,128)(2,1)} %bitcast.106, bf16[768,1536]{1,0:T(8,128)(2,1)} %collective-permute-done.26.refs_1_, bf16[768,1536]{1,0:T(8,128)(2,1)} %collective-permute-done.27.refs_2_, ...), custom_call_target="tpu_custom_call" | custom-call | flops 14495514624 | bytes 20000000 | tf_op jit(solution)/shard_map/pallas_call | solution.py:451
  461.8 2.2 add_convert_fusion.1
  465.7 2.4 collective-permute-start.37
  468.0 2.4 fusion.27
  471.4 16.4 %shard_map.229 = (f32[208,768]{1,0:T(8,128)}, bf16[4,2,192,768]{3,2,1,0:T(8,128)(2,1)}, bf16[4,2,192,768]{3,2,1,0:T(8,128)(2,1)}, f32[40,768]{1,0:T(8,128)}) custom-call(f32[208,768]{1,0:T(8,128)} %get-tuple-element.161.refs_0_, bf16[768,768]{1,0:T(8,128)(2,1)} %bitcast.121, f32[208,768]{1,0:T(8,128)} %pad_convert_fusion.refs_8_.refs_2_, ...), custom_call_target="tpu_custom_call" | custom-call | flops 4000000000 | bytes 20000000 | tf_op jit(solution)/shard_map/pallas_call | solution.py:677
  487.9 6.3 %collective-permute-done.35 = bf16[384,768]{1,0:T(8,128)(2,1)} collective-permute-done((bf16[384,768]{1,0:T(8,128)(2,1)}, bf16[384,768]{1,0:T(8,128)(2,1)}, u32[]{:S(2)}, u32[]{:S(2)}) %collective-permute-start.35) | collective-permute-done | bytes 589856 | tf_op jit(solution)/shard_map/ppermute | solution.py:470
  494.5 1.7 fusion.5
  499.0 3.0 collective-permute-done.42
  502.1 2.2 add_convert_fusion
  504.6 3.2 collective-permute-start.44
  508.0 24.7 %shard_map.230 = (f32[2,768,768]{2,1,0:T(8,128)}, f32[2,768,1]{2,1,0:T(8,128)}, f32[2,768,768]{2,1,0:T(8,128)}, f32[2,1,768]{2,1,0:T(1,128)}) custom-call(bf16[768,768]{1,0:T(8,128)(2,1)} %bitcast.13.refs_0_, bf16[768,768]{1,0:T(8,128)(2,1)} %bitcast.117, ...), custom_call_target="tpu_custom_call", output_to_operand_aliasing={{0}: (13, {}), {1}: (14, {}), {2}: (15, {}), {3}: (16, {})} | custom-call | flops 14495514624 | bytes 20000000 | tf_op jit(solution)/shard_map/pallas_call | solution.py:451
  532.8 3.9 collective-permute-done.44
  537.3 24.7 %all_to_all.45 = bf16[16,51,768]{2,1,0:T(8,128)(2,1)S(1)} all-to-all(bf16[16,51,768]{2,1,0:T(8,128)(2,1)S(1)} %pad_maximum_fusion.1), channel_id=1, replica_groups={{0,8,16,24,32,40,48,56,64,72,80,88,96,104,112,120},{4,12,20,28,36,44,52..., dimensions={0} | all-to-all | bytes 2506752 | tf_op jit(solution)/shard_map/all_to_all | solution.py:777
  562.3 20.9 %all_to_all.46.mine_ref = bf16[16,51,768]{2,1,0:T(8,128)(2,1)S(1)} all-to-all(bf16[16,51,768]{2,1,0:T(8,128)(2,1)S(1)} %broadcast_in_dim.24), channel_id=1, replica_groups={{0,8,16,24,32,40,48,56,64,72,80,88,96,104,112,120},{4,12,20,28,36,44,52..., dimensions={0} | all-to-all | bytes 2506752 | tf_op jit(solution)/shard_map/all_to_all | solution.py:781
  584.6 4.3 collective-permute-start.46
  588.9 1.7 slice.208
  590.6 1.9 slice.214
  594.9 4.4 shard_map.231
  (237 shorter events, 64.5 us)
Async XLA Ops:
  3.4 16.9 %collective-permute-start = (bf16[2,192,768]{2,1,0:T(8,128)(2,1)}, bf16[2,192,768]{2,1,0:T(8,128)(2,1)}, u32[]{:S(2)}, u32[]{:S(2)}) collective-permute-start(bf16[2,192,768]{2,1,0:T(8,128)(2,1)} %fusion.16), channel_id=1, source_target_pairs={{1,0},{2,1},{3,2},{0,3},{5,4},{6,5},{7,6},{4,7},{9,8},{10,9},{11,1... | collective-permute-start | bytes 1769480 | tf_op jit(solution)/shard_map/ppermute | solution.py:470
  6.7 15.4 %collective-permute-start.2 = (bf16[2,192,768]{2,1,0:T(8,128)(2,1)}, bf16[2,192,768]{2,1,0:T(8,128)(2,1)}, u32[]{:S(2)}, u32[]{:S(2)}) collective-permute-start(bf16[2,192,768]{2,1,0:T(8,128)(2,1)} %fusion.16), channel_id=1, source_target_pairs={{3,0},{0,1},{1,2},{2,3},{7,4},{4,5},{5,6},{6,7},{11,8},{8,9},{9,10... | collective-permute-start | bytes 1769480 | tf_op jit(solution)/shard_map/ppermute | solution.py:470
  7.6 23.4 %all-to-all-start = ((bf16[4,88,192]{2,1,0:T(8,128)(2,1)}), bf16[4,88,192]{2,1,0:T(8,128)(2,1)S(1)}, u32[]{:S(2)}, u32[]{:S(2)}) async-start(bf16[4,88,192]{2,1,0:T(8,128)(2,1)} %broadcast_in_dim.21), calls=%async_computation | async-start | bytes 360448 | tf_op jit(solution)/shard_map/all_to_all | solution.py:547
  15.7 100.7 %copy-start.1 = (bf16[4,192,768]{2,1,0:T(8,128)(2,1)}, bf16[4,192,768]{2,1,0:T(8,128)(2,1)S(1)}, u32[]{:S(2)}) copy-start(bf16[4,192,768]{2,1,0:T(8,128)(2,1)S(1)} %pad_maximum_fusion.2.refs_1_) | copy-start | bytes 3538948
  16.8 9.3 %copy-start.18 = (s32[2,208]{0,1:T(8,128)S(1)}, s32[2,208]{0,1:T(8,128)}, u32[]{:S(2)}) copy-start(s32[2,208]{0,1:T(8,128)} %get-tuple-element.286) | copy-start | bytes 4996
  20.3 40.2 %copy-start.10 = (bf16[768,768]{1,0:T(8,128)(2,1)}, bf16[768,768]{1,0:T(8,128)(2,1)S(1)}, u32[]{:S(2)}) copy-start(bf16[768,768]{1,0:T(8,128)(2,1)S(1)} %get-tuple-element.125.refs_4_.refs_2_.refs_12_) | copy-start | bytes 3538948
  20.3 19.4 %collective-permute-start.4 = (bf16[2,192,768]{2,1,0:T(8,128)(2,1)}, bf16[2,192,768]{2,1,0:T(8,128)(2,1)}, u32[]{:S(2)}, u32[]{:S(2)}) collective-permute-start(bf16[2,192,768]{2,1,0:T(8,128)(2,1)} %collective-permute-done.refs_2_), channel_id=1, source_target_pairs={{4,0},{0,4},{12,8},{8,12},{20,16},{16,20},{28,24},{24,28},{36,32},... | collective-permute-start | bytes 1769480 | tf_op jit(solution)/shard_map/ppermute | solution.py:475
  22.1 17.6 %collective-permute-start.5 = (bf16[2,192,768]{2,1,0:T(8,128)(2,1)}, bf16[2,192,768]{2,1,0:T(8,128)(2,1)}, u32[]{:S(2)}, u32[]{:S(2)}) collective-permute-start(bf16[2,192,768]{2,1,0:T(8,128)(2,1)} %collective-permute-done.2.refs_4_), channel_id=1, source_target_pairs={{4,0},{0,4},{12,8},{8,12},{20,16},{16,20},{28,24},{24,28},{36,32},... | collective-permute-start | bytes 1769480 | tf_op jit(solution)/shard_map/ppermute | solution.py:475
  28.4 8.8 %collective-permute-start.1 = (bf16[1,192,768]{2,1,0:T(8,128)(2,1)S(1)}, bf16[1,192,768]{2,1,0:T(8,128)(2,1)}, u32[]{:S(2)}, u32[]{:S(2)}) collective-permute-start(bf16[1,192,768]{2,1,0:T(8,128)(2,1)S(1)} %slice.229), channel_id=1, source_target_pairs={{1,0},{2,1},{3,2},{0,3},{5,4},{6,5},{7,6},{4,7},{9,8},{10,9},{11,1... | collective-permute-start | bytes 884744 | tf_op jit(solution)/shard_map/ppermute | solution.py:470
  29.5 9.1 %collective-permute-start.3 = (bf16[1,192,768]{2,1,0:T(8,128)(2,1)S(1)}, bf16[1,192,768]{2,1,0:T(8,128)(2,1)}, u32[]{:S(2)}, u32[]{:S(2)}) collective-permute-start(bf16[1,192,768]{2,1,0:T(8,128)(2,1)S(1)} %slice.230), channel_id=1, source_target_pairs={{3,0},{0,1},{1,2},{2,3},{7,4},{4,5},{5,6},{6,7},{11,8},{8,9},{9,10... | collective-permute-start | bytes 884744 | tf_op jit(solution)/shard_map/ppermute | solution.py:470
  39.8 4.5 collective-permute-start.6
  51.9 26.7 %all-to-all-start.1 = ((bf16[32,24,768]{2,1,0:T(8,128)(2,1)}), bf16[32,24,768]{2,1,0:T(8,128)(2,1)}, u32[]{:S(2)}, u32[]{:S(2)}) async-start(bf16[32,24,768]{2,1,0:T(8,128)(2,1)} %bitcast.122), calls=%async_computation.1 | async-start | bytes 2359296 | tf_op jit(solution)/shard_map/all_to_all | solution.py:498
  60.2 28.6 %collective-permute-start.10 = (bf16[768,768]{1,0:T(8,128)(2,1)S(1)}, bf16[768,768]{1,0:T(8,128)(2,1)}, u32[]{:S(2)}, u32[]{:S(2)}) collective-permute-start(bf16[768,768]{1,0:T(8,128)(2,1)S(1)} %get-tuple-element.125.refs_4_.refs_2_.refs_12_), channel_id=1, source_target_pairs={{3,0},{0,1},{1,2},{2,3},{7,4},{4,5},{5,6},{6,7},{11,8},{8,9},{9,10... | collective-permute-start | bytes 3538952 | tf_op jit(solution)/shard_map/ppermute | solution.py:470
  60.5 52.6 %collective-permute-start.8 = (bf16[768,768]{1,0:T(8,128)(2,1)S(1)}, bf16[768,768]{1,0:T(8,128)(2,1)}, u32[]{:S(2)}, u32[]{:S(2)}) collective-permute-start(bf16[768,768]{1,0:T(8,128)(2,1)S(1)} %get-tuple-element.125.refs_4_.refs_2_.refs_12_), channel_id=1, source_target_pairs={{1,0},{2,1},{3,2},{0,3},{5,4},{6,5},{7,6},{4,7},{9,8},{10,9},{11,1... | collective-permute-start | bytes 3538952 | tf_op jit(solution)/shard_map/ppermute | solution.py:470
  62.9 50.1 %collective-permute-start.7 = (bf16[768,768]{1,0:T(8,128)(2,1)}, bf16[768,768]{1,0:T(8,128)(2,1)}, u32[]{:S(2)}, u32[]{:S(2)}) collective-permute-start(bf16[768,768]{1,0:T(8,128)(2,1)} %get-tuple-element.124.refs_3_.refs_1_.refs_10_), channel_id=1, source_target_pairs={{1,0},{2,1},{3,2},{0,3},{5,4},{6,5},{7,6},{4,7},{9,8},{10,9},{11,1... | collective-permute-start | bytes 3538952 | tf_op jit(solution)/shard_map/ppermute | solution.py:470
  63.0 51.1 %collective-permute-start.9 = (bf16[768,768]{1,0:T(8,128)(2,1)}, bf16[768,768]{1,0:T(8,128)(2,1)}, u32[]{:S(2)}, u32[]{:S(2)}) collective-permute-start(bf16[768,768]{1,0:T(8,128)(2,1)} %get-tuple-element.124.refs_3_.refs_1_.refs_10_), channel_id=1, source_target_pairs={{3,0},{0,1},{1,2},{2,3},{7,4},{4,5},{5,6},{6,7},{11,8},{8,9},{9,10... | collective-permute-start | bytes 3538952 | tf_op jit(solution)/shard_map/ppermute | solution.py:470
  114.1 45.1 %collective-permute-start.17 = (bf16[768,768]{1,0:T(8,128)(2,1)}, bf16[768,768]{1,0:T(8,128)(2,1)}, u32[]{:S(2)}, u32[]{:S(2)}) collective-permute-start(bf16[768,768]{1,0:T(8,128)(2,1)} %collective-permute-done.7.refs_3_), channel_id=1, source_target_pairs={{1,0},{2,1},{3,2},{0,3},{5,4},{6,5},{7,6},{4,7},{9,8},{10,9},{11,1... | collective-permute-start | bytes 3538952 | tf_op jit(solution)/shard_map/ppermute | solution.py:470
  116.5 44.0 %collective-permute-start.19 = (bf16[768,768]{1,0:T(8,128)(2,1)}, bf16[768,768]{1,0:T(8,128)(2,1)}, u32[]{:S(2)}, u32[]{:S(2)}) collective-permute-start(bf16[768,768]{1,0:T(8,128)(2,1)} %collective-permute-done.10.refs_6_), channel_id=1, source_target_pairs={{3,0},{0,1},{1,2},{2,3},{7,4},{4,5},{5,6},{6,7},{11,8},{8,9},{9,10... | collective-permute-start | bytes 3538952 | tf_op jit(solution)/shard_map/ppermute | solution.py:470
  116.5 36.8 %collective-permute-start.11 = (bf16[2,192,768]{2,1,0:T(8,128)(2,1)S(1)}, bf16[2,192,768]{2,1,0:T(8,128)(2,1)S(1)}, u32[]{:S(2)}, u32[]{:S(2)}) collective-permute-start(bf16[2,192,768]{2,1,0:T(8,128)(2,1)S(1)} %constant_dynamic-slice_fusion.3), channel_id=1, source_target_pairs={{1,0},{2,1},{3,2},{0,3},{5,4},{6,5},{7,6},{4,7},{9,8},{10,9},{11,1... | collective-permute-start | bytes 1769480 | tf_op jit(solution)/shard_map/ppermute | solution.py:470
  119.3 37.0 %collective-permute-start.12 = (bf16[2,192,768]{2,1,0:T(8,128)(2,1)S(1)}, bf16[2,192,768]{2,1,0:T(8,128)(2,1)S(1)}, u32[]{:S(2)}, u32[]{:S(2)}) collective-permute-start(bf16[2,192,768]{2,1,0:T(8,128)(2,1)S(1)} %constant_dynamic-slice_fusion.3), channel_id=1, source_target_pairs={{3,0},{0,1},{1,2},{2,3},{7,4},{4,5},{5,6},{6,7},{11,8},{8,9},{9,10... | collective-permute-start | bytes 1769480 | tf_op jit(solution)/shard_map/ppermute | solution.py:470
  153.3 14.4 %copy-start.8 = (bf16[2,192,768]{2,1,0:T(8,128)(2,1)}, bf16[2,192,768]{2,1,0:T(8,128)(2,1)S(1)}, u32[]{:S(2)}) copy-start(bf16[2,192,768]{2,1,0:T(8,128)(2,1)S(1)} %collective-permute-done.11.refs_2_) | copy-start | bytes 1769476
  156.3 11.4 %copy-start.9 = (bf16[2,192,768]{2,1,0:T(8,128)(2,1)}, bf16[2,192,768]{2,1,0:T(8,128)(2,1)S(1)}, u32[]{:S(2)}) copy-start(bf16[2,192,768]{2,1,0:T(8,128)(2,1)S(1)} %collective-permute-done.12.refs_4_) | copy-start | bytes 1769476
  156.3 21.1 %collective-permute-start.15 = (bf16[2,192,768]{2,1,0:T(8,128)(2,1)S(1)}, bf16[2,192,768]{2,1,0:T(8,128)(2,1)}, u32[]{:S(2)}, u32[]{:S(2)}) collective-permute-start(bf16[2,192,768]{2,1,0:T(8,128)(2,1)S(1)} %collective-permute-done.11.refs_2_), channel_id=1, source_target_pairs={{4,0},{0,4},{12,8},{8,12},{20,16},{16,20},{28,24},{24,28},{36,32},... | collective-permute-start | bytes 1769480 | tf_op jit(solution)/shard_map/ppermute | solution.py:475
  158.9 18.5 %collective-permute-start.16 = (bf16[2,192,768]{2,1,0:T(8,128)(2,1)S(1)}, bf16[2,192,768]{2,1,0:T(8,128)(2,1)}, u32[]{:S(2)}, u32[]{:S(2)}) collective-permute-start(bf16[2,192,768]{2,1,0:T(8,128)(2,1)S(1)} %collective-permute-done.12.refs_4_), channel_id=1, source_target_pairs={{4,0},{0,4},{12,8},{8,12},{20,16},{16,20},{28,24},{24,28},{36,32},... | collective-permute-start | bytes 1769480 | tf_op jit(solution)/shard_map/ppermute | solution.py:475
  159.0 17.2 %collective-permute-start.13 = (bf16[1,192,768]{2,1,0:T(8,128)(2,1)S(1)}, bf16[1,192,768]{2,1,0:T(8,128)(2,1)}, u32[]{:S(2)}, u32[]{:S(2)}) collective-permute-start(bf16[1,192,768]{2,1,0:T(8,128)(2,1)S(1)} %slice.196), channel_id=1, source_target_pairs={{1,0},{2,1},{3,2},{0,3},{5,4},{6,5},{7,6},{4,7},{9,8},{10,9},{11,1... | collective-permute-start | bytes 884744 | tf_op jit(solution)/shard_map/ppermute | solution.py:470
  159.2 17.0 %collective-permute-start.14 = (bf16[1,192,768]{2,1,0:T(8,128)(2,1)S(1)}, bf16[1,192,768]{2,1,0:T(8,128)(2,1)}, u32[]{:S(2)}, u32[]{:S(2)}) collective-permute-start(bf16[1,192,768]{2,1,0:T(8,128)(2,1)S(1)} %slice.197), channel_id=1, source_target_pairs={{3,0},{0,1},{1,2},{2,3},{7,4},{4,5},{5,6},{6,7},{11,8},{8,9},{9,10... | collective-permute-start | bytes 884744 | tf_op jit(solution)/shard_map/ppermute | solution.py:470
  167.7 26.8 %all-to-all-start.2 = ((bf16[32,24,768]{2,1,0:T(8,128)(2,1)}), bf16[32,24,768]{2,1,0:T(8,128)(2,1)S(1)}, u32[]{:S(2)}, u32[]{:S(2)}) async-start(bf16[32,24,768]{2,1,0:T(8,128)(2,1)} %bitcast.120), calls=%async_computation.2 | async-start | bytes 2359296 | tf_op jit(solution)/shard_map/all_to_all | solution.py:498
  177.4 28.4 %collective-permute-start.20 = (bf16[768,768]{1,0:T(8,128)(2,1)}, bf16[768,768]{1,0:T(8,128)(2,1)}, u32[]{:S(2)}, u32[]{:S(2)}) collective-permute-start(bf16[768,768]{1,0:T(8,128)(2,1)} %get-tuple-element.144.refs_3_.refs_5_), channel_id=1, source_target_pairs={{1,0},{2,1},{3,2},{0,3},{5,4},{6,5},{7,6},{4,7},{9,8},{10,9},{11,1... | collective-permute-start | bytes 3538952 | tf_op jit(solution)/shard_map/ppermute | solution.py:470
  178.7 28.5 %collective-permute-start.21 = (bf16[768,768]{1,0:T(8,128)(2,1)}, bf16[768,768]{1,0:T(8,128)(2,1)}, u32[]{:S(2)}, u32[]{:S(2)}) collective-permute-start(bf16[768,768]{1,0:T(8,128)(2,1)} %get-tuple-element.145.refs_4_.refs_7_), channel_id=1, source_target_pairs={{3,0},{0,1},{1,2},{2,3},{7,4},{4,5},{5,6},{6,7},{11,8},{8,9},{9,10... | collective-permute-start | bytes 3538952 | tf_op jit(solution)/shard_map/ppermute | solution.py:470
  179.2 6.2 %collective-permute-start.18 = (bf16[2,192,768]{2,1,0:T(8,128)(2,1)S(1)}, bf16[2,192,768]{2,1,0:T(8,128)(2,1)S(1)}, u32[]{:S(2)}, u32[]{:S(2)}) collective-permute-start(bf16[2,192,768]{2,1,0:T(8,128)(2,1)S(1)} %pad_maximum_fusion.4.refs_3_), channel_id=1, source_target_pairs={{4,0},{0,4},{12,8},{8,12},{20,16},{16,20},{28,24},{24,28},{36,32},... | collective-permute-start | bytes 1769480 | tf_op jit(solution)/shard_map/ppermute | solution.py:475
  185.4 9.1 %copy-start.15 = (bf16[2,192,768]{2,1,0:T(8,128)(2,1)}, bf16[2,192,768]{2,1,0:T(8,128)(2,1)S(1)}, u32[]{:S(2)}) copy-start(bf16[2,192,768]{2,1,0:T(8,128)(2,1)S(1)} %collective-permute-done.18.refs_6_) | copy-start | bytes 1769476
  207.3 39.7 %all-to-all-start.3 = ((bf16[32,24,1536]{2,1,0:T(8,128)(2,1)}), bf16[32,24,1536]{2,1,0:T(8,128)(2,1)S(1)}, u32[]{:S(2)}, u32[]{:S(2)}) async-start(bf16[32,24,1536]{2,1,0:T(8,128)(2,1)} %bitcast.107), calls=%async_computation.3 | async-start | bytes 4718592 | tf_op jit(solution)/shard_map/all_to_all | solution.py:498
  215.8 31.1 %collective-permute-start.22 = (bf16[768,768]{1,0:T(8,128)(2,1)S(1)}, bf16[768,768]{1,0:T(8,128)(2,1)}, u32[]{:S(2)}, u32[]{:S(2)}) collective-permute-start(bf16[768,768]{1,0:T(8,128)(2,1)S(1)} %copy-done.11), channel_id=1, source_target_pairs={{1,0},{2,1},{3,2},{0,3},{5,4},{6,5},{7,6},{4,7},{9,8},{10,9},{11,1... | collective-permute-start | bytes 3538952 | tf_op jit(solution)/shard_map/ppermute | solution.py:470
  215.9 32.7 %collective-permute-start.25 = (bf16[768,768]{1,0:T(8,128)(2,1)}, bf16[768,768]{1,0:T(8,128)(2,1)}, u32[]{:S(2)}, u32[]{:S(2)}) collective-permute-start(bf16[768,768]{1,0:T(8,128)(2,1)} %get-tuple-element.144.refs_3_.refs_5_), channel_id=1, source_target_pairs={{3,0},{0,1},{1,2},{2,3},{7,4},{4,5},{5,6},{6,7},{11,8},{8,9},{9,10... | collective-permute-start | bytes 3538952 | tf_op jit(solution)/shard_map/ppermute | solution.py:470
  217.4 51.3 %collective-permute-start.23 = (bf16[768,768]{1,0:T(8,128)(2,1)}, bf16[768,768]{1,0:T(8,128)(2,1)}, u32[]{:S(2)}, u32[]{:S(2)}) collective-permute-start(bf16[768,768]{1,0:T(8,128)(2,1)} %collective-permute-done.20.refs_5_), channel_id=1, source_target_pairs={{1,0},{2,1},{3,2},{0,3},{5,4},{6,5},{7,6},{4,7},{9,8},{10,9},{11,1... | collective-permute-start | bytes 3538952 | tf_op jit(solution)/shard_map/ppermute | solution.py:470
  218.7 51.2 %collective-permute-start.24 = (bf16[768,768]{1,0:T(8,128)(2,1)}, bf16[768,768]{1,0:T(8,128)(2,1)}, u32[]{:S(2)}, u32[]{:S(2)}) collective-permute-start(bf16[768,768]{1,0:T(8,128)(2,1)} %collective-permute-done.21.refs_10_), channel_id=1, source_target_pairs={{3,0},{0,1},{1,2},{2,3},{7,4},{4,5},{5,6},{6,7},{11,8},{8,9},{9,10... | collective-permute-start | bytes 3538952 | tf_op jit(solution)/shard_map/ppermute | solution.py:470
  246.9 22.9 %copy-start.6 = (bf16[32,24,1536]{2,1,0:T(8,128)(2,1)}, bf16[32,24,1536]{2,1,0:T(8,128)(2,1)S(1)}, u32[]{:S(2)}) copy-start(bf16[32,24,1536]{2,1,0:T(8,128)(2,1)S(1)} %all-to-all-done.3) | copy-start | bytes 7077892
  246.9 84.7 %collective-permute-start.26 = (bf16[768,1536]{1,0:T(8,128)(2,1)S(1)}, bf16[768,1536]{1,0:T(8,128)(2,1)}, u32[]{:S(2)}, u32[]{:S(2)}) collective-permute-start(bf16[768,1536]{1,0:T(8,128)(2,1)S(1)} %bitcast.103), channel_id=1, source_target_pairs={{1,0},{2,1},{3,2},{0,3},{5,4},{6,5},{7,6},{4,7},{9,8},{10,9},{11,1... | collective-permute-start | bytes 7077896 | tf_op jit(solution)/shard_map/ppermute | solution.py:470
  247.0 84.7 %collective-permute-start.27 = (bf16[768,1536]{1,0:T(8,128)(2,1)S(1)}, bf16[768,1536]{1,0:T(8,128)(2,1)}, u32[]{:S(2)}, u32[]{:S(2)}) collective-permute-start(bf16[768,1536]{1,0:T(8,128)(2,1)S(1)} %bitcast.104), channel_id=1, source_target_pairs={{3,0},{0,1},{1,2},{2,3},{7,4},{4,5},{5,6},{6,7},{11,8},{8,9},{9,10... | collective-permute-start | bytes 7077896 | tf_op jit(solution)/shard_map/ppermute | solution.py:470
  291.1 40.6 %all-to-all-start.4 = ((bf16[32,24,1536]{2,1,0:T(8,128)(2,1)}), bf16[32,24,1536]{2,1,0:T(8,128)(2,1)}, u32[]{:S(2)}, u32[]{:S(2)}) async-start(bf16[32,24,1536]{2,1,0:T(8,128)(2,1)} %bitcast.108), calls=%async_computation.4 | async-start | bytes 4718592 | tf_op jit(solution)/shard_map/all_to_all | solution.py:498
  300.5 47.9 %collective-permute-start.28 = (bf16[768,768]{1,0:T(8,128)(2,1)}, bf16[768,768]{1,0:T(8,128)(2,1)S(1)}, u32[]{:S(2)}, u32[]{:S(2)}) collective-permute-start(bf16[768,768]{1,0:T(8,128)(2,1)} %bitcast.13.refs_0_), channel_id=1, source_target_pairs={{1,0},{2,1},{3,2},{0,3},{5,4},{6,5},{7,6},{4,7},{9,8},{10,9},{11,1... | collective-permute-start | bytes 3538952 | tf_op jit(solution)/shard_map/ppermute | solution.py:470
  300.6 47.9 %collective-permute-start.29 = (bf16[768,768]{1,0:T(8,128)(2,1)}, bf16[768,768]{1,0:T(8,128)(2,1)}, u32[]{:S(2)}, u32[]{:S(2)}) collective-permute-start(bf16[768,768]{1,0:T(8,128)(2,1)} %bitcast.13.refs_0_), channel_id=1, source_target_pairs={{3,0},{0,1},{1,2},{2,3},{7,4},{4,5},{5,6},{6,7},{11,8},{8,9},{9,10... | collective-permute-start | bytes 3538952 | tf_op jit(solution)/shard_map/ppermute | solution.py:470
  349.5 23.0 %all-to-all-start.5 = ((bf16[32,24,768]{2,1,0:T(8,128)(2,1)}), bf16[32,24,768]{2,1,0:T(8,128)(2,1)S(1)}, u32[]{:S(2)}, u32[]{:S(2)}) async-start(bf16[32,24,768]{2,1,0:T(8,128)(2,1)} %bitcast.118), calls=%async_computation.5 | async-start | bytes 2359296 | tf_op jit(solution)/shard_map/all_to_all | solution.py:498
  356.4 32.0 %collective-permute-start.30 = (bf16[384,1536]{1,0:T(8,128)(2,1)}, bf16[384,1536]{1,0:T(8,128)(2,1)}, u32[]{:S(2)}, u32[]{:S(2)}) collective-permute-start(bf16[384,1536]{1,0:T(8,128)(2,1)} %slice.209), channel_id=1, source_target_pairs={{1,0},{2,1},{3,2},{0,3},{5,4},{6,5},{7,6},{4,7},{9,8},{10,9},{11,1... | collective-permute-start | bytes 3538952 | tf_op jit(solution)/shard_map/ppermute | solution.py:470
  359.4 29.6 %collective-permute-start.31 = (bf16[384,1536]{1,0:T(8,128)(2,1)}, bf16[384,1536]{1,0:T(8,128)(2,1)}, u32[]{:S(2)}, u32[]{:S(2)}) collective-permute-start(bf16[384,1536]{1,0:T(8,128)(2,1)} %slice.210), channel_id=1, source_target_pairs={{3,0},{0,1},{1,2},{2,3},{7,4},{4,5},{5,6},{6,7},{11,8},{8,9},{9,10... | collective-permute-start | bytes 3538952 | tf_op jit(solution)/shard_map/ppermute | solution.py:470
  360.2 100.2 %collective-permute-start.34 = (bf16[4,2,192,768]{3,2,1,0:T(8,128)(2,1)}, bf16[4,2,192,768]{3,2,1,0:T(8,128)(2,1)S(1)}, u32[]{:S(2)}, u32[]{:S(2)}) collective-permute-start(bf16[4,2,192,768]{3,2,1,0:T(8,128)(2,1)} %get-tuple-element.195), channel_id=1, source_target_pairs={{4,0},{0,4},{12,8},{8,12},{20,16},{16,20},{28,24},{24,28},{36,32},... | collective-permute-start | bytes 7077896 | tf_op jit(solution)/shard_map/ppermute | solution.py:475
  364.0 32.7 %collective-permute-start.32 = (bf16[384,768]{1,0:T(8,128)(2,1)}, bf16[384,768]{1,0:T(8,128)(2,1)}, u32[]{:S(2)}, u32[]{:S(2)}) collective-permute-start(bf16[384,768]{1,0:T(8,128)(2,1)} %slice.211), channel_id=1, source_target_pairs={{1,0},{2,1},{3,2},{0,3},{5,4},{6,5},{7,6},{4,7},{9,8},{10,9},{11,1... | collective-permute-start | bytes 1769480 | tf_op jit(solution)/shard_map/ppermute | solution.py:470
  367.7 57.5 %collective-permute-start.33 = (bf16[384,768]{1,0:T(8,128)(2,1)}, bf16[384,768]{1,0:T(8,128)(2,1)}, u32[]{:S(2)}, u32[]{:S(2)}) collective-permute-start(bf16[384,768]{1,0:T(8,128)(2,1)} %slice.212), channel_id=1, source_target_pairs={{3,0},{0,1},{1,2},{2,3},{7,4},{4,5},{5,6},{6,7},{11,8},{8,9},{9,10... | collective-permute-start | bytes 1769480 | tf_op jit(solution)/shard_map/ppermute | solution.py:470
  388.4 77.2 %collective-permute-start.40 = (bf16[768,768]{1,0:T(8,128)(2,1)}, bf16[768,768]{1,0:T(8,128)(2,1)}, u32[]{:S(2)}, u32[]{:S(2)}) collective-permute-start(bf16[768,768]{1,0:T(8,128)(2,1)} %bitcast.114), channel_id=1, source_target_pairs={{2,0},{3,1},{0,2},{1,3},{6,4},{7,5},{4,6},{5,7},{10,8},{11,9},{8,1... | collective-permute-start | bytes 3538952 | tf_op jit(solution)/shard_map/ppermute | solution.py:470
  389.0 107.3 %collective-permute-start.38 = (bf16[768,768]{1,0:T(8,128)(2,1)}, bf16[768,768]{1,0:T(8,128)(2,1)}, u32[]{:S(2)}, u32[]{:S(2)}) collective-permute-start(bf16[768,768]{1,0:T(8,128)(2,1)} %bitcast.115), channel_id=1, source_target_pairs={{1,0},{2,1},{3,2},{0,3},{5,4},{6,5},{7,6},{4,7},{9,8},{10,9},{11,1... | collective-permute-start | bytes 3538952 | tf_op jit(solution)/shard_map/ppermute | solution.py:470
  396.6 99.6 %collective-permute-start.39 = (bf16[768,768]{1,0:T(8,128)(2,1)}, bf16[768,768]{1,0:T(8,128)(2,1)}, u32[]{:S(2)}, u32[]{:S(2)}) collective-permute-start(bf16[768,768]{1,0:T(8,128)(2,1)} %bitcast.116), channel_id=1, source_target_pairs={{3,0},{0,1},{1,2},{2,3},{7,4},{4,5},{5,6},{6,7},{11,8},{8,9},{9,10... | collective-permute-start | bytes 3538952 | tf_op jit(solution)/shard_map/ppermute | solution.py:470
  425.2 45.2 %all-to-all-start.6 = ((bf16[32,24,768]{2,1,0:T(8,128)(2,1)}), bf16[32,24,768]{2,1,0:T(8,128)(2,1)S(1)}, u32[]{:S(2)}, u32[]{:S(2)}) async-start(bf16[32,24,768]{2,1,0:T(8,128)(2,1)} %bitcast.119), calls=%async_computation.6 | async-start | bytes 2359296 | tf_op jit(solution)/shard_map/all_to_all | solution.py:498
  435.4 26.5 %copy-start.4 = (bf16[4,2,192,768]{3,2,1,0:T(8,128)(2,1)S(1)}, bf16[4,2,192,768]{3,2,1,0:T(8,128)(2,1)}, u32[]{:S(2)}) copy-start(bf16[4,2,192,768]{3,2,1,0:T(8,128)(2,1)} %get-tuple-element.194) | copy-start | bytes 7077892
  465.3 28.9 %collective-permute-start.35 = (bf16[384,768]{1,0:T(8,128)(2,1)}, bf16[384,768]{1,0:T(8,128)(2,1)}, u32[]{:S(2)}, u32[]{:S(2)}) collective-permute-start(bf16[384,768]{1,0:T(8,128)(2,1)} %get-tuple-element.268), channel_id=1, source_target_pairs={{3,0},{0,1},{1,2},{2,3},{7,4},{4,5},{5,6},{6,7},{11,8},{8,9},{9,10... | collective-permute-start | bytes 1769480 | tf_op jit(solution)/shard_map/ppermute | solution.py:470
  465.3 28.9 %collective-permute-start.36 = (bf16[384,768]{1,0:T(8,128)(2,1)}, bf16[384,768]{1,0:T(8,128)(2,1)}, u32[]{:S(2)}, u32[]{:S(2)}) collective-permute-start(bf16[384,768]{1,0:T(8,128)(2,1)} %get-tuple-element.270), channel_id=1, source_target_pairs={{2,0},{3,1},{0,2},{1,3},{6,4},{7,5},{4,6},{5,7},{10,8},{11,9},{8,1... | collective-permute-start | bytes 1769480 | tf_op jit(solution)/shard_map/ppermute | solution.py:470
  465.7 28.9 %collective-permute-start.37 = (bf16[384,768]{1,0:T(8,128)(2,1)}, bf16[384,768]{1,0:T(8,128)(2,1)}, u32[]{:S(2)}, u32[]{:S(2)}) collective-permute-start(bf16[384,768]{1,0:T(8,128)(2,1)} %get-tuple-element.269), channel_id=1, source_target_pairs={{1,0},{2,1},{3,2},{0,3},{5,4},{6,5},{7,6},{4,7},{9,8},{10,9},{11,1... | collective-permute-start | bytes 1769480 | tf_op jit(solution)/shard_map/ppermute | solution.py:470
  487.8 9.9 %copy-start.24 = (f32[40,768]{1,0:T(8,128)S(1)}, f32[40,768]{1,0:T(8,128)}, u32[]{:S(2)}) copy-start(f32[40,768]{1,0:T(8,128)} %get-tuple-element.199) | copy-start | bytes 368644
  487.8 9.9 %copy-start.25 = (f32[40,768]{1,0:T(8,128)S(1)}, f32[40,768]{1,0:T(8,128)}, u32[]{:S(2)}) copy-start(f32[40,768]{1,0:T(8,128)} %get-tuple-element.198) | copy-start | bytes 368644
  496.3 5.8 collective-permute-start.41
  497.9 4.0 collective-permute-start.42
  504.5 28.3 %collective-permute-start.43 = (bf16[432,768]{1,0:T(8,128)(2,1)S(1)}, bf16[432,768]{1,0:T(8,128)(2,1)S(1)}, u32[]{:S(2)}, u32[]{:S(2)}) collective-permute-start(bf16[432,768]{1,0:T(8,128)(2,1)S(1)} %get-tuple-element.265), channel_id=1, source_target_pairs={{3,0},{0,1},{1,2},{2,3},{7,4},{4,5},{5,6},{6,7},{11,8},{8,9},{9,10... | collective-permute-start | bytes 1990664 | tf_op jit(solution)/shard_map/ppermute | solution.py:470
  504.6 32.1 %collective-permute-start.44 = (bf16[432,768]{1,0:T(8,128)(2,1)S(1)}, bf16[432,768]{1,0:T(8,128)(2,1)S(1)}, u32[]{:S(2)}, u32[]{:S(2)}) collective-permute-start(bf16[432,768]{1,0:T(8,128)(2,1)S(1)} %get-tuple-element.266), channel_id=1, source_target_pairs={{2,0},{3,1},{0,2},{1,3},{6,4},{7,5},{4,6},{5,7},{10,8},{11,9},{8,1... | collective-permute-start | bytes 1990664 | tf_op jit(solution)/shard_map/ppermute | solution.py:470
  507.8 28.9 %collective-permute-start.45 = (bf16[432,768]{1,0:T(8,128)(2,1)S(1)}, bf16[432,768]{1,0:T(8,128)(2,1)S(1)}, u32[]{:S(2)}, u32[]{:S(2)}) collective-permute-start(bf16[432,768]{1,0:T(8,128)(2,1)S(1)} %get-tuple-element.267), channel_id=1, source_target_pairs={{1,0},{2,1},{3,2},{0,3},{5,4},{6,5},{7,6},{4,7},{9,8},{10,9},{11,1... | collective-permute-start | bytes 1990664 | tf_op jit(solution)/shard_map/ppermute | solution.py:470
  584.6 8.9 %collective-permute-start.46 = (bf16[16,51,768]{2,0,1:T(8,128)(2,1)}, bf16[16,51,768]{2,0,1:T(8,128)(2,1)S(1)}, u32[]{:S(2)}, u32[]{:S(2)}) collective-permute-start(bf16[16,51,768]{2,0,1:T(8,128)(2,1)} %copy.70), channel_id=1, source_target_pairs={{4,0},{0,4},{12,8},{8,12},{20,16},{16,20},{28,24},{24,28},{36,32},... | collective-permute-start | bytes 3760136 | tf_op jit(solution)/shard_map/ppermute | solution.py:475
  (23 other events, 90.8 us)

commit v4 on v3

--- a/solution.py
+++ b/solution.py
@@ -571,7 +571,7 @@
     after, before = ahead(half, 1), ahead(half, 3)
     far = far_weights(after, before)
     theirs = [other_core(after), other_core(before)]
-    far, *theirs, in0, out0 = tie(far, *theirs, expert_in[0, 0], expert_out[0, 0])
+    *theirs, in0, out0 = tie(*theirs, expert_in[0, 0], expert_out[0, 0])
     weights0 = [packed[0], after, far, before, theirs[0], other_core(far), theirs[1]]
     next_in, last_out = ahead(in0, 1), ahead(out0, 3)
     next_out, last_in = ahead(out0, 1), ahead(in0, 3)
@@ -737,11 +737,10 @@
     )
     bias_columns = expert_in_bias[:, 0].astype(F32)[:, :, None]
     back0, *joint1 = tie(back0, *joint1)
-    back0, *rows_pieces = tie(back0, *rows_pieces)
     own = expert_grads(joint1, expert_in[1, 0], bias_columns[1], expert_out[1, 0], 1)
-    far_rows = ahead(grads0, 2)
-    grads_pieces = [grads0, ahead(grads0, 1), ahead(grads0, 3)]
-    grads_pieces += [far_rows[: rows // 2], far_rows[rows // 2 :]]
+    after_g, before_g, far_g = ring_rows(grads0)
+    after_g, before_g, *own = tie(after_g, before_g, *own)
+    grads_pieces = [grads0, after_g, before_g, *far_g(after_g, before_g)]
     back0 = swap(back0, stride)
     back0, *own = tie(back0, *own)
     q, k, v, m, lse, probs, gates = kept0
@@ -752,7 +751,8 @@
         [full_rows, half_shape, half_shape, small_shape],
     )
 
-    keep0, give0, line1, *grads_pieces = tie(keep0, give0, line1, *grads_pieces)
+    keep0, give0, line1, *rows_pieces = tie(keep0, give0, line1, *rows_pieces)
+    keep0, give0, *grads_pieces = tie(keep0, give0, *grads_pieces)
     own = expert_grads(
         list(zip(rows_pieces, grads_pieces)),
         expert_in[0, 0],

time: 613 us -> 580 us (0.946)
  waiting for transfers between devices: 215 us -> 184 us
    ppermute x37 -> x38, waiting for transfers between devices: 129 us -> 94.8 us  [ahead(): lax.ppermute(value, axis, [((i + steps) % size, i) for i in range(size)])]
    ppermute x37 -> x38, starting transfers between devices: 36.3 us -> 37 us  [ahead(): lax.ppermute(value, axis, [((i + steps) % size, i) for i in range(size)])]
  transfers between devices with their start and end apart: 54 -> 55, of which waited for: 23 -> 22; matrix products, arithmetic and copies ran while one was open for 8% -> 9% of each run, Pallas kernels for 25% -> 27%
where the time goes in v4:
time: 580 us; the launch traced here: 570 us
  waiting for transfers between devices  184 us (32%)
  Pallas kernels  166 us (29%)
  starting transfers between devices  104 us (18%)
  local copies, waits for them, and re-layouts  54.1 us (9%)
  blocking collectives  45.1 us (8%)
  other arithmetic  15.4 us (3%)
    ppermute x38, waiting for transfers between devices, ahead(): lax.ppermute(value, axis, [((i + steps) % size, i) for i in range(size)])  94.8 us
    all_to_all x6, waiting for transfers between devices, swap(): lax.all_to_all(rows.reshape(-1, stride, width), 'expert', split_axis=0, c...  85.6 us
    pallas_call x5, Pallas kernels, expert_pieces(): pl.pallas_call(body, out_shape=[s for _, s in shapes], in_specs=[pl.Block...  60.5 us
    pallas_call x2, Pallas kernels, expert_grads(): pl.pallas_call(body, grid=(1,), in_specs=[pl.BlockSpec(memory_space=pl.AN...  49.6 us
    all_to_all x6, starting transfers between devices, swap(): lax.all_to_all(rows.reshape(-1, stride, width), 'expert', split_axis=0, c...  46.9 us
    ppermute x38, starting transfers between devices, ahead(): lax.ppermute(value, axis, [((i + steps) % size, i) for i in range(size)])  37 us
    pallas_call x2, Pallas kernels, mixer_backward(): pl.pallas_call(functools.partial(mixer_backward_body, last, count, scale,...  33.2 us
    all_to_all x1, blocking collectives, shards(): lax.all_to_all(lines, 'expert', split_axis=0, concat_axis=0, tiled=True,...  24.5 us
  transfers between devices with their start and end apart: 55, of which 22 were waited for; matrix products, arithmetic and copies ran while one was open for 9% of the time, Pallas kernels for 27%

profile of v4, /device:TPU:1, one launch (start us, length us, event | category | flops | bytes accessed | tf_op | source)
XLA Modules:
  0.0 569.7 jit_solution(3348294474984884949)
XLA Ops:
  0.7 1.6 slice_bitcast_fusion.4
  4.1 3.3 collective-permute-start
  8.3 4.1 all-to-all-start
  15.8 4.3 slice_bitcast_fusion
  20.2 1.7 copy.60.refs_13_.refs_17_
  24.8 2.7 collective-permute-start.1
  29.3 2.1 collective-permute-start.4
  32.8 3.5 collective-permute-done.3
  37.0 3.0 collective-permute-start.6
  42.8 7.6 %shard_map.220 = (f32[208,768]{1,0:T(8,128)}, bf16[768,768]{1,0:T(8,128)(2,1)}, bf16[208,768]{1,0:T(8,128)(2,1)}, bf16[208,768]{1,0:T(8,128)(2,1)}, bf16[208,768...) custom-call(s32[2]{0:T(128)} %pad_add_fusion.refs_0_.refs_13_.here_r, ...), custom_call_target="tpu_custom_call" | custom-call | flops 2000000000 | bytes 20000000 | tf_op jit(solution)/shard_map/pallas_call | solution.py:600
  50.4 8.3 %all-to-all-start.1 = ((bf16[32,24,768]{2,1,0:T(8,128)(2,1)}), bf16[32,24,768]{2,1,0:T(8,128)(2,1)}, u32[]{:S(2)}, u32[]{:S(2)}) async-start(bf16[32,24,768]{2,1,0:T(8,128)(2,1)} %bitcast.120), calls=%async_computation.1 | async-start | bytes 2359296 | tf_op jit(solution)/shard_map/all_to_all | solution.py:498
  58.8 2.7 collective-permute-start.8
  61.5 1.6 collective-permute-start.9
  65.6 11.5 %all-to-all-done.1 = bf16[32,24,768]{2,1,0:T(8,128)(2,1)} async-done(((bf16[32,24,768]{2,1,0:T(8,128)(2,1)}), bf16[32,24,768]{2,1,0:T(8,128)(2,1)}, u32[]{:S(2)}, u32[]{:S(2)}) %all-to-all-start.1) | async-done | bytes 1179680 | tf_op jit(solution)/shard_map/all_to_all | solution.py:498
  77.1 6.8 %shard_map.221 = (f32[768,768]{1,0:T(8,128)}, bf16[1,768,768]{2,1,0:T(8,128)(2,1)}) custom-call(bf16[768,768]{1,0:T(8,128)(2,1)} %bitcast.13.refs_0_, f32[1,768]{1,0:T(1,128)} %get-tuple-element.302.refs_1_, f32[1,768]{1,0:T(1,128)} %get-tuple-element.308.refs_2_, bf16[768,768]{1,0:T(8,128)(2,1)} %get-tuple-element.129.refs_3_.refs_1_.refs_10_, ...), custom_call_target="tpu_custom_call" | custom-call | flops 1811939328 | bytes 20000000 | tf_op jit(solution)/shard_map/pallas_call | solution.py:394
  83.9 3.4 collective-permute-done.10.refs_6_
  87.3 24.2 %collective-permute-done.7.refs_3_ = bf16[768,768]{1,0:T(8,128)(2,1)} collective-permute-done((bf16[768,768]{1,0:T(8,128)(2,1)}, bf16[768,768]{1,0:T(8,128)(2,1)}, u32[]{:S(2)}, u32[]{:S(2)}) %collective-permute-start.7) | collective-permute-done | bytes 1179680 | tf_op jit(solution)/shard_map/ppermute | solution.py:470
  112.6 2.4 collective-permute-start.17
  115.0 2.7 collective-permute-start.11
  118.4 10.3 %shard_map.222 = (f32[768,768]{1,0:T(8,128)}, bf16[2,768,768]{2,1,0:T(8,128)(2,1)}) custom-call(bf16[768,768]{1,0:T(8,128)(2,1)} %bitcast.13.refs_0_, f32[2,768]{1,0:T(2,128)} %slice.193.refs_1_, f32[768,768]{1,0:T(8,128)} %get-tuple-element.132.refs_2_, bf16[768,768]{1,0:T(8,128)(2,1)} %collective-permute-done.7.refs_3_, ...), custom_call_target="tpu_custom_call" | custom-call | flops 3623878656 | bytes 20000000 | tf_op jit(solution)/shard_map/pallas_call | solution.py:394
  128.7 23.1 %collective-permute-done.11.refs_2_ = bf16[2,192,768]{2,1,0:T(8,128)(2,1)S(1)} collective-permute-done((bf16[2,192,768]{2,1,0:T(8,128)(2,1)S(1)}, bf16[2,192,768]{2,1,0:T(8,128)(2,1)S(1)}, u32[]{:S(2)}, u32[]{:S(2)}) %collective-permute-start.11) | collective-permute-done | bytes 589856 | tf_op jit(solution)/shard_map/ppermute | solution.py:470
  151.8 3.0 collective-permute-done.12.refs_4_
  154.8 2.6 collective-permute-start.15
  159.0 7.2 %shard_map.223 = (bf16[768,768]{1,0:T(8,128)(2,1)}, bf16[1,768,768]{2,1,0:T(8,128)(2,1)}) custom-call(bf16[768,768]{1,0:T(8,128)(2,1)} %bitcast.13.refs_0_, f32[1,768]{1,0:T(1,128)} %get-tuple-element.301.refs_1_, f32[768,768]{1,0:T(8,128)} %get-tuple-element.145.refs_2_, bf16[768,768]{1,0:T(8,128)(2,1)} %collective-permute-done.17.refs_3_.refs_7_, ...), custom_call_target="tpu_custom_call" | custom-call | flops 1811939328 | bytes 20000000 | tf_op jit(solution)/shard_map/pallas_call | solution.py:394
  166.2 8.4 %all-to-all-start.2 = ((bf16[32,24,768]{2,1,0:T(8,128)(2,1)}), bf16[32,24,768]{2,1,0:T(8,128)(2,1)S(1)}, u32[]{:S(2)}, u32[]{:S(2)}) async-start(bf16[32,24,768]{2,1,0:T(8,128)(2,1)} %bitcast.118), calls=%async_computation.2 | async-start | bytes 2359296 | tf_op jit(solution)/shard_map/all_to_all | solution.py:498
  183.9 9.1 %all-to-all-done.2 = bf16[32,24,768]{2,1,0:T(8,128)(2,1)S(1)} async-done(((bf16[32,24,768]{2,1,0:T(8,128)(2,1)}), bf16[32,24,768]{2,1,0:T(8,128)(2,1)S(1)}, u32[]{:S(2)}, u32[]{:S(2)}) %all-to-all-start.2) | async-done | bytes 1179680 | tf_op jit(solution)/shard_map/all_to_all | solution.py:498
  194.1 10.2 %shard_map.224 = (f32[208,768]{1,0:T(8,128)}, bf16[768,1536]{1,0:T(8,128)(2,1)}, bf16[208,768]{1,0:T(8,128)(2,1)}, bf16[208,768]{1,0:T(8,128)(2,1)}, bf16[208,76...) custom-call(s32[2]{0:T(128)} %pad_add_fusion.refs_0_.refs_13_.here_r, ...), custom_call_target="tpu_custom_call" | custom-call | flops 2000000000 | bytes 20000000 | tf_op jit(solution)/shard_map/pallas_call | solution.py:600
  204.3 1.5 collective-permute-done.21.refs_10_
  205.8 8.5 %all-to-all-start.3 = ((bf16[32,24,1536]{2,1,0:T(8,128)(2,1)}), bf16[32,24,1536]{2,1,0:T(8,128)(2,1)S(1)}, u32[]{:S(2)}, u32[]{:S(2)}) async-start(bf16[32,24,1536]{2,1,0:T(8,128)(2,1)} %bitcast.107), calls=%async_computation.3 | async-start | bytes 4718592 | tf_op jit(solution)/shard_map/all_to_all | solution.py:498
  217.3 28.1 %all-to-all-done.3 = bf16[32,24,1536]{2,1,0:T(8,128)(2,1)S(1)} async-done(((bf16[32,24,1536]{2,1,0:T(8,128)(2,1)}), bf16[32,24,1536]{2,1,0:T(8,128)(2,1)S(1)}, u32[]{:S(2)}, u32[]{:S(2)}) %all-to-all-start.3) | async-done | bytes 2359328 | tf_op jit(solution)/shard_map/all_to_all | solution.py:498
  245.5 1.6 collective-permute-start.27
  247.1 20.0 %collective-permute-done.23.refs_7_ = bf16[768,768]{1,0:T(8,128)(2,1)} collective-permute-done((bf16[768,768]{1,0:T(8,128)(2,1)}, bf16[768,768]{1,0:T(8,128)(2,1)}, u32[]{:S(2)}, u32[]{:S(2)}) %collective-permute-start.23) | collective-permute-done | bytes 1179680 | tf_op jit(solution)/shard_map/ppermute | solution.py:470
  268.4 21.2 %shard_map.225 = bf16[768,1536]{1,0:T(8,128)(2,1)} custom-call(bf16[768,1536]{1,0:T(8,128)(2,1)} %bitcast.105, f32[4,768]{1,0:T(4,128)} %get-tuple-element.309.refs_1_, f32[1,768]{1,0:T(1,128)} %get-tuple-element.307.refs_2_, bf16[768,768]{1,0:T(8,128)(2,1)} %get-tuple-element.149.refs_3_.refs_5_, bf16[768,768]{1,0:T(8,128)(2,1)} %get-tuple-element.150.refs_4_.refs_7_, ...), custom_call_target="tpu_custom_call" | custom-call | flops 14495514624 | bytes 20000000 | tf_op jit(solution)/shard_map/pallas_call | solution.py:394
  289.6 9.4 %all-to-all-start.4 = ((bf16[32,24,1536]{2,1,0:T(8,128)(2,1)}), bf16[32,24,1536]{2,1,0:T(8,128)(2,1)}, u32[]{:S(2)}, u32[]{:S(2)}) async-start(bf16[32,24,1536]{2,1,0:T(8,128)(2,1)} %bitcast.108), calls=%async_computation.4 | async-start | bytes 4718592 | tf_op jit(solution)/shard_map/all_to_all | solution.py:498
  300.5 29.7 %all-to-all-done.4 = bf16[32,24,1536]{2,1,0:T(8,128)(2,1)} async-done(((bf16[32,24,1536]{2,1,0:T(8,128)(2,1)}), bf16[32,24,1536]{2,1,0:T(8,128)(2,1)}, u32[]{:S(2)}, u32[]{:S(2)}) %all-to-all-start.4) | async-done | bytes 2359328 | tf_op jit(solution)/shard_map/all_to_all | solution.py:498
  330.2 16.8 %shard_map.226 = (f32[208,768]{1,0:T(8,128)}, bf16[4,2,192,768]{3,2,1,0:T(8,128)(2,1)}, bf16[4,2,192,768]{3,2,1,0:T(8,128)(2,1)}, f32[40,768]{1,0:T(8,128)}, bf1...) custom-call(f32[208,768]{1,0:T(8,128)} %pad_convert_fusion.1.refs_12_.refs_0_, bf16[768,1536]{1,0:T(8,128)(2,1)} %bitcast.27.refs_1_, ...), custom_call_target="tpu_custom_call" | custom-call | flops 4000000000 | bytes 20000000 | tf_op jit(solution)/shard_map/pallas_call | solution.py:677
  348.9 3.7 all-to-all-start.5
  352.6 2.4 slice.209
  355.5 2.4 slice.210
  359.7 2.0 slice.213
  361.7 1.9 slice.214
  363.6 7.3 %all-to-all-done.5 = bf16[32,24,768]{2,1,0:T(8,128)(2,1)S(1)} async-done(((bf16[32,24,768]{2,1,0:T(8,128)(2,1)}), bf16[32,24,768]{2,1,0:T(8,128)(2,1)S(1)}, u32[]{:S(2)}, u32[]{:S(2)}) %all-to-all-start.5) | async-done | bytes 1179680 | tf_op jit(solution)/shard_map/all_to_all | solution.py:498
  372.4 15.0 %shard_map.227 = bf16[768,768]{1,0:T(8,128)(2,1)} custom-call(bf16[768,768]{1,0:T(8,128)(2,1)} %bitcast.115, bf16[768,768]{1,0:T(8,128)(2,1)} %get-tuple-element.129.refs_3_.refs_1_.refs_10_, bf16[768,768]{1,0:T(8,128)(2,1)} %copy-done.8, bf16[768,768]{1,0:T(8,128)(2,1)} %collective-permute-done.7.refs_3_, bf16[768,768]{1,0:T(8,128)(2,1)} %collective-permute-done.8.refs_4_, ...), custom_call_target="tpu_custom_call" | custom-call | flops 7247757312 | bytes 20000000 | tf_op jit(solution)/shard_map/pallas_call | solution.py:394
  387.4 8.6 %all-to-all-start.6 = ((bf16[32,24,768]{2,1,0:T(8,128)(2,1)}), bf16[32,24,768]{2,1,0:T(8,128)(2,1)}, u32[]{:S(2)}, u32[]{:S(2)}) async-start(bf16[32,24,768]{2,1,0:T(8,128)(2,1)} %bitcast.119), calls=%async_computation.6 | async-start | bytes 2359296 | tf_op jit(solution)/shard_map/all_to_all | solution.py:498
  397.4 2.9 add_convert_fusion.1
  402.1 2.4 collective-permute-start.37
  404.5 24.9 %shard_map.228 = (f32[2,768,768]{2,1,0:T(8,128)}, f32[2,768,1]{2,1,0:T(8,128)}, f32[2,768,768]{2,1,0:T(8,128)}, f32[2,1,768]{2,1,0:T(1,128)}) custom-call(bf16[768,1536]{1,0:T(8,128)(2,1)} %bitcast.106, bf16[768,1536]{1,0:T(8,128)(2,1)} %collective-permute-done.26.refs_1_, bf16[768,1536]{1,0:T(8,128)(2,1)} %collective-permute-done.27.refs_2_, ...), custom_call_target="tpu_custom_call" | custom-call | flops 14495514624 | bytes 20000000 | tf_op jit(solution)/shard_map/pallas_call | solution.py:451
  433.2 3.2 collective-permute-done.35
  437.8 16.4 %shard_map.229 = (f32[208,768]{1,0:T(8,128)}, bf16[4,2,192,768]{3,2,1,0:T(8,128)(2,1)}, bf16[4,2,192,768]{3,2,1,0:T(8,128)(2,1)}, f32[40,768]{1,0:T(8,128)}) custom-call(f32[208,768]{1,0:T(8,128)} %get-tuple-element.166.refs_0_, bf16[768,768]{1,0:T(8,128)(2,1)} %bitcast.31.refs_1_, f32[208,768]{1,0:T(8,128)} %pad_convert_fusion.refs_8_.refs_2_, ...), custom_call_target="tpu_custom_call" | custom-call | flops 4000000000 | bytes 20000000 | tf_op jit(solution)/shard_map/pallas_call | solution.py:677
  454.3 1.8 fusion.5
  456.1 2.3 collective-permute-done.40.refs_7_
  458.4 3.8 collective-permute-done.41.refs_9_
  465.6 3.0 collective-permute-done.43
  468.8 2.2 add_convert_fusion
  472.5 2.2 collective-permute-start.46
  474.7 24.7 %shard_map.230 = (f32[2,768,768]{2,1,0:T(8,128)}, f32[2,768,1]{2,1,0:T(8,128)}, f32[2,768,768]{2,1,0:T(8,128)}, f32[2,1,768]{2,1,0:T(1,128)}) custom-call(bf16[768,768]{1,0:T(8,128)(2,1)} %bitcast.13.refs_0_, bf16[768,768]{1,0:T(8,128)(2,1)} %bitcast.116, ...), custom_call_target="tpu_custom_call", output_to_operand_aliasing={{0}: (13, {}), {1}: (14, {}), {2}: (15, {}), {3}: (16, {})} | custom-call | flops 14495514624 | bytes 20000000 | tf_op jit(solution)/shard_map/pallas_call | solution.py:451
  499.4 3.5 collective-permute-done.44
  503.8 24.5 %all_to_all.45 = bf16[16,51,768]{2,1,0:T(8,128)(2,1)S(1)} all-to-all(bf16[16,51,768]{2,1,0:T(8,128)(2,1)S(1)} %pad_maximum_fusion.1), channel_id=1, replica_groups={{0,8,16,24,32,40,48,56,64,72,80,88,96,104,112,120},{4,12,20,28,36,44,52..., dimensions={0} | all-to-all | bytes 2506752 | tf_op jit(solution)/shard_map/all_to_all | solution.py:777
  528.5 20.6 %all_to_all.46.mine_ref = bf16[16,51,768]{2,1,0:T(8,128)(2,1)S(1)} all-to-all(bf16[16,51,768]{2,1,0:T(8,128)(2,1)S(1)} %broadcast_in_dim.24), channel_id=1, replica_groups={{0,8,16,24,32,40,48,56,64,72,80,88,96,104,112,120},{4,12,20,28,36,44,52..., dimensions={0} | all-to-all | bytes 2506752 | tf_op jit(solution)/shard_map/all_to_all | solution.py:781
  550.6 4.6 collective-permute-start.47
  555.2 1.7 slice.208
  556.9 1.9 slice.212
  559.7 1.5 copy.71.theirs_ref
  561.2 4.4 shard_map.231
  (237 shorter events, 64.0 us)
Async XLA Ops:
  4.1 19.7 %collective-permute-start = (bf16[2,192,768]{2,1,0:T(8,128)(2,1)}, bf16[2,192,768]{2,1,0:T(8,128)(2,1)}, u32[]{:S(2)}, u32[]{:S(2)}) collective-permute-start(bf16[2,192,768]{2,1,0:T(8,128)(2,1)} %fusion.16), channel_id=1, source_target_pairs={{1,0},{2,1},{3,2},{0,3},{5,4},{6,5},{7,6},{4,7},{9,8},{10,9},{11,1... | collective-permute-start | bytes 1769480 | tf_op jit(solution)/shard_map/ppermute | solution.py:470
  7.4 20.2 %collective-permute-start.2 = (bf16[2,192,768]{2,1,0:T(8,128)(2,1)}, bf16[2,192,768]{2,1,0:T(8,128)(2,1)}, u32[]{:S(2)}, u32[]{:S(2)}) collective-permute-start(bf16[2,192,768]{2,1,0:T(8,128)(2,1)} %fusion.16), channel_id=1, source_target_pairs={{3,0},{0,1},{1,2},{2,3},{7,4},{4,5},{5,6},{6,7},{11,8},{8,9},{9,10... | collective-permute-start | bytes 1769480 | tf_op jit(solution)/shard_map/ppermute | solution.py:470
  8.3 19.2 %all-to-all-start = ((bf16[4,88,192]{2,1,0:T(8,128)(2,1)}), bf16[4,88,192]{2,1,0:T(8,128)(2,1)S(1)}, u32[]{:S(2)}, u32[]{:S(2)}) async-start(bf16[4,88,192]{2,1,0:T(8,128)(2,1)} %broadcast_in_dim.21), calls=%async_computation | async-start | bytes 360448 | tf_op jit(solution)/shard_map/all_to_all | solution.py:547
  20.1 38.7 %copy-start.8 = (bf16[768,768]{1,0:T(8,128)(2,1)}, bf16[768,768]{1,0:T(8,128)(2,1)S(1)}, u32[]{:S(2)}) copy-start(bf16[768,768]{1,0:T(8,128)(2,1)S(1)} %get-tuple-element.130.refs_4_.refs_2_.refs_12_) | copy-start | bytes 3538948
  20.2 94.8 %copy-start.1 = (bf16[4,192,768]{2,1,0:T(8,128)(2,1)}, bf16[4,192,768]{2,1,0:T(8,128)(2,1)S(1)}, u32[]{:S(2)}) copy-start(bf16[4,192,768]{2,1,0:T(8,128)(2,1)S(1)} %pad_maximum_fusion.2.refs_1_) | copy-start | bytes 3538948
  24.8 7.2 %collective-permute-start.1 = (bf16[1,192,768]{2,1,0:T(8,128)(2,1)S(1)}, bf16[1,192,768]{2,1,0:T(8,128)(2,1)S(1)}, u32[]{:S(2)}, u32[]{:S(2)}) collective-permute-start(bf16[1,192,768]{2,1,0:T(8,128)(2,1)S(1)} %slice.229), channel_id=1, source_target_pairs={{1,0},{2,1},{3,2},{0,3},{5,4},{6,5},{7,6},{4,7},{9,8},{10,9},{11,1... | collective-permute-start | bytes 884744 | tf_op jit(solution)/shard_map/ppermute | solution.py:470
  28.6 7.7 %collective-permute-start.3 = (bf16[1,192,768]{2,1,0:T(8,128)(2,1)S(1)}, bf16[1,192,768]{2,1,0:T(8,128)(2,1)S(1)}, u32[]{:S(2)}, u32[]{:S(2)}) collective-permute-start(bf16[1,192,768]{2,1,0:T(8,128)(2,1)S(1)} %slice.230), channel_id=1, source_target_pairs={{3,0},{0,1},{1,2},{2,3},{7,4},{4,5},{5,6},{6,7},{11,8},{8,9},{9,10... | collective-permute-start | bytes 884744 | tf_op jit(solution)/shard_map/ppermute | solution.py:470
  29.3 13.4 %collective-permute-start.4 = (bf16[2,192,768]{2,1,0:T(8,128)(2,1)}, bf16[2,192,768]{2,1,0:T(8,128)(2,1)}, u32[]{:S(2)}, u32[]{:S(2)}) collective-permute-start(bf16[2,192,768]{2,1,0:T(8,128)(2,1)} %collective-permute-done.refs_2_), channel_id=1, source_target_pairs={{4,0},{0,4},{12,8},{8,12},{20,16},{16,20},{28,24},{24,28},{36,32},... | collective-permute-start | bytes 1769480 | tf_op jit(solution)/shard_map/ppermute | solution.py:475
  31.4 11.4 %collective-permute-start.5 = (bf16[2,192,768]{2,1,0:T(8,128)(2,1)}, bf16[2,192,768]{2,1,0:T(8,128)(2,1)}, u32[]{:S(2)}, u32[]{:S(2)}) collective-permute-start(bf16[2,192,768]{2,1,0:T(8,128)(2,1)} %collective-permute-done.2.refs_4_), channel_id=1, source_target_pairs={{4,0},{0,4},{12,8},{8,12},{20,16},{16,20},{28,24},{24,28},{36,32},... | collective-permute-start | bytes 1769480 | tf_op jit(solution)/shard_map/ppermute | solution.py:475
  37.0 5.8 %collective-permute-start.6 = (bf16[2,192,768]{2,1,0:T(8,128)(2,1)}, bf16[2,192,768]{2,1,0:T(8,128)(2,1)}, u32[]{:S(2)}, u32[]{:S(2)}) collective-permute-start(bf16[2,192,768]{2,1,0:T(8,128)(2,1)} %constant_dynamic-update-slice_fusion.refs_3_), channel_id=1, source_target_pairs={{4,0},{0,4},{12,8},{8,12},{20,16},{16,20},{28,24},{24,28},{36,32},... | collective-permute-start | bytes 1769480 | tf_op jit(solution)/shard_map/ppermute | solution.py:475
  50.4 26.7 %all-to-all-start.1 = ((bf16[32,24,768]{2,1,0:T(8,128)(2,1)}), bf16[32,24,768]{2,1,0:T(8,128)(2,1)}, u32[]{:S(2)}, u32[]{:S(2)}) async-start(bf16[32,24,768]{2,1,0:T(8,128)(2,1)} %bitcast.120), calls=%async_computation.1 | async-start | bytes 2359296 | tf_op jit(solution)/shard_map/all_to_all | solution.py:498
  58.7 28.6 %collective-permute-start.10 = (bf16[768,768]{1,0:T(8,128)(2,1)S(1)}, bf16[768,768]{1,0:T(8,128)(2,1)}, u32[]{:S(2)}, u32[]{:S(2)}) collective-permute-start(bf16[768,768]{1,0:T(8,128)(2,1)S(1)} %get-tuple-element.130.refs_4_.refs_2_.refs_12_), channel_id=1, source_target_pairs={{3,0},{0,1},{1,2},{2,3},{7,4},{4,5},{5,6},{6,7},{11,8},{8,9},{9,10... | collective-permute-start | bytes 3538952 | tf_op jit(solution)/shard_map/ppermute | solution.py:470
  58.8 52.8 %collective-permute-start.8 = (bf16[768,768]{1,0:T(8,128)(2,1)S(1)}, bf16[768,768]{1,0:T(8,128)(2,1)}, u32[]{:S(2)}, u32[]{:S(2)}) collective-permute-start(bf16[768,768]{1,0:T(8,128)(2,1)S(1)} %get-tuple-element.130.refs_4_.refs_2_.refs_12_), channel_id=1, source_target_pairs={{1,0},{2,1},{3,2},{0,3},{5,4},{6,5},{7,6},{4,7},{9,8},{10,9},{11,1... | collective-permute-start | bytes 3538952 | tf_op jit(solution)/shard_map/ppermute | solution.py:470
  61.4 50.1 %collective-permute-start.7 = (bf16[768,768]{1,0:T(8,128)(2,1)}, bf16[768,768]{1,0:T(8,128)(2,1)}, u32[]{:S(2)}, u32[]{:S(2)}) collective-permute-start(bf16[768,768]{1,0:T(8,128)(2,1)} %get-tuple-element.129.refs_3_.refs_1_.refs_10_), channel_id=1, source_target_pairs={{1,0},{2,1},{3,2},{0,3},{5,4},{6,5},{7,6},{4,7},{9,8},{10,9},{11,1... | collective-permute-start | bytes 3538952 | tf_op jit(solution)/shard_map/ppermute | solution.py:470
  61.5 51.1 %collective-permute-start.9 = (bf16[768,768]{1,0:T(8,128)(2,1)}, bf16[768,768]{1,0:T(8,128)(2,1)}, u32[]{:S(2)}, u32[]{:S(2)}) collective-permute-start(bf16[768,768]{1,0:T(8,128)(2,1)} %get-tuple-element.129.refs_3_.refs_1_.refs_10_), channel_id=1, source_target_pairs={{3,0},{0,1},{1,2},{2,3},{7,4},{4,5},{5,6},{6,7},{11,8},{8,9},{9,10... | collective-permute-start | bytes 3538952 | tf_op jit(solution)/shard_map/ppermute | solution.py:470
  112.6 45.1 %collective-permute-start.17 = (bf16[768,768]{1,0:T(8,128)(2,1)}, bf16[768,768]{1,0:T(8,128)(2,1)}, u32[]{:S(2)}, u32[]{:S(2)}) collective-permute-start(bf16[768,768]{1,0:T(8,128)(2,1)} %collective-permute-done.7.refs_3_), channel_id=1, source_target_pairs={{1,0},{2,1},{3,2},{0,3},{5,4},{6,5},{7,6},{4,7},{9,8},{10,9},{11,1... | collective-permute-start | bytes 3538952 | tf_op jit(solution)/shard_map/ppermute | solution.py:470
  115.0 44.0 %collective-permute-start.19 = (bf16[768,768]{1,0:T(8,128)(2,1)}, bf16[768,768]{1,0:T(8,128)(2,1)}, u32[]{:S(2)}, u32[]{:S(2)}) collective-permute-start(bf16[768,768]{1,0:T(8,128)(2,1)} %collective-permute-done.10.refs_6_), channel_id=1, source_target_pairs={{3,0},{0,1},{1,2},{2,3},{7,4},{4,5},{5,6},{6,7},{11,8},{8,9},{9,10... | collective-permute-start | bytes 3538952 | tf_op jit(solution)/shard_map/ppermute | solution.py:470
  115.0 36.8 %collective-permute-start.11 = (bf16[2,192,768]{2,1,0:T(8,128)(2,1)S(1)}, bf16[2,192,768]{2,1,0:T(8,128)(2,1)S(1)}, u32[]{:S(2)}, u32[]{:S(2)}) collective-permute-start(bf16[2,192,768]{2,1,0:T(8,128)(2,1)S(1)} %constant_dynamic-slice_fusion.3), channel_id=1, source_target_pairs={{1,0},{2,1},{3,2},{0,3},{5,4},{6,5},{7,6},{4,7},{9,8},{10,9},{11,1... | collective-permute-start | bytes 1769480 | tf_op jit(solution)/shard_map/ppermute | solution.py:470
  117.8 37.0 %collective-permute-start.12 = (bf16[2,192,768]{2,1,0:T(8,128)(2,1)S(1)}, bf16[2,192,768]{2,1,0:T(8,128)(2,1)S(1)}, u32[]{:S(2)}, u32[]{:S(2)}) collective-permute-start(bf16[2,192,768]{2,1,0:T(8,128)(2,1)S(1)} %constant_dynamic-slice_fusion.3), channel_id=1, source_target_pairs={{3,0},{0,1},{1,2},{2,3},{7,4},{4,5},{5,6},{6,7},{11,8},{8,9},{9,10... | collective-permute-start | bytes 1769480 | tf_op jit(solution)/shard_map/ppermute | solution.py:470
  151.8 14.4 %copy-start.6 = (bf16[2,192,768]{2,1,0:T(8,128)(2,1)}, bf16[2,192,768]{2,1,0:T(8,128)(2,1)S(1)}, u32[]{:S(2)}) copy-start(bf16[2,192,768]{2,1,0:T(8,128)(2,1)S(1)} %collective-permute-done.11.refs_2_) | copy-start | bytes 1769476
  154.8 11.4 %copy-start.7 = (bf16[2,192,768]{2,1,0:T(8,128)(2,1)}, bf16[2,192,768]{2,1,0:T(8,128)(2,1)S(1)}, u32[]{:S(2)}) copy-start(bf16[2,192,768]{2,1,0:T(8,128)(2,1)S(1)} %collective-permute-done.12.refs_4_) | copy-start | bytes 1769476
  154.8 21.1 %collective-permute-start.15 = (bf16[2,192,768]{2,1,0:T(8,128)(2,1)S(1)}, bf16[2,192,768]{2,1,0:T(8,128)(2,1)}, u32[]{:S(2)}, u32[]{:S(2)}) collective-permute-start(bf16[2,192,768]{2,1,0:T(8,128)(2,1)S(1)} %collective-permute-done.11.refs_2_), channel_id=1, source_target_pairs={{4,0},{0,4},{12,8},{8,12},{20,16},{16,20},{28,24},{24,28},{36,32},... | collective-permute-start | bytes 1769480 | tf_op jit(solution)/shard_map/ppermute | solution.py:475
  157.4 18.5 %collective-permute-start.16 = (bf16[2,192,768]{2,1,0:T(8,128)(2,1)S(1)}, bf16[2,192,768]{2,1,0:T(8,128)(2,1)}, u32[]{:S(2)}, u32[]{:S(2)}) collective-permute-start(bf16[2,192,768]{2,1,0:T(8,128)(2,1)S(1)} %collective-permute-done.12.refs_4_), channel_id=1, source_target_pairs={{4,0},{0,4},{12,8},{8,12},{20,16},{16,20},{28,24},{24,28},{36,32},... | collective-permute-start | bytes 1769480 | tf_op jit(solution)/shard_map/ppermute | solution.py:475
  157.5 17.2 %collective-permute-start.13 = (bf16[1,192,768]{2,1,0:T(8,128)(2,1)S(1)}, bf16[1,192,768]{2,1,0:T(8,128)(2,1)}, u32[]{:S(2)}, u32[]{:S(2)}) collective-permute-start(bf16[1,192,768]{2,1,0:T(8,128)(2,1)S(1)} %slice.196), channel_id=1, source_target_pairs={{1,0},{2,1},{3,2},{0,3},{5,4},{6,5},{7,6},{4,7},{9,8},{10,9},{11,1... | collective-permute-start | bytes 884744 | tf_op jit(solution)/shard_map/ppermute | solution.py:470
  157.7 17.0 %collective-permute-start.14 = (bf16[1,192,768]{2,1,0:T(8,128)(2,1)S(1)}, bf16[1,192,768]{2,1,0:T(8,128)(2,1)}, u32[]{:S(2)}, u32[]{:S(2)}) collective-permute-start(bf16[1,192,768]{2,1,0:T(8,128)(2,1)S(1)} %slice.197), channel_id=1, source_target_pairs={{3,0},{0,1},{1,2},{2,3},{7,4},{4,5},{5,6},{6,7},{11,8},{8,9},{9,10... | collective-permute-start | bytes 884744 | tf_op jit(solution)/shard_map/ppermute | solution.py:470
  166.2 26.8 %all-to-all-start.2 = ((bf16[32,24,768]{2,1,0:T(8,128)(2,1)}), bf16[32,24,768]{2,1,0:T(8,128)(2,1)S(1)}, u32[]{:S(2)}, u32[]{:S(2)}) async-start(bf16[32,24,768]{2,1,0:T(8,128)(2,1)} %bitcast.118), calls=%async_computation.2 | async-start | bytes 2359296 | tf_op jit(solution)/shard_map/all_to_all | solution.py:498
  175.9 28.4 %collective-permute-start.20 = (bf16[768,768]{1,0:T(8,128)(2,1)}, bf16[768,768]{1,0:T(8,128)(2,1)}, u32[]{:S(2)}, u32[]{:S(2)}) collective-permute-start(bf16[768,768]{1,0:T(8,128)(2,1)} %get-tuple-element.149.refs_3_.refs_5_), channel_id=1, source_target_pairs={{1,0},{2,1},{3,2},{0,3},{5,4},{6,5},{7,6},{4,7},{9,8},{10,9},{11,1... | collective-permute-start | bytes 3538952 | tf_op jit(solution)/shard_map/ppermute | solution.py:470
  177.3 28.5 %collective-permute-start.21 = (bf16[768,768]{1,0:T(8,128)(2,1)}, bf16[768,768]{1,0:T(8,128)(2,1)}, u32[]{:S(2)}, u32[]{:S(2)}) collective-permute-start(bf16[768,768]{1,0:T(8,128)(2,1)} %get-tuple-element.150.refs_4_.refs_7_), channel_id=1, source_target_pairs={{3,0},{0,1},{1,2},{2,3},{7,4},{4,5},{5,6},{6,7},{11,8},{8,9},{9,10... | collective-permute-start | bytes 3538952 | tf_op jit(solution)/shard_map/ppermute | solution.py:470
  177.7 6.2 %collective-permute-start.18 = (bf16[2,192,768]{2,1,0:T(8,128)(2,1)S(1)}, bf16[2,192,768]{2,1,0:T(8,128)(2,1)S(1)}, u32[]{:S(2)}, u32[]{:S(2)}) collective-permute-start(bf16[2,192,768]{2,1,0:T(8,128)(2,1)S(1)} %pad_maximum_fusion.3.refs_3_), channel_id=1, source_target_pairs={{4,0},{0,4},{12,8},{8,12},{20,16},{16,20},{28,24},{24,28},{36,32},... | collective-permute-start | bytes 1769480 | tf_op jit(solution)/shard_map/ppermute | solution.py:475
  183.9 9.1 %copy-start.13 = (bf16[2,192,768]{2,1,0:T(8,128)(2,1)}, bf16[2,192,768]{2,1,0:T(8,128)(2,1)S(1)}, u32[]{:S(2)}) copy-start(bf16[2,192,768]{2,1,0:T(8,128)(2,1)S(1)} %collective-permute-done.18.refs_6_) | copy-start | bytes 1769476
  205.8 8.5 %copy-start.9 = (bf16[768,768]{1,0:T(8,128)(2,1)S(1)}, bf16[768,768]{1,0:T(8,128)(2,1)}, u32[]{:S(2)}) copy-start(bf16[768,768]{1,0:T(8,128)(2,1)} %get-tuple-element.150.refs_4_.refs_7_) | copy-start | bytes 3538948
  205.8 39.7 %all-to-all-start.3 = ((bf16[32,24,1536]{2,1,0:T(8,128)(2,1)}), bf16[32,24,1536]{2,1,0:T(8,128)(2,1)S(1)}, u32[]{:S(2)}, u32[]{:S(2)}) async-start(bf16[32,24,1536]{2,1,0:T(8,128)(2,1)} %bitcast.107), calls=%async_computation.3 | async-start | bytes 4718592 | tf_op jit(solution)/shard_map/all_to_all | solution.py:498
  214.3 31.1 %collective-permute-start.22 = (bf16[768,768]{1,0:T(8,128)(2,1)S(1)}, bf16[768,768]{1,0:T(8,128)(2,1)}, u32[]{:S(2)}, u32[]{:S(2)}) collective-permute-start(bf16[768,768]{1,0:T(8,128)(2,1)S(1)} %copy-done.9), channel_id=1, source_target_pairs={{1,0},{2,1},{3,2},{0,3},{5,4},{6,5},{7,6},{4,7},{9,8},{10,9},{11,1... | collective-permute-start | bytes 3538952 | tf_op jit(solution)/shard_map/ppermute | solution.py:470
  214.4 32.7 %collective-permute-start.25 = (bf16[768,768]{1,0:T(8,128)(2,1)}, bf16[768,768]{1,0:T(8,128)(2,1)}, u32[]{:S(2)}, u32[]{:S(2)}) collective-permute-start(bf16[768,768]{1,0:T(8,128)(2,1)} %get-tuple-element.149.refs_3_.refs_5_), channel_id=1, source_target_pairs={{3,0},{0,1},{1,2},{2,3},{7,4},{4,5},{5,6},{6,7},{11,8},{8,9},{9,10... | collective-permute-start | bytes 3538952 | tf_op jit(solution)/shard_map/ppermute | solution.py:470
  215.9 51.3 %collective-permute-start.23 = (bf16[768,768]{1,0:T(8,128)(2,1)}, bf16[768,768]{1,0:T(8,128)(2,1)}, u32[]{:S(2)}, u32[]{:S(2)}) collective-permute-start(bf16[768,768]{1,0:T(8,128)(2,1)} %collective-permute-done.20.refs_5_), channel_id=1, source_target_pairs={{1,0},{2,1},{3,2},{0,3},{5,4},{6,5},{7,6},{4,7},{9,8},{10,9},{11,1... | collective-permute-start | bytes 3538952 | tf_op jit(solution)/shard_map/ppermute | solution.py:470
  217.2 51.2 %collective-permute-start.24 = (bf16[768,768]{1,0:T(8,128)(2,1)}, bf16[768,768]{1,0:T(8,128)(2,1)}, u32[]{:S(2)}, u32[]{:S(2)}) collective-permute-start(bf16[768,768]{1,0:T(8,128)(2,1)} %collective-permute-done.21.refs_10_), channel_id=1, source_target_pairs={{3,0},{0,1},{1,2},{2,3},{7,4},{4,5},{5,6},{6,7},{11,8},{8,9},{9,10... | collective-permute-start | bytes 3538952 | tf_op jit(solution)/shard_map/ppermute | solution.py:470
  245.5 22.9 %copy-start.5 = (bf16[32,24,1536]{2,1,0:T(8,128)(2,1)}, bf16[32,24,1536]{2,1,0:T(8,128)(2,1)S(1)}, u32[]{:S(2)}) copy-start(bf16[32,24,1536]{2,1,0:T(8,128)(2,1)S(1)} %all-to-all-done.3) | copy-start | bytes 7077892
  245.5 84.7 %collective-permute-start.26 = (bf16[768,1536]{1,0:T(8,128)(2,1)S(1)}, bf16[768,1536]{1,0:T(8,128)(2,1)}, u32[]{:S(2)}, u32[]{:S(2)}) collective-permute-start(bf16[768,1536]{1,0:T(8,128)(2,1)S(1)} %bitcast.103), channel_id=1, source_target_pairs={{1,0},{2,1},{3,2},{0,3},{5,4},{6,5},{7,6},{4,7},{9,8},{10,9},{11,1... | collective-permute-start | bytes 7077896 | tf_op jit(solution)/shard_map/ppermute | solution.py:470
  245.5 84.7 %collective-permute-start.27 = (bf16[768,1536]{1,0:T(8,128)(2,1)S(1)}, bf16[768,1536]{1,0:T(8,128)(2,1)}, u32[]{:S(2)}, u32[]{:S(2)}) collective-permute-start(bf16[768,1536]{1,0:T(8,128)(2,1)S(1)} %bitcast.104), channel_id=1, source_target_pairs={{3,0},{0,1},{1,2},{2,3},{7,4},{4,5},{5,6},{6,7},{11,8},{8,9},{9,10... | collective-permute-start | bytes 7077896 | tf_op jit(solution)/shard_map/ppermute | solution.py:470
  289.6 40.6 %all-to-all-start.4 = ((bf16[32,24,1536]{2,1,0:T(8,128)(2,1)}), bf16[32,24,1536]{2,1,0:T(8,128)(2,1)}, u32[]{:S(2)}, u32[]{:S(2)}) async-start(bf16[32,24,1536]{2,1,0:T(8,128)(2,1)} %bitcast.108), calls=%async_computation.4 | async-start | bytes 4718592 | tf_op jit(solution)/shard_map/all_to_all | solution.py:498
  299.0 48.9 %collective-permute-start.28 = (bf16[768,768]{1,0:T(8,128)(2,1)}, bf16[768,768]{1,0:T(8,128)(2,1)S(1)}, u32[]{:S(2)}, u32[]{:S(2)}) collective-permute-start(bf16[768,768]{1,0:T(8,128)(2,1)} %bitcast.13.refs_0_), channel_id=1, source_target_pairs={{1,0},{2,1},{3,2},{0,3},{5,4},{6,5},{7,6},{4,7},{9,8},{10,9},{11,1... | collective-permute-start | bytes 3538952 | tf_op jit(solution)/shard_map/ppermute | solution.py:470
  299.1 48.8 %collective-permute-start.29 = (bf16[768,768]{1,0:T(8,128)(2,1)}, bf16[768,768]{1,0:T(8,128)(2,1)}, u32[]{:S(2)}, u32[]{:S(2)}) collective-permute-start(bf16[768,768]{1,0:T(8,128)(2,1)} %bitcast.13.refs_0_), channel_id=1, source_target_pairs={{3,0},{0,1},{1,2},{2,3},{7,4},{4,5},{5,6},{6,7},{11,8},{8,9},{9,10... | collective-permute-start | bytes 3538952 | tf_op jit(solution)/shard_map/ppermute | solution.py:470
  346.9 49.1 %collective-permute-start.34 = (bf16[4,2,192,768]{3,2,1,0:T(8,128)(2,1)}, bf16[4,2,192,768]{3,2,1,0:T(8,128)(2,1)S(1)}, u32[]{:S(2)}, u32[]{:S(2)}) collective-permute-start(bf16[4,2,192,768]{3,2,1,0:T(8,128)(2,1)} %get-tuple-element.201), channel_id=1, source_target_pairs={{4,0},{0,4},{12,8},{8,12},{20,16},{16,20},{28,24},{24,28},{36,32},... | collective-permute-start | bytes 7077896 | tf_op jit(solution)/shard_map/ppermute | solution.py:475
  348.9 22.1 %all-to-all-start.5 = ((bf16[32,24,768]{2,1,0:T(8,128)(2,1)}), bf16[32,24,768]{2,1,0:T(8,128)(2,1)S(1)}, u32[]{:S(2)}, u32[]{:S(2)}) async-start(bf16[32,24,768]{2,1,0:T(8,128)(2,1)} %bitcast.117), calls=%async_computation.5 | async-start | bytes 2359296 | tf_op jit(solution)/shard_map/all_to_all | solution.py:498
  354.9 32.5 %collective-permute-start.30 = (bf16[384,1536]{1,0:T(8,128)(2,1)}, bf16[384,1536]{1,0:T(8,128)(2,1)}, u32[]{:S(2)}, u32[]{:S(2)}) collective-permute-start(bf16[384,1536]{1,0:T(8,128)(2,1)} %slice.209), channel_id=1, source_target_pairs={{1,0},{2,1},{3,2},{0,3},{5,4},{6,5},{7,6},{4,7},{9,8},{10,9},{11,1... | collective-permute-start | bytes 3538952 | tf_op jit(solution)/shard_map/ppermute | solution.py:470
  357.9 29.5 %collective-permute-start.31 = (bf16[384,1536]{1,0:T(8,128)(2,1)}, bf16[384,1536]{1,0:T(8,128)(2,1)}, u32[]{:S(2)}, u32[]{:S(2)}) collective-permute-start(bf16[384,1536]{1,0:T(8,128)(2,1)} %slice.210), channel_id=1, source_target_pairs={{3,0},{0,1},{1,2},{2,3},{7,4},{4,5},{5,6},{6,7},{11,8},{8,9},{9,10... | collective-permute-start | bytes 3538952 | tf_op jit(solution)/shard_map/ppermute | solution.py:470
  370.9 58.5 %collective-permute-start.32 = (bf16[768,768]{1,0:T(8,128)(2,1)S(1)}, bf16[768,768]{1,0:T(8,128)(2,1)}, u32[]{:S(2)}, u32[]{:S(2)}) collective-permute-start(bf16[768,768]{1,0:T(8,128)(2,1)S(1)} %bitcast.113), channel_id=1, source_target_pairs={{1,0},{2,1},{3,2},{0,3},{5,4},{6,5},{7,6},{4,7},{9,8},{10,9},{11,1... | collective-permute-start | bytes 3538952 | tf_op jit(solution)/shard_map/ppermute | solution.py:470
  371.5 58.5 %collective-permute-start.33 = (bf16[768,768]{1,0:T(8,128)(2,1)S(1)}, bf16[768,768]{1,0:T(8,128)(2,1)}, u32[]{:S(2)}, u32[]{:S(2)}) collective-permute-start(bf16[768,768]{1,0:T(8,128)(2,1)S(1)} %bitcast.114), channel_id=1, source_target_pairs={{3,0},{0,1},{1,2},{2,3},{7,4},{4,5},{5,6},{6,7},{11,8},{8,9},{9,10... | collective-permute-start | bytes 3538952 | tf_op jit(solution)/shard_map/ppermute | solution.py:470
  387.4 43.5 %all-to-all-start.6 = ((bf16[32,24,768]{2,1,0:T(8,128)(2,1)}), bf16[32,24,768]{2,1,0:T(8,128)(2,1)}, u32[]{:S(2)}, u32[]{:S(2)}) async-start(bf16[32,24,768]{2,1,0:T(8,128)(2,1)} %bitcast.119), calls=%async_computation.6 | async-start | bytes 2359296 | tf_op jit(solution)/shard_map/all_to_all | solution.py:498
  401.6 34.7 %collective-permute-start.35 = (bf16[384,768]{1,0:T(8,128)(2,1)}, bf16[384,768]{1,0:T(8,128)(2,1)}, u32[]{:S(2)}, u32[]{:S(2)}) collective-permute-start(bf16[384,768]{1,0:T(8,128)(2,1)} %get-tuple-element.280), channel_id=1, source_target_pairs={{3,0},{0,1},{1,2},{2,3},{7,4},{4,5},{5,6},{6,7},{11,8},{8,9},{9,10... | collective-permute-start | bytes 1769480 | tf_op jit(solution)/shard_map/ppermute | solution.py:470
  401.6 34.7 %collective-permute-start.36 = (bf16[384,768]{1,0:T(8,128)(2,1)}, bf16[384,768]{1,0:T(8,128)(2,1)}, u32[]{:S(2)}, u32[]{:S(2)}) collective-permute-start(bf16[384,768]{1,0:T(8,128)(2,1)} %get-tuple-element.282), channel_id=1, source_target_pairs={{2,0},{3,1},{0,2},{1,3},{6,4},{7,5},{4,6},{5,7},{10,8},{11,9},{8,1... | collective-permute-start | bytes 1769480 | tf_op jit(solution)/shard_map/ppermute | solution.py:470
  402.1 52.2 %collective-permute-start.37 = (bf16[384,768]{1,0:T(8,128)(2,1)}, bf16[384,768]{1,0:T(8,128)(2,1)}, u32[]{:S(2)}, u32[]{:S(2)}) collective-permute-start(bf16[384,768]{1,0:T(8,128)(2,1)} %get-tuple-element.281), channel_id=1, source_target_pairs={{1,0},{2,1},{3,2},{0,3},{5,4},{6,5},{7,6},{4,7},{9,8},{10,9},{11,1... | collective-permute-start | bytes 1769480 | tf_op jit(solution)/shard_map/ppermute | solution.py:470
  429.4 26.7 %collective-permute-start.38 = (bf16[384,768]{1,0:T(8,128)(2,1)}, bf16[384,768]{1,0:T(8,128)(2,1)}, u32[]{:S(2)}, u32[]{:S(2)}) collective-permute-start(bf16[384,768]{1,0:T(8,128)(2,1)} %slice.213), channel_id=1, source_target_pairs={{1,0},{2,1},{3,2},{0,3},{5,4},{6,5},{7,6},{4,7},{9,8},{10,9},{11,1... | collective-permute-start | bytes 1769480 | tf_op jit(solution)/shard_map/ppermute | solution.py:470
  430.0 26.0 %collective-permute-start.39 = (bf16[384,768]{1,0:T(8,128)(2,1)}, bf16[384,768]{1,0:T(8,128)(2,1)}, u32[]{:S(2)}, u32[]{:S(2)}) collective-permute-start(bf16[384,768]{1,0:T(8,128)(2,1)} %slice.214), channel_id=1, source_target_pairs={{3,0},{0,1},{1,2},{2,3},{7,4},{4,5},{5,6},{6,7},{11,8},{8,9},{9,10... | collective-permute-start | bytes 1769480 | tf_op jit(solution)/shard_map/ppermute | solution.py:470
  436.4 22.0 %collective-permute-start.40 = (bf16[384,768]{1,0:T(8,128)(2,1)S(1)}, bf16[384,768]{1,0:T(8,128)(2,1)S(1)}, u32[]{:S(2)}, u32[]{:S(2)}) collective-permute-start(bf16[384,768]{1,0:T(8,128)(2,1)S(1)} %slice.215), channel_id=1, source_target_pairs={{1,0},{2,1},{3,2},{0,3},{5,4},{6,5},{7,6},{4,7},{9,8},{10,9},{11,1... | collective-permute-start | bytes 1769480 | tf_op jit(solution)/shard_map/ppermute | solution.py:470
  436.4 25.8 %collective-permute-start.41 = (bf16[384,768]{1,0:T(8,128)(2,1)S(1)}, bf16[384,768]{1,0:T(8,128)(2,1)S(1)}, u32[]{:S(2)}, u32[]{:S(2)}) collective-permute-start(bf16[384,768]{1,0:T(8,128)(2,1)S(1)} %slice.216), channel_id=1, source_target_pairs={{3,0},{0,1},{1,2},{2,3},{7,4},{4,5},{5,6},{6,7},{11,8},{8,9},{9,10... | collective-permute-start | bytes 1769480 | tf_op jit(solution)/shard_map/ppermute | solution.py:470
  454.3 10.2 %copy-start.20 = (f32[40,768]{1,0:T(8,128)S(1)}, f32[40,768]{1,0:T(8,128)}, u32[]{:S(2)}) copy-start(f32[40,768]{1,0:T(8,128)} %get-tuple-element.211) | copy-start | bytes 368644
  454.3 10.2 %copy-start.21 = (f32[40,768]{1,0:T(8,128)S(1)}, f32[40,768]{1,0:T(8,128)}, u32[]{:S(2)}) copy-start(f32[40,768]{1,0:T(8,128)} %get-tuple-element.210) | copy-start | bytes 368644
  463.0 5.8 %collective-permute-start.42 = (bf16[4,2,192,768]{3,2,1,0:T(8,128)(2,1)}, bf16[4,2,192,768]{3,2,1,0:T(8,128)(2,1)S(1)}, u32[]{:S(2)}, u32[]{:S(2)}) collective-permute-start(bf16[4,2,192,768]{3,2,1,0:T(8,128)(2,1)} %get-tuple-element.209), channel_id=1, source_target_pairs={{4,0},{0,4},{12,8},{8,12},{20,16},{16,20},{28,24},{24,28},{36,32},... | collective-permute-start | bytes 7077896 | tf_op jit(solution)/shard_map/ppermute | solution.py:475
  464.6 4.0 collective-permute-start.43
  471.2 31.6 %collective-permute-start.44 = (bf16[432,768]{1,0:T(8,128)(2,1)S(1)}, bf16[432,768]{1,0:T(8,128)(2,1)S(1)}, u32[]{:S(2)}, u32[]{:S(2)}) collective-permute-start(bf16[432,768]{1,0:T(8,128)(2,1)S(1)} %get-tuple-element.277), channel_id=1, source_target_pairs={{3,0},{0,1},{1,2},{2,3},{7,4},{4,5},{5,6},{6,7},{11,8},{8,9},{9,10... | collective-permute-start | bytes 1990664 | tf_op jit(solution)/shard_map/ppermute | solution.py:470
  471.3 31.5 %collective-permute-start.45 = (bf16[432,768]{1,0:T(8,128)(2,1)S(1)}, bf16[432,768]{1,0:T(8,128)(2,1)S(1)}, u32[]{:S(2)}, u32[]{:S(2)}) collective-permute-start(bf16[432,768]{1,0:T(8,128)(2,1)S(1)} %get-tuple-element.278), channel_id=1, source_target_pairs={{2,0},{3,1},{0,2},{1,3},{6,4},{7,5},{4,6},{5,7},{10,8},{11,9},{8,1... | collective-permute-start | bytes 1990664 | tf_op jit(solution)/shard_map/ppermute | solution.py:470
  472.5 30.7 %collective-permute-start.46 = (bf16[432,768]{1,0:T(8,128)(2,1)S(1)}, bf16[432,768]{1,0:T(8,128)(2,1)S(1)}, u32[]{:S(2)}, u32[]{:S(2)}) collective-permute-start(bf16[432,768]{1,0:T(8,128)(2,1)S(1)} %get-tuple-element.279), channel_id=1, source_target_pairs={{1,0},{2,1},{3,2},{0,3},{5,4},{6,5},{7,6},{4,7},{9,8},{10,9},{11,1... | collective-permute-start | bytes 1990664 | tf_op jit(solution)/shard_map/ppermute | solution.py:470
  550.6 9.1 %collective-permute-start.47 = (bf16[16,51,768]{2,0,1:T(8,128)(2,1)}, bf16[16,51,768]{2,0,1:T(8,128)(2,1)S(1)}, u32[]{:S(2)}, u32[]{:S(2)}) collective-permute-start(bf16[16,51,768]{2,0,1:T(8,128)(2,1)} %copy.70), channel_id=1, source_target_pairs={{4,0},{0,4},{12,8},{8,12},{20,16},{16,20},{28,24},{24,28},{36,32},... | collective-permute-start | bytes 3760136 | tf_op jit(solution)/shard_map/ppermute | solution.py:475
  (22 other events, 89.9 us)

commit v5 on v4

--- a/solution.py
+++ b/solution.py
@@ -357,9 +357,10 @@
         y_sum = refs.pop(0) if forward else None
         d_sum = refs.pop(0) if backward else None
         if forward:
-            y_sum[...] = jnp.broadcast_to(at["total"][...], y_sum.shape)
+            y_sum[...] = jnp.broadcast_to(at["total"][:, :width], y_sum.shape)
         if backward:
-            d_sum[...] = jnp.zeros_like(d_sum)
+            resumed = forward and total.shape[1] > width
+            d_sum[...] = at["total"][:, width:] if resumed else jnp.zeros_like(d_sum)
         for i in range(len(pieces)):
             in_ref, out_ref = held_refs[2 * i], held_refs[2 * i + 1]
             fetch.wait(2 * i, 2 * i + 1)
@@ -659,7 +660,17 @@
     far_in, far_out = ahead(next_in, 1), ahead(last_out, 3)
     both1 = swap(send, stride)
     wide1 = [(in1, out1), (next_in, next_out), (far_in, far_out), (last_in, last_out)]
-    (both,) = expert_pieces(both1, both1, wide1, hidden_bias[1], None, bias_out[1], True)
+    bias = hidden_bias[1]
+    (sums,) = expert_pieces(
+        both1,
+        both1,
+        [wide1[i] for i in (0, 1, 3)],
+        jnp.concatenate([bias[:2], bias[3:]]),
+        None,
+        bias_out[1],
+        False,
+    )
+    (both,) = expert_pieces(both1, both1, [wide1[2]], bias[2:3], None, sums, True)
     after1, before1, far1 = ring_rows(both1)
     early, _ = tie(rows0, both1)
     after0, before0, far0 = ring_rows(early)

time: 580 us -> 580 us (level)
  waiting for transfers between devices: 184 us -> 172 us
  Pallas kernels: 166 us -> 172 us
    ppermute x38, waiting for transfers between devices: 94.8 us -> 83.8 us  [ahead(): lax.ppermute(value, axis, [((i + steps) % size, i) for i in range(size)])]
    pallas_call x5 -> x6, Pallas kernels: 60.5 us -> 67.3 us  [expert_pieces(): pl.pallas_call(body, out_shape=[s for _, s in shapes], in_specs=[pl.Block...]
  transfers between devices with their start and end apart: 55 -> 55, of which waited for: 22 -> 24; matrix products, arithmetic and copies ran while one was open for 9% -> 9% of each run, Pallas kernels for 27% -> 28%
where the time goes in v5:
time: 580 us; the launch traced here: 570 us
  waiting for transfers between devices  172 us (30%)
  Pallas kernels  172 us (30%)
  starting transfers between devices  109 us (19%)
  local copies, waits for them, and re-layouts  53.7 us (9%)
  blocking collectives  45.1 us (8%)
  other arithmetic  15.3 us (3%)
    all_to_all x6, waiting for transfers between devices, swap(): lax.all_to_all(rows.reshape(-1, stride, width), 'expert', split_axis=0, c...  85.1 us
    ppermute x38, waiting for transfers between devices, ahead(): lax.ppermute(value, axis, [((i + steps) % size, i) for i in range(size)])  83.8 us
    pallas_call x6, Pallas kernels, expert_pieces(): pl.pallas_call(body, out_shape=[s for _, s in shapes], in_specs=[pl.Block...  67.3 us
    all_to_all x6, starting transfers between devices, swap(): lax.all_to_all(rows.reshape(-1, stride, width), 'expert', split_axis=0, c...  51.5 us
    pallas_call x2, Pallas kernels, expert_grads(): pl.pallas_call(body, grid=(1,), in_specs=[pl.BlockSpec(memory_space=pl.AN...  49.6 us
    ppermute x38, starting transfers between devices, ahead(): lax.ppermute(value, axis, [((i + steps) % size, i) for i in range(size)])  37 us
    pallas_call x2, Pallas kernels, mixer_backward(): pl.pallas_call(functools.partial(mixer_backward_body, last, count, scale,...  33.1 us
    all_to_all x1, blocking collectives, shards(): lax.all_to_all(lines, 'expert', split_axis=0, concat_axis=0, tiled=True,...  24.5 us
  transfers between devices with their start and end apart: 55, of which 24 were waited for; matrix products, arithmetic and copies ran while one was open for 9% of the time, Pallas kernels for 28%

profile of v5, /device:TPU:1, one launch (start us, length us, event | category | flops | bytes accessed | tf_op | source)
XLA Modules:
  0.0 569.6 jit_solution(17112578292587174761)
XLA Ops:
  4.1 3.3 collective-permute-start
  8.3 4.1 all-to-all-start
  15.8 4.3 slice_bitcast_fusion
  20.2 1.7 copy.60.refs_13_.refs_17_
  24.7 2.7 collective-permute-start.1
  29.2 2.1 collective-permute-start.4
  32.7 3.5 collective-permute-done.3
  36.9 3.0 collective-permute-start.6
  42.7 7.6 %shard_map.220 = (f32[208,768]{1,0:T(8,128)}, bf16[768,768]{1,0:T(8,128)(2,1)}, bf16[208,768]{1,0:T(8,128)(2,1)}, bf16[208,768]{1,0:T(8,128)(2,1)}, bf16[208,768...) custom-call(s32[2]{0:T(128)} %pad_add_fusion.refs_0_.refs_13_.here_r, ...), custom_call_target="tpu_custom_call" | custom-call | flops 2000000000 | bytes 20000000 | tf_op jit(solution)/shard_map/pallas_call | solution.py:601
  50.3 8.3 %all-to-all-start.1 = ((bf16[32,24,768]{2,1,0:T(8,128)(2,1)}), bf16[32,24,768]{2,1,0:T(8,128)(2,1)}, u32[]{:S(2)}, u32[]{:S(2)}) async-start(bf16[32,24,768]{2,1,0:T(8,128)(2,1)} %bitcast.121), calls=%async_computation.1 | async-start | bytes 2359296 | tf_op jit(solution)/shard_map/all_to_all | solution.py:499
  58.7 2.7 collective-permute-start.8
  61.4 1.6 collective-permute-start.9
  64.9 12.1 %all-to-all-done.1 = bf16[32,24,768]{2,1,0:T(8,128)(2,1)} async-done(((bf16[32,24,768]{2,1,0:T(8,128)(2,1)}), bf16[32,24,768]{2,1,0:T(8,128)(2,1)}, u32[]{:S(2)}, u32[]{:S(2)}) %all-to-all-start.1) | async-done | bytes 1179680 | tf_op jit(solution)/shard_map/all_to_all | solution.py:499
  77.0 6.8 %shard_map.221 = (f32[768,768]{1,0:T(8,128)}, bf16[1,768,768]{2,1,0:T(8,128)(2,1)}) custom-call(bf16[768,768]{1,0:T(8,128)(2,1)} %bitcast.13.refs_0_, f32[1,768]{1,0:T(1,128)} %get-tuple-element.304.refs_1_, f32[1,768]{1,0:T(1,128)} %get-tuple-element.310.refs_2_, bf16[768,768]{1,0:T(8,128)(2,1)} %get-tuple-element.129.refs_3_.refs_1_.refs_10_, ...), custom_call_target="tpu_custom_call" | custom-call | flops 1811939328 | bytes 20000000 | tf_op jit(solution)/shard_map/pallas_call | solution.py:395
  83.8 3.4 collective-permute-done.10.refs_6_
  87.3 24.2 %collective-permute-done.7.refs_3_ = bf16[768,768]{1,0:T(8,128)(2,1)} collective-permute-done((bf16[768,768]{1,0:T(8,128)(2,1)}, bf16[768,768]{1,0:T(8,128)(2,1)}, u32[]{:S(2)}, u32[]{:S(2)}) %collective-permute-start.7) | collective-permute-done | bytes 1179680 | tf_op jit(solution)/shard_map/ppermute | solution.py:471
  112.5 2.4 collective-permute-start.17
  114.9 2.7 collective-permute-start.11
  118.3 10.3 %shard_map.222 = (f32[768,768]{1,0:T(8,128)}, bf16[2,768,768]{2,1,0:T(8,128)(2,1)}) custom-call(bf16[768,768]{1,0:T(8,128)(2,1)} %bitcast.13.refs_0_, f32[2,768]{1,0:T(2,128)} %slice.202.refs_1_, f32[768,768]{1,0:T(8,128)} %get-tuple-element.132.refs_2_, bf16[768,768]{1,0:T(8,128)(2,1)} %collective-permute-done.7.refs_3_, ...), custom_call_target="tpu_custom_call" | custom-call | flops 3623878656 | bytes 20000000 | tf_op jit(solution)/shard_map/pallas_call | solution.py:395
  128.6 23.1 %collective-permute-done.11.refs_2_ = bf16[2,192,768]{2,1,0:T(8,128)(2,1)S(1)} collective-permute-done((bf16[2,192,768]{2,1,0:T(8,128)(2,1)S(1)}, bf16[2,192,768]{2,1,0:T(8,128)(2,1)S(1)}, u32[]{:S(2)}, u32[]{:S(2)}) %collective-permute-start.11) | collective-permute-done | bytes 589856 | tf_op jit(solution)/shard_map/ppermute | solution.py:471
  151.7 3.0 collective-permute-done.12.refs_4_
  154.7 2.6 collective-permute-start.15
  158.9 7.2 %shard_map.223 = (bf16[768,768]{1,0:T(8,128)(2,1)}, bf16[1,768,768]{2,1,0:T(8,128)(2,1)}) custom-call(bf16[768,768]{1,0:T(8,128)(2,1)} %bitcast.13.refs_0_, f32[1,768]{1,0:T(1,128)} %get-tuple-element.303.refs_1_, f32[768,768]{1,0:T(8,128)} %get-tuple-element.145.refs_2_, bf16[768,768]{1,0:T(8,128)(2,1)} %collective-permute-done.17.refs_3_.refs_7_, ...), custom_call_target="tpu_custom_call" | custom-call | flops 1811939328 | bytes 20000000 | tf_op jit(solution)/shard_map/pallas_call | solution.py:395
  166.1 8.4 %all-to-all-start.2 = ((bf16[32,24,768]{2,1,0:T(8,128)(2,1)}), bf16[32,24,768]{2,1,0:T(8,128)(2,1)S(1)}, u32[]{:S(2)}, u32[]{:S(2)}) async-start(bf16[32,24,768]{2,1,0:T(8,128)(2,1)} %bitcast.119), calls=%async_computation.2 | async-start | bytes 2359296 | tf_op jit(solution)/shard_map/all_to_all | solution.py:499
  183.9 9.1 %all-to-all-done.2 = bf16[32,24,768]{2,1,0:T(8,128)(2,1)S(1)} async-done(((bf16[32,24,768]{2,1,0:T(8,128)(2,1)}), bf16[32,24,768]{2,1,0:T(8,128)(2,1)S(1)}, u32[]{:S(2)}, u32[]{:S(2)}) %all-to-all-start.2) | async-done | bytes 1179680 | tf_op jit(solution)/shard_map/all_to_all | solution.py:499
  194.0 10.3 %shard_map.224 = (f32[208,768]{1,0:T(8,128)}, bf16[768,1536]{1,0:T(8,128)(2,1)}, bf16[208,768]{1,0:T(8,128)(2,1)}, bf16[208,768]{1,0:T(8,128)(2,1)}, bf16[208,76...) custom-call(s32[2]{0:T(128)} %pad_add_fusion.refs_0_.refs_13_.here_r, ...), custom_call_target="tpu_custom_call" | custom-call | flops 2000000000 | bytes 20000000 | tf_op jit(solution)/shard_map/pallas_call | solution.py:601
  205.7 8.5 %all-to-all-start.3 = ((bf16[32,24,1536]{2,1,0:T(8,128)(2,1)}), bf16[32,24,1536]{2,1,0:T(8,128)(2,1)S(1)}, u32[]{:S(2)}, u32[]{:S(2)}) async-start(bf16[32,24,1536]{2,1,0:T(8,128)(2,1)} %bitcast.108), calls=%async_computation.3 | async-start | bytes 4718592 | tf_op jit(solution)/shard_map/all_to_all | solution.py:499
  218.5 26.9 %all-to-all-done.3 = bf16[32,24,1536]{2,1,0:T(8,128)(2,1)S(1)} async-done(((bf16[32,24,1536]{2,1,0:T(8,128)(2,1)}), bf16[32,24,1536]{2,1,0:T(8,128)(2,1)S(1)}, u32[]{:S(2)}, u32[]{:S(2)}) %all-to-all-start.3) | async-done | bytes 2359328 | tf_op jit(solution)/shard_map/all_to_all | solution.py:499
  245.4 1.6 collective-permute-start.27
  247.0 17.5 %shard_map.225.refs_2_ = f32[768,1536]{1,0:T(8,128)} custom-call(bf16[768,1536]{1,0:T(8,128)(2,1)} %bitcast.105, f32[3,768]{1,0:T(4,128)} %pad_maximum_fusion.4.refs_1_, f32[1,768]{1,0:T(1,128)} %get-tuple-element.309.refs_2_, bf16[768,768]{1,0:T(8,128)(2,1)} %get-tuple-element.149.refs_3_.refs_5_, bf16[768,768]{1,0:T(8,128)(2,1)} %get-tuple-element.150.refs_4_.refs_7_, ...), custom_call_target="tpu_custom_call" | custom-call | flops 10871635968 | bytes 20000000 | tf_op jit(solution)/shard_map/pallas_call | solution.py:395
  264.5 2.6 collective-permute-done.24.refs_3_
  268.3 10.5 %shard_map.226 = bf16[768,1536]{1,0:T(8,128)(2,1)} custom-call(bf16[768,1536]{1,0:T(8,128)(2,1)} %bitcast.106, f32[1,768]{1,0:T(1,128)} %get-tuple-element.302.refs_1_, f32[768,1536]{1,0:T(8,128)} %shard_map.225.refs_2_, bf16[768,768]{1,0:T(8,128)(2,1)} %collective-permute-done.24.refs_3_, bf16[768,768]{1,0:T(8,128)(2,1)} %collective-permute-done.25.refs_4_), custom_call_target="tpu_custom_call" | custom-call | flops 3623878656 | bytes 20000000 | tf_op jit(solution)/shard_map/pallas_call | solution.py:395
  278.9 9.4 %all-to-all-start.4 = ((bf16[32,24,1536]{2,1,0:T(8,128)(2,1)}), bf16[32,24,1536]{2,1,0:T(8,128)(2,1)}, u32[]{:S(2)}, u32[]{:S(2)}) async-start(bf16[32,24,1536]{2,1,0:T(8,128)(2,1)} %bitcast.109), calls=%async_computation.4 | async-start | bytes 4718592 | tf_op jit(solution)/shard_map/all_to_all | solution.py:499
  289.8 29.7 %all-to-all-done.4 = bf16[32,24,1536]{2,1,0:T(8,128)(2,1)} async-done(((bf16[32,24,1536]{2,1,0:T(8,128)(2,1)}), bf16[32,24,1536]{2,1,0:T(8,128)(2,1)}, u32[]{:S(2)}, u32[]{:S(2)}) %all-to-all-start.4) | async-done | bytes 2359328 | tf_op jit(solution)/shard_map/all_to_all | solution.py:499
  319.4 16.7 %shard_map.227 = (f32[208,768]{1,0:T(8,128)}, bf16[4,2,192,768]{3,2,1,0:T(8,128)(2,1)}, bf16[4,2,192,768]{3,2,1,0:T(8,128)(2,1)}, f32[40,768]{1,0:T(8,128)}, bf1...) custom-call(f32[208,768]{1,0:T(8,128)} %pad_convert_fusion.1.refs_12_.refs_0_, bf16[768,1536]{1,0:T(8,128)(2,1)} %bitcast.27.refs_1_, ...), custom_call_target="tpu_custom_call" | custom-call | flops 4000000000 | bytes 20000000 | tf_op jit(solution)/shard_map/pallas_call | solution.py:688
  336.2 1.6 collective-permute-start.34
  337.8 5.1 collective-permute-done.28.refs_2_
  344.2 8.3 %all-to-all-start.5 = ((bf16[32,24,768]{2,1,0:T(8,128)(2,1)}), bf16[32,24,768]{2,1,0:T(8,128)(2,1)S(1)}, u32[]{:S(2)}, u32[]{:S(2)}) async-start(bf16[32,24,768]{2,1,0:T(8,128)(2,1)} %bitcast.118), calls=%async_computation.5 | async-start | bytes 2359296 | tf_op jit(solution)/shard_map/all_to_all | solution.py:499
  352.5 2.4 slice.221
  355.5 2.3 slice.222
  359.6 2.0 slice.225
  361.6 1.9 slice.226
  363.5 7.3 %all-to-all-done.5 = bf16[32,24,768]{2,1,0:T(8,128)(2,1)S(1)} async-done(((bf16[32,24,768]{2,1,0:T(8,128)(2,1)}), bf16[32,24,768]{2,1,0:T(8,128)(2,1)S(1)}, u32[]{:S(2)}, u32[]{:S(2)}) %all-to-all-start.5) | async-done | bytes 1179680 | tf_op jit(solution)/shard_map/all_to_all | solution.py:499
  372.3 15.0 %shard_map.228 = bf16[768,768]{1,0:T(8,128)(2,1)} custom-call(bf16[768,768]{1,0:T(8,128)(2,1)} %bitcast.116, bf16[768,768]{1,0:T(8,128)(2,1)} %get-tuple-element.129.refs_3_.refs_1_.refs_10_, bf16[768,768]{1,0:T(8,128)(2,1)} %copy-done.8, bf16[768,768]{1,0:T(8,128)(2,1)} %collective-permute-done.7.refs_3_, bf16[768,768]{1,0:T(8,128)(2,1)} %collective-permute-done.8.refs_4_, ...), custom_call_target="tpu_custom_call" | custom-call | flops 7247757312 | bytes 20000000 | tf_op jit(solution)/shard_map/pallas_call | solution.py:395
  387.3 8.6 %all-to-all-start.6 = ((bf16[32,24,768]{2,1,0:T(8,128)(2,1)}), bf16[32,24,768]{2,1,0:T(8,128)(2,1)}, u32[]{:S(2)}, u32[]{:S(2)}) async-start(bf16[32,24,768]{2,1,0:T(8,128)(2,1)} %bitcast.120), calls=%async_computation.6 | async-start | bytes 2359296 | tf_op jit(solution)/shard_map/all_to_all | solution.py:499
  397.3 2.9 add_convert_fusion.1
  402.0 2.4 collective-permute-start.37
  404.4 24.9 %shard_map.229 = (f32[2,768,768]{2,1,0:T(8,128)}, f32[2,768,1]{2,1,0:T(8,128)}, f32[2,768,768]{2,1,0:T(8,128)}, f32[2,1,768]{2,1,0:T(1,128)}) custom-call(bf16[768,1536]{1,0:T(8,128)(2,1)} %bitcast.107, bf16[768,1536]{1,0:T(8,128)(2,1)} %collective-permute-done.26.refs_1_, bf16[768,1536]{1,0:T(8,128)(2,1)} %collective-permute-done.27.refs_2_, ...), custom_call_target="tpu_custom_call" | custom-call | flops 14495514624 | bytes 20000000 | tf_op jit(solution)/shard_map/pallas_call | solution.py:452
  433.1 3.2 collective-permute-done.35
  437.7 16.4 %shard_map.230 = (f32[208,768]{1,0:T(8,128)}, bf16[4,2,192,768]{3,2,1,0:T(8,128)(2,1)}, bf16[4,2,192,768]{3,2,1,0:T(8,128)(2,1)}, f32[40,768]{1,0:T(8,128)}) custom-call(f32[208,768]{1,0:T(8,128)} %get-tuple-element.166.refs_0_, bf16[768,768]{1,0:T(8,128)(2,1)} %bitcast.31.refs_1_, f32[208,768]{1,0:T(8,128)} %pad_convert_fusion.refs_8_.refs_2_, ...), custom_call_target="tpu_custom_call" | custom-call | flops 4000000000 | bytes 20000000 | tf_op jit(solution)/shard_map/pallas_call | solution.py:688
  454.1 1.8 fusion.5
  455.9 2.3 collective-permute-done.40.refs_7_
  458.3 3.8 collective-permute-done.41.refs_9_
  465.6 2.9 collective-permute-done.43
  468.7 2.2 add_convert_fusion
  472.4 2.2 collective-permute-start.46
  474.5 24.7 %shard_map.231 = (f32[2,768,768]{2,1,0:T(8,128)}, f32[2,768,1]{2,1,0:T(8,128)}, f32[2,768,768]{2,1,0:T(8,128)}, f32[2,1,768]{2,1,0:T(1,128)}) custom-call(bf16[768,768]{1,0:T(8,128)(2,1)} %bitcast.13.refs_0_, bf16[768,768]{1,0:T(8,128)(2,1)} %bitcast.117, ...), custom_call_target="tpu_custom_call", output_to_operand_aliasing={{0}: (13, {}), {1}: (14, {}), {2}: (15, {}), {3}: (16, {})} | custom-call | flops 14495514624 | bytes 20000000 | tf_op jit(solution)/shard_map/pallas_call | solution.py:452
  499.3 3.5 collective-permute-done.44
  503.7 24.5 %all_to_all.45 = bf16[16,51,768]{2,1,0:T(8,128)(2,1)S(1)} all-to-all(bf16[16,51,768]{2,1,0:T(8,128)(2,1)S(1)} %pad_maximum_fusion.1), channel_id=1, replica_groups={{0,8,16,24,32,40,48,56,64,72,80,88,96,104,112,120},{4,12,20,28,36,44,52..., dimensions={0} | all-to-all | bytes 2506752 | tf_op jit(solution)/shard_map/all_to_all | solution.py:788
  528.4 20.6 %all_to_all.46.mine_ref = bf16[16,51,768]{2,1,0:T(8,128)(2,1)S(1)} all-to-all(bf16[16,51,768]{2,1,0:T(8,128)(2,1)S(1)} %broadcast_in_dim.24), channel_id=1, replica_groups={{0,8,16,24,32,40,48,56,64,72,80,88,96,104,112,120},{4,12,20,28,36,44,52..., dimensions={0} | all-to-all | bytes 2506752 | tf_op jit(solution)/shard_map/all_to_all | solution.py:792
  550.5 4.6 collective-permute-start.47
  555.1 1.7 slice.220
  556.8 1.9 slice.224
  561.1 4.4 shard_map.232
  (241 shorter events, 68.4 us)
Async XLA Ops:
  4.1 19.6 %collective-permute-start = (bf16[2,192,768]{2,1,0:T(8,128)(2,1)}, bf16[2,192,768]{2,1,0:T(8,128)(2,1)}, u32[]{:S(2)}, u32[]{:S(2)}) collective-permute-start(bf16[2,192,768]{2,1,0:T(8,128)(2,1)} %fusion.16), channel_id=1, source_target_pairs={{1,0},{2,1},{3,2},{0,3},{5,4},{6,5},{7,6},{4,7},{9,8},{10,9},{11,1... | collective-permute-start | bytes 1769480 | tf_op jit(solution)/shard_map/ppermute | solution.py:471
  7.4 20.0 %collective-permute-start.2 = (bf16[2,192,768]{2,1,0:T(8,128)(2,1)}, bf16[2,192,768]{2,1,0:T(8,128)(2,1)}, u32[]{:S(2)}, u32[]{:S(2)}) collective-permute-start(bf16[2,192,768]{2,1,0:T(8,128)(2,1)} %fusion.16), channel_id=1, source_target_pairs={{3,0},{0,1},{1,2},{2,3},{7,4},{4,5},{5,6},{6,7},{11,8},{8,9},{9,10... | collective-permute-start | bytes 1769480 | tf_op jit(solution)/shard_map/ppermute | solution.py:471
  8.3 19.1 %all-to-all-start = ((bf16[4,88,192]{2,1,0:T(8,128)(2,1)}), bf16[4,88,192]{2,1,0:T(8,128)(2,1)S(1)}, u32[]{:S(2)}, u32[]{:S(2)}) async-start(bf16[4,88,192]{2,1,0:T(8,128)(2,1)} %broadcast_in_dim.21), calls=%async_computation | async-start | bytes 360448 | tf_op jit(solution)/shard_map/all_to_all | solution.py:548
  20.1 38.6 %copy-start.8 = (bf16[768,768]{1,0:T(8,128)(2,1)}, bf16[768,768]{1,0:T(8,128)(2,1)S(1)}, u32[]{:S(2)}) copy-start(bf16[768,768]{1,0:T(8,128)(2,1)S(1)} %get-tuple-element.130.refs_4_.refs_2_.refs_12_) | copy-start | bytes 3538948
  20.2 94.7 %copy-start.1 = (bf16[4,192,768]{2,1,0:T(8,128)(2,1)}, bf16[4,192,768]{2,1,0:T(8,128)(2,1)S(1)}, u32[]{:S(2)}) copy-start(bf16[4,192,768]{2,1,0:T(8,128)(2,1)S(1)} %pad_maximum_fusion.2.refs_1_) | copy-start | bytes 3538948
  24.7 7.2 %collective-permute-start.1 = (bf16[1,192,768]{2,1,0:T(8,128)(2,1)S(1)}, bf16[1,192,768]{2,1,0:T(8,128)(2,1)S(1)}, u32[]{:S(2)}, u32[]{:S(2)}) collective-permute-start(bf16[1,192,768]{2,1,0:T(8,128)(2,1)S(1)} %slice.241), channel_id=1, source_target_pairs={{1,0},{2,1},{3,2},{0,3},{5,4},{6,5},{7,6},{4,7},{9,8},{10,9},{11,1... | collective-permute-start | bytes 884744 | tf_op jit(solution)/shard_map/ppermute | solution.py:471
  28.5 7.7 %collective-permute-start.3 = (bf16[1,192,768]{2,1,0:T(8,128)(2,1)S(1)}, bf16[1,192,768]{2,1,0:T(8,128)(2,1)S(1)}, u32[]{:S(2)}, u32[]{:S(2)}) collective-permute-start(bf16[1,192,768]{2,1,0:T(8,128)(2,1)S(1)} %slice.242), channel_id=1, source_target_pairs={{3,0},{0,1},{1,2},{2,3},{7,4},{4,5},{5,6},{6,7},{11,8},{8,9},{9,10... | collective-permute-start | bytes 884744 | tf_op jit(solution)/shard_map/ppermute | solution.py:471
  29.2 13.5 %collective-permute-start.4 = (bf16[2,192,768]{2,1,0:T(8,128)(2,1)}, bf16[2,192,768]{2,1,0:T(8,128)(2,1)}, u32[]{:S(2)}, u32[]{:S(2)}) collective-permute-start(bf16[2,192,768]{2,1,0:T(8,128)(2,1)} %collective-permute-done.refs_2_), channel_id=1, source_target_pairs={{4,0},{0,4},{12,8},{8,12},{20,16},{16,20},{28,24},{24,28},{36,32},... | collective-permute-start | bytes 1769480 | tf_op jit(solution)/shard_map/ppermute | solution.py:476
  31.3 11.4 %collective-permute-start.5 = (bf16[2,192,768]{2,1,0:T(8,128)(2,1)}, bf16[2,192,768]{2,1,0:T(8,128)(2,1)}, u32[]{:S(2)}, u32[]{:S(2)}) collective-permute-start(bf16[2,192,768]{2,1,0:T(8,128)(2,1)} %collective-permute-done.2.refs_4_), channel_id=1, source_target_pairs={{4,0},{0,4},{12,8},{8,12},{20,16},{16,20},{28,24},{24,28},{36,32},... | collective-permute-start | bytes 1769480 | tf_op jit(solution)/shard_map/ppermute | solution.py:476
  36.9 5.8 %collective-permute-start.6 = (bf16[2,192,768]{2,1,0:T(8,128)(2,1)}, bf16[2,192,768]{2,1,0:T(8,128)(2,1)}, u32[]{:S(2)}, u32[]{:S(2)}) collective-permute-start(bf16[2,192,768]{2,1,0:T(8,128)(2,1)} %constant_dynamic-update-slice_fusion.refs_3_), channel_id=1, source_target_pairs={{4,0},{0,4},{12,8},{8,12},{20,16},{16,20},{28,24},{24,28},{36,32},... | collective-permute-start | bytes 1769480 | tf_op jit(solution)/shard_map/ppermute | solution.py:476
  50.3 26.7 %all-to-all-start.1 = ((bf16[32,24,768]{2,1,0:T(8,128)(2,1)}), bf16[32,24,768]{2,1,0:T(8,128)(2,1)}, u32[]{:S(2)}, u32[]{:S(2)}) async-start(bf16[32,24,768]{2,1,0:T(8,128)(2,1)} %bitcast.121), calls=%async_computation.1 | async-start | bytes 2359296 | tf_op jit(solution)/shard_map/all_to_all | solution.py:499
  58.6 28.6 %collective-permute-start.10 = (bf16[768,768]{1,0:T(8,128)(2,1)S(1)}, bf16[768,768]{1,0:T(8,128)(2,1)}, u32[]{:S(2)}, u32[]{:S(2)}) collective-permute-start(bf16[768,768]{1,0:T(8,128)(2,1)S(1)} %get-tuple-element.130.refs_4_.refs_2_.refs_12_), channel_id=1, source_target_pairs={{3,0},{0,1},{1,2},{2,3},{7,4},{4,5},{5,6},{6,7},{11,8},{8,9},{9,10... | collective-permute-start | bytes 3538952 | tf_op jit(solution)/shard_map/ppermute | solution.py:471
  58.7 52.8 %collective-permute-start.8 = (bf16[768,768]{1,0:T(8,128)(2,1)S(1)}, bf16[768,768]{1,0:T(8,128)(2,1)}, u32[]{:S(2)}, u32[]{:S(2)}) collective-permute-start(bf16[768,768]{1,0:T(8,128)(2,1)S(1)} %get-tuple-element.130.refs_4_.refs_2_.refs_12_), channel_id=1, source_target_pairs={{1,0},{2,1},{3,2},{0,3},{5,4},{6,5},{7,6},{4,7},{9,8},{10,9},{11,1... | collective-permute-start | bytes 3538952 | tf_op jit(solution)/shard_map/ppermute | solution.py:471
  61.4 50.1 %collective-permute-start.7 = (bf16[768,768]{1,0:T(8,128)(2,1)}, bf16[768,768]{1,0:T(8,128)(2,1)}, u32[]{:S(2)}, u32[]{:S(2)}) collective-permute-start(bf16[768,768]{1,0:T(8,128)(2,1)} %get-tuple-element.129.refs_3_.refs_1_.refs_10_), channel_id=1, source_target_pairs={{1,0},{2,1},{3,2},{0,3},{5,4},{6,5},{7,6},{4,7},{9,8},{10,9},{11,1... | collective-permute-start | bytes 3538952 | tf_op jit(solution)/shard_map/ppermute | solution.py:471
  61.4 51.1 %collective-permute-start.9 = (bf16[768,768]{1,0:T(8,128)(2,1)}, bf16[768,768]{1,0:T(8,128)(2,1)}, u32[]{:S(2)}, u32[]{:S(2)}) collective-permute-start(bf16[768,768]{1,0:T(8,128)(2,1)} %get-tuple-element.129.refs_3_.refs_1_.refs_10_), channel_id=1, source_target_pairs={{3,0},{0,1},{1,2},{2,3},{7,4},{4,5},{5,6},{6,7},{11,8},{8,9},{9,10... | collective-permute-start | bytes 3538952 | tf_op jit(solution)/shard_map/ppermute | solution.py:471
  112.5 45.1 %collective-permute-start.17 = (bf16[768,768]{1,0:T(8,128)(2,1)}, bf16[768,768]{1,0:T(8,128)(2,1)}, u32[]{:S(2)}, u32[]{:S(2)}) collective-permute-start(bf16[768,768]{1,0:T(8,128)(2,1)} %collective-permute-done.7.refs_3_), channel_id=1, source_target_pairs={{1,0},{2,1},{3,2},{0,3},{5,4},{6,5},{7,6},{4,7},{9,8},{10,9},{11,1... | collective-permute-start | bytes 3538952 | tf_op jit(solution)/shard_map/ppermute | solution.py:471
  114.9 44.0 %collective-permute-start.19 = (bf16[768,768]{1,0:T(8,128)(2,1)}, bf16[768,768]{1,0:T(8,128)(2,1)}, u32[]{:S(2)}, u32[]{:S(2)}) collective-permute-start(bf16[768,768]{1,0:T(8,128)(2,1)} %collective-permute-done.10.refs_6_), channel_id=1, source_target_pairs={{3,0},{0,1},{1,2},{2,3},{7,4},{4,5},{5,6},{6,7},{11,8},{8,9},{9,10... | collective-permute-start | bytes 3538952 | tf_op jit(solution)/shard_map/ppermute | solution.py:471
  114.9 36.8 %collective-permute-start.11 = (bf16[2,192,768]{2,1,0:T(8,128)(2,1)S(1)}, bf16[2,192,768]{2,1,0:T(8,128)(2,1)S(1)}, u32[]{:S(2)}, u32[]{:S(2)}) collective-permute-start(bf16[2,192,768]{2,1,0:T(8,128)(2,1)S(1)} %constant_dynamic-slice_fusion.3), channel_id=1, source_target_pairs={{1,0},{2,1},{3,2},{0,3},{5,4},{6,5},{7,6},{4,7},{9,8},{10,9},{11,1... | collective-permute-start | bytes 1769480 | tf_op jit(solution)/shard_map/ppermute | solution.py:471
  117.7 37.0 %collective-permute-start.12 = (bf16[2,192,768]{2,1,0:T(8,128)(2,1)S(1)}, bf16[2,192,768]{2,1,0:T(8,128)(2,1)S(1)}, u32[]{:S(2)}, u32[]{:S(2)}) collective-permute-start(bf16[2,192,768]{2,1,0:T(8,128)(2,1)S(1)} %constant_dynamic-slice_fusion.3), channel_id=1, source_target_pairs={{3,0},{0,1},{1,2},{2,3},{7,4},{4,5},{5,6},{6,7},{11,8},{8,9},{9,10... | collective-permute-start | bytes 1769480 | tf_op jit(solution)/shard_map/ppermute | solution.py:471
  151.7 14.4 %copy-start.6 = (bf16[2,192,768]{2,1,0:T(8,128)(2,1)}, bf16[2,192,768]{2,1,0:T(8,128)(2,1)S(1)}, u32[]{:S(2)}) copy-start(bf16[2,192,768]{2,1,0:T(8,128)(2,1)S(1)} %collective-permute-done.11.refs_2_) | copy-start | bytes 1769476
  154.7 11.4 %copy-start.7 = (bf16[2,192,768]{2,1,0:T(8,128)(2,1)}, bf16[2,192,768]{2,1,0:T(8,128)(2,1)S(1)}, u32[]{:S(2)}) copy-start(bf16[2,192,768]{2,1,0:T(8,128)(2,1)S(1)} %collective-permute-done.12.refs_4_) | copy-start | bytes 1769476
  154.7 21.1 %collective-permute-start.15 = (bf16[2,192,768]{2,1,0:T(8,128)(2,1)S(1)}, bf16[2,192,768]{2,1,0:T(8,128)(2,1)}, u32[]{:S(2)}, u32[]{:S(2)}) collective-permute-start(bf16[2,192,768]{2,1,0:T(8,128)(2,1)S(1)} %collective-permute-done.11.refs_2_), channel_id=1, source_target_pairs={{4,0},{0,4},{12,8},{8,12},{20,16},{16,20},{28,24},{24,28},{36,32},... | collective-permute-start | bytes 1769480 | tf_op jit(solution)/shard_map/ppermute | solution.py:476
  157.3 18.5 %collective-permute-start.16 = (bf16[2,192,768]{2,1,0:T(8,128)(2,1)S(1)}, bf16[2,192,768]{2,1,0:T(8,128)(2,1)}, u32[]{:S(2)}, u32[]{:S(2)}) collective-permute-start(bf16[2,192,768]{2,1,0:T(8,128)(2,1)S(1)} %collective-permute-done.12.refs_4_), channel_id=1, source_target_pairs={{4,0},{0,4},{12,8},{8,12},{20,16},{16,20},{28,24},{24,28},{36,32},... | collective-permute-start | bytes 1769480 | tf_op jit(solution)/shard_map/ppermute | solution.py:476
  157.4 17.2 %collective-permute-start.13 = (bf16[1,192,768]{2,1,0:T(8,128)(2,1)S(1)}, bf16[1,192,768]{2,1,0:T(8,128)(2,1)}, u32[]{:S(2)}, u32[]{:S(2)}) collective-permute-start(bf16[1,192,768]{2,1,0:T(8,128)(2,1)S(1)} %slice.205), channel_id=1, source_target_pairs={{1,0},{2,1},{3,2},{0,3},{5,4},{6,5},{7,6},{4,7},{9,8},{10,9},{11,1... | collective-permute-start | bytes 884744 | tf_op jit(solution)/shard_map/ppermute | solution.py:471
  157.6 17.0 %collective-permute-start.14 = (bf16[1,192,768]{2,1,0:T(8,128)(2,1)S(1)}, bf16[1,192,768]{2,1,0:T(8,128)(2,1)}, u32[]{:S(2)}, u32[]{:S(2)}) collective-permute-start(bf16[1,192,768]{2,1,0:T(8,128)(2,1)S(1)} %slice.206), channel_id=1, source_target_pairs={{3,0},{0,1},{1,2},{2,3},{7,4},{4,5},{5,6},{6,7},{11,8},{8,9},{9,10... | collective-permute-start | bytes 884744 | tf_op jit(solution)/shard_map/ppermute | solution.py:471
  166.1 26.8 %all-to-all-start.2 = ((bf16[32,24,768]{2,1,0:T(8,128)(2,1)}), bf16[32,24,768]{2,1,0:T(8,128)(2,1)S(1)}, u32[]{:S(2)}, u32[]{:S(2)}) async-start(bf16[32,24,768]{2,1,0:T(8,128)(2,1)} %bitcast.119), calls=%async_computation.2 | async-start | bytes 2359296 | tf_op jit(solution)/shard_map/all_to_all | solution.py:499
  175.8 28.4 %collective-permute-start.20 = (bf16[768,768]{1,0:T(8,128)(2,1)}, bf16[768,768]{1,0:T(8,128)(2,1)}, u32[]{:S(2)}, u32[]{:S(2)}) collective-permute-start(bf16[768,768]{1,0:T(8,128)(2,1)} %get-tuple-element.149.refs_3_.refs_5_), channel_id=1, source_target_pairs={{1,0},{2,1},{3,2},{0,3},{5,4},{6,5},{7,6},{4,7},{9,8},{10,9},{11,1... | collective-permute-start | bytes 3538952 | tf_op jit(solution)/shard_map/ppermute | solution.py:471
  177.2 28.5 %collective-permute-start.21 = (bf16[768,768]{1,0:T(8,128)(2,1)}, bf16[768,768]{1,0:T(8,128)(2,1)}, u32[]{:S(2)}, u32[]{:S(2)}) collective-permute-start(bf16[768,768]{1,0:T(8,128)(2,1)} %get-tuple-element.150.refs_4_.refs_7_), channel_id=1, source_target_pairs={{3,0},{0,1},{1,2},{2,3},{7,4},{4,5},{5,6},{6,7},{11,8},{8,9},{9,10... | collective-permute-start | bytes 3538952 | tf_op jit(solution)/shard_map/ppermute | solution.py:471
  177.6 6.2 %collective-permute-start.18 = (bf16[2,192,768]{2,1,0:T(8,128)(2,1)S(1)}, bf16[2,192,768]{2,1,0:T(8,128)(2,1)S(1)}, u32[]{:S(2)}, u32[]{:S(2)}) collective-permute-start(bf16[2,192,768]{2,1,0:T(8,128)(2,1)S(1)} %pad_maximum_fusion.3.refs_3_), channel_id=1, source_target_pairs={{4,0},{0,4},{12,8},{8,12},{20,16},{16,20},{28,24},{24,28},{36,32},... | collective-permute-start | bytes 1769480 | tf_op jit(solution)/shard_map/ppermute | solution.py:476
  183.9 9.1 %copy-start.13 = (bf16[2,192,768]{2,1,0:T(8,128)(2,1)}, bf16[2,192,768]{2,1,0:T(8,128)(2,1)S(1)}, u32[]{:S(2)}) copy-start(bf16[2,192,768]{2,1,0:T(8,128)(2,1)S(1)} %collective-permute-done.18.refs_6_) | copy-start | bytes 1769476
  205.7 8.5 %copy-start.9 = (bf16[768,768]{1,0:T(8,128)(2,1)S(1)}, bf16[768,768]{1,0:T(8,128)(2,1)}, u32[]{:S(2)}) copy-start(bf16[768,768]{1,0:T(8,128)(2,1)} %get-tuple-element.150.refs_4_.refs_7_) | copy-start | bytes 3538948
  205.7 39.7 %all-to-all-start.3 = ((bf16[32,24,1536]{2,1,0:T(8,128)(2,1)}), bf16[32,24,1536]{2,1,0:T(8,128)(2,1)S(1)}, u32[]{:S(2)}, u32[]{:S(2)}) async-start(bf16[32,24,1536]{2,1,0:T(8,128)(2,1)} %bitcast.108), calls=%async_computation.3 | async-start | bytes 4718592 | tf_op jit(solution)/shard_map/all_to_all | solution.py:499
  214.3 31.1 %collective-permute-start.22 = (bf16[768,768]{1,0:T(8,128)(2,1)S(1)}, bf16[768,768]{1,0:T(8,128)(2,1)}, u32[]{:S(2)}, u32[]{:S(2)}) collective-permute-start(bf16[768,768]{1,0:T(8,128)(2,1)S(1)} %copy-done.9), channel_id=1, source_target_pairs={{1,0},{2,1},{3,2},{0,3},{5,4},{6,5},{7,6},{4,7},{9,8},{10,9},{11,1... | collective-permute-start | bytes 3538952 | tf_op jit(solution)/shard_map/ppermute | solution.py:471
  214.3 32.7 %collective-permute-start.23 = (bf16[768,768]{1,0:T(8,128)(2,1)}, bf16[768,768]{1,0:T(8,128)(2,1)}, u32[]{:S(2)}, u32[]{:S(2)}) collective-permute-start(bf16[768,768]{1,0:T(8,128)(2,1)} %get-tuple-element.149.refs_3_.refs_5_), channel_id=1, source_target_pairs={{3,0},{0,1},{1,2},{2,3},{7,4},{4,5},{5,6},{6,7},{11,8},{8,9},{9,10... | collective-permute-start | bytes 3538952 | tf_op jit(solution)/shard_map/ppermute | solution.py:471
  215.8 51.3 %collective-permute-start.24 = (bf16[768,768]{1,0:T(8,128)(2,1)}, bf16[768,768]{1,0:T(8,128)(2,1)}, u32[]{:S(2)}, u32[]{:S(2)}) collective-permute-start(bf16[768,768]{1,0:T(8,128)(2,1)} %collective-permute-done.20.refs_5_), channel_id=1, source_target_pairs={{1,0},{2,1},{3,2},{0,3},{5,4},{6,5},{7,6},{4,7},{9,8},{10,9},{11,1... | collective-permute-start | bytes 3538952 | tf_op jit(solution)/shard_map/ppermute | solution.py:471
  217.1 51.2 %collective-permute-start.25 = (bf16[768,768]{1,0:T(8,128)(2,1)}, bf16[768,768]{1,0:T(8,128)(2,1)}, u32[]{:S(2)}, u32[]{:S(2)}) collective-permute-start(bf16[768,768]{1,0:T(8,128)(2,1)} %collective-permute-done.21.refs_8_), channel_id=1, source_target_pairs={{3,0},{0,1},{1,2},{2,3},{7,4},{4,5},{5,6},{6,7},{11,8},{8,9},{9,10... | collective-permute-start | bytes 3538952 | tf_op jit(solution)/shard_map/ppermute | solution.py:471
  245.4 74.1 %collective-permute-start.26 = (bf16[768,1536]{1,0:T(8,128)(2,1)S(1)}, bf16[768,1536]{1,0:T(8,128)(2,1)}, u32[]{:S(2)}, u32[]{:S(2)}) collective-permute-start(bf16[768,1536]{1,0:T(8,128)(2,1)S(1)} %bitcast.103), channel_id=1, source_target_pairs={{1,0},{2,1},{3,2},{0,3},{5,4},{6,5},{7,6},{4,7},{9,8},{10,9},{11,1... | collective-permute-start | bytes 7077896 | tf_op jit(solution)/shard_map/ppermute | solution.py:471
  245.4 74.0 %collective-permute-start.27 = (bf16[768,1536]{1,0:T(8,128)(2,1)S(1)}, bf16[768,1536]{1,0:T(8,128)(2,1)}, u32[]{:S(2)}, u32[]{:S(2)}) collective-permute-start(bf16[768,1536]{1,0:T(8,128)(2,1)S(1)} %bitcast.104), channel_id=1, source_target_pairs={{3,0},{0,1},{1,2},{2,3},{7,4},{4,5},{5,6},{6,7},{11,8},{8,9},{9,10... | collective-permute-start | bytes 7077896 | tf_op jit(solution)/shard_map/ppermute | solution.py:471
  278.9 40.6 %all-to-all-start.4 = ((bf16[32,24,1536]{2,1,0:T(8,128)(2,1)}), bf16[32,24,1536]{2,1,0:T(8,128)(2,1)}, u32[]{:S(2)}, u32[]{:S(2)}) async-start(bf16[32,24,1536]{2,1,0:T(8,128)(2,1)} %bitcast.109), calls=%async_computation.4 | async-start | bytes 4718592 | tf_op jit(solution)/shard_map/all_to_all | solution.py:499
  288.2 54.6 %collective-permute-start.28 = (bf16[768,768]{1,0:T(8,128)(2,1)}, bf16[768,768]{1,0:T(8,128)(2,1)S(1)}, u32[]{:S(2)}, u32[]{:S(2)}) collective-permute-start(bf16[768,768]{1,0:T(8,128)(2,1)} %bitcast.13.refs_0_), channel_id=1, source_target_pairs={{1,0},{2,1},{3,2},{0,3},{5,4},{6,5},{7,6},{4,7},{9,8},{10,9},{11,1... | collective-permute-start | bytes 3538952 | tf_op jit(solution)/shard_map/ppermute | solution.py:471
  288.3 55.8 %collective-permute-start.29 = (bf16[768,768]{1,0:T(8,128)(2,1)}, bf16[768,768]{1,0:T(8,128)(2,1)}, u32[]{:S(2)}, u32[]{:S(2)}) collective-permute-start(bf16[768,768]{1,0:T(8,128)(2,1)} %bitcast.13.refs_0_), channel_id=1, source_target_pairs={{3,0},{0,1},{1,2},{2,3},{7,4},{4,5},{5,6},{6,7},{11,8},{8,9},{9,10... | collective-permute-start | bytes 3538952 | tf_op jit(solution)/shard_map/ppermute | solution.py:471
  336.2 59.7 %collective-permute-start.34 = (bf16[4,2,192,768]{3,2,1,0:T(8,128)(2,1)}, bf16[4,2,192,768]{3,2,1,0:T(8,128)(2,1)S(1)}, u32[]{:S(2)}, u32[]{:S(2)}) collective-permute-start(bf16[4,2,192,768]{3,2,1,0:T(8,128)(2,1)} %get-tuple-element.201), channel_id=1, source_target_pairs={{4,0},{0,4},{12,8},{8,12},{20,16},{16,20},{28,24},{24,28},{36,32},... | collective-permute-start | bytes 7077896 | tf_op jit(solution)/shard_map/ppermute | solution.py:476
  344.2 26.7 %all-to-all-start.5 = ((bf16[32,24,768]{2,1,0:T(8,128)(2,1)}), bf16[32,24,768]{2,1,0:T(8,128)(2,1)S(1)}, u32[]{:S(2)}, u32[]{:S(2)}) async-start(bf16[32,24,768]{2,1,0:T(8,128)(2,1)} %bitcast.118), calls=%async_computation.5 | async-start | bytes 2359296 | tf_op jit(solution)/shard_map/all_to_all | solution.py:499
  354.8 32.5 %collective-permute-start.30 = (bf16[384,1536]{1,0:T(8,128)(2,1)}, bf16[384,1536]{1,0:T(8,128)(2,1)}, u32[]{:S(2)}, u32[]{:S(2)}) collective-permute-start(bf16[384,1536]{1,0:T(8,128)(2,1)} %slice.221), channel_id=1, source_target_pairs={{1,0},{2,1},{3,2},{0,3},{5,4},{6,5},{7,6},{4,7},{9,8},{10,9},{11,1... | collective-permute-start | bytes 3538952 | tf_op jit(solution)/shard_map/ppermute | solution.py:471
  357.8 29.5 %collective-permute-start.31 = (bf16[384,1536]{1,0:T(8,128)(2,1)}, bf16[384,1536]{1,0:T(8,128)(2,1)}, u32[]{:S(2)}, u32[]{:S(2)}) collective-permute-start(bf16[384,1536]{1,0:T(8,128)(2,1)} %slice.222), channel_id=1, source_target_pairs={{3,0},{0,1},{1,2},{2,3},{7,4},{4,5},{5,6},{6,7},{11,8},{8,9},{9,10... | collective-permute-start | bytes 3538952 | tf_op jit(solution)/shard_map/ppermute | solution.py:471
  370.8 58.5 %collective-permute-start.32 = (bf16[768,768]{1,0:T(8,128)(2,1)S(1)}, bf16[768,768]{1,0:T(8,128)(2,1)}, u32[]{:S(2)}, u32[]{:S(2)}) collective-permute-start(bf16[768,768]{1,0:T(8,128)(2,1)S(1)} %bitcast.114), channel_id=1, source_target_pairs={{1,0},{2,1},{3,2},{0,3},{5,4},{6,5},{7,6},{4,7},{9,8},{10,9},{11,1... | collective-permute-start | bytes 3538952 | tf_op jit(solution)/shard_map/ppermute | solution.py:471
  371.5 58.5 %collective-permute-start.33 = (bf16[768,768]{1,0:T(8,128)(2,1)S(1)}, bf16[768,768]{1,0:T(8,128)(2,1)}, u32[]{:S(2)}, u32[]{:S(2)}) collective-permute-start(bf16[768,768]{1,0:T(8,128)(2,1)S(1)} %bitcast.115), channel_id=1, source_target_pairs={{3,0},{0,1},{1,2},{2,3},{7,4},{4,5},{5,6},{6,7},{11,8},{8,9},{9,10... | collective-permute-start | bytes 3538952 | tf_op jit(solution)/shard_map/ppermute | solution.py:471
  387.3 43.5 %all-to-all-start.6 = ((bf16[32,24,768]{2,1,0:T(8,128)(2,1)}), bf16[32,24,768]{2,1,0:T(8,128)(2,1)}, u32[]{:S(2)}, u32[]{:S(2)}) async-start(bf16[32,24,768]{2,1,0:T(8,128)(2,1)} %bitcast.120), calls=%async_computation.6 | async-start | bytes 2359296 | tf_op jit(solution)/shard_map/all_to_all | solution.py:499
  401.5 34.7 %collective-permute-start.35 = (bf16[384,768]{1,0:T(8,128)(2,1)}, bf16[384,768]{1,0:T(8,128)(2,1)}, u32[]{:S(2)}, u32[]{:S(2)}) collective-permute-start(bf16[384,768]{1,0:T(8,128)(2,1)} %get-tuple-element.280), channel_id=1, source_target_pairs={{3,0},{0,1},{1,2},{2,3},{7,4},{4,5},{5,6},{6,7},{11,8},{8,9},{9,10... | collective-permute-start | bytes 1769480 | tf_op jit(solution)/shard_map/ppermute | solution.py:471
  401.5 34.7 %collective-permute-start.36 = (bf16[384,768]{1,0:T(8,128)(2,1)}, bf16[384,768]{1,0:T(8,128)(2,1)}, u32[]{:S(2)}, u32[]{:S(2)}) collective-permute-start(bf16[384,768]{1,0:T(8,128)(2,1)} %get-tuple-element.282), channel_id=1, source_target_pairs={{2,0},{3,1},{0,2},{1,3},{6,4},{7,5},{4,6},{5,7},{10,8},{11,9},{8,1... | collective-permute-start | bytes 1769480 | tf_op jit(solution)/shard_map/ppermute | solution.py:471
  402.0 52.2 %collective-permute-start.37 = (bf16[384,768]{1,0:T(8,128)(2,1)}, bf16[384,768]{1,0:T(8,128)(2,1)}, u32[]{:S(2)}, u32[]{:S(2)}) collective-permute-start(bf16[384,768]{1,0:T(8,128)(2,1)} %get-tuple-element.281), channel_id=1, source_target_pairs={{1,0},{2,1},{3,2},{0,3},{5,4},{6,5},{7,6},{4,7},{9,8},{10,9},{11,1... | collective-permute-start | bytes 1769480 | tf_op jit(solution)/shard_map/ppermute | solution.py:471
  429.3 26.6 %collective-permute-start.38 = (bf16[384,768]{1,0:T(8,128)(2,1)}, bf16[384,768]{1,0:T(8,128)(2,1)}, u32[]{:S(2)}, u32[]{:S(2)}) collective-permute-start(bf16[384,768]{1,0:T(8,128)(2,1)} %slice.225), channel_id=1, source_target_pairs={{1,0},{2,1},{3,2},{0,3},{5,4},{6,5},{7,6},{4,7},{9,8},{10,9},{11,1... | collective-permute-start | bytes 1769480 | tf_op jit(solution)/shard_map/ppermute | solution.py:471
  430.0 26.0 %collective-permute-start.39 = (bf16[384,768]{1,0:T(8,128)(2,1)}, bf16[384,768]{1,0:T(8,128)(2,1)}, u32[]{:S(2)}, u32[]{:S(2)}) collective-permute-start(bf16[384,768]{1,0:T(8,128)(2,1)} %slice.226), channel_id=1, source_target_pairs={{3,0},{0,1},{1,2},{2,3},{7,4},{4,5},{5,6},{6,7},{11,8},{8,9},{9,10... | collective-permute-start | bytes 1769480 | tf_op jit(solution)/shard_map/ppermute | solution.py:471
  436.3 22.0 %collective-permute-start.40 = (bf16[384,768]{1,0:T(8,128)(2,1)S(1)}, bf16[384,768]{1,0:T(8,128)(2,1)S(1)}, u32[]{:S(2)}, u32[]{:S(2)}) collective-permute-start(bf16[384,768]{1,0:T(8,128)(2,1)S(1)} %slice.227), channel_id=1, source_target_pairs={{1,0},{2,1},{3,2},{0,3},{5,4},{6,5},{7,6},{4,7},{9,8},{10,9},{11,1... | collective-permute-start | bytes 1769480 | tf_op jit(solution)/shard_map/ppermute | solution.py:471
  436.3 25.8 %collective-permute-start.41 = (bf16[384,768]{1,0:T(8,128)(2,1)S(1)}, bf16[384,768]{1,0:T(8,128)(2,1)S(1)}, u32[]{:S(2)}, u32[]{:S(2)}) collective-permute-start(bf16[384,768]{1,0:T(8,128)(2,1)S(1)} %slice.228), channel_id=1, source_target_pairs={{3,0},{0,1},{1,2},{2,3},{7,4},{4,5},{5,6},{6,7},{11,8},{8,9},{9,10... | collective-permute-start | bytes 1769480 | tf_op jit(solution)/shard_map/ppermute | solution.py:471
  454.1 10.3 %copy-start.20 = (f32[40,768]{1,0:T(8,128)S(1)}, f32[40,768]{1,0:T(8,128)}, u32[]{:S(2)}) copy-start(f32[40,768]{1,0:T(8,128)} %get-tuple-element.211) | copy-start | bytes 368644
  454.1 10.3 %copy-start.21 = (f32[40,768]{1,0:T(8,128)S(1)}, f32[40,768]{1,0:T(8,128)}, u32[]{:S(2)}) copy-start(f32[40,768]{1,0:T(8,128)} %get-tuple-element.210) | copy-start | bytes 368644
  462.9 5.8 %collective-permute-start.42 = (bf16[4,2,192,768]{3,2,1,0:T(8,128)(2,1)}, bf16[4,2,192,768]{3,2,1,0:T(8,128)(2,1)S(1)}, u32[]{:S(2)}, u32[]{:S(2)}) collective-permute-start(bf16[4,2,192,768]{3,2,1,0:T(8,128)(2,1)} %get-tuple-element.209), channel_id=1, source_target_pairs={{4,0},{0,4},{12,8},{8,12},{20,16},{16,20},{28,24},{24,28},{36,32},... | collective-permute-start | bytes 7077896 | tf_op jit(solution)/shard_map/ppermute | solution.py:476
  464.5 4.0 collective-permute-start.43
  471.2 31.6 %collective-permute-start.44 = (bf16[432,768]{1,0:T(8,128)(2,1)S(1)}, bf16[432,768]{1,0:T(8,128)(2,1)S(1)}, u32[]{:S(2)}, u32[]{:S(2)}) collective-permute-start(bf16[432,768]{1,0:T(8,128)(2,1)S(1)} %get-tuple-element.277), channel_id=1, source_target_pairs={{3,0},{0,1},{1,2},{2,3},{7,4},{4,5},{5,6},{6,7},{11,8},{8,9},{9,10... | collective-permute-start | bytes 1990664 | tf_op jit(solution)/shard_map/ppermute | solution.py:471
  471.2 31.5 %collective-permute-start.45 = (bf16[432,768]{1,0:T(8,128)(2,1)S(1)}, bf16[432,768]{1,0:T(8,128)(2,1)S(1)}, u32[]{:S(2)}, u32[]{:S(2)}) collective-permute-start(bf16[432,768]{1,0:T(8,128)(2,1)S(1)} %get-tuple-element.278), channel_id=1, source_target_pairs={{2,0},{3,1},{0,2},{1,3},{6,4},{7,5},{4,6},{5,7},{10,8},{11,9},{8,1... | collective-permute-start | bytes 1990664 | tf_op jit(solution)/shard_map/ppermute | solution.py:471
  472.4 30.7 %collective-permute-start.46 = (bf16[432,768]{1,0:T(8,128)(2,1)S(1)}, bf16[432,768]{1,0:T(8,128)(2,1)S(1)}, u32[]{:S(2)}, u32[]{:S(2)}) collective-permute-start(bf16[432,768]{1,0:T(8,128)(2,1)S(1)} %get-tuple-element.279), channel_id=1, source_target_pairs={{1,0},{2,1},{3,2},{0,3},{5,4},{6,5},{7,6},{4,7},{9,8},{10,9},{11,1... | collective-permute-start | bytes 1990664 | tf_op jit(solution)/shard_map/ppermute | solution.py:471
  550.5 8.2 %copy-start.12 = (f32[2,768,1]{2,1,0:T(8,128)S(1)}, f32[2,768,1]{2,1,0:T(8,128)}, u32[]{:S(2)}) copy-start(f32[2,768,1]{2,1,0:T(8,128)} %get-tuple-element.236) | copy-start | bytes 18436
  550.5 9.1 %collective-permute-start.47 = (bf16[16,51,768]{2,0,1:T(8,128)(2,1)}, bf16[16,51,768]{2,0,1:T(8,128)(2,1)S(1)}, u32[]{:S(2)}, u32[]{:S(2)}) collective-permute-start(bf16[16,51,768]{2,0,1:T(8,128)(2,1)} %copy.70), channel_id=1, source_target_pairs={{4,0},{0,4},{12,8},{8,12},{20,16},{16,20},{28,24},{24,28},{36,32},... | collective-permute-start | bytes 3760136 | tf_op jit(solution)/shard_map/ppermute | solution.py:476
  (22 other events, 83.6 us)
